TPU v7x, 32 devices: a whole 2x2x4 slice. The times are simulated.
32 devices in a mesh: gx: 4 (over z), gy: 8 (over y, x, core).
Axes of the slice: x: 2, y: 2, z: 4, core: 2. Of those that a mesh axis runs over, the one named last changes fastest.
Arguments:
- cotangent: float32 [6, 128, 128, 128], P(None, 'gx', 'gy'), may hold values from -3000 to 3000
- diffusion: float32 [128, 128, 128], P('gx', 'gy'), may hold values from 50 to 2000
- phase: int32 [128, 128, 128], P('gx', 'gy'), may hold values 0 or 1
- courant: float32 [3, 128, 128, 128], P(None, 'gx', 'gy'), may hold values from 0.02 to 0.3
- upwind: int32 [3, 128, 128, 128], P(None, 'gx', 'gy'), may hold values 0 or 1
Outputs:
- grad: float32 [6, 128, 128, 128], P(None, 'gx', 'gy')
All inputs are finite; a program needn't handle non-finite values. No bound on the sum of `phase` or of `upwind` on one device may be relied on, other than what follows from the above.
Results may differ from a plain program's by a relative error of at most 0.00019.
Values sent between devices are 32-bit elements; how exact they have to be, the bound alone decides.
No kernel may reach another device: no remote copies, remote signals or barrier semaphores. Data moves between devices by JAX's collectives and lax.ppermute only.
A program may use at most 128 MiB of HBM per device.

v0:
```python
import functools

import jax
import jax.numpy as jnp
from jax import lax
from jax.experimental import pallas as pl
from jax.experimental.pallas import tpu as pltpu
from jax.sharding import PartitionSpec as P

COMPS = 6
LANES = 128
TILE = 8
VMEM_BYTES = 24 * 1024 * 1024


def round_up(count, step):
    return (count + step - 1) // step * step


def weight_of(diffusion, phase):
    return 1.0 / (diffusion * (1.0 + 3.0 * phase.astype(jnp.float32)))


def growing_step(value, slope, weight):
    slope = slope + weight * value
    return value + slope, slope


def split3(cells):
    high = cells.astype(jnp.bfloat16)
    rest = cells - high.astype(jnp.float32)
    middle = rest.astype(jnp.bfloat16)
    low = (rest - middle.astype(jnp.float32)).astype(jnp.bfloat16)
    return high, middle, low


def sum_matrix():
    row = lax.broadcasted_iota(jnp.int32, (2 * LANES, 2 * LANES), 0)
    col = lax.broadcasted_iota(jnp.int32, (2 * LANES, 2 * LANES), 1)
    before = (row < LANES) & (col < LANES) & (row <= col)
    after = (row >= LANES) & (col >= LANES) & (row > col)
    return jnp.where(before | after, 1.0, 0.0).astype(jnp.bfloat16)


def z_kernel(
    dims, cot_any, diffusion, phase, az_any, send, w_out, inv_out,
    cot, az, wt, pht, pst, phi, psi, left, right, in_sems, out_sems,
):
    nx, ny, py, width = dims
    rows = nx * ny
    tiles = rows // LANES
    owned = nx // py
    for c in range(COMPS):
        pltpu.make_async_copy(cot_any.at[c], cot.at[c], in_sems.at[c]).start()

    w_out[...] = weight_of(diffusion[...], phase[...])
    for t in range(tiles):
        span = pl.ds(t * LANES, LANES)
        wt[span, :] = w_out[span, :].T
    ones = jnp.ones((tiles, LANES), jnp.float32)
    value, slope = ones, ones
    back, fall = ones, ones
    for k in range(LANES):
        here = pl.ds(k, tiles, stride=LANES)
        pht[here, :] = value
        value, slope = growing_step(value, slope, wt[here, :])
        there = pl.ds(LANES - 1 - k, tiles, stride=LANES)
        pst[there, :] = back
        back, fall = growing_step(back, fall, wt[there, :])
    scale = 1.0 / value
    for t in range(tiles):
        span = pl.ds(t * LANES, LANES)
        phi[span, :] = pht[span, :].T
        psi[span, :] = (pst[span, :] * scale[t : t + 1]).T

    one = jnp.ones((nx, LANES), jnp.float32)
    value, slope, chain = one, one, []
    weights = [w_out[pl.ds(y, nx, stride=ny), :] for y in range(ny)]
    for y in range(ny):
        chain.append(value)
        value, slope = growing_step(value, slope, weights[y])
    total = 1.0 / value
    chain.append(value)
    back, fall = one, one
    for y in reversed(range(ny)):
        span = pl.ds(y * nx, nx)
        left[span, :] = back * total
        right[span, :] = chain[y] * total
        inv_out[span, :] = chain[y] / chain[y + 1]
        back, fall = growing_step(back, fall, weights[y])

    def post(index, cells):
        for r in range(owned):
            send[pl.ds(index * owned + r, py, stride=width), :] = cells[r * py : (r + 1) * py]

    post(2 * COMPS, left[pl.ds(0, nx), :])
    post(2 * COMPS + 1, right[pl.ds(0, nx), :])
    post(2 * COMPS + 2, right[pl.ds((ny - 1) * nx, nx), :])

    sums = sum_matrix()
    for c in range(COMPS):
        pltpu.make_async_copy(cot_any.at[c], cot.at[c], in_sems.at[c]).wait()
        for t in range(tiles):
            span = pl.ds(t * LANES, LANES)
            cells, up, down = cot[c, span, :], phi[span, :], psi[span, :]
            wide = jnp.concatenate([up * cells, down * cells], axis=1)
            found = sum(
                jnp.dot(part, sums, preferred_element_type=jnp.float32) for part in split3(wide)
            )
            az[c, span, :] = w_out[span, :] * (down * found[:, :LANES] + up * found[:, LANES:])
        pltpu.make_async_copy(az.at[c], az_any.at[c], out_sems.at[c]).start()
        first = jnp.zeros((nx, LANES), jnp.float32)
        last = jnp.zeros((nx, LANES), jnp.float32)
        for y in range(ny):
            cells = az[c, pl.ds(y, nx, stride=ny), :]
            span = pl.ds(y * nx, nx)
            first = first + left[span, :] * cells
            last = last + right[span, :] * cells
        post(c, first)
        post(COMPS + c, last)
    for c in range(COMPS):
        pltpu.make_async_copy(az.at[c], az_any.at[c], out_sems.at[c]).wait()


def owner_kernel(dims, got, send):
    owned, py, width, out_width = dims
    group = COMPS * owned

    def spread(row, p):
        piece = got[pl.ds(p * width + row, owned), :]
        return jnp.concatenate([piece] * COMPS, axis=0)

    zero = jnp.zeros((group, LANES), jnp.float32)
    tail, tail_edge = zero, zero
    chains = []
    for p in range(py):
        yfirst = got[pl.ds(p * width, group), :]
        ylast = got[pl.ds(p * width + group, group), :]
        corner = spread(2 * group, p)
        cross = spread(2 * group + owned, p)
        far = spread(2 * group + 2 * owned, p)
        pivot = 1.0 / (1.0 - corner * tail_edge)
        lead = (yfirst + corner * tail) * pivot
        lead_edge = cross * pivot
        linked = cross * tail_edge
        tail, tail_edge = ylast + cross * tail + linked * lead, far + linked * lead_edge
        chains.append((lead, lead_edge, tail, tail_edge))
    later = zero
    for p in reversed(range(py)):
        lead, lead_edge, tail, tail_edge = chains[p]
        send[pl.ds(p * out_width + group, group), :] = later
        if p + 1 < py:
            send[pl.ds((p + 1) * out_width, group), :] = tail + tail_edge * later
        later = lead + lead_edge * later
    send[pl.ds(0, group), :] = zero


def sides(before, after, x):
    return jnp.concatenate(
        [
            jnp.broadcast_to(before[pl.ds(x, 1), :], (TILE, LANES)),
            jnp.broadcast_to(after[pl.ds(x, 1), :], (TILE, LANES)),
        ],
        axis=0,
    )


def state_kernel(dims, me_ref, w, before, after, xend, send):
    nx, ny, px, width = dims
    me = me_ref[0]
    rows = ny + 2 * TILE
    one = jnp.ones((rows, LANES), jnp.float32)
    zero = jnp.zeros((rows, LANES), jnp.float32)
    states = [(one, zero), (zero, one)]
    for x in range(nx):
        weight = jnp.concatenate([w[pl.ds(x * ny, ny), :], sides(before, after, x)], axis=0)
        states = [growing_step(value, slope, weight) for value, slope in states]
    entries = [states[0][0], states[1][0], states[0][1], states[1][1]]
    for p in range(px):
        base = p * width
        for e, entry in enumerate(entries):
            send[pl.ds(base + e * ny, ny), :] = entry[:ny]
            send[pl.ds(base + 4 * ny + 2 * e, 1), :] = entry[ny : ny + 1]
            send[pl.ds(base + 4 * ny + 2 * e + 1, 1), :] = entry[ny + TILE : ny + TILE + 1]
        send[pl.ds(base + 4 * ny + TILE, ny), :] = jnp.where(
            jnp.full((ny, LANES), p, jnp.int32) < me, xend[pl.ds(0, ny), :], xend[pl.ds(ny, ny), :]
        )


def y_kernel(
    dims, me_ref, az, got, w, inv, before, after, states,
    ay, ghost, send, total_out, xinv, misc, back_all,
):
    nx, ny, py, px, out_width, state_width, x_width = dims
    me = me_ref[0]
    owned = nx // py
    rows = ny + 2 * TILE
    gbase = COMPS * ny

    ghost[...] = jnp.zeros(ghost.shape, jnp.float32)
    for c in range(COMPS):
        for r in range(owned):
            part = pl.ds(r * py, py)
            fb = got[pl.ds(c * owned + r, py, stride=out_width), :]
            fa = got[pl.ds((COMPS + c) * owned + r, py, stride=out_width), :]
            ghost[pl.ds(r * py * 2 * TILE + c, py, stride=2 * TILE), :] = before[part, :] * fb
            ghost[pl.ds(r * py * 2 * TILE + TILE + c, py, stride=2 * TILE), :] = after[part, :] * fa
            swept = fb
            chain = []
            for y in range(ny):
                cells = az[c, pl.ds(r * py * ny + y, py, stride=ny), :]
                swept = (cells + swept) * inv[pl.ds(y * nx + r * py, py), :]
                chain.append(swept)
            later = fa
            for y in reversed(range(ny)):
                where = pl.ds(r * py * ny + y, py, stride=ny)
                later = chain[y] + inv[pl.ds(y * nx + r * py, py), :] * later
                ay[c, where, :] = later * w[where, :]

    def entry(p, e):
        base = p * state_width
        row = base + 4 * ny + 2 * e
        return jnp.concatenate(
            [
                states[pl.ds(base + e * ny, ny), :],
                jnp.broadcast_to(states[pl.ds(row, 1), :], (TILE, LANES)),
                jnp.broadcast_to(states[pl.ds(row + 1, 1), :], (TILE, LANES)),
            ],
            axis=0,
        )

    maps = [[entry(p, e) for e in range(4)] for p in range(px)]
    one = jnp.ones((rows, LANES), jnp.float32)
    value, slope = one, one
    start_value, start_slope = one, one
    for p in range(px):
        a, b, c, d = maps[p]
        keep = jnp.full((rows, LANES), p, jnp.int32) == me
        start_value = jnp.where(keep, value, start_value)
        start_slope = jnp.where(keep, slope, start_slope)
        value, slope = a * value + b * slope, c * value + d * slope
    scale = 1.0 / value
    back, fall = scale, scale
    for p in reversed(range(px)):
        a, b, c, d = maps[p]
        past = jnp.full((rows, LANES), p, jnp.int32) > me
        new_back = (c + d) * back + (a + b - c - d) * fall
        new_fall = c * back + (a - c) * fall
        back = jnp.where(past, new_back, back)
        fall = jnp.where(past, new_fall, fall)

    inverse = 1.0 / start_value
    misc[pl.ds(0, rows), :] = inverse
    misc[pl.ds(rows, rows), :] = (start_value - start_slope) * inverse
    misc[pl.ds(2 * rows, rows), :] = back - fall

    def weight_at(x):
        return jnp.concatenate([w[pl.ds(x * ny, ny), :], sides(before, after, x)], axis=0)

    for x in reversed(range(nx)):
        back_all[pl.ds(x * rows, rows), :] = back
        back, fall = growing_step(back, fall, weight_at(x))
    value, slope = start_value, start_slope
    zero = jnp.zeros((ny, LANES), jnp.float32)
    ups = [zero] * COMPS
    downs = [zero] * COMPS
    gup = jnp.zeros((2 * TILE, LANES), jnp.float32)
    gdown = gup
    for x in range(nx):
        down = back_all[pl.ds(x * rows, rows), :]
        for c in range(COMPS):
            cells = ay[c, pl.ds(x * ny, ny), :]
            ups[c] = ups[c] + value[:ny] * cells
            downs[c] = downs[c] + down[:ny] * cells
        cells = ghost[pl.ds(x * 2 * TILE, 2 * TILE), :]
        gup = gup + value[ny:] * cells
        gdown = gdown + down[ny:] * cells
        new_value, slope = growing_step(value, slope, weight_at(x))
        xinv[pl.ds(x * rows, rows), :] = value / new_value
        value = new_value
    misc[pl.ds(3 * rows, rows), :] = value
    for c in range(COMPS):
        total_out[pl.ds(c * ny, ny), :] = ups[c]
    total_out[pl.ds(gbase, 2 * TILE), :] = gup
    for p in range(px):
        base = p * x_width
        later = jnp.full((ny, LANES), p, jnp.int32) > me
        for c in range(COMPS):
            send[pl.ds(base + c * ny, ny), :] = jnp.where(later, ups[c], downs[c])
        later = jnp.full((2 * TILE, LANES), p, jnp.int32) > me
        send[pl.ds(base + gbase, 2 * TILE), :] = jnp.where(later, gup, gdown)


def x_kernel(
    dims, me_ref, got, total, misc, xinv, ay, ghost, w, before, after, states, courant, upwind,
    out, swept_all, gswept, sums,
):
    nx, ny, px, state_width, x_width = dims
    me = me_ref[0]
    rows = ny + 2 * TILE
    gbase = COMPS * ny

    pre = jnp.zeros((x_width, LANES), jnp.float32)
    suf = pre
    for p in range(px):
        chunk = got[pl.ds(p * x_width, x_width), :]
        index = jnp.full((x_width, LANES), p, jnp.int32)
        pre = pre + jnp.where(index < me, chunk, 0.0)
        suf = suf + jnp.where(index > me, chunk, 0.0)
    sums[pl.ds(0, x_width), :] = pre
    sums[pl.ds(x_width, x_width), :] = suf

    inverse = misc[pl.ds(0, ny), :]
    reach = misc[pl.ds(rows, ny), :]
    psi_next = misc[pl.ds(2 * rows, ny), :]
    phi_next = misc[pl.ds(3 * rows, ny), :]
    g_inverse = misc[pl.ds(ny, 2 * TILE), :]
    g_psi_next = misc[pl.ds(2 * rows + ny, 2 * TILE), :]
    g_phi_next = misc[pl.ds(3 * rows + ny, 2 * TILE), :]

    starts = [sums[pl.ds(c * ny, ny), :] * inverse for c in range(COMPS)]
    gstart = sums[pl.ds(gbase, 2 * TILE), :] * g_inverse
    nexts = [
        psi_next * (sums[pl.ds(c * ny, ny), :] + total[pl.ds(c * ny, ny), :])
        + phi_next * sums[pl.ds(x_width + c * ny, ny), :]
        for c in range(COMPS)
    ]
    gnext = g_psi_next * (
        sums[pl.ds(gbase, 2 * TILE), :] + total[pl.ds(gbase, 2 * TILE), :]
    ) + g_phi_next * sums[pl.ds(x_width + gbase, 2 * TILE), :]

    def sweep(x, carry):
        cells, gcells = carry
        factor = xinv[pl.ds(x * rows, rows), :]
        span = pl.ds(x * ny, ny)
        new = []
        for c in range(COMPS):
            value = (ay[c, span, :] + cells[c]) * factor[:ny]
            swept_all[c, span, :] = value
            new.append(value)
        gspan = pl.ds(x * 2 * TILE, 2 * TILE)
        gvalue = (ghost[gspan, :] + gcells) * factor[ny:]
        gswept[gspan, :] = gvalue
        return tuple(new), gvalue

    lax.fori_loop(0, nx, sweep, (tuple(starts), gstart), unroll=4)

    lane = lax.broadcasted_iota(jnp.int32, (ny, LANES), 1)
    line = lax.broadcasted_iota(jnp.int32, (ny, LANES), 0)
    has_left = jnp.where(me > 0, 1.0, 0.0)
    has_right = jnp.where(me < px - 1, 1.0, 0.0)
    left_row = jnp.maximum(me - 1, 0) * state_width + 4 * ny + TILE
    right_row = jnp.minimum(me + 1, px - 1) * state_width + 4 * ny + TILE
    near = states[pl.ds(pl.multiple_of(left_row, TILE), ny), :] * has_left
    far = states[pl.ds(pl.multiple_of(right_row, TILE), ny), :] * has_right

    def finish(step, carry):
        cells, fluxes, gcells = carry
        x = nx - 1 - step
        span = pl.ds(x * ny, ny)
        factor = xinv[pl.ds(x * rows, rows), :]
        weight = w[span, :]
        ahead, behind = [], []
        own = jnp.ones((ny, LANES), jnp.float32)
        for d in range(3):
            flow = courant[d, span, :]
            up = flow * upwind[d, span, :].astype(jnp.float32)
            down = flow - up
            own = own + (down - up)
            ahead.append(up)
            behind.append(down)
        ahead_y = jnp.where(line == 0, 0.0, ahead[1])
        behind_y = jnp.where(line == ny - 1, 0.0, behind[1])
        ahead_z = jnp.where(lane == 0, 0.0, ahead[2])
        behind_z = jnp.where(lane == LANES - 1, 0.0, behind[2])
        gspan = pl.ds(x * 2 * TILE, 2 * TILE)
        gvalue = gswept[gspan, :] + factor[ny:] * gcells
        gflux = gvalue * sides_of(before, after, x)
        new_cells, new_fluxes = [], []
        for c in range(COMPS):
            solved = swept_all[c, span, :] + factor[:ny] * cells[c]
            grad = weight * solved
            part = own * grad + fluxes[c]
            part = part + pltpu.roll(ahead_y * grad, ny - 1, 0) - pltpu.roll(behind_y * grad, 1, 0)
            part = part + pltpu.roll(ahead_z * grad, LANES - 1, 1) - pltpu.roll(behind_z * grad, 1, 1)
            part = part - jnp.where(line == 0, gflux[c : c + 1], 0.0)
            part = part + jnp.where(line == ny - 1, gflux[TILE + c : TILE + c + 1], 0.0)
            out[c, span, :] = part
            upper = pl.ds((x + 1) * ny, ny)
            out[c, upper, :] = out[c, upper, :] - behind[0] * grad
            new_cells.append(solved)
            new_fluxes.append(ahead[0] * grad)
        return tuple(new_cells), tuple(new_fluxes), gvalue

    def sides_of(lower, upper, x):
        return jnp.concatenate(
            [
                jnp.broadcast_to(lower[pl.ds(nx + x, 1), :], (TILE, LANES)),
                jnp.broadcast_to(upper[pl.ds(nx + x, 1), :], (TILE, LANES)),
            ],
            axis=0,
        )

    fluxes = tuple(far * nexts[c] for c in range(COMPS))
    solved, _, _ = lax.fori_loop(0, nx, finish, (tuple(nexts), fluxes, gnext))
    top = pl.ds(0, ny)
    for c in range(COMPS):
        entering = starts[c] + reach * solved[c]
        out[c, top, :] = out[c, top, :] - near * entering


def call(kernel, name, operands, outs, scratch=(), spaces=None, out_spaces=None, ops=0):
    params = pltpu.CompilerParams(vmem_limit_bytes=VMEM_BYTES)
    vmem = pl.BlockSpec(memory_space=pltpu.VMEM)
    anywhere = pl.BlockSpec(memory_space=pl.ANY)
    smem = pl.BlockSpec(memory_space=pltpu.SMEM)
    pick = {"v": vmem, "a": anywhere, "s": smem}
    spaces = spaces or "v" * len(operands)
    out_spaces = out_spaces or "v" * len(outs)
    moved = sum(4 * math_prod(shape) for shape in outs) + sum(4 * o.size for o in operands)
    return pl.pallas_call(
        kernel,
        name=name,
        out_shape=[jax.ShapeDtypeStruct(shape, jnp.float32) for shape in outs],
        in_specs=[pick[s] for s in spaces],
        out_specs=[pick[s] for s in out_spaces],
        scratch_shapes=list(scratch),
        compiler_params=params,
        cost_estimate=pl.CostEstimate(flops=ops, bytes_accessed=moved, transcendentals=0),
    )(*operands)


def math_prod(shape):
    size = 1
    for extent in shape:
        size *= extent
    return size


def on_device(cotangent, diffusion, phase, courant, upwind):
    comps, nx, ny, nz = cotangent.shape
    px, py = lax.axis_size("gx"), lax.axis_size("gy")
    rows = nx * ny
    owned = nx // py
    group = comps * owned
    width = round_up(2 * group + 3 * owned, TILE)
    out_width = round_up(2 * group, TILE)
    state_width = 5 * ny + TILE
    x_width = comps * ny + 2 * TILE
    wide = ny + 2 * TILE
    me = lax.axis_index("gx").astype(jnp.int32).reshape(1)
    f32 = jnp.float32
    vmem = lambda *shape: pltpu.VMEM(shape, f32)

    flat_w = (diffusion.reshape(rows, nz), phase.reshape(rows, nz))
    cot = cotangent.reshape(comps, rows, nz)
    cour = courant.reshape(3, rows, nz)
    upw = upwind.reshape(3, rows, nz)

    def y_edge(y, toward):
        weight = weight_of(diffusion[:, y], phase[:, y])
        up = courant[1, :, y] * upwind[1, :, y].astype(f32)
        flow = up if toward else courant[1, :, y] - up
        return jnp.concatenate([weight, weight * flow], axis=0)

    after = lax.ppermute(y_edge(0, True), "gy", [(i + 1, i) for i in range(py - 1)])
    before = lax.ppermute(y_edge(ny - 1, False), "gy", [(i, i + 1) for i in range(py - 1)])

    def x_edge(x, toward):
        weight = weight_of(diffusion[x], phase[x])
        up = courant[0, x] * upwind[0, x].astype(f32)
        return weight * (up if toward else courant[0, x] - up)

    xend = jnp.concatenate([x_edge(0, True), x_edge(nx - 1, False)], axis=0)

    az, posted, w, inv = call(
        functools.partial(z_kernel, (nx, ny, py, width)),
        "z_solve",
        (cot,) + flat_w,
        [(comps, rows, nz), (py * width, nz), (rows, nz), (rows, nz)],
        [
            vmem(comps, rows, nz), vmem(comps, rows, nz), vmem(rows, nz), vmem(rows, nz),
            vmem(rows, nz), vmem(rows, nz), vmem(rows, nz), vmem(rows, nz), vmem(rows, nz),
            pltpu.SemaphoreType.DMA((comps,)), pltpu.SemaphoreType.DMA((comps,)),
        ],
        spaces="avv",
        out_spaces="avvv",
    )
    got = lax.all_to_all(posted, "gy", 0, 0, tiled=True)
    (states_send,) = call(
        functools.partial(state_kernel, (nx, ny, px, state_width)),
        "x_states",
        (me, w, before, after, xend),
        [(px * state_width, nz)],
        spaces="svvvv",
    )
    states = lax.all_to_all(states_send, "gx", 0, 0, tiled=True)
    (answers,) = call(
        functools.partial(owner_kernel, (owned, py, width, out_width)),
        "y_reduced",
        (got,),
        [(py * out_width, nz)],
    )
    edges = lax.all_to_all(answers, "gy", 0, 0, tiled=True)
    ay, ghost, x_send, total, xinv, misc = call(
        functools.partial(y_kernel, (nx, ny, py, px, out_width, state_width, x_width)),
        "y_solve",
        (me, az, edges, w, inv, before, after, states),
        [
            (comps, rows, nz), (nx * 2 * TILE, nz), (px * x_width, nz), (x_width, nz),
            (nx * wide, nz), (4 * wide, nz),
        ],
        [vmem(nx * wide, nz)],
        spaces="svvvvvvv",
    )
    x_got = lax.all_to_all(x_send, "gx", 0, 0, tiled=True)
    (grad,) = call(
        functools.partial(x_kernel, (nx, ny, px, state_width, x_width)),
        "x_solve",
        (me, x_got, total, misc, xinv, ay, ghost, w, before, after, states, cour, upw),
        [(comps, rows + ny, nz)],
        [vmem(comps, rows, nz), vmem(nx * 2 * TILE, nz), vmem(2 * x_width, nz)],
        spaces="s" + "v" * 12,
    )
    return grad[:, :rows].reshape(comps, nx, ny, nz)


def solution(mesh):
    placed = (
        P(None, "gx", "gy", None),
        P("gx", "gy", None),
        P("gx", "gy", None),
        P(None, "gx", "gy", None),
        P(None, "gx", "gy", None),
    )
    return jax.shard_map(
        on_device, mesh=mesh, in_specs=placed, out_specs=P(None, "gx", "gy", None), check_vma=False
    )
```

profile of v0, /device:TPU:0, one launch (start us, length us, event | category | flops | bytes accessed | tf_op | source)
XLA Modules:
  0.0 69.3 jit_solution(17938444115221530207)
XLA Ops:
  0.0 1.0 %fusion.5 = (f32[32,1,128]{2,1,0:T(1,128)S(1)}, f32[32,1,128]{2,1,0:T(1,128)S(1)}) fusion(f32[32,16,128]{2,1,0:T(8,128)} %param.6), kind=kLoop, calls=%fused_computation.14 | loop fusion | bytes 65536 | tf_op jit(solution)/shard_map/slice | solution.py:461
  1.0 1.0 %fusion.4 = (s32[32,1,128]{2,1,0:T(1,128)S(1)}, s32[32,1,128]{2,1,0:T(1,128)S(1)}) fusion(s32[32,16,128]{2,1,0:T(8,128)} %param.7), kind=kLoop, calls=%fused_computation.13 | loop fusion | bytes 65536 | tf_op jit(solution)/shard_map/slice | solution.py:461
  2.0 1.0 %fusion.3 = (f32[1,32,1,128]{3,2,1,0:T(1,128)S(1)}, f32[1,32,1,128]{3,2,1,0:T(1,128)S(1)}) fusion(f32[3,32,16,128]{3,2,1,0:T(8,128)} %param.8), kind=kLoop, calls=%fused_computation.12 | loop fusion | bytes 65536 | tf_op jit(solution)/shard_map/slice | solution.py:462
  3.0 1.0 %fusion.2 = (s32[1,32,1,128]{3,2,1,0:T(1,128)S(1)}, s32[1,32,1,128]{3,2,1,0:T(1,128)S(1)}) fusion(s32[3,32,16,128]{3,2,1,0:T(8,128)} %param.9), kind=kLoop, calls=%fused_computation.11 | loop fusion | bytes 65536 | tf_op jit(solution)/shard_map/slice | solution.py:462
  4.0 2.4 %collective-permute-start = (f32[64,128]{1,0:T(8,128)S(1)}, f32[64,128]{1,0:T(8,128)S(1)}, u32[]{:S(2)}, u32[]{:S(2)}) collective-permute-start(f32[64,128]{1,0:T(8,128)S(1)} %pad_maximum_fusion), channel_id=1, source_target_pairs={{0,1},{1,2},{2,3},{3,4},{4,5},{5,6},{6,7},{8,9},{9,10},{10,11},{11... | collective-permute-start | bytes 98312 | tf_op jit(solution)/shard_map/ppermute | solution.py:467
  6.4 1.3 %collective-permute-start.1 = (f32[64,128]{1,0:T(8,128)S(1)}, f32[64,128]{1,0:T(8,128)S(1)}, u32[]{:S(2)}, u32[]{:S(2)}) collective-permute-start(f32[64,128]{1,0:T(8,128)S(1)} %pad_maximum_fusion.1), channel_id=1, source_target_pairs={{1,0},{2,1},{3,2},{4,3},{5,4},{6,5},{7,6},{9,8},{10,9},{11,10},{12... | collective-permute-start | bytes 98312 | tf_op jit(solution)/shard_map/ppermute | solution.py:466
  7.7 1.4 %copy-done = f32[6,32,16,128]{3,2,1,0:T(8,128)S(1)} copy-done((f32[6,32,16,128]{3,2,1,0:T(8,128)S(1)}, f32[6,32,16,128]{3,2,1,0:T(8,128)}, u32[]{:S(2)}) %copy-start) | copy-done | bytes 1572888
  9.1 0.9 %copy-done.3 = f32[32,16,128]{2,1,0:T(8,128)S(1)} copy-done((f32[32,16,128]{2,1,0:T(8,128)S(1)}, f32[32,16,128]{2,1,0:T(8,128)}, u32[]{:S(2)}) %copy-start.3) | copy-done | bytes 262168
  10.1 0.9 %copy-done.4 = s32[32,16,128]{2,1,0:T(8,128)S(1)} copy-done((s32[32,16,128]{2,1,0:T(8,128)S(1)}, s32[32,16,128]{2,1,0:T(8,128)}, u32[]{:S(2)}) %copy-start.4) | copy-done | bytes 262168
  11.0 5.1 %z_solve.1 = (f32[6,512,128]{2,1,0:T(8,128)S(1)}, f32[512,128]{1,0:T(8,128)}, f32[512,128]{1,0:T(8,128)S(1)}, f32[512,128]{1,0:T(8,128)S(1)}) custom-call(f32[6,512,128]{2,1,0:T(8,128)S(1)} %bitcast.47, f32[512,128]{1,0:T(8,128)S(1)} %bitcast.54, s32[512,128]{1,0:T(8,128)S(1)} %bitcast.55), custom_call_target="tpu_custom_call" | custom-call | bytes 4456448 | tf_op jit(solution)/shard_map/z_solve/pallas_call | solution.py:421
  16.2 0.7 copy-done.5
  16.9 7.1 %all-to-all-start = ((f32[8,64,128]{2,1,0:T(8,128)}), f32[8,64,128]{2,1,0:T(8,128)S(1)}, u32[]{:S(2)}, u32[]{:S(2)}) async-start(f32[8,64,128]{2,1,0:T(8,128)} %bitcast.4), calls=%async_computation | async-start | bytes 524288 | tf_op jit(solution)/shard_map/all_to_all | solution.py:489
  24.0 0.8 %bitcast_multiply_fusion.1 = (f32[16,128]{1,0:T(8,128)S(1)}, f32[16,128]{1,0:T(8,128)S(1)}) fusion(s32[3,32,16,128]{3,2,1,0:T(8,128)} %param.9, f32[3,32,16,128]{3,2,1,0:T(8,128)S(1)} %copy-done.1, s32[32,16,128]{2,1,0:T(8,128)} %param.7, f32[32,16,128]{2,1,0:T(8,128)} %param.6), kind=kLoop, calls=%fused_computation.10 | loop fusion | flops 34816 | bytes 81920 | tf_op jit(solution)/shard_map/mul | solution.py:472
  24.8 0.8 %x_states.1 = f32[352,128]{1,0:T(8,128)} custom-call(s32[1]{0:T(128)} %bitcast.me_ref, f32[512,128]{1,0:T(8,128)S(1)} %get-tuple-element.17.w, f32[64,128]{1,0:T(8,128)S(1)} %collective-permute-done.before, f32[64,128]{1,0:T(8,128)S(1)} %collective-permute-done.1.after, f32[32,128]{1,0:T(8,128)S(1)} %pad_maximum_fusion.2.xend), custom_call_target="tpu_custom_call" | custom-call | bytes 524292 | tf_op jit(solution)/shard_map/x_states/pallas_call | solution.py:421
  25.6 5.3 %all-to-all-done = f32[8,64,128]{2,1,0:T(8,128)S(1)} async-done(((f32[8,64,128]{2,1,0:T(8,128)}), f32[8,64,128]{2,1,0:T(8,128)S(1)}, u32[]{:S(2)}, u32[]{:S(2)}) %all-to-all-start) | async-done | bytes 262176 | tf_op jit(solution)/shard_map/all_to_all | solution.py:489
  30.9 4.9 %all-to-all-start.2 = ((f32[4,88,128]{2,1,0:T(8,128)}), f32[4,88,128]{2,1,0:T(8,128)S(1)}, u32[]{:S(2)}, u32[]{:S(2)}) async-start(f32[4,88,128]{2,1,0:T(8,128)} %bitcast.18), calls=%async_computation.2 | async-start | bytes 360448 | tf_op jit(solution)/shard_map/all_to_all | solution.py:497
  35.8 0.1 y_reduced.1
  35.9 6.3 %all-to-all-done.2 = f32[4,88,128]{2,1,0:T(8,128)S(1)} async-done(((f32[4,88,128]{2,1,0:T(8,128)}), f32[4,88,128]{2,1,0:T(8,128)S(1)}, u32[]{:S(2)}, u32[]{:S(2)}) %all-to-all-start.2) | async-done | bytes 180256 | tf_op jit(solution)/shard_map/all_to_all | solution.py:497
  42.2 8.7 %all_to_all.44 = f32[8,48,128]{2,1,0:T(8,128)S(1)} all-to-all(f32[8,48,128]{2,1,0:T(8,128)S(1)} %bitcast.52), channel_id=1, replica_groups=mesh['gx'=4,'gy'=8] {'gy'}, dimensions={0} | all-to-all | bytes 393216 | tf_op jit(solution)/shard_map/all_to_all | solution.py:504
  50.8 1.0 %copy-done.6 = f32[512,128]{1,0:T(8,128)S(1)} copy-done((f32[512,128]{1,0:T(8,128)S(1)}, f32[512,128]{1,0:T(8,128)}, u32[]{:S(2)}) %copy-start.6) | copy-done | bytes 262168
  51.9 1.9 %y_solve.1 = (f32[6,512,128]{2,1,0:T(8,128)S(1)}, f32[512,128]{1,0:T(8,128)S(1)}, f32[448,128]{1,0:T(8,128)S(1)}, f32[112,128]{1,0:T(8,128)S(1)}, f32[1024,128]{1,0:T(8,128)S(1)}, /*index=5*/f32[128,128]{1,0:T(8,128)S(1)}) custom-call(s32[1]{0:T(128)} %bitcast.me_ref, f32[6,512,128]{2,1,0:T(8,128)S(1)} %get-tuple-element.15.az, f32[384,128]{1,0:T(8,128)S(1)} %bitcast.53, ...), custom_call_target="tpu_custom_call" | custom-call | bytes 5251076 | tf_op jit(solution)/shard_map/y_solve/pallas_call | solution.py:421
  53.7 10.5 %all_to_all.45 = f32[4,112,128]{2,1,0:T(8,128)S(1)} all-to-all(f32[4,112,128]{2,1,0:T(8,128)S(1)} %bitcast.56), channel_id=1, replica_groups=mesh['gx'=4,'gy'=8] {'gx'}, dimensions={0} | all-to-all | bytes 458752 | tf_op jit(solution)/shard_map/all_to_all | solution.py:516
  64.3 3.7 %x_solve.1 = f32[6,528,128]{2,1,0:T(8,128)S(1)} custom-call(s32[1]{0:T(128)} %bitcast.me_ref, f32[448,128]{1,0:T(8,128)S(1)} %bitcast.49, f32[112,128]{1,0:T(8,128)S(1)} %get-tuple-element.20.total, f32[128,128]{1,0:T(8,128)S(1)} %get-tuple-element.21.misc, f32[1024,128]{1,0:T(8,128)S(1)} %get-tuple-element.22.xinv, ...), custom_call_target="tpu_custom_call" | custom-call | bytes 6414340 | tf_op jit(solution)/shard_map/x_solve/pallas_call | solution.py:421
  68.0 1.2 %slice.70 = f32[6,512,128]{2,1,0:T(8,128)} slice(f32[6,528,128]{2,1,0:T(8,128)S(1)} %x_solve.1), slice={[0:6], [0:512], [0:128]} | slice | bytes 3145728 | tf_op jit(solution)/shard_map/slice | solution.py:525
  (16 shorter events, 0.1 us)
Async XLA Ops:
  4.0 20.7 %collective-permute-start = (f32[64,128]{1,0:T(8,128)S(1)}, f32[64,128]{1,0:T(8,128)S(1)}, u32[]{:S(2)}, u32[]{:S(2)}) collective-permute-start(f32[64,128]{1,0:T(8,128)S(1)} %pad_maximum_fusion), channel_id=1, source_target_pairs={{0,1},{1,2},{2,3},{3,4},{4,5},{5,6},{6,7},{8,9},{9,10},{10,11},{11... | collective-permute-start | bytes 98312 | tf_op jit(solution)/shard_map/ppermute | solution.py:467
  6.4 18.4 %collective-permute-start.1 = (f32[64,128]{1,0:T(8,128)S(1)}, f32[64,128]{1,0:T(8,128)S(1)}, u32[]{:S(2)}, u32[]{:S(2)}) collective-permute-start(f32[64,128]{1,0:T(8,128)S(1)} %pad_maximum_fusion.1), channel_id=1, source_target_pairs={{1,0},{2,1},{3,2},{4,3},{5,4},{6,5},{7,6},{9,8},{10,9},{11,10},{12... | collective-permute-start | bytes 98312 | tf_op jit(solution)/shard_map/ppermute | solution.py:466
  7.7 1.4 %copy-start = (f32[6,32,16,128]{3,2,1,0:T(8,128)S(1)}, f32[6,32,16,128]{3,2,1,0:T(8,128)}, u32[]{:S(2)}) copy-start(f32[6,32,16,128]{3,2,1,0:T(8,128)} %param.5) | copy-start | bytes 4718596
  9.1 0.9 %copy-start.3 = (f32[32,16,128]{2,1,0:T(8,128)S(1)}, f32[32,16,128]{2,1,0:T(8,128)}, u32[]{:S(2)}) copy-start(f32[32,16,128]{2,1,0:T(8,128)} %param.6) | copy-start | bytes 786436
  10.1 0.9 %copy-start.4 = (s32[32,16,128]{2,1,0:T(8,128)S(1)}, s32[32,16,128]{2,1,0:T(8,128)}, u32[]{:S(2)}) copy-start(s32[32,16,128]{2,1,0:T(8,128)} %param.7) | copy-start | bytes 786436
  11.0 12.9 %copy-start.1 = (f32[3,32,16,128]{3,2,1,0:T(8,128)S(1)}, f32[3,32,16,128]{3,2,1,0:T(8,128)}, u32[]{:S(2)}) copy-start(f32[3,32,16,128]{3,2,1,0:T(8,128)} %param.8) | copy-start | bytes 2359300
  16.2 0.7 %copy-start.5 = (f32[512,128]{1,0:T(8,128)}, f32[512,128]{1,0:T(8,128)S(1)}, u32[]{:S(2)}) copy-start(f32[512,128]{1,0:T(8,128)S(1)} %get-tuple-element.18.inv) | copy-start | bytes 786436
  16.9 14.0 %all-to-all-start = ((f32[8,64,128]{2,1,0:T(8,128)}), f32[8,64,128]{2,1,0:T(8,128)S(1)}, u32[]{:S(2)}, u32[]{:S(2)}) async-start(f32[8,64,128]{2,1,0:T(8,128)} %bitcast.4), calls=%async_computation | async-start | bytes 524288 | tf_op jit(solution)/shard_map/all_to_all | solution.py:489
  30.9 11.3 %all-to-all-start.2 = ((f32[4,88,128]{2,1,0:T(8,128)}), f32[4,88,128]{2,1,0:T(8,128)S(1)}, u32[]{:S(2)}, u32[]{:S(2)}) async-start(f32[4,88,128]{2,1,0:T(8,128)} %bitcast.18), calls=%async_computation.2 | async-start | bytes 360448 | tf_op jit(solution)/shard_map/all_to_all | solution.py:497
  50.8 13.5 %copy-start.2 = (s32[3,32,16,128]{3,2,1,0:T(8,128)S(1)}, s32[3,32,16,128]{3,2,1,0:T(8,128)}, u32[]{:S(2)}) copy-start(s32[3,32,16,128]{3,2,1,0:T(8,128)} %param.9) | copy-start | bytes 2359300
  50.8 1.0 %copy-start.6 = (f32[512,128]{1,0:T(8,128)S(1)}, f32[512,128]{1,0:T(8,128)}, u32[]{:S(2)}) copy-start(f32[512,128]{1,0:T(8,128)} %copy-done.5) | copy-start | bytes 786436
where the time goes:
time: 69.9 us; the launch traced here: 69.3 us
  blocking collectives  19.2 us (27%)
  starting transfers between devices  15.6 us (22%)
  Pallas kernels  11.6 us (17%)
  waiting for transfers between devices  11.6 us (17%)
  local copies, waits for them, and re-layouts  10.2 us (15%)
  other arithmetic  0.84 us (1%)
    pallas_call x5, Pallas kernels, call(): pl.pallas_call(kernel, name=name, out_shape=[jax.ShapeDtypeStruct(shape,...  11.6 us
    all_to_all x1, blocking collectives, on_device(): x_got = lax.all_to_all(x_send, 'gx', 0, 0, tiled=True)  10.5 us
    all_to_all x1, blocking collectives, on_device(): edges = lax.all_to_all(answers, 'gy', 0, 0, tiled=True)  8.67 us
    all_to_all x1, starting transfers between devices, on_device(): got = lax.all_to_all(posted, 'gy', 0, 0, tiled=True)  7.06 us
    all_to_all x1, waiting for transfers between devices, on_device(): states = lax.all_to_all(states_send, 'gx', 0, 0, tiled=True)  6.29 us
    all_to_all x1, waiting for transfers between devices, on_device(): got = lax.all_to_all(posted, 'gy', 0, 0, tiled=True)  5.3 us
    unnamed x14, local copies, waits for them, and re-layouts  5.02 us
    all_to_all x1, starting transfers between devices, on_device(): states = lax.all_to_all(states_send, 'gx', 0, 0, tiled=True)  4.88 us
  transfers between devices with their start and end apart: 4, of which 2 were waited for; matrix products, arithmetic and copies ran while one was open for 1% of the time, Pallas kernels for 9%

commit v1 on v0

v1 whole, which is shorter than its diff:
```python
import functools

import jax
import jax.numpy as jnp
from jax import lax
from jax.experimental import pallas as pl
from jax.experimental.pallas import tpu as pltpu
from jax.sharding import PartitionSpec as P

COMPS = 6
LANES = 128
TILE = 8
VMEM_BYTES = 24 * 1024 * 1024


def weight_of(diffusion, phase):
    return 1.0 / (diffusion * (1.0 + 3.0 * phase.astype(jnp.float32)))


def growing_step(value, slope, weight):
    slope = slope + weight * value
    return value + slope, slope


def split3(cells):
    high = cells.astype(jnp.bfloat16)
    rest = cells - high.astype(jnp.float32)
    middle = rest.astype(jnp.bfloat16)
    low = (rest - middle.astype(jnp.float32)).astype(jnp.bfloat16)
    return high, middle, low


def sum_matrix():
    row = lax.broadcasted_iota(jnp.int32, (2 * LANES, 2 * LANES), 0)
    col = lax.broadcasted_iota(jnp.int32, (2 * LANES, 2 * LANES), 1)
    before = (row < LANES) & (col < LANES) & (row <= col)
    after = (row >= LANES) & (col >= LANES) & (row > col)
    return jnp.where(before | after, 1.0, 0.0).astype(jnp.bfloat16)


class Layout:
    def __init__(self, pieces, groups, edges, lines):
        self.pieces, self.groups, self.edges, self.lines = pieces, groups, edges, lines
        self.couple = pieces * lines * 2
        self.packed = self.couple + 3 * lines
        self.edge = self.packed + (TILE if groups > 1 else 0)
        self.rows = self.edge + 2 * edges * lines
        self.side_couple = pieces * lines
        self.side_packed = self.side_couple + lines
        self.side_edge = self.side_packed + (TILE if groups > 1 else 0)
        self.side_rows = self.side_edge + edges * lines
        self.answer_rows = 2 * (pieces + edges) * lines

    def group(self, piece):
        return 0 if piece < COMPS else 1


def read_rows(ref, base, count, lines):
    return [ref[pl.ds(base + i * lines, lines), :] for i in range(count)]


def write_rows(ref, base, values, lines):
    for i, value in enumerate(values):
        ref[pl.ds(base + i * lines, lines), :] = value


def read_pair(ref, row):
    return jnp.concatenate(
        [jnp.broadcast_to(ref[pl.ds(row + i, 1), :], (TILE, LANES)) for i in range(2)], axis=0
    )


def write_pair(ref, row, value):
    ref[pl.ds(row, 1), :] = value[:1]
    ref[pl.ds(row + 1, 1), :] = value[TILE : TILE + 1]


def read_block(lay, ref, base=0):
    n, m = lay.lines, lay.pieces
    couple = []
    for e in range(3):
        entry = [ref[pl.ds(base + lay.couple + e * n, n), :]]
        if lay.groups > 1:
            entry.append(read_pair(ref, base + lay.packed + 2 * e))
        couple.append(entry)
    return {
        "first": read_rows(ref, base, m, n),
        "last": read_rows(ref, base + m * n, m, n),
        "near": couple[0],
        "cross": couple[1],
        "far": couple[2],
        "head": read_rows(ref, base + lay.edge, lay.edges, n),
        "tail": read_rows(ref, base + lay.edge + lay.edges * n, lay.edges, n),
    }


def write_block(lay, ref, block, base=0):
    n, m = lay.lines, lay.pieces
    write_rows(ref, base, block["first"], n)
    write_rows(ref, base + m * n, block["last"], n)
    for e, name in enumerate(("near", "cross", "far")):
        ref[pl.ds(base + lay.couple + e * n, n), :] = block[name][0]
        if lay.groups > 1:
            write_pair(ref, base + lay.packed + 2 * e, block[name][1])
    write_rows(ref, base + lay.edge, block["head"], n)
    write_rows(ref, base + lay.edge + lay.edges * n, block["tail"], n)


def write_side(lay, ref, block, upper):
    n = lay.lines

    def facing(low, high):
        return jnp.where(jnp.full(low.shape, upper, jnp.int32) == 1, high, low)

    write_rows(ref, 0, [facing(a, b) for a, b in zip(block["last"], block["first"])], n)
    pair = [facing(a, b) for a, b in zip(block["far"], block["near"])]
    ref[pl.ds(lay.side_couple, n), :] = pair[0]
    if lay.groups > 1:
        write_pair(ref, lay.side_packed, pair[1])
    write_rows(ref, lay.side_edge, [facing(a, b) for a, b in zip(block["tail"], block["head"])], n)


def read_side(lay, ref):
    n = lay.lines
    couple = [ref[pl.ds(lay.side_couple, n), :]]
    if lay.groups > 1:
        couple.append(read_pair(ref, lay.side_packed))
    return (
        read_rows(ref, 0, lay.pieces, n),
        couple,
        read_rows(ref, lay.side_edge, lay.edges, n),
    )


def pick(upper, low, high):
    if isinstance(low, list):
        return [pick(upper, a, b) for a, b in zip(low, high)]
    return jnp.where(jnp.full(low.shape, upper, jnp.int32) == 1, high, low)


def ordered(upper, own, other):
    low = {name: pick(upper, own[name], other[name]) for name in own}
    high = {name: pick(upper, other[name], own[name]) for name in own}
    return low, high


def joint(lay, low, high):
    return [
        1.0 / (1.0 - low["far"][g] * high["near"][g]) for g in range(lay.groups)
    ]


def merge(lay, low, high):
    shrink = joint(lay, low, high)
    to_low = [low["cross"][g] * shrink[g] for g in range(lay.groups)]
    to_high = [high["cross"][g] * shrink[g] for g in range(lay.groups)]
    span = range(lay.pieces)
    of = lay.group
    return {
        "first": [
            low["first"][i]
            + to_low[of(i)] * (high["first"][i] + high["near"][of(i)] * low["last"][i])
            for i in span
        ],
        "last": [
            high["last"][i]
            + to_high[of(i)] * (low["last"][i] + low["far"][of(i)] * high["first"][i])
            for i in span
        ],
        "near": [
            low["near"][g] + to_low[g] * low["cross"][g] * high["near"][g]
            for g in range(lay.groups)
        ],
        "cross": [to_low[g] * high["cross"][g] for g in range(lay.groups)],
        "far": [
            high["far"][g] + to_high[g] * high["cross"][g] * low["far"][g]
            for g in range(lay.groups)
        ],
        "head": low["head"],
        "tail": high["tail"],
    }


def inner(lay, low, high, before, after):
    shrink = joint(lay, low, high)
    low_last, high_first = [], []
    for i in range(lay.pieces):
        g = lay.group(i)
        left = low["last"][i] + low["cross"][g] * before[i]
        right = high["first"][i] + high["cross"][g] * after[i]
        low_last.append((left + low["far"][g] * right) * shrink[g])
        high_first.append((right + high["near"][g] * left) * shrink[g])
    return low_last, high_first


def merge_kernel(lay, bit, top, me_ref, own, other, out, *side):
    upper = (me_ref[0] >> bit) & 1
    low, high = ordered(upper, read_block(lay, own), read_block(lay, other))
    block = merge(lay, low, high)
    write_block(lay, out, block)
    if top:
        write_side(lay, side[0], block, (me_ref[0] >> (bit + 1)) & 1)


def descend(lay, me, levels, own_refs, got_refs):
    top = levels - 1
    upper = (me >> top) & 1
    own = read_block(lay, own_refs[top])
    met, met_couple, met_edge = read_side(lay, got_refs[top])
    facing = pick(upper, own["last"], own["first"])
    couple = pick(upper, own["far"], own["near"])
    found = []
    for i in range(lay.pieces):
        g = lay.group(i)
        found.append((met[i] + met_couple[g] * facing[i]) / (1.0 - met_couple[g] * couple[g]))
    zeros = [jnp.zeros_like(v) for v in found]
    edge_zeros = [jnp.zeros_like(v) for v in met_edge]
    before, after = pick(upper, zeros, found), pick(upper, found, zeros)
    behind, ahead = pick(upper, edge_zeros, met_edge), pick(upper, met_edge, edge_zeros)
    return before, after, behind, ahead


def narrow(lay, upper, low, high, before, after, behind, ahead):
    low_last, high_first = inner(lay, low, high, before, after)
    return (
        pick(upper, before, low_last),
        pick(upper, high_first, after),
        pick(upper, behind, low["tail"]),
        pick(upper, high["head"], ahead),
    )


def write_answer(lay, ref, before, after, behind, ahead):
    write_rows(ref, 0, before + after + behind + ahead, lay.lines)


def solve_kernel(lay, levels, split, me_ref, *refs):
    me = me_ref[0]
    own_refs, got_refs = refs[:levels], refs[levels : 2 * levels]
    outs = refs[2 * levels :]
    state = descend(lay, me, levels, own_refs, got_refs)
    for level in reversed(range(levels - 1)):
        upper = (me >> level) & 1
        low, high = ordered(
            upper, read_block(lay, own_refs[level]), read_block(lay, got_refs[level])
        )
        if level == 0 and split:
            write_answer(lay, outs[1], *narrow(lay, 1 - upper, low, high, *state))
        state = narrow(lay, upper, low, high, *state)
    write_answer(lay, outs[0], *state)


def corners(weights):
    one = jnp.ones_like(weights[0])
    value, slope, chain = one, one, [one]
    for weight in weights:
        value, slope = growing_step(value, slope, weight)
        chain.append(value)
    total = 1.0 / value
    back, fall, backs = one, one, []
    for weight in reversed(weights):
        backs.append(back)
        back, fall = growing_step(back, fall, weight)
    backs.reverse()
    return chain, backs, total


def z_kernel(
    dims, lay, me_ref, cot_any, diff_any, phase_any, cour_any, upw_any, az, w_out, inv_out, keep, send,
    cot, diff, phase, cour, upw, wt, pht, pst, phi, psi, left, right, both, in_sems, sems,
):
    nx, ny = dims
    rows = nx * ny
    tiles = rows // LANES
    half = nx // 2
    small = [(diff_any, diff), (phase_any, phase), (cour_any.at[1], cour), (upw_any.at[1], upw)]
    for i, (source, target) in enumerate(small):
        pltpu.make_async_copy(source, target, sems.at[i]).start()
    for c in range(COMPS):
        pltpu.make_async_copy(cot_any.at[c], cot.at[c], in_sems.at[c]).start()

    for i, (source, target) in enumerate(small[:2]):
        pltpu.make_async_copy(source, target, sems.at[i]).wait()
    w_out[...] = weight_of(diff[...], phase[...])
    for t in range(tiles):
        span = pl.ds(t * LANES, LANES)
        wt[span, :] = w_out[span, :].T
    ones = jnp.ones((tiles, LANES), jnp.float32)
    value, slope = ones, ones
    back, fall = ones, ones
    for k in range(LANES):
        here = pl.ds(k, tiles, stride=LANES)
        pht[here, :] = value
        value, slope = growing_step(value, slope, wt[here, :])
        there = pl.ds(LANES - 1 - k, tiles, stride=LANES)
        pst[there, :] = back
        back, fall = growing_step(back, fall, wt[there, :])
    scale = 1.0 / value
    for t in range(tiles):
        span = pl.ds(t * LANES, LANES)
        phi[span, :] = pht[span, :].T
        psi[span, :] = (pst[span, :] * scale[t : t + 1]).T

    chain, backs, total = corners([w_out[pl.ds(y, nx, stride=ny), :] for y in range(ny)])
    for y in range(ny):
        span = pl.ds(y * nx, nx)
        left[span, :] = backs[y] * total
        right[span, :] = chain[y] * total
        inv_out[span, :] = chain[y] / chain[y + 1]

    def post(row, cells):
        for h in range(2):
            both[pl.ds(h * lay.rows + row, half), :] = cells[h * half : (h + 1) * half]

    post(lay.couple, left[pl.ds(0, nx), :])
    post(lay.couple + half, total)
    post(lay.couple + 2 * half, right[pl.ds((ny - 1) * nx, nx), :])
    for i, (source, target) in enumerate(small[2:]):
        pltpu.make_async_copy(source, target, sems.at[2 + i]).wait()
    for e, y in enumerate((0, ny - 1)):
        edge = pl.ds(y, nx, stride=ny)
        weight = w_out[edge, :]
        up = cour[edge, :] * upw[edge, :].astype(jnp.float32)
        flow = up if e == 0 else cour[edge, :] - up
        post(lay.edge + 2 * e * half, weight)
        post(lay.edge + (2 * e + 1) * half, weight * flow)

    sums = sum_matrix()
    for c in range(COMPS):
        pltpu.make_async_copy(cot_any.at[c], cot.at[c], in_sems.at[c]).wait()
        for t in range(tiles):
            span = pl.ds(t * LANES, LANES)
            cells, up, down = cot[c, span, :], phi[span, :], psi[span, :]
            wide = jnp.concatenate([up * cells, down * cells], axis=1)
            found = sum(
                jnp.dot(part, sums, preferred_element_type=jnp.float32) for part in split3(wide)
            )
            az[c, span, :] = w_out[span, :] * (down * found[:, :LANES] + up * found[:, LANES:])
        first = jnp.zeros((nx, LANES), jnp.float32)
        last = jnp.zeros((nx, LANES), jnp.float32)
        for y in range(ny):
            cells = az[c, pl.ds(y, nx, stride=ny), :]
            span = pl.ds(y * nx, nx)
            first = first + left[span, :] * cells
            last = last + right[span, :] * cells
        post(c * half, first)
        post((COMPS + c) * half, last)
    mine = me_ref[0] & 1
    keep[...] = both[pl.ds(pl.multiple_of(mine * lay.rows, TILE), lay.rows), :]
    send[...] = both[pl.ds(pl.multiple_of((1 - mine) * lay.rows, TILE), lay.rows), :]


def sides(before, after, x):
    return jnp.concatenate(
        [
            jnp.broadcast_to(before[pl.ds(x, 1), :], (TILE, LANES)),
            jnp.broadcast_to(after[pl.ds(x, 1), :], (TILE, LANES)),
        ],
        axis=0,
    )


def y_kernel(
    dims, ylay, xlay, me_ref, az, own, got, w, inv, cour, upw,
    ay, ghost, block, xinv, before, after, joined, left_all,
):
    nx, ny = dims
    half = nx // 2
    rows = ny + 2 * TILE
    mine = me_ref[0] & 1
    span = ylay.answer_rows
    joined[pl.ds(pl.multiple_of(mine * span, TILE), span), :] = own[...]
    joined[pl.ds(pl.multiple_of((1 - mine) * span, TILE), span), :] = got[...]
    for h in range(2):
        for e in range(2):
            where = pl.ds(e * nx + h * half, half)
            row = h * span + 2 * COMPS * half + e * half
            before[where, :] = joined[pl.ds(row, half), :]
            after[where, :] = joined[pl.ds(row + 2 * half, half), :]

    ghost[...] = jnp.zeros(ghost.shape, jnp.float32)
    for c in range(COMPS):
        for h in range(2):
            part = pl.ds(h * half, half)
            fb = joined[pl.ds(h * span + c * half, half), :]
            fa = joined[pl.ds(h * span + (COMPS + c) * half, half), :]
            deep = 2 * TILE
            ghost[pl.ds(h * half * deep + c, half, stride=deep), :] = before[part, :] * fb
            ghost[pl.ds(h * half * deep + TILE + c, half, stride=deep), :] = after[part, :] * fa
            swept, chain = fb, []
            for y in range(ny):
                cells = az[c, pl.ds(h * half * ny + y, half, stride=ny), :]
                swept = (cells + swept) * inv[pl.ds(y * nx + h * half, half), :]
                chain.append(swept)
            later = fa
            for y in reversed(range(ny)):
                where = pl.ds(h * half * ny + y, half, stride=ny)
                later = chain[y] + inv[pl.ds(y * nx + h * half, half), :] * later
                ay[c, where, :] = later * w[where, :]

    def weight_at(x):
        return jnp.concatenate([w[pl.ds(x * ny, ny), :], sides(before, after, x)], axis=0)

    one = jnp.ones((rows, LANES), jnp.float32)
    back, fall = one, one
    for x in reversed(range(nx)):
        left_all[pl.ds(x * rows, rows), :] = back
        back, fall = growing_step(back, fall, weight_at(x))
    total = 1.0 / back
    value, slope = one, one
    zero = jnp.zeros((ny, LANES), jnp.float32)
    pieces = xlay.pieces
    firsts, lasts = [zero] * pieces, [zero] * pieces
    corner = left_all[pl.ds(0, rows), :]
    for x in range(nx):
        down = left_all[pl.ds(x * rows, rows), :]
        for i in range(pieces):
            part = slice(0, ny) if i < COMPS else slice(ny, rows)
            cells = ay[i, pl.ds(x * ny, ny), :] if i < COMPS else ghost[pl.ds(x * 2 * TILE, 2 * TILE), :]
            lasts[i] = lasts[i] + value[part] * cells
            firsts[i] = firsts[i] + down[part] * cells
        new_value, slope = growing_step(value, slope, weight_at(x))
        xinv[pl.ds(x * rows, rows), :] = value / new_value
        end, value = value, new_value

    def halves(cells):
        return [cells[:ny], cells[ny:]]

    scale = halves(total)
    edges = []
    for e, x in enumerate((0, nx - 1)):
        where = pl.ds(x * ny, ny)
        up = cour[0, where, :] * upw[0, where, :].astype(jnp.float32)
        edges.append(w[where, :] * (up if e == 0 else cour[0, where, :] - up))
    write_block(
        xlay,
        block,
        {
            "first": [v * scale[xlay.group(i)] for i, v in enumerate(firsts)],
            "last": [v * scale[xlay.group(i)] for i, v in enumerate(lasts)],
            "near": halves(corner * total),
            "cross": scale,
            "far": halves(end * total),
            "head": edges[:1],
            "tail": edges[1:],
        },
    )
    if xlay.edge > xlay.packed + 6:
        block[pl.ds(xlay.packed + 6, 2), :] = jnp.zeros((2, LANES), jnp.float32)


def x_kernel(
    dims, lay, levels, me_ref, *refs
):
    nx, ny = dims
    own_refs, got_refs = refs[:levels], refs[levels : 2 * levels]
    (xinv, ay, ghost, w, lower, upper_edge, courant, upwind,
     out_any, out, swept_all, gswept, answer, sems) = refs[2 * levels :]
    rows = ny + 2 * TILE
    solve_kernel(lay, levels, False, me_ref, *own_refs, *got_refs, answer)
    n = lay.pieces
    starts = read_rows(answer, 0, n, ny)
    nexts = read_rows(answer, n * ny, n, ny)
    near = answer[pl.ds(2 * n * ny, ny), :]
    far = answer[pl.ds((2 * n + 1) * ny, ny), :]

    def sweep(x, carry):
        factor = xinv[pl.ds(x * rows, rows), :]
        span = pl.ds(x * ny, ny)
        new = []
        for c in range(COMPS):
            value = (ay[c, span, :] + carry[c]) * factor[:ny]
            swept_all[c, span, :] = value
            new.append(value)
        gspan = pl.ds(x * 2 * TILE, 2 * TILE)
        gvalue = (ghost[gspan, :] + carry[COMPS]) * factor[ny:]
        gswept[gspan, :] = gvalue
        return tuple(new) + (gvalue,)

    lax.fori_loop(0, nx, sweep, tuple(starts), unroll=4)

    lane = lax.broadcasted_iota(jnp.int32, (ny, LANES), 1)
    line = lax.broadcasted_iota(jnp.int32, (ny, LANES), 0)

    def finish(step, carry):
        cells, fluxes, gcells = carry
        x = nx - 1 - step
        span = pl.ds(x * ny, ny)
        factor = xinv[pl.ds(x * rows, rows), :]
        weight = w[span, :]
        ahead, behind = [], []
        own = jnp.ones((ny, LANES), jnp.float32)
        for d in range(3):
            flow = courant[d, span, :]
            up = flow * upwind[d, span, :].astype(jnp.float32)
            down = flow - up
            own = own + (down - up)
            ahead.append(up)
            behind.append(down)
        ahead_y = jnp.where(line == 0, 0.0, ahead[1])
        behind_y = jnp.where(line == ny - 1, 0.0, behind[1])
        ahead_z = jnp.where(lane == 0, 0.0, ahead[2])
        behind_z = jnp.where(lane == LANES - 1, 0.0, behind[2])
        gspan = pl.ds(x * 2 * TILE, 2 * TILE)
        gvalue = gswept[gspan, :] + factor[ny:] * gcells
        gflux = gvalue * jnp.concatenate(
            [
                jnp.broadcast_to(lower[pl.ds(nx + x, 1), :], (TILE, LANES)),
                jnp.broadcast_to(upper_edge[pl.ds(nx + x, 1), :], (TILE, LANES)),
            ],
            axis=0,
        )
        new_cells, new_fluxes = [], []
        for c in range(COMPS):
            solved = swept_all[c, span, :] + factor[:ny] * cells[c]
            grad = weight * solved
            part = own * grad + fluxes[c]
            part = part + pltpu.roll(ahead_y * grad, ny - 1, 0) - pltpu.roll(behind_y * grad, 1, 0)
            part = part + pltpu.roll(ahead_z * grad, LANES - 1, 1) - pltpu.roll(behind_z * grad, 1, 1)
            part = part - jnp.where(line == 0, gflux[c : c + 1], 0.0)
            part = part + jnp.where(line == ny - 1, gflux[TILE + c : TILE + c + 1], 0.0)
            out[c, span, :] = part
            above = pl.ds((x + 1) * ny, ny)
            out[c, above, :] = out[c, above, :] - behind[0] * grad
            new_cells.append(solved)
            new_fluxes.append(ahead[0] * grad)
        return tuple(new_cells), tuple(new_fluxes), gvalue

    out[:, pl.ds(nx * ny, ny), :] = jnp.zeros((COMPS, ny, LANES), jnp.float32)
    state = (tuple(nexts[:COMPS]), tuple(far * nexts[c] for c in range(COMPS)), nexts[COMPS])
    parts = 4
    deep = nx // parts

    def copy(part):
        span = pl.ds(part * deep * ny, deep * ny)
        return pltpu.make_async_copy(out.at[:, span, :], out_any.at[:, span, :], sems.at[part])

    for part in reversed(range(parts)):
        first = (parts - 1 - part) * deep
        state = lax.fori_loop(first, first + deep, finish, state)
        if part + 1 < parts:
            copy(part + 1).start()
    top = pl.ds(0, ny)
    for c in range(COMPS):
        out[c, top, :] = out[c, top, :] - near * starts[c]
    copy(0).start()
    for part in range(parts):
        copy(part).wait()


def call(kernel, name, operands, outs, scratch=(), spaces=None, out_spaces=None):
    params = pltpu.CompilerParams(vmem_limit_bytes=VMEM_BYTES)
    pick_space = {
        "v": pl.BlockSpec(memory_space=pltpu.VMEM),
        "h": pl.BlockSpec(memory_space=pltpu.HBM),
        "s": pl.BlockSpec(memory_space=pltpu.SMEM),
    }
    spaces = spaces or "s" + "v" * (len(operands) - 1)
    out_spaces = out_spaces or "v" * len(outs)
    return pl.pallas_call(
        kernel,
        name=name,
        out_shape=[jax.ShapeDtypeStruct(shape, jnp.float32) for shape in outs],
        in_specs=[pick_space[s] for s in spaces],
        out_specs=[pick_space[s] for s in out_spaces],
        scratch_shapes=list(scratch),
        compiler_params=params,
    )(*operands)


def exchange(rows, axis, bit):
    count = lax.axis_size(axis)
    return lax.ppermute(rows, axis, [(i, i ^ (1 << bit)) for i in range(count)])


def climb(lay, axis, levels, me, own):
    owns, gots = [own], []
    for level in range(levels - 1):
        gots.append(exchange(owns[-1][0], axis, level))
        top = level == levels - 2
        shapes = [(lay.rows, LANES)] + ([(lay.side_rows, LANES)] if top else [])
        merged = call(
            functools.partial(merge_kernel, lay, level, top),
            axis + "_merge_" + str(level),
            (me, owns[-1][1], gots[-1]),
            shapes,
        )
        owns.append((merged[-1], merged[0]))
    gots.append(exchange(owns[-1][0], axis, levels - 1))
    return [block for _, block in owns], gots


def on_device(cotangent, diffusion, phase, courant, upwind):
    comps, nx, ny, nz = cotangent.shape
    x_levels = (lax.axis_size("gx") - 1).bit_length()
    y_levels = (lax.axis_size("gy") - 1).bit_length()
    rows = nx * ny
    half = nx // 2
    wide = ny + 2 * TILE
    ylay = Layout(comps, 1, 2, half)
    xlay = Layout(comps + 1, 2, 1, ny)
    me_x = lax.axis_index("gx").astype(jnp.int32).reshape(1)
    me_y = lax.axis_index("gy").astype(jnp.int32).reshape(1)

    def vmem(*shape, dtype=jnp.float32):
        return pltpu.VMEM(shape, dtype)

    cot = cotangent.reshape(comps, rows, nz)
    cour = courant.reshape(3, rows, nz)
    upw = upwind.reshape(3, rows, nz)
    az, w, inv, keep, send = call(
        functools.partial(z_kernel, (nx, ny), ylay),
        "z_solve",
        (me_y, cot, diffusion.reshape(rows, nz), phase.reshape(rows, nz), cour, upw),
        [(comps, rows, nz), (rows, nz), (rows, nz), (ylay.rows, nz), (ylay.rows, nz)],
        [
            vmem(comps, rows, nz), vmem(rows, nz), vmem(rows, nz, dtype=jnp.int32),
            vmem(rows, nz), vmem(rows, nz, dtype=jnp.int32),
            vmem(rows, nz), vmem(rows, nz), vmem(rows, nz), vmem(rows, nz), vmem(rows, nz),
            vmem(rows, nz), vmem(rows, nz), vmem(2 * ylay.rows, nz),
            pltpu.SemaphoreType.DMA((comps,)), pltpu.SemaphoreType.DMA((4,)),
        ],
        spaces="shhhhh",
    )
    y_owns, y_gots = climb(ylay, "gy", y_levels, me_y, (send, keep))
    answer, passed = call(
        functools.partial(solve_kernel, ylay, y_levels, True),
        "y_reduced",
        (me_y, *y_owns, *y_gots),
        [(ylay.answer_rows, nz), (ylay.answer_rows, nz)],
    )
    met = exchange(passed, "gy", 0)
    ay, ghost, block, xinv, before, after = call(
        functools.partial(y_kernel, (nx, ny), ylay, xlay),
        "y_solve",
        (me_y, az, answer, met, w, inv, cour, upw),
        [
            (comps, rows, nz), (nx * 2 * TILE, nz), (xlay.rows, nz), (nx * wide, nz),
            (2 * nx, nz), (2 * nx, nz),
        ],
        [vmem(2 * ylay.answer_rows, nz), vmem(nx * wide, nz)],
    )
    x_owns, x_gots = climb(xlay, "gx", x_levels, me_x, (block, block))
    (grad,) = call(
        functools.partial(x_kernel, (nx, ny), xlay, x_levels),
        "x_solve",
        (me_x, *x_owns, *x_gots, xinv, ay, ghost, w, before, after, cour, upw),
        [(comps, rows, nz)],
        [
            vmem(comps, rows + ny, nz), vmem(comps, rows, nz), vmem(nx * 2 * TILE, nz),
            vmem(xlay.answer_rows, nz), pltpu.SemaphoreType.DMA((4,)),
        ],
        out_spaces="h",
    )
    return grad.reshape(comps, nx, ny, nz)


def solution(mesh):
    placed = (
        P(None, "gx", "gy", None),
        P("gx", "gy", None),
        P("gx", "gy", None),
        P(None, "gx", "gy", None),
        P(None, "gx", "gy", None),
    )
    return jax.shard_map(
        on_device, mesh=mesh, in_specs=placed, out_specs=P(None, "gx", "gy", None), check_vma=False
    )
```

time: 69.9 us -> 49.9 us (0.71)
  blocking collectives: 19.2 us -> 0 us
  starting transfers between devices: 15.6 us -> 10 us
  waiting for transfers between devices: 11.6 us -> 16.9 us
  Pallas kernels: 11.6 us -> 13.5 us
  local copies, waits for them, and re-layouts: 10.2 us -> 9.06 us
  other arithmetic: 0.84 us -> 0 us
    all_to_all x2 -> x0, blocking collectives: 19.2 us -> none  [the longest x1 10.5 us: on_device(): x_got = lax.all_to_all(x_send, 'gx', 0, 0, tiled=True)]
    ppermute x2 -> x6, waiting for transfers between devices: 0.01 us -> 16.9 us  [exchange(): return lax.ppermute(rows, axis, [(i, i ^ 1 << bit) for i in range(count)])]
    all_to_all x2 -> x0, starting transfers between devices: 11.9 us -> none  [the longest x1 7.06 us: on_device(): got = lax.all_to_all(posted, 'gy', 0, 0, tiled=True)]
    all_to_all x2 -> x0, waiting for transfers between devices: 11.6 us -> none  [the longest x1 6.29 us: on_device(): states = lax.all_to_all(states_send, 'gx', 0, 0, tiled=True)]
    ppermute x2 -> x6, starting transfers between devices: 3.65 us -> 10 us  [exchange(): return lax.ppermute(rows, axis, [(i, i ^ 1 << bit) for i in range(count)])]
    slice x5 -> x0, local copies, waits for them, and re-layouts: 5.22 us -> none  [the longest x2 1.99 us: y_edge(): up = courant[1, :, y] * upwind[1, :, y].astype(f32)]
    unnamed x14 -> x22, local copies, waits for them, and re-layouts: 5.02 us -> 9.06 us
    pallas_call x5 -> x7, Pallas kernels: 11.6 us -> 13.5 us  [call(): pl.pallas_call(kernel, name=name, out_shape=[jax.ShapeDtypeStruct(shape,...]
  transfers between devices with their start and end apart: 4 -> 6, of which waited for: 2 -> 6; matrix products, arithmetic and copies ran while one was open for 1% -> 0% of each run, Pallas kernels for 9% -> 0%
where the time goes in v1:
time: 49.9 us; the launch traced here: 49.5 us
  waiting for transfers between devices  16.9 us (34%)
  Pallas kernels  13.5 us (27%)
  starting transfers between devices  10 us (20%)
  local copies, waits for them, and re-layouts  9.06 us (18%)
    ppermute x6, waiting for transfers between devices, exchange(): return lax.ppermute(rows, axis, [(i, i ^ 1 << bit) for i in range(count)])  16.9 us
    pallas_call x7, Pallas kernels, call(): pl.pallas_call(kernel, name=name, out_shape=[jax.ShapeDtypeStruct(shape,...  13.5 us
    ppermute x6, starting transfers between devices, exchange(): return lax.ppermute(rows, axis, [(i, i ^ 1 << bit) for i in range(count)])  10 us
    unnamed x22, local copies, waits for them, and re-layouts  9.06 us
  transfers between devices with their start and end apart: 6, of which 6 were waited for; matrix products, arithmetic and copies ran while one was open for 0% of the time, Pallas kernels for 0%

profile of v1, /device:TPU:0, one launch (start us, length us, event | category | flops | bytes accessed | tf_op | source)
XLA Modules:
  0.0 49.5 jit_solution(6092413892433146019)
XLA Ops:
  0.0 1.1 %copy-done = f32[3,32,16,128]{3,2,1,0:T(8,128)S(1)} copy-done((f32[3,32,16,128]{3,2,1,0:T(8,128)S(1)}, f32[3,32,16,128]{3,2,1,0:T(8,128)}, u32[]{:S(2)}) %copy-start) | copy-done | bytes 786456
  1.1 1.1 %copy-done.2 = s32[3,32,16,128]{3,2,1,0:T(8,128)S(1)} copy-done((s32[3,32,16,128]{3,2,1,0:T(8,128)S(1)}, s32[3,32,16,128]{3,2,1,0:T(8,128)}, u32[]{:S(2)}) %copy-start.2) | copy-done | bytes 786456
  2.3 1.4 %copy-done.4 = f32[6,32,16,128]{3,2,1,0:T(8,128)S(1)} copy-done((f32[6,32,16,128]{3,2,1,0:T(8,128)S(1)}, f32[6,32,16,128]{3,2,1,0:T(8,128)}, u32[]{:S(2)}) %copy-start.4) | copy-done | bytes 1572888
  3.7 0.9 %copy-done.9 = f32[32,16,128]{2,1,0:T(8,128)S(1)} copy-done((f32[32,16,128]{2,1,0:T(8,128)S(1)}, f32[32,16,128]{2,1,0:T(8,128)}, u32[]{:S(2)}) %copy-start.9) | copy-done | bytes 262168
  4.6 0.9 %copy-done.10 = s32[32,16,128]{2,1,0:T(8,128)S(1)} copy-done((s32[32,16,128]{2,1,0:T(8,128)S(1)}, s32[32,16,128]{2,1,0:T(8,128)}, u32[]{:S(2)}) %copy-start.10) | copy-done | bytes 262168
  5.6 4.0 %z_solve.1 = (f32[6,512,128]{2,1,0:T(8,128)S(1)}, f32[512,128]{1,0:T(8,128)S(1)}, f32[512,128]{1,0:T(8,128)S(1)}, f32[304,128]{1,0:T(8,128)S(1)}, f32[304,128]{1,0:T(8,128)S(1)}) custom-call(s32[1]{0:T(128)} %bitcast.1.me_ref, f32[6,512,128]{2,1,0:T(8,128)S(1)} %bitcast.14, f32[512,128]{1,0:T(8,128)S(1)} %bitcast.15, s32[512,128]{1,0:T(8,128)S(1)} %bitcast.16, ...), custom_call_target="tpu_custom_call" | custom-call | tf_op jit(solution)/shard_map/z_solve/pallas_call | solution.py:560
  9.6 0.5 %collective-permute-start = (f32[304,128]{1,0:T(8,128)S(1)}, f32[304,128]{1,0:T(8,128)S(1)}, u32[]{:S(2)}, u32[]{:S(2)}) collective-permute-start(f32[304,128]{1,0:T(8,128)S(1)} %get-tuple-element.24), channel_id=1, source_target_pairs={{0,1},{1,0},{2,3},{3,2},{4,5},{5,4},{6,7},{7,6},{8,9},{9,8},{10,11... | collective-permute-start | bytes 466952 | tf_op jit(solution)/shard_map/ppermute | solution.py:573
  10.1 1.0 %collective-permute-done.other.refs_3_ = f32[304,128]{1,0:T(8,128)S(1)} collective-permute-done((f32[304,128]{1,0:T(8,128)S(1)}, f32[304,128]{1,0:T(8,128)S(1)}, u32[]{:S(2)}, u32[]{:S(2)}) %collective-permute-start) | collective-permute-done | bytes 155680 | tf_op jit(solution)/shard_map/ppermute | solution.py:573
  11.2 2.9 %collective-permute-start.1 = (f32[304,128]{1,0:T(8,128)S(1)}, f32[304,128]{1,0:T(8,128)S(1)}, u32[]{:S(2)}, u32[]{:S(2)}) collective-permute-start(f32[304,128]{1,0:T(8,128)S(1)} %gy_merge_0.1.own.refs_1_), channel_id=1, source_target_pairs={{0,2},{1,3},{2,0},{3,1},{4,6},{5,7},{6,4},{7,5},{8,10},{9,11},{10,... | collective-permute-start | bytes 466952 | tf_op jit(solution)/shard_map/ppermute | solution.py:573
  14.1 4.3 %collective-permute-done.1.other.refs_4_ = f32[304,128]{1,0:T(8,128)S(1)} collective-permute-done((f32[304,128]{1,0:T(8,128)S(1)}, f32[304,128]{1,0:T(8,128)S(1)}, u32[]{:S(2)}, u32[]{:S(2)}) %collective-permute-start.1) | collective-permute-done | bytes 155680 | tf_op jit(solution)/shard_map/ppermute | solution.py:573
  18.4 1.9 %collective-permute-start.2 = (f32[144,128]{1,0:T(8,128)S(1)}, f32[144,128]{1,0:T(8,128)S(1)}, u32[]{:S(2)}, u32[]{:S(2)}) collective-permute-start(f32[144,128]{1,0:T(8,128)S(1)} %get-tuple-element.26), channel_id=1, source_target_pairs={{0,4},{1,5},{2,6},{3,7},{4,0},{5,1},{6,2},{7,3},{8,12},{9,13},{10,... | collective-permute-start | bytes 221192 | tf_op jit(solution)/shard_map/ppermute | solution.py:573
  20.3 2.6 %collective-permute-done.2.refs_5_ = f32[144,128]{1,0:T(8,128)S(1)} collective-permute-done((f32[144,128]{1,0:T(8,128)S(1)}, f32[144,128]{1,0:T(8,128)S(1)}, u32[]{:S(2)}, u32[]{:S(2)}) %collective-permute-start.2) | collective-permute-done | bytes 73760 | tf_op jit(solution)/shard_map/ppermute | solution.py:573
  23.0 1.3 %collective-permute-done.3.got = f32[256,128]{1,0:T(8,128)S(1)} collective-permute-done((f32[256,128]{1,0:T(8,128)S(1)}, f32[256,128]{1,0:T(8,128)S(1)}, u32[]{:S(2)}, u32[]{:S(2)}) %collective-permute-start.3) | collective-permute-done | bytes 131104 | tf_op jit(solution)/shard_map/ppermute | solution.py:573
  24.4 2.7 %y_solve.1 = (f32[6,512,128]{2,1,0:T(8,128)S(1)}, f32[512,128]{1,0:T(8,128)S(1)}, f32[312,128]{1,0:T(8,128)}, f32[1024,128]{1,0:T(8,128)S(1)}, f32[64,128]{1,0:T(8,128)S(1)}, /*index=5*/f32[64,128]{1,0:T(8,128)S(1)}) custom-call(s32[1]{0:T(128)} %bitcast.1.me_ref, f32[6,512,128]{2,1,0:T(8,128)S(1)} %get-tuple-element.22.az, ...), custom_call_target="tpu_custom_call" | custom-call | tf_op jit(solution)/shard_map/y_solve/pallas_call | solution.py:560
  27.1 0.8 %copy-done.5 = f32[1024,128]{1,0:T(8,128)} copy-done((f32[1024,128]{1,0:T(8,128)}, f32[1024,128]{1,0:T(8,128)S(1)}, u32[]{:S(2)}) %copy-start.5) | copy-done | bytes 524312
  27.9 0.7 %copy-done.7 = f32[512,128]{1,0:T(8,128)} copy-done((f32[512,128]{1,0:T(8,128)}, f32[512,128]{1,0:T(8,128)S(1)}, u32[]{:S(2)}) %copy-start.7) | copy-done | bytes 262168
  28.6 1.9 %collective-permute-start.4 = (f32[312,128]{1,0:T(8,128)}, f32[312,128]{1,0:T(8,128)}, u32[]{:S(2)}, u32[]{:S(2)}) collective-permute-start(f32[312,128]{1,0:T(8,128)} %get-tuple-element.31.own.refs_0_), channel_id=1, source_target_pairs={{0,8},{8,0},{16,24},{24,16},{1,9},{9,1},{17,25},{25,17},{2,10},{10... | collective-permute-start | bytes 479240 | tf_op jit(solution)/shard_map/ppermute | solution.py:573
  30.4 4.7 %collective-permute-done.4.other.refs_2_ = f32[312,128]{1,0:T(8,128)} collective-permute-done((f32[312,128]{1,0:T(8,128)}, f32[312,128]{1,0:T(8,128)}, u32[]{:S(2)}, u32[]{:S(2)}) %collective-permute-start.4) | collective-permute-done | bytes 159776 | tf_op jit(solution)/shard_map/ppermute | solution.py:573
  35.2 1.0 %gx_merge_0.1 = (f32[312,128]{1,0:T(8,128)S(1)}, f32[152,128]{1,0:T(8,128)S(1)}) custom-call(s32[1]{0:T(128)} %bitcast.me_ref, f32[312,128]{1,0:T(8,128)} %get-tuple-element.31.own.refs_0_, f32[312,128]{1,0:T(8,128)} %collective-permute-done.4.other.refs_2_), custom_call_target="tpu_custom_call" | custom-call | tf_op jit(solution)/shard_map/gx_merge_0/pallas_call | solution.py:560
  36.2 2.8 %collective-permute-start.5 = (f32[152,128]{1,0:T(8,128)S(1)}, f32[152,128]{1,0:T(8,128)S(1)}, u32[]{:S(2)}, u32[]{:S(2)}) collective-permute-start(f32[152,128]{1,0:T(8,128)S(1)} %get-tuple-element.33), channel_id=1, source_target_pairs={{0,16},{8,24},{16,0},{24,8},{1,17},{9,25},{17,1},{25,9},{2,18},{10... | collective-permute-start | bytes 233480 | tf_op jit(solution)/shard_map/ppermute | solution.py:573
  39.0 2.9 %collective-permute-done.5.refs_3_ = f32[152,128]{1,0:T(8,128)S(1)} collective-permute-done((f32[152,128]{1,0:T(8,128)S(1)}, f32[152,128]{1,0:T(8,128)S(1)}, u32[]{:S(2)}, u32[]{:S(2)}) %collective-permute-start.5) | collective-permute-done | bytes 77856 | tf_op jit(solution)/shard_map/ppermute | solution.py:573
  41.9 1.0 %copy-done.6 = f32[1024,128]{1,0:T(8,128)S(1)} copy-done((f32[1024,128]{1,0:T(8,128)S(1)}, f32[1024,128]{1,0:T(8,128)}, u32[]{:S(2)}) %copy-start.6) | copy-done | bytes 524312
  43.0 0.9 %copy-done.8 = f32[512,128]{1,0:T(8,128)S(1)} copy-done((f32[512,128]{1,0:T(8,128)S(1)}, f32[512,128]{1,0:T(8,128)}, u32[]{:S(2)}) %copy-start.8) | copy-done | bytes 262168
  43.9 5.6 %x_solve.1 = f32[6,512,128]{2,1,0:T(8,128)} custom-call(s32[1]{0:T(128)} %bitcast.me_ref, f32[312,128]{1,0:T(8,128)} %get-tuple-element.31.own.refs_0_, f32[312,128]{1,0:T(8,128)S(1)} %get-tuple-element.32.refs_1_, f32[312,128]{1,0:T(8,128)} %collective-permute-done.4.other.refs_2_, f32[152,128]{1,0:T(8,128)S(1)} %collective-permute-done.5.refs_3_, ...), custom_call_target="tpu_custom_call" | custom-call | tf_op jit(solution)/shard_map/x_solve/pallas_call | solution.py:560
  (17 shorter events, 0.3 us)
Async XLA Ops:
  0.0 1.1 %copy-start = (f32[3,32,16,128]{3,2,1,0:T(8,128)S(1)}, f32[3,32,16,128]{3,2,1,0:T(8,128)}, u32[]{:S(2)}) copy-start(f32[3,32,16,128]{3,2,1,0:T(8,128)} %param.8) | copy-start | bytes 2359300
  1.1 1.1 %copy-start.2 = (s32[3,32,16,128]{3,2,1,0:T(8,128)S(1)}, s32[3,32,16,128]{3,2,1,0:T(8,128)}, u32[]{:S(2)}) copy-start(s32[3,32,16,128]{3,2,1,0:T(8,128)} %param.9) | copy-start | bytes 2359300
  2.3 1.4 %copy-start.4 = (f32[6,32,16,128]{3,2,1,0:T(8,128)S(1)}, f32[6,32,16,128]{3,2,1,0:T(8,128)}, u32[]{:S(2)}) copy-start(f32[6,32,16,128]{3,2,1,0:T(8,128)} %param.5) | copy-start | bytes 4718596
  3.7 0.9 %copy-start.9 = (f32[32,16,128]{2,1,0:T(8,128)S(1)}, f32[32,16,128]{2,1,0:T(8,128)}, u32[]{:S(2)}) copy-start(f32[32,16,128]{2,1,0:T(8,128)} %param.6) | copy-start | bytes 786436
  4.6 0.9 %copy-start.10 = (s32[32,16,128]{2,1,0:T(8,128)S(1)}, s32[32,16,128]{2,1,0:T(8,128)}, u32[]{:S(2)}) copy-start(s32[32,16,128]{2,1,0:T(8,128)} %param.7) | copy-start | bytes 786436
  9.6 14.8 %copy-start.1 = (f32[3,32,16,128]{3,2,1,0:T(8,128)S(1)}, f32[3,32,16,128]{3,2,1,0:T(8,128)}, u32[]{:S(2)}) copy-start(f32[3,32,16,128]{3,2,1,0:T(8,128)} %param.8) | copy-start | bytes 2359300
  9.6 14.8 %copy-start.3 = (s32[3,32,16,128]{3,2,1,0:T(8,128)S(1)}, s32[3,32,16,128]{3,2,1,0:T(8,128)}, u32[]{:S(2)}) copy-start(s32[3,32,16,128]{3,2,1,0:T(8,128)} %param.9) | copy-start | bytes 2359300
  9.6 1.5 %collective-permute-start = (f32[304,128]{1,0:T(8,128)S(1)}, f32[304,128]{1,0:T(8,128)S(1)}, u32[]{:S(2)}, u32[]{:S(2)}) collective-permute-start(f32[304,128]{1,0:T(8,128)S(1)} %get-tuple-element.24), channel_id=1, source_target_pairs={{0,1},{1,0},{2,3},{3,2},{4,5},{5,4},{6,7},{7,6},{8,9},{9,8},{10,11... | collective-permute-start | bytes 466952 | tf_op jit(solution)/shard_map/ppermute | solution.py:573
  11.2 7.2 %collective-permute-start.1 = (f32[304,128]{1,0:T(8,128)S(1)}, f32[304,128]{1,0:T(8,128)S(1)}, u32[]{:S(2)}, u32[]{:S(2)}) collective-permute-start(f32[304,128]{1,0:T(8,128)S(1)} %gy_merge_0.1.own.refs_1_), channel_id=1, source_target_pairs={{0,2},{1,3},{2,0},{3,1},{4,6},{5,7},{6,4},{7,5},{8,10},{9,11},{10,... | collective-permute-start | bytes 466952 | tf_op jit(solution)/shard_map/ppermute | solution.py:573
  18.4 4.4 %collective-permute-start.2 = (f32[144,128]{1,0:T(8,128)S(1)}, f32[144,128]{1,0:T(8,128)S(1)}, u32[]{:S(2)}, u32[]{:S(2)}) collective-permute-start(f32[144,128]{1,0:T(8,128)S(1)} %get-tuple-element.26), channel_id=1, source_target_pairs={{0,4},{1,5},{2,6},{3,7},{4,0},{5,1},{6,2},{7,3},{8,12},{9,13},{10,... | collective-permute-start | bytes 221192 | tf_op jit(solution)/shard_map/ppermute | solution.py:573
  23.0 1.4 %collective-permute-start.3 = (f32[256,128]{1,0:T(8,128)S(1)}, f32[256,128]{1,0:T(8,128)S(1)}, u32[]{:S(2)}, u32[]{:S(2)}) collective-permute-start(f32[256,128]{1,0:T(8,128)S(1)} %get-tuple-element.28), channel_id=1, source_target_pairs={{0,1},{1,0},{2,3},{3,2},{4,5},{5,4},{6,7},{7,6},{8,9},{9,8},{10,11... | collective-permute-start | bytes 393224 | tf_op jit(solution)/shard_map/ppermute | solution.py:573
  27.1 0.8 %copy-start.5 = (f32[1024,128]{1,0:T(8,128)}, f32[1024,128]{1,0:T(8,128)S(1)}, u32[]{:S(2)}) copy-start(f32[1024,128]{1,0:T(8,128)S(1)} %get-tuple-element.34.refs_4_) | copy-start | bytes 1572868
  27.9 0.7 %copy-start.7 = (f32[512,128]{1,0:T(8,128)}, f32[512,128]{1,0:T(8,128)S(1)}, u32[]{:S(2)}) copy-start(f32[512,128]{1,0:T(8,128)S(1)} %get-tuple-element.36.refs_6_) | copy-start | bytes 786436
  28.6 6.6 %collective-permute-start.4 = (f32[312,128]{1,0:T(8,128)}, f32[312,128]{1,0:T(8,128)}, u32[]{:S(2)}, u32[]{:S(2)}) collective-permute-start(f32[312,128]{1,0:T(8,128)} %get-tuple-element.31.own.refs_0_), channel_id=1, source_target_pairs={{0,8},{8,0},{16,24},{24,16},{1,9},{9,1},{17,25},{25,17},{2,10},{10... | collective-permute-start | bytes 479240 | tf_op jit(solution)/shard_map/ppermute | solution.py:573
  36.2 5.7 %collective-permute-start.5 = (f32[152,128]{1,0:T(8,128)S(1)}, f32[152,128]{1,0:T(8,128)S(1)}, u32[]{:S(2)}, u32[]{:S(2)}) collective-permute-start(f32[152,128]{1,0:T(8,128)S(1)} %get-tuple-element.33), channel_id=1, source_target_pairs={{0,16},{8,24},{16,0},{24,8},{1,17},{9,25},{17,1},{25,9},{2,18},{10... | collective-permute-start | bytes 233480 | tf_op jit(solution)/shard_map/ppermute | solution.py:573
  41.9 1.0 %copy-start.6 = (f32[1024,128]{1,0:T(8,128)S(1)}, f32[1024,128]{1,0:T(8,128)}, u32[]{:S(2)}) copy-start(f32[1024,128]{1,0:T(8,128)} %copy-done.5) | copy-start | bytes 1572868
  43.0 0.9 %copy-start.8 = (f32[512,128]{1,0:T(8,128)S(1)}, f32[512,128]{1,0:T(8,128)}, u32[]{:S(2)}) copy-start(f32[512,128]{1,0:T(8,128)} %copy-done.7) | copy-start | bytes 786436

commit v2 on v1

--- a/solution.py
+++ b/solution.py
@@ -10,7 +10,6 @@
 COMPS = 6
 LANES = 128
 TILE = 8
-VMEM_BYTES = 24 * 1024 * 1024
 
 
 def weight_of(diffusion, phase):
@@ -193,7 +192,8 @@
     return low_last, high_first
 
 
-def merge_kernel(lay, bit, top, me_ref, own, other, out, *side):
+def merge_kernel(lay, bit, top, me_ref, own, other, *refs):
+    out, *side = refs[-2:] if top else refs[-1:]
     upper = (me_ref[0] >> bit) & 1
     low, high = ordered(upper, read_block(lay, own), read_block(lay, other))
     block = merge(lay, low, high)
@@ -360,13 +360,59 @@
     )
 
 
+def coef_kernel(dims, w, courant, upwind, after, block, xinv, left, right, flows):
+    del after
+    nx, ny = dims
+    rows = nx * ny
+    one = jnp.ones((ny, LANES), jnp.float32)
+    value, slope, back, fall = one, one, one, one
+    for k in range(nx):
+        low, high = pl.ds(k * ny, ny), pl.ds((nx - 1 - k) * ny, ny)
+        right[low, :] = value
+        left[high, :] = back
+        new_value, slope = growing_step(value, slope, w[low, :])
+        xinv[low, :] = value / new_value
+        end, value = value, new_value
+        corner = back
+        back, fall = growing_step(back, fall, w[high, :])
+    total = 1.0 / value
+    block[pl.ds(0, ny), :] = corner * total
+    block[pl.ds(ny, ny), :] = total
+    block[pl.ds(2 * ny, ny), :] = end * total
+
+    lane = lax.broadcasted_iota(jnp.int32, (ny, LANES), 1)
+
+    def plane(x, carry):
+        span = pl.ds(x * ny, ny)
+        left[span, :] = left[span, :] * total
+        right[span, :] = right[span, :] * total
+        own = one
+        for d in range(3):
+            flow = courant[d, span, :]
+            up = flow * upwind[d, span, :].astype(jnp.float32)
+            down = flow - up
+            own = own + (down - up)
+            if d == 2:
+                up = jnp.where(lane == 0, 0.0, up)
+                down = jnp.where(lane == LANES - 1, 0.0, down)
+            flows[pl.ds((1 + 2 * d) * rows + x * ny, ny), :] = up
+            flows[pl.ds((2 + 2 * d) * rows + x * ny, ny), :] = down
+        flows[span, :] = own
+        return carry
+
+    lax.fori_loop(0, nx, plane, 0, unroll=4)
+    first, last = pl.ds(0, ny), pl.ds(rows - ny, ny)
+    block[pl.ds(3 * ny, ny), :] = w[first, :] * flows[pl.ds(rows, ny), :]
+    block[pl.ds(4 * ny, ny), :] = w[last, :] * flows[pl.ds(2 * rows + rows - ny, ny), :]
+
+
 def y_kernel(
-    dims, ylay, xlay, me_ref, az, own, got, w, inv, cour, upw,
-    ay, ghost, block, xinv, before, after, joined, left_all,
+    dims, ylay, xlay, me_ref, az, own, got, w, inv, left, right, part,
+    ay, ghost, block, ginv, before, after, joined, back_all,
 ):
     nx, ny = dims
     half = nx // 2
-    rows = ny + 2 * TILE
+    deep = 2 * TILE
     mine = me_ref[0] & 1
     span = ylay.answer_rows
     joined[pl.ds(pl.multiple_of(mine * span, TILE), span), :] = own[...]
@@ -381,12 +427,11 @@
     ghost[...] = jnp.zeros(ghost.shape, jnp.float32)
     for c in range(COMPS):
         for h in range(2):
-            part = pl.ds(h * half, half)
+            piece = pl.ds(h * half, half)
             fb = joined[pl.ds(h * span + c * half, half), :]
             fa = joined[pl.ds(h * span + (COMPS + c) * half, half), :]
-            deep = 2 * TILE
-            ghost[pl.ds(h * half * deep + c, half, stride=deep), :] = before[part, :] * fb
-            ghost[pl.ds(h * half * deep + TILE + c, half, stride=deep), :] = after[part, :] * fa
+            ghost[pl.ds(h * half * deep + c, half, stride=deep), :] = before[piece, :] * fb
+            ghost[pl.ds(h * half * deep + TILE + c, half, stride=deep), :] = after[piece, :] * fa
             swept, chain = fb, []
             for y in range(ny):
                 cells = az[c, pl.ds(h * half * ny + y, half, stride=ny), :]
@@ -398,65 +443,57 @@
                 later = chain[y] + inv[pl.ds(y * nx + h * half, half), :] * later
                 ay[c, where, :] = later * w[where, :]
 
-    def weight_at(x):
-        return jnp.concatenate([w[pl.ds(x * ny, ny), :], sides(before, after, x)], axis=0)
-
-    one = jnp.ones((rows, LANES), jnp.float32)
+    one = jnp.ones((deep, LANES), jnp.float32)
     back, fall = one, one
     for x in reversed(range(nx)):
-        left_all[pl.ds(x * rows, rows), :] = back
-        back, fall = growing_step(back, fall, weight_at(x))
+        back_all[pl.ds(x * deep, deep), :] = back
+        corner = back
+        back, fall = growing_step(back, fall, sides(before, after, x))
     total = 1.0 / back
     value, slope = one, one
     zero = jnp.zeros((ny, LANES), jnp.float32)
-    pieces = xlay.pieces
-    firsts, lasts = [zero] * pieces, [zero] * pieces
-    corner = left_all[pl.ds(0, rows), :]
+    firsts, lasts = [zero] * xlay.pieces, [zero] * xlay.pieces
     for x in range(nx):
-        down = left_all[pl.ds(x * rows, rows), :]
-        for i in range(pieces):
-            part = slice(0, ny) if i < COMPS else slice(ny, rows)
-            cells = ay[i, pl.ds(x * ny, ny), :] if i < COMPS else ghost[pl.ds(x * 2 * TILE, 2 * TILE), :]
-            lasts[i] = lasts[i] + value[part] * cells
-            firsts[i] = firsts[i] + down[part] * cells
-        new_value, slope = growing_step(value, slope, weight_at(x))
-        xinv[pl.ds(x * rows, rows), :] = value / new_value
+        here = pl.ds(x * ny, ny)
+        near, far = left[here, :], right[here, :]
+        for c in range(COMPS):
+            cells = ay[c, here, :]
+            firsts[c] = firsts[c] + near * cells
+            lasts[c] = lasts[c] + far * cells
+        here = pl.ds(x * deep, deep)
+        cells = ghost[here, :]
+        firsts[COMPS] = firsts[COMPS] + back_all[here, :] * cells
+        lasts[COMPS] = lasts[COMPS] + value * cells
+        new_value, slope = growing_step(value, slope, sides(before, after, x))
+        ginv[here, :] = value / new_value
         end, value = value, new_value
-
-    def halves(cells):
-        return [cells[:ny], cells[ny:]]
-
-    scale = halves(total)
-    edges = []
-    for e, x in enumerate((0, nx - 1)):
-        where = pl.ds(x * ny, ny)
-        up = cour[0, where, :] * upw[0, where, :].astype(jnp.float32)
-        edges.append(w[where, :] * (up if e == 0 else cour[0, where, :] - up))
+    firsts[COMPS] = firsts[COMPS] * total
+    lasts[COMPS] = lasts[COMPS] * total
+    pieces = [part[pl.ds(i * ny, ny), :] for i in range(5)]
     write_block(
         xlay,
         block,
         {
-            "first": [v * scale[xlay.group(i)] for i, v in enumerate(firsts)],
-            "last": [v * scale[xlay.group(i)] for i, v in enumerate(lasts)],
-            "near": halves(corner * total),
-            "cross": scale,
-            "far": halves(end * total),
-            "head": edges[:1],
-            "tail": edges[1:],
+            "first": firsts,
+            "last": lasts,
+            "near": [pieces[0], corner * total],
+            "cross": [pieces[1], total],
+            "far": [pieces[2], end * total],
+            "head": pieces[3:4],
+            "tail": pieces[4:5],
         },
     )
-    if xlay.edge > xlay.packed + 6:
-        block[pl.ds(xlay.packed + 6, 2), :] = jnp.zeros((2, LANES), jnp.float32)
-
-
-def x_kernel(
-    dims, lay, levels, me_ref, *refs
-):
+    block[pl.ds(xlay.packed + 6, 2), :] = jnp.zeros((2, LANES), jnp.float32)
+
+
+def x_kernel(dims, lay, levels, me_ref, *refs):
     nx, ny = dims
     own_refs, got_refs = refs[:levels], refs[levels : 2 * levels]
-    (xinv, ay, ghost, w, lower, upper_edge, courant, upwind,
-     out_any, out, swept_all, gswept, answer, sems) = refs[2 * levels :]
-    rows = ny + 2 * TILE
+    (xinv, ginv, ay, ghost, w, lower, higher, flows,
+     out_any, out, field, fluxes, answer, sems) = refs[2 * levels :]
+    rows = nx * ny
+    deep = 2 * TILE
+    tiles = ny // TILE
     solve_kernel(lay, levels, False, me_ref, *own_refs, *got_refs, answer)
     n = lay.pieces
     starts = read_rows(answer, 0, n, ny)
@@ -465,91 +502,110 @@
     far = answer[pl.ds((2 * n + 1) * ny, ny), :]
 
     def sweep(x, carry):
-        factor = xinv[pl.ds(x * rows, rows), :]
-        span = pl.ds(x * ny, ny)
+        span, above = pl.ds(x * ny, ny), pl.ds((x + 1) * ny, ny)
+        factor = xinv[span, :]
         new = []
         for c in range(COMPS):
-            value = (ay[c, span, :] + carry[c]) * factor[:ny]
-            swept_all[c, span, :] = value
+            value = (ay[c, span, :] + carry[c]) * factor
+            field[c, above, :] = value
             new.append(value)
-        gspan = pl.ds(x * 2 * TILE, 2 * TILE)
-        gvalue = (ghost[gspan, :] + carry[COMPS]) * factor[ny:]
-        gswept[gspan, :] = gvalue
-        return tuple(new) + (gvalue,)
-
-    lax.fori_loop(0, nx, sweep, tuple(starts), unroll=4)
-
-    lane = lax.broadcasted_iota(jnp.int32, (ny, LANES), 1)
-    line = lax.broadcasted_iota(jnp.int32, (ny, LANES), 0)
-
-    def finish(step, carry):
-        cells, fluxes, gcells = carry
+        here = pl.ds(x * deep, deep)
+        edge = (ghost[here, :] + carry[COMPS]) * ginv[here, :]
+        fluxes[here, :] = edge
+        return tuple(new) + (edge,)
+
+    lax.fori_loop(0, nx, sweep, tuple(starts), unroll=8)
+
+    def back(step, carry):
         x = nx - 1 - step
-        span = pl.ds(x * ny, ny)
-        factor = xinv[pl.ds(x * rows, rows), :]
+        span, above = pl.ds(x * ny, ny), pl.ds((x + 1) * ny, ny)
+        factor = xinv[span, :]
         weight = w[span, :]
-        ahead, behind = [], []
-        own = jnp.ones((ny, LANES), jnp.float32)
-        for d in range(3):
-            flow = courant[d, span, :]
-            up = flow * upwind[d, span, :].astype(jnp.float32)
-            down = flow - up
-            own = own + (down - up)
-            ahead.append(up)
-            behind.append(down)
-        ahead_y = jnp.where(line == 0, 0.0, ahead[1])
-        behind_y = jnp.where(line == ny - 1, 0.0, behind[1])
-        ahead_z = jnp.where(lane == 0, 0.0, ahead[2])
-        behind_z = jnp.where(lane == LANES - 1, 0.0, behind[2])
-        gspan = pl.ds(x * 2 * TILE, 2 * TILE)
-        gvalue = gswept[gspan, :] + factor[ny:] * gcells
-        gflux = gvalue * jnp.concatenate(
+        new = []
+        for c in range(COMPS):
+            value = field[c, above, :] + factor * carry[c]
+            field[c, above, :] = value * weight
+            new.append(value)
+        here = pl.ds(x * deep, deep)
+        edge = fluxes[here, :] + ginv[here, :] * carry[COMPS]
+        scale = jnp.concatenate(
             [
                 jnp.broadcast_to(lower[pl.ds(nx + x, 1), :], (TILE, LANES)),
-                jnp.broadcast_to(upper_edge[pl.ds(nx + x, 1), :], (TILE, LANES)),
+                jnp.broadcast_to(higher[pl.ds(nx + x, 1), :], (TILE, LANES)),
             ],
             axis=0,
         )
-        new_cells, new_fluxes = [], []
+        fluxes[here, :] = edge * scale
+        return tuple(new) + (edge,)
+
+    lax.fori_loop(0, nx, back, tuple(nexts), unroll=8)
+    blank = jnp.zeros((COMPS, ny, LANES), jnp.float32)
+    field[:, pl.ds(0, ny), :] = blank
+    field[:, pl.ds((nx + 1) * ny, ny), :] = blank
+
+    line = lax.broadcasted_iota(jnp.int32, (TILE, LANES), 0)
+
+    def advect(x, carry):
+        before = jnp.maximum(x - 1, 0)
+        beyond = jnp.minimum(x + 1, nx - 1)
+
+        def flow(kind, plane, t):
+            start = pl.multiple_of(kind * rows + plane * ny + t * TILE, TILE)
+            return flows[pl.ds(start, TILE), :]
+
+        own = [flow(0, x, t) for t in range(tiles)]
+        ahead_x = [flow(1, beyond, t) for t in range(tiles)]
+        behind_x = [flow(2, before, t) for t in range(tiles)]
+        ahead_y = [flow(3, x, t) for t in range(tiles)]
+        behind_y = [flow(4, x, t) for t in range(tiles)]
+        ahead_z = [flow(5, x, t) for t in range(tiles)]
+        behind_z = [flow(6, x, t) for t in range(tiles)]
         for c in range(COMPS):
-            solved = swept_all[c, span, :] + factor[:ny] * cells[c]
-            grad = weight * solved
-            part = own * grad + fluxes[c]
-            part = part + pltpu.roll(ahead_y * grad, ny - 1, 0) - pltpu.roll(behind_y * grad, 1, 0)
-            part = part + pltpu.roll(ahead_z * grad, LANES - 1, 1) - pltpu.roll(behind_z * grad, 1, 1)
-            part = part - jnp.where(line == 0, gflux[c : c + 1], 0.0)
-            part = part + jnp.where(line == ny - 1, gflux[TILE + c : TILE + c + 1], 0.0)
-            out[c, span, :] = part
-            above = pl.ds((x + 1) * ny, ny)
-            out[c, above, :] = out[c, above, :] - behind[0] * grad
-            new_cells.append(solved)
-            new_fluxes.append(ahead[0] * grad)
-        return tuple(new_cells), tuple(new_fluxes), gvalue
-
-    out[:, pl.ds(nx * ny, ny), :] = jnp.zeros((COMPS, ny, LANES), jnp.float32)
-    state = (tuple(nexts[:COMPS]), tuple(far * nexts[c] for c in range(COMPS)), nexts[COMPS])
+
+            def cells(plane, t):
+                start = pl.multiple_of((plane + 1) * ny + t * TILE, TILE)
+                return field[c, pl.ds(start, TILE), :]
+
+            grad = [cells(x, t) for t in range(tiles)]
+            ups = [pltpu.roll(ahead_y[t] * grad[t], TILE - 1, 0) for t in range(tiles)]
+            downs = [pltpu.roll(behind_y[t] * grad[t], 1, 0) for t in range(tiles)]
+            lowest = fluxes[pl.ds(x * deep + c, 1), :]
+            highest = fluxes[pl.ds(x * deep + TILE + c, 1), :]
+            for t in range(tiles):
+                part = own[t] * grad[t]
+                part = part + ahead_x[t] * cells(x + 1, t) - behind_x[t] * cells(x - 1, t)
+                enter = ups[t + 1] if t + 1 < tiles else jnp.broadcast_to(highest, (TILE, LANES))
+                part = part + jnp.where(line == TILE - 1, enter, ups[t])
+                enter = downs[t - 1] if t > 0 else jnp.broadcast_to(lowest, (TILE, LANES))
+                part = part - jnp.where(line == 0, enter, downs[t])
+                part = part + pltpu.roll(ahead_z[t] * grad[t], LANES - 1, 1)
+                part = part - pltpu.roll(behind_z[t] * grad[t], 1, 1)
+                start = pl.multiple_of(x * ny + t * TILE, TILE)
+                out[c, pl.ds(start, TILE), :] = part
+        return carry
+
     parts = 4
-    deep = nx // parts
+    share = nx // parts
 
     def copy(part):
-        span = pl.ds(part * deep * ny, deep * ny)
+        span = pl.ds(part * share * ny, share * ny)
         return pltpu.make_async_copy(out.at[:, span, :], out_any.at[:, span, :], sems.at[part])
 
-    for part in reversed(range(parts)):
-        first = (parts - 1 - part) * deep
-        state = lax.fori_loop(first, first + deep, finish, state)
-        if part + 1 < parts:
-            copy(part + 1).start()
-    top = pl.ds(0, ny)
-    for c in range(COMPS):
-        out[c, top, :] = out[c, top, :] - near * starts[c]
-    copy(0).start()
+    top, bottom = pl.ds(0, ny), pl.ds(rows - ny, ny)
+    for part in range(parts):
+        lax.fori_loop(part * share, (part + 1) * share, advect, 0, unroll=2)
+        for c in range(COMPS):
+            if part == 0:
+                out[c, top, :] = out[c, top, :] - near * starts[c]
+            if part == parts - 1:
+                out[c, bottom, :] = out[c, bottom, :] + far * nexts[c]
+        copy(part).start()
     for part in range(parts):
         copy(part).wait()
 
 
-def call(kernel, name, operands, outs, scratch=(), spaces=None, out_spaces=None):
-    params = pltpu.CompilerParams(vmem_limit_bytes=VMEM_BYTES)
+def call(kernel, name, operands, outs, scratch=(), spaces=None, out_spaces=None, mebibytes=4):
+    params = pltpu.CompilerParams(vmem_limit_bytes=mebibytes * 1024 * 1024)
     pick_space = {
         "v": pl.BlockSpec(memory_space=pltpu.VMEM),
         "h": pl.BlockSpec(memory_space=pltpu.HBM),
@@ -557,6 +613,10 @@
     }
     spaces = spaces or "s" + "v" * (len(operands) - 1)
     out_spaces = out_spaces or "v" * len(outs)
+    operands = [
+        pltpu.with_memory_space_constraint(o, pltpu.HBM) if s == "h" else o
+        for o, s in zip(operands, spaces)
+    ]
     return pl.pallas_call(
         kernel,
         name=name,
@@ -573,21 +633,23 @@
     return lax.ppermute(rows, axis, [(i, i ^ (1 << bit)) for i in range(count)])
 
 
-def climb(lay, axis, levels, me, own):
-    owns, gots = [own], []
+def climb(lay, axis, levels, me, own, beside=None):
+    owns, gots, extra = [own], [], ()
     for level in range(levels - 1):
         gots.append(exchange(owns[-1][0], axis, level))
         top = level == levels - 2
+        if beside is not None and top:
+            extra = beside(owns[-1][1])
         shapes = [(lay.rows, LANES)] + ([(lay.side_rows, LANES)] if top else [])
         merged = call(
             functools.partial(merge_kernel, lay, level, top),
             axis + "_merge_" + str(level),
-            (me, owns[-1][1], gots[-1]),
+            (me, owns[-1][1], gots[-1]) + tuple(extra[:1]),
             shapes,
         )
         owns.append((merged[-1], merged[0]))
     gots.append(exchange(owns[-1][0], axis, levels - 1))
-    return [block for _, block in owns], gots
+    return [block for _, block in owns], gots, extra
 
 
 def on_device(cotangent, diffusion, phase, courant, upwind):
@@ -596,7 +658,6 @@
     y_levels = (lax.axis_size("gy") - 1).bit_length()
     rows = nx * ny
     half = nx // 2
-    wide = ny + 2 * TILE
     ylay = Layout(comps, 1, 2, half)
     xlay = Layout(comps + 1, 2, 1, ny)
     me_x = lax.axis_index("gx").astype(jnp.int32).reshape(1)
@@ -621,8 +682,20 @@
             pltpu.SemaphoreType.DMA((comps,)), pltpu.SemaphoreType.DMA((4,)),
         ],
         spaces="shhhhh",
-    )
-    y_owns, y_gots = climb(ylay, "gy", y_levels, me_y, (send, keep))
+        mebibytes=16,
+    )
+    def coefficients(after):
+        return call(
+            functools.partial(coef_kernel, (nx, ny)),
+            "x_coefficients",
+            (w, cour, upw, after),
+            [(5 * ny, nz), (rows, nz), (rows, nz), (rows, nz), (7 * rows, nz)],
+            spaces="vvvv",
+            mebibytes=8,
+        )
+
+    y_owns, y_gots, found = climb(ylay, "gy", y_levels, me_y, (send, keep), coefficients)
+    part, xinv, left, right, flows = found
     answer, passed = call(
         functools.partial(solve_kernel, ylay, y_levels, True),
         "y_reduced",
@@ -630,27 +703,29 @@
         [(ylay.answer_rows, nz), (ylay.answer_rows, nz)],
     )
     met = exchange(passed, "gy", 0)
-    ay, ghost, block, xinv, before, after = call(
+    ay, ghost, block, ginv, before, after = call(
         functools.partial(y_kernel, (nx, ny), ylay, xlay),
         "y_solve",
-        (me_y, az, answer, met, w, inv, cour, upw),
+        (me_y, az, answer, met, w, inv, left, right, part),
         [
-            (comps, rows, nz), (nx * 2 * TILE, nz), (xlay.rows, nz), (nx * wide, nz),
+            (comps, rows, nz), (nx * 2 * TILE, nz), (xlay.rows, nz), (nx * 2 * TILE, nz),
             (2 * nx, nz), (2 * nx, nz),
         ],
-        [vmem(2 * ylay.answer_rows, nz), vmem(nx * wide, nz)],
-    )
-    x_owns, x_gots = climb(xlay, "gx", x_levels, me_x, (block, block))
+        [vmem(2 * ylay.answer_rows, nz), vmem(nx * 2 * TILE, nz)],
+        mebibytes=8,
+    )
+    x_owns, x_gots, _ = climb(xlay, "gx", x_levels, me_x, (block, block))
     (grad,) = call(
         functools.partial(x_kernel, (nx, ny), xlay, x_levels),
         "x_solve",
-        (me_x, *x_owns, *x_gots, xinv, ay, ghost, w, before, after, cour, upw),
+        (me_x, *x_owns, *x_gots, xinv, ginv, ay, ghost, w, before, after, flows),
         [(comps, rows, nz)],
         [
-            vmem(comps, rows + ny, nz), vmem(comps, rows, nz), vmem(nx * 2 * TILE, nz),
+            vmem(comps, rows, nz), vmem(comps, rows + 2 * ny, nz), vmem(nx * 2 * TILE, nz),
             vmem(xlay.answer_rows, nz), pltpu.SemaphoreType.DMA((4,)),
         ],
         out_spaces="h",
+        mebibytes=12,
     )
     return grad.reshape(comps, nx, ny, nz)
 

time: 49.9 us -> 40 us (0.80)
  local copies, waits for them, and re-layouts: 9.06 us -> 2.55 us
  Pallas kernels: 13.5 us -> 11 us
  waiting for transfers between devices: 16.9 us -> 16.2 us
    unnamed x22 -> x8, local copies, waits for them, and re-layouts: 9.06 us -> 2.55 us
    pallas_call x7 -> x8, Pallas kernels: 13.5 us -> 11 us  [call(): pl.pallas_call(kernel, name=name, out_shape=[jax.ShapeDtypeStruct(shape,...]
    ppermute x6, waiting for transfers between devices: 16.9 us -> 16.2 us  [exchange(): return lax.ppermute(rows, axis, [(i, i ^ 1 << bit) for i in range(count)])]
  transfers between devices with their start and end apart: 6 -> 6, of which waited for: 6 -> 6; matrix products, arithmetic and copies ran while one was open for 0% -> 0% of each run, Pallas kernels for 0% -> 1%
where the time goes in v2:
time: 40 us; the launch traced here: 39.8 us
  waiting for transfers between devices  16.2 us (40%)
  Pallas kernels  11 us (28%)
  starting transfers between devices  10 us (25%)
  local copies, waits for them, and re-layouts  2.55 us (6%)
    ppermute x6, waiting for transfers between devices, exchange(): return lax.ppermute(rows, axis, [(i, i ^ 1 << bit) for i in range(count)])  16.2 us
    pallas_call x8, Pallas kernels, call(): pl.pallas_call(kernel, name=name, out_shape=[jax.ShapeDtypeStruct(shape,...  11 us
    ppermute x6, starting transfers between devices, exchange(): return lax.ppermute(rows, axis, [(i, i ^ 1 << bit) for i in range(count)])  10 us
    unnamed x8, local copies, waits for them, and re-layouts  2.55 us
  transfers between devices with their start and end apart: 6, of which 6 were waited for; matrix products, arithmetic and copies ran while one was open for 0% of the time, Pallas kernels for 1%

profile of v2, /device:TPU:0, one launch (start us, length us, event | category | flops | bytes accessed | tf_op | source)
XLA Modules:
  0.0 39.8 jit_solution(12784195434532903729)
XLA Ops:
  0.0 0.0 copy-start
  0.0 5.3 %z_solve.1 = (f32[6,512,128]{2,1,0:T(8,128)S(1)}, f32[512,128]{1,0:T(8,128)S(1)}, f32[512,128]{1,0:T(8,128)S(1)}, f32[304,128]{1,0:T(8,128)S(1)}, f32[304,128]{1,0:T(8,128)S(1)}) custom-call(s32[1]{0:T(128)} %bitcast.1.me_ref, f32[6,512,128]{2,1,0:T(8,128)} %bitcast.12, f32[512,128]{1,0:T(8,128)} %bitcast.13, s32[512,128]{1,0:T(8,128)} %bitcast.14, ...), custom_call_target="tpu_custom_call" | custom-call | tf_op jit(solution)/shard_map/z_solve/pallas_call | solution.py:620
  5.3 0.5 %collective-permute-start = (f32[304,128]{1,0:T(8,128)S(1)}, f32[304,128]{1,0:T(8,128)S(1)}, u32[]{:S(2)}, u32[]{:S(2)}) collective-permute-start(f32[304,128]{1,0:T(8,128)S(1)} %get-tuple-element.29), channel_id=1, source_target_pairs={{0,1},{1,0},{2,3},{3,2},{4,5},{5,4},{6,7},{7,6},{8,9},{9,8},{10,11... | collective-permute-start | bytes 466952 | tf_op jit(solution)/shard_map/ppermute | solution.py:633
  5.8 1.0 %collective-permute-done.other.refs_3_ = f32[304,128]{1,0:T(8,128)S(1)} collective-permute-done((f32[304,128]{1,0:T(8,128)S(1)}, f32[304,128]{1,0:T(8,128)S(1)}, u32[]{:S(2)}, u32[]{:S(2)}) %collective-permute-start) | collective-permute-done | bytes 155680 | tf_op jit(solution)/shard_map/ppermute | solution.py:633
  6.9 2.9 %collective-permute-start.1 = (f32[304,128]{1,0:T(8,128)S(1)}, f32[304,128]{1,0:T(8,128)S(1)}, u32[]{:S(2)}, u32[]{:S(2)}) collective-permute-start(f32[304,128]{1,0:T(8,128)S(1)} %gy_merge_0.1.after.own.refs_1_), channel_id=1, source_target_pairs={{0,2},{1,3},{2,0},{3,1},{4,6},{5,7},{6,4},{7,5},{8,10},{9,11},{10,... | collective-permute-start | bytes 466952 | tf_op jit(solution)/shard_map/ppermute | solution.py:633
  9.8 0.0 copy-done
  9.8 0.0 copy-done.1
  9.8 0.3 x_coefficients.1
  10.1 4.0 %collective-permute-done.1.other.refs_4_ = f32[304,128]{1,0:T(8,128)S(1)} collective-permute-done((f32[304,128]{1,0:T(8,128)S(1)}, f32[304,128]{1,0:T(8,128)S(1)}, u32[]{:S(2)}, u32[]{:S(2)}) %collective-permute-start.1) | collective-permute-done | bytes 155680 | tf_op jit(solution)/shard_map/ppermute | solution.py:633
  14.1 1.9 %collective-permute-start.2 = (f32[144,128]{1,0:T(8,128)S(1)}, f32[144,128]{1,0:T(8,128)S(1)}, u32[]{:S(2)}, u32[]{:S(2)}) collective-permute-start(f32[144,128]{1,0:T(8,128)S(1)} %get-tuple-element.33), channel_id=1, source_target_pairs={{0,4},{1,5},{2,6},{3,7},{4,0},{5,1},{6,2},{7,3},{8,12},{9,13},{10,... | collective-permute-start | bytes 221192 | tf_op jit(solution)/shard_map/ppermute | solution.py:633
  16.0 2.6 %collective-permute-done.2.refs_5_ = f32[144,128]{1,0:T(8,128)S(1)} collective-permute-done((f32[144,128]{1,0:T(8,128)S(1)}, f32[144,128]{1,0:T(8,128)S(1)}, u32[]{:S(2)}, u32[]{:S(2)}) %collective-permute-start.2) | collective-permute-done | bytes 73760 | tf_op jit(solution)/shard_map/ppermute | solution.py:633
  18.6 0.1 y_reduced.1
  18.7 0.1 collective-permute-start.3
  18.7 1.3 %collective-permute-done.3.got = f32[256,128]{1,0:T(8,128)S(1)} collective-permute-done((f32[256,128]{1,0:T(8,128)S(1)}, f32[256,128]{1,0:T(8,128)S(1)}, u32[]{:S(2)}, u32[]{:S(2)}) %collective-permute-start.3) | collective-permute-done | bytes 131104 | tf_op jit(solution)/shard_map/ppermute | solution.py:633
  20.1 1.9 %y_solve.1 = (f32[6,512,128]{2,1,0:T(8,128)S(1)}, f32[512,128]{1,0:T(8,128)S(1)}, f32[312,128]{1,0:T(8,128)S(1)}, f32[512,128]{1,0:T(8,128)S(1)}, f32[64,128]{1,0:T(8,128)S(1)}, /*index=5*/f32[64,128]{1,0:T(8,128)S(1)}) custom-call(s32[1]{0:T(128)} %bitcast.1.me_ref, f32[6,512,128]{2,1,0:T(8,128)S(1)} %get-tuple-element.27.az, ...), custom_call_target="tpu_custom_call" | custom-call | tf_op jit(solution)/shard_map/y_solve/pallas_call | solution.py:620
  22.0 0.0 copy-start.2
  22.0 1.1 %copy-done.2 = f32[6,512,128]{2,1,0:T(8,128)} copy-done((f32[6,512,128]{2,1,0:T(8,128)}, f32[6,512,128]{2,1,0:T(8,128)S(1)}, u32[]{:S(2)}) %copy-start.2) | copy-done | bytes 1572888
  23.1 1.8 %collective-permute-start.4 = (f32[312,128]{1,0:T(8,128)S(1)}, f32[312,128]{1,0:T(8,128)S(1)}, u32[]{:S(2)}, u32[]{:S(2)}) collective-permute-start(f32[312,128]{1,0:T(8,128)S(1)} %get-tuple-element.39.own.refs_0_), channel_id=1, source_target_pairs={{0,8},{8,0},{16,24},{24,16},{1,9},{9,1},{17,25},{25,17},{2,10},{10... | collective-permute-start | bytes 479240 | tf_op jit(solution)/shard_map/ppermute | solution.py:633
  24.9 4.4 %collective-permute-done.4.other.refs_2_ = f32[312,128]{1,0:T(8,128)S(1)} collective-permute-done((f32[312,128]{1,0:T(8,128)S(1)}, f32[312,128]{1,0:T(8,128)S(1)}, u32[]{:S(2)}, u32[]{:S(2)}) %collective-permute-start.4) | collective-permute-done | bytes 159776 | tf_op jit(solution)/shard_map/ppermute | solution.py:633
  29.4 0.1 gx_merge_0.1
  29.4 2.9 %collective-permute-start.5 = (f32[152,128]{1,0:T(8,128)S(1)}, f32[152,128]{1,0:T(8,128)S(1)}, u32[]{:S(2)}, u32[]{:S(2)}) collective-permute-start(f32[152,128]{1,0:T(8,128)S(1)} %get-tuple-element.41), channel_id=1, source_target_pairs={{0,16},{8,24},{16,0},{24,8},{1,17},{9,25},{17,1},{25,9},{2,18},{10... | collective-permute-start | bytes 233480 | tf_op jit(solution)/shard_map/ppermute | solution.py:633
  32.3 2.9 %collective-permute-done.5.refs_3_ = f32[152,128]{1,0:T(8,128)S(1)} collective-permute-done((f32[152,128]{1,0:T(8,128)S(1)}, f32[152,128]{1,0:T(8,128)S(1)}, u32[]{:S(2)}, u32[]{:S(2)}) %collective-permute-start.5) | collective-permute-done | bytes 77856 | tf_op jit(solution)/shard_map/ppermute | solution.py:633
  35.1 1.4 %copy-done.3 = f32[6,512,128]{2,1,0:T(8,128)S(1)} copy-done((f32[6,512,128]{2,1,0:T(8,128)S(1)}, f32[6,512,128]{2,1,0:T(8,128)}, u32[]{:S(2)}) %copy-start.3) | copy-done | bytes 1572888
  36.6 3.3 %x_solve.1 = f32[6,512,128]{2,1,0:T(8,128)} custom-call(s32[1]{0:T(128)} %bitcast.me_ref, f32[312,128]{1,0:T(8,128)S(1)} %get-tuple-element.39.own.refs_0_, f32[312,128]{1,0:T(8,128)S(1)} %get-tuple-element.40.refs_1_, f32[312,128]{1,0:T(8,128)S(1)} %collective-permute-done.4.other.refs_2_, f32[152,128]{1,0:T(8,128)S(1)} %collective-permute-done.5.refs_3_, ...), custom_call_target="tpu_custom_call" | custom-call | tf_op jit(solution)/shard_map/x_solve/pallas_call | solution.py:620
  (4 shorter events, 0.1 us)
Async XLA Ops:
  0.0 9.8 %copy-start = (f32[3,32,16,128]{3,2,1,0:T(8,128)S(1)}, f32[3,32,16,128]{3,2,1,0:T(8,128)}, u32[]{:S(2)}) copy-start(f32[3,32,16,128]{3,2,1,0:T(8,128)} %param.8) | copy-start | bytes 2359300
  0.0 9.8 %copy-start.1 = (s32[3,32,16,128]{3,2,1,0:T(8,128)S(1)}, s32[3,32,16,128]{3,2,1,0:T(8,128)}, u32[]{:S(2)}) copy-start(s32[3,32,16,128]{3,2,1,0:T(8,128)} %param.9) | copy-start | bytes 2359300
  5.3 1.5 %collective-permute-start = (f32[304,128]{1,0:T(8,128)S(1)}, f32[304,128]{1,0:T(8,128)S(1)}, u32[]{:S(2)}, u32[]{:S(2)}) collective-permute-start(f32[304,128]{1,0:T(8,128)S(1)} %get-tuple-element.29), channel_id=1, source_target_pairs={{0,1},{1,0},{2,3},{3,2},{4,5},{5,4},{6,7},{7,6},{8,9},{9,8},{10,11... | collective-permute-start | bytes 466952 | tf_op jit(solution)/shard_map/ppermute | solution.py:633
  6.9 7.2 %collective-permute-start.1 = (f32[304,128]{1,0:T(8,128)S(1)}, f32[304,128]{1,0:T(8,128)S(1)}, u32[]{:S(2)}, u32[]{:S(2)}) collective-permute-start(f32[304,128]{1,0:T(8,128)S(1)} %gy_merge_0.1.after.own.refs_1_), channel_id=1, source_target_pairs={{0,2},{1,3},{2,0},{3,1},{4,6},{5,7},{6,4},{7,5},{8,10},{9,11},{10,... | collective-permute-start | bytes 466952 | tf_op jit(solution)/shard_map/ppermute | solution.py:633
  14.1 4.4 %collective-permute-start.2 = (f32[144,128]{1,0:T(8,128)S(1)}, f32[144,128]{1,0:T(8,128)S(1)}, u32[]{:S(2)}, u32[]{:S(2)}) collective-permute-start(f32[144,128]{1,0:T(8,128)S(1)} %get-tuple-element.33), channel_id=1, source_target_pairs={{0,4},{1,5},{2,6},{3,7},{4,0},{5,1},{6,2},{7,3},{8,12},{9,13},{10,... | collective-permute-start | bytes 221192 | tf_op jit(solution)/shard_map/ppermute | solution.py:633
  18.7 1.4 %collective-permute-start.3 = (f32[256,128]{1,0:T(8,128)S(1)}, f32[256,128]{1,0:T(8,128)S(1)}, u32[]{:S(2)}, u32[]{:S(2)}) collective-permute-start(f32[256,128]{1,0:T(8,128)S(1)} %get-tuple-element.35), channel_id=1, source_target_pairs={{0,1},{1,0},{2,3},{3,2},{4,5},{5,4},{6,7},{7,6},{8,9},{9,8},{10,11... | collective-permute-start | bytes 393224 | tf_op jit(solution)/shard_map/ppermute | solution.py:633
  22.0 1.1 %copy-start.2 = (f32[6,512,128]{2,1,0:T(8,128)}, f32[6,512,128]{2,1,0:T(8,128)S(1)}, u32[]{:S(2)}) copy-start(f32[6,512,128]{2,1,0:T(8,128)S(1)} %get-tuple-element.44.refs_6_) | copy-start | bytes 4718596
  23.1 6.2 %collective-permute-start.4 = (f32[312,128]{1,0:T(8,128)S(1)}, f32[312,128]{1,0:T(8,128)S(1)}, u32[]{:S(2)}, u32[]{:S(2)}) collective-permute-start(f32[312,128]{1,0:T(8,128)S(1)} %get-tuple-element.39.own.refs_0_), channel_id=1, source_target_pairs={{0,8},{8,0},{16,24},{24,16},{1,9},{9,1},{17,25},{25,17},{2,10},{10... | collective-permute-start | bytes 479240 | tf_op jit(solution)/shard_map/ppermute | solution.py:633
  29.4 5.7 %collective-permute-start.5 = (f32[152,128]{1,0:T(8,128)S(1)}, f32[152,128]{1,0:T(8,128)S(1)}, u32[]{:S(2)}, u32[]{:S(2)}) collective-permute-start(f32[152,128]{1,0:T(8,128)S(1)} %get-tuple-element.41), channel_id=1, source_target_pairs={{0,16},{8,24},{16,0},{24,8},{1,17},{9,25},{17,1},{25,9},{2,18},{10... | collective-permute-start | bytes 233480 | tf_op jit(solution)/shard_map/ppermute | solution.py:633
  35.1 1.4 %copy-start.3 = (f32[6,512,128]{2,1,0:T(8,128)S(1)}, f32[6,512,128]{2,1,0:T(8,128)}, u32[]{:S(2)}) copy-start(f32[6,512,128]{2,1,0:T(8,128)} %copy-done.2) | copy-start | bytes 4718596

commit v3 on v2

--- a/solution.py
+++ b/solution.py
@@ -325,17 +325,15 @@
         post(lay.edge + 2 * e * half, weight)
         post(lay.edge + (2 * e + 1) * half, weight * flow)
 
-    sums = sum_matrix()
+    sums = jnp.concatenate([sum_matrix()] * 3, axis=0)
     for c in range(COMPS):
         pltpu.make_async_copy(cot_any.at[c], cot.at[c], in_sems.at[c]).wait()
-        for t in range(tiles):
-            span = pl.ds(t * LANES, LANES)
-            cells, up, down = cot[c, span, :], phi[span, :], psi[span, :]
-            wide = jnp.concatenate([up * cells, down * cells], axis=1)
-            found = sum(
-                jnp.dot(part, sums, preferred_element_type=jnp.float32) for part in split3(wide)
-            )
-            az[c, span, :] = w_out[span, :] * (down * found[:, :LANES] + up * found[:, LANES:])
+        cells, up, down = cot[c], phi[...], psi[...]
+        high, middle, low = split3(jnp.concatenate([up * cells, down * cells], axis=1))
+        found = jnp.dot(
+            jnp.concatenate([high, middle, low], axis=1), sums, preferred_element_type=jnp.float32
+        )
+        az[c] = w_out[...] * (down * found[:, :LANES] + up * found[:, LANES:])
         first = jnp.zeros((nx, LANES), jnp.float32)
         last = jnp.zeros((nx, LANES), jnp.float32)
         for y in range(ny):
@@ -610,17 +608,22 @@
         "v": pl.BlockSpec(memory_space=pltpu.VMEM),
         "h": pl.BlockSpec(memory_space=pltpu.HBM),
         "s": pl.BlockSpec(memory_space=pltpu.SMEM),
+        "k": pl.BlockSpec(memory_space=pltpu.VMEM),
     }
+    held = {"h": pltpu.HBM, "k": pltpu.VMEM}
     spaces = spaces or "s" + "v" * (len(operands) - 1)
     out_spaces = out_spaces or "v" * len(outs)
     operands = [
-        pltpu.with_memory_space_constraint(o, pltpu.HBM) if s == "h" else o
+        pltpu.with_memory_space_constraint(o, held[s]) if s in held else o
         for o, s in zip(operands, spaces)
     ]
     return pl.pallas_call(
         kernel,
         name=name,
-        out_shape=[jax.ShapeDtypeStruct(shape, jnp.float32) for shape in outs],
+        out_shape=[
+            held[s](shape, jnp.float32) if s in held else jax.ShapeDtypeStruct(shape, jnp.float32)
+            for shape, s in zip(outs, out_spaces)
+        ],
         in_specs=[pick_space[s] for s in spaces],
         out_specs=[pick_space[s] for s in out_spaces],
         scratch_shapes=list(scratch),
@@ -712,6 +715,7 @@
             (2 * nx, nz), (2 * nx, nz),
         ],
         [vmem(2 * ylay.answer_rows, nz), vmem(nx * 2 * TILE, nz)],
+        out_spaces="kvvvvv",
         mebibytes=8,
     )
     x_owns, x_gots, _ = climb(xlay, "gx", x_levels, me_x, (block, block))
@@ -724,6 +728,7 @@
             vmem(comps, rows, nz), vmem(comps, rows + 2 * ny, nz), vmem(nx * 2 * TILE, nz),
             vmem(xlay.answer_rows, nz), pltpu.SemaphoreType.DMA((4,)),
         ],
+        spaces="s" + "v" * (2 * x_levels + 2) + "k" + "v" * 5,
         out_spaces="h",
         mebibytes=12,
     )

time: 40 us -> 40.9 us (1.022)
  Pallas kernels: 11 us -> 11.9 us
    pallas_call x8, Pallas kernels: 11 us -> 11.9 us  [call(): pl.pallas_call(kernel, name=name, out_shape=[held[s](shape, jnp.float32)...]
where the time goes in v3:
time: 40.9 us; the launch traced here: 40.8 us
  waiting for transfers between devices  16.3 us (40%)
  Pallas kernels  11.9 us (29%)
  starting transfers between devices  9.99 us (24%)
  local copies, waits for them, and re-layouts  2.55 us (6%)
    ppermute x6, waiting for transfers between devices, exchange(): return lax.ppermute(rows, axis, [(i, i ^ 1 << bit) for i in range(count)])  16.3 us
    pallas_call x8, Pallas kernels, call(): pl.pallas_call(kernel, name=name, out_shape=[held[s](shape, jnp.float32)...  11.9 us
    ppermute x6, starting transfers between devices, exchange(): return lax.ppermute(rows, axis, [(i, i ^ 1 << bit) for i in range(count)])  9.99 us
    unnamed x8, local copies, waits for them, and re-layouts  2.55 us
  transfers between devices with their start and end apart: 6, of which 6 were waited for; matrix products, arithmetic and copies ran while one was open for 0% of the time, Pallas kernels for 1%

profile of v3, /device:TPU:0, one launch (start us, length us, event | category | flops | bytes accessed | tf_op | source)
XLA Modules:
  0.0 40.8 jit_solution(1749144839151567335)
XLA Ops:
  0.0 0.0 copy-start
  0.0 6.2 %z_solve.1 = (f32[6,512,128]{2,1,0:T(8,128)S(1)}, f32[512,128]{1,0:T(8,128)S(1)}, f32[512,128]{1,0:T(8,128)S(1)}, f32[304,128]{1,0:T(8,128)S(1)}, f32[304,128]{1,0:T(8,128)S(1)}) custom-call(s32[1]{0:T(128)} %bitcast.1.me_ref, f32[6,512,128]{2,1,0:T(8,128)} %bitcast.12, f32[512,128]{1,0:T(8,128)} %bitcast.13, s32[512,128]{1,0:T(8,128)} %bitcast.14, ...), custom_call_target="tpu_custom_call" | custom-call | tf_op jit(solution)/shard_map/z_solve/pallas_call | solution.py:620
  6.2 0.5 %collective-permute-start = (f32[304,128]{1,0:T(8,128)S(1)}, f32[304,128]{1,0:T(8,128)S(1)}, u32[]{:S(2)}, u32[]{:S(2)}) collective-permute-start(f32[304,128]{1,0:T(8,128)S(1)} %get-tuple-element.29), channel_id=1, source_target_pairs={{0,1},{1,0},{2,3},{3,2},{4,5},{5,4},{6,7},{7,6},{8,9},{9,8},{10,11... | collective-permute-start | bytes 466952 | tf_op jit(solution)/shard_map/ppermute | solution.py:636
  6.7 1.0 %collective-permute-done.other.refs_3_ = f32[304,128]{1,0:T(8,128)S(1)} collective-permute-done((f32[304,128]{1,0:T(8,128)S(1)}, f32[304,128]{1,0:T(8,128)S(1)}, u32[]{:S(2)}, u32[]{:S(2)}) %collective-permute-start) | collective-permute-done | bytes 155680 | tf_op jit(solution)/shard_map/ppermute | solution.py:636
  7.8 2.9 %collective-permute-start.1 = (f32[304,128]{1,0:T(8,128)S(1)}, f32[304,128]{1,0:T(8,128)S(1)}, u32[]{:S(2)}, u32[]{:S(2)}) collective-permute-start(f32[304,128]{1,0:T(8,128)S(1)} %gy_merge_0.1.after.own.refs_1_), channel_id=1, source_target_pairs={{0,2},{1,3},{2,0},{3,1},{4,6},{5,7},{6,4},{7,5},{8,10},{9,11},{10,... | collective-permute-start | bytes 466952 | tf_op jit(solution)/shard_map/ppermute | solution.py:636
  10.7 0.0 copy-done
  10.7 0.0 copy-done.1
  10.7 0.3 x_coefficients.1
  11.0 4.0 %collective-permute-done.1.other.refs_4_ = f32[304,128]{1,0:T(8,128)S(1)} collective-permute-done((f32[304,128]{1,0:T(8,128)S(1)}, f32[304,128]{1,0:T(8,128)S(1)}, u32[]{:S(2)}, u32[]{:S(2)}) %collective-permute-start.1) | collective-permute-done | bytes 155680 | tf_op jit(solution)/shard_map/ppermute | solution.py:636
  15.1 1.8 %collective-permute-start.2 = (f32[144,128]{1,0:T(8,128)S(1)}, f32[144,128]{1,0:T(8,128)S(1)}, u32[]{:S(2)}, u32[]{:S(2)}) collective-permute-start(f32[144,128]{1,0:T(8,128)S(1)} %get-tuple-element.33), channel_id=1, source_target_pairs={{0,4},{1,5},{2,6},{3,7},{4,0},{5,1},{6,2},{7,3},{8,12},{9,13},{10,... | collective-permute-start | bytes 221192 | tf_op jit(solution)/shard_map/ppermute | solution.py:636
  16.9 2.6 %collective-permute-done.2.refs_5_ = f32[144,128]{1,0:T(8,128)S(1)} collective-permute-done((f32[144,128]{1,0:T(8,128)S(1)}, f32[144,128]{1,0:T(8,128)S(1)}, u32[]{:S(2)}, u32[]{:S(2)}) %collective-permute-start.2) | collective-permute-done | bytes 73760 | tf_op jit(solution)/shard_map/ppermute | solution.py:636
  19.5 0.1 y_reduced.1
  19.6 0.1 collective-permute-start.3
  19.7 1.3 %collective-permute-done.3.got = f32[256,128]{1,0:T(8,128)S(1)} collective-permute-done((f32[256,128]{1,0:T(8,128)S(1)}, f32[256,128]{1,0:T(8,128)S(1)}, u32[]{:S(2)}, u32[]{:S(2)}) %collective-permute-start.3) | collective-permute-done | bytes 131104 | tf_op jit(solution)/shard_map/ppermute | solution.py:636
  21.0 1.9 %y_solve.1 = (f32[6,512,128]{2,1,0:T(8,128)S(1)}, f32[512,128]{1,0:T(8,128)S(1)}, f32[312,128]{1,0:T(8,128)S(1)}, f32[512,128]{1,0:T(8,128)S(1)}, f32[64,128]{1,0:T(8,128)S(1)}, /*index=5*/f32[64,128]{1,0:T(8,128)S(1)}) custom-call(s32[1]{0:T(128)} %bitcast.1.me_ref, f32[6,512,128]{2,1,0:T(8,128)S(1)} %get-tuple-element.27.az, ...), custom_call_target="tpu_custom_call" | custom-call | tf_op jit(solution)/shard_map/y_solve/pallas_call | solution.py:620
  22.9 0.0 copy-start.2
  22.9 1.1 %copy-done.2 = f32[6,512,128]{2,1,0:T(8,128)} copy-done((f32[6,512,128]{2,1,0:T(8,128)}, f32[6,512,128]{2,1,0:T(8,128)S(1)}, u32[]{:S(2)}) %copy-start.2) | copy-done | bytes 1572888
  24.0 1.8 %collective-permute-start.4 = (f32[312,128]{1,0:T(8,128)S(1)}, f32[312,128]{1,0:T(8,128)S(1)}, u32[]{:S(2)}, u32[]{:S(2)}) collective-permute-start(f32[312,128]{1,0:T(8,128)S(1)} %get-tuple-element.39.own.refs_0_), channel_id=1, source_target_pairs={{0,8},{8,0},{16,24},{24,16},{1,9},{9,1},{17,25},{25,17},{2,10},{10... | collective-permute-start | bytes 479240 | tf_op jit(solution)/shard_map/ppermute | solution.py:636
  25.9 4.4 %collective-permute-done.4.other.refs_2_ = f32[312,128]{1,0:T(8,128)S(1)} collective-permute-done((f32[312,128]{1,0:T(8,128)S(1)}, f32[312,128]{1,0:T(8,128)S(1)}, u32[]{:S(2)}, u32[]{:S(2)}) %collective-permute-start.4) | collective-permute-done | bytes 159776 | tf_op jit(solution)/shard_map/ppermute | solution.py:636
  30.3 0.1 gx_merge_0.1
  30.3 2.8 %collective-permute-start.5 = (f32[152,128]{1,0:T(8,128)S(1)}, f32[152,128]{1,0:T(8,128)S(1)}, u32[]{:S(2)}, u32[]{:S(2)}) collective-permute-start(f32[152,128]{1,0:T(8,128)S(1)} %get-tuple-element.41), channel_id=1, source_target_pairs={{0,16},{8,24},{16,0},{24,8},{1,17},{9,25},{17,1},{25,9},{2,18},{10... | collective-permute-start | bytes 233480 | tf_op jit(solution)/shard_map/ppermute | solution.py:636
  33.2 2.9 %collective-permute-done.5.refs_3_ = f32[152,128]{1,0:T(8,128)S(1)} collective-permute-done((f32[152,128]{1,0:T(8,128)S(1)}, f32[152,128]{1,0:T(8,128)S(1)}, u32[]{:S(2)}, u32[]{:S(2)}) %collective-permute-start.5) | collective-permute-done | bytes 77856 | tf_op jit(solution)/shard_map/ppermute | solution.py:636
  36.1 1.4 %copy-done.3 = f32[6,512,128]{2,1,0:T(8,128)S(1)} copy-done((f32[6,512,128]{2,1,0:T(8,128)S(1)}, f32[6,512,128]{2,1,0:T(8,128)}, u32[]{:S(2)}) %copy-start.3) | copy-done | bytes 1572888
  37.5 3.3 %x_solve.1 = f32[6,512,128]{2,1,0:T(8,128)} custom-call(s32[1]{0:T(128)} %bitcast.me_ref, f32[312,128]{1,0:T(8,128)S(1)} %get-tuple-element.39.own.refs_0_, f32[312,128]{1,0:T(8,128)S(1)} %get-tuple-element.40.refs_1_, f32[312,128]{1,0:T(8,128)S(1)} %collective-permute-done.4.other.refs_2_, f32[152,128]{1,0:T(8,128)S(1)} %collective-permute-done.5.refs_3_, ...), custom_call_target="tpu_custom_call" | custom-call | tf_op jit(solution)/shard_map/x_solve/pallas_call | solution.py:620
  (4 shorter events, 0.1 us)
Async XLA Ops:
  0.0 10.7 %copy-start = (f32[3,32,16,128]{3,2,1,0:T(8,128)S(1)}, f32[3,32,16,128]{3,2,1,0:T(8,128)}, u32[]{:S(2)}) copy-start(f32[3,32,16,128]{3,2,1,0:T(8,128)} %param.8) | copy-start | bytes 2359300
  0.0 10.7 %copy-start.1 = (s32[3,32,16,128]{3,2,1,0:T(8,128)S(1)}, s32[3,32,16,128]{3,2,1,0:T(8,128)}, u32[]{:S(2)}) copy-start(s32[3,32,16,128]{3,2,1,0:T(8,128)} %param.9) | copy-start | bytes 2359300
  6.2 1.5 %collective-permute-start = (f32[304,128]{1,0:T(8,128)S(1)}, f32[304,128]{1,0:T(8,128)S(1)}, u32[]{:S(2)}, u32[]{:S(2)}) collective-permute-start(f32[304,128]{1,0:T(8,128)S(1)} %get-tuple-element.29), channel_id=1, source_target_pairs={{0,1},{1,0},{2,3},{3,2},{4,5},{5,4},{6,7},{7,6},{8,9},{9,8},{10,11... | collective-permute-start | bytes 466952 | tf_op jit(solution)/shard_map/ppermute | solution.py:636
  7.8 7.3 %collective-permute-start.1 = (f32[304,128]{1,0:T(8,128)S(1)}, f32[304,128]{1,0:T(8,128)S(1)}, u32[]{:S(2)}, u32[]{:S(2)}) collective-permute-start(f32[304,128]{1,0:T(8,128)S(1)} %gy_merge_0.1.after.own.refs_1_), channel_id=1, source_target_pairs={{0,2},{1,3},{2,0},{3,1},{4,6},{5,7},{6,4},{7,5},{8,10},{9,11},{10,... | collective-permute-start | bytes 466952 | tf_op jit(solution)/shard_map/ppermute | solution.py:636
  15.1 4.4 %collective-permute-start.2 = (f32[144,128]{1,0:T(8,128)S(1)}, f32[144,128]{1,0:T(8,128)S(1)}, u32[]{:S(2)}, u32[]{:S(2)}) collective-permute-start(f32[144,128]{1,0:T(8,128)S(1)} %get-tuple-element.33), channel_id=1, source_target_pairs={{0,4},{1,5},{2,6},{3,7},{4,0},{5,1},{6,2},{7,3},{8,12},{9,13},{10,... | collective-permute-start | bytes 221192 | tf_op jit(solution)/shard_map/ppermute | solution.py:636
  19.6 1.4 %collective-permute-start.3 = (f32[256,128]{1,0:T(8,128)S(1)}, f32[256,128]{1,0:T(8,128)S(1)}, u32[]{:S(2)}, u32[]{:S(2)}) collective-permute-start(f32[256,128]{1,0:T(8,128)S(1)} %get-tuple-element.35), channel_id=1, source_target_pairs={{0,1},{1,0},{2,3},{3,2},{4,5},{5,4},{6,7},{7,6},{8,9},{9,8},{10,11... | collective-permute-start | bytes 393224 | tf_op jit(solution)/shard_map/ppermute | solution.py:636
  22.9 1.1 %copy-start.2 = (f32[6,512,128]{2,1,0:T(8,128)}, f32[6,512,128]{2,1,0:T(8,128)S(1)}, u32[]{:S(2)}) copy-start(f32[6,512,128]{2,1,0:T(8,128)S(1)} %get-tuple-element.44.refs_6_) | copy-start | bytes 4718596
  24.0 6.2 %collective-permute-start.4 = (f32[312,128]{1,0:T(8,128)S(1)}, f32[312,128]{1,0:T(8,128)S(1)}, u32[]{:S(2)}, u32[]{:S(2)}) collective-permute-start(f32[312,128]{1,0:T(8,128)S(1)} %get-tuple-element.39.own.refs_0_), channel_id=1, source_target_pairs={{0,8},{8,0},{16,24},{24,16},{1,9},{9,1},{17,25},{25,17},{2,10},{10... | collective-permute-start | bytes 479240 | tf_op jit(solution)/shard_map/ppermute | solution.py:636
  30.3 5.7 %collective-permute-start.5 = (f32[152,128]{1,0:T(8,128)S(1)}, f32[152,128]{1,0:T(8,128)S(1)}, u32[]{:S(2)}, u32[]{:S(2)}) collective-permute-start(f32[152,128]{1,0:T(8,128)S(1)} %get-tuple-element.41), channel_id=1, source_target_pairs={{0,16},{8,24},{16,0},{24,8},{1,17},{9,25},{17,1},{25,9},{2,18},{10... | collective-permute-start | bytes 233480 | tf_op jit(solution)/shard_map/ppermute | solution.py:636
  36.1 1.4 %copy-start.3 = (f32[6,512,128]{2,1,0:T(8,128)S(1)}, f32[6,512,128]{2,1,0:T(8,128)}, u32[]{:S(2)}) copy-start(f32[6,512,128]{2,1,0:T(8,128)} %copy-done.2) | copy-start | bytes 4718596

commit v4 on v3

v4 whole, which is shorter than its diff:
```python
import functools

import jax
import jax.numpy as jnp
from jax import lax
from jax.experimental import pallas as pl
from jax.experimental.pallas import tpu as pltpu
from jax.sharding import PartitionSpec as P

COMPS = 6
LANES = 128
TILE = 8
SIDE = TILE // 2


def weight_of(diffusion, phase):
    return 1.0 / (diffusion * (1.0 + 3.0 * phase.astype(jnp.float32)))


def growing_step(value, slope, weight):
    slope = slope + weight * value
    return value + slope, slope


def split3(cells):
    high = cells.astype(jnp.bfloat16)
    rest = cells - high.astype(jnp.float32)
    middle = rest.astype(jnp.bfloat16)
    low = (rest - middle.astype(jnp.float32)).astype(jnp.bfloat16)
    return high, middle, low


def sum_matrix():
    row = lax.broadcasted_iota(jnp.int32, (2 * LANES, 2 * LANES), 0)
    col = lax.broadcasted_iota(jnp.int32, (2 * LANES, 2 * LANES), 1)
    before = (row < LANES) & (col < LANES) & (row <= col)
    after = (row >= LANES) & (col >= LANES) & (row > col)
    return jnp.where(before | after, 1.0, 0.0).astype(jnp.bfloat16)


class Layout:
    def __init__(self, sizes, groups, edges, lines, leads):
        self.sizes, self.groups, self.edges, self.lines, self.leads = sizes, groups, edges, lines, leads
        self.offsets = [sum(sizes[:i]) for i in range(len(sizes))]
        self.total = sum(sizes)
        packed = TILE if groups > 1 else 0
        self.couple = 2 * self.total
        self.packed = self.couple + 3 * lines
        self.edge = self.packed + packed
        self.side_couple = self.total
        self.side_packed = self.side_couple + lines
        self.side_edge = self.side_packed + packed
        extra = 2 * edges * lines
        self.rows = self.edge + extra if leads else self.couple
        self.side_rows = self.side_edge + extra // 2 if leads else self.total
        self.answer_rows = 2 * self.total + (extra if leads else 0)

    def group(self, piece):
        return 1 if self.groups > 1 and piece == len(self.sizes) - 1 else 0


def read_pieces(lay, ref, base=0):
    return [ref[pl.ds(base + o, n), :] for o, n in zip(lay.offsets, lay.sizes)]


def write_pieces(lay, ref, values, base=0):
    for o, n, value in zip(lay.offsets, lay.sizes, values):
        ref[pl.ds(base + o, n), :] = value


def read_rows(ref, base, count, lines):
    return [ref[pl.ds(base + i * lines, lines), :] for i in range(count)]


def write_rows(ref, base, values, lines):
    for i, value in enumerate(values):
        ref[pl.ds(base + i * lines, lines), :] = value


def two_sides(low, high):
    return jnp.concatenate(
        [jnp.broadcast_to(low, (SIDE, LANES)), jnp.broadcast_to(high, (SIDE, LANES))], axis=0
    )


def read_pair(ref, row):
    return two_sides(ref[pl.ds(row, 1), :], ref[pl.ds(row + 1, 1), :])


def write_pair(ref, row, value):
    ref[pl.ds(row, 1), :] = value[:1]
    ref[pl.ds(row + 1, 1), :] = value[SIDE : SIDE + 1]


def read_block(lay, ref, lead, lead_ref):
    n = lead.lines
    block = {"first": read_pieces(lay, ref), "last": read_pieces(lay, ref, lay.total)}
    for e, name in enumerate(("near", "cross", "far")):
        entry = [lead_ref[pl.ds(lead.couple + e * n, n), :]]
        if lead.groups > 1:
            entry.append(read_pair(lead_ref, lead.packed + 2 * e))
        block[name] = entry
    block["head"] = read_rows(lead_ref, lead.edge, lead.edges, n)
    block["tail"] = read_rows(lead_ref, lead.edge + lead.edges * n, lead.edges, n)
    return block


def write_block(lay, ref, block):
    n = lay.lines
    write_pieces(lay, ref, block["first"])
    write_pieces(lay, ref, block["last"], lay.total)
    if not lay.leads:
        return
    for e, name in enumerate(("near", "cross", "far")):
        ref[pl.ds(lay.couple + e * n, n), :] = block[name][0]
        if lay.groups > 1:
            write_pair(ref, lay.packed + 2 * e, block[name][1])
    if lay.groups > 1:
        ref[pl.ds(lay.packed + 6, 2), :] = jnp.zeros((2, LANES), jnp.float32)
    write_rows(ref, lay.edge, block["head"], n)
    write_rows(ref, lay.edge + lay.edges * n, block["tail"], n)


def pick(upper, low, high):
    if isinstance(low, list):
        return [pick(upper, a, b) for a, b in zip(low, high)]
    return jnp.where(jnp.full(low.shape, upper, jnp.int32) == 1, high, low)


def write_side(lay, ref, block, upper):
    n = lay.lines
    write_pieces(lay, ref, pick(upper, block["last"], block["first"]))
    if not lay.leads:
        return
    pair = pick(upper, block["far"], block["near"])
    ref[pl.ds(lay.side_couple, n), :] = pair[0]
    if lay.groups > 1:
        ref[pl.ds(lay.side_packed, TILE), :] = pair[1]
    write_rows(ref, lay.side_edge, pick(upper, block["tail"], block["head"]), n)


def read_side(lay, ref, lead, lead_ref):
    n = lead.lines
    couple = [lead_ref[pl.ds(lead.side_couple, n), :]]
    if lead.groups > 1:
        couple.append(lead_ref[pl.ds(lead.side_packed, TILE), :])
    return read_pieces(lay, ref), couple, read_rows(lead_ref, lead.side_edge, lead.edges, n)


def ordered(upper, own, other):
    low = {name: pick(upper, own[name], other[name]) for name in own}
    high = {name: pick(upper, other[name], own[name]) for name in own}
    return low, high


def joint(low, high):
    return [1.0 / (1.0 - far * near) for far, near in zip(low["far"], high["near"])]


def merge(lay, low, high):
    shrink = joint(low, high)
    groups = range(len(shrink))
    to_low = [low["cross"][g] * shrink[g] for g in groups]
    to_high = [high["cross"][g] * shrink[g] for g in groups]
    span = range(len(lay.sizes))
    of = lay.group
    block = {
        "first": [
            low["first"][i]
            + to_low[of(i)] * (high["first"][i] + high["near"][of(i)] * low["last"][i])
            for i in span
        ],
        "last": [
            high["last"][i]
            + to_high[of(i)] * (low["last"][i] + low["far"][of(i)] * high["first"][i])
            for i in span
        ],
    }
    block["near"] = [low["near"][g] + to_low[g] * low["cross"][g] * high["near"][g] for g in groups]
    block["cross"] = [to_low[g] * high["cross"][g] for g in groups]
    block["far"] = [high["far"][g] + to_high[g] * high["cross"][g] * low["far"][g] for g in groups]
    block["head"] = low["head"]
    block["tail"] = high["tail"]
    return block


def inner(lay, low, high, before, after):
    shrink = joint(low, high)
    low_last, high_first = [], []
    for i in range(len(lay.sizes)):
        g = lay.group(i)
        left = low["last"][i] + low["cross"][g] * before[i]
        right = high["first"][i] + high["cross"][g] * after[i]
        low_last.append((left + low["far"][g] * right) * shrink[g])
        high_first.append((right + high["near"][g] * left) * shrink[g])
    return low_last, high_first


def merge_kernel(lay, lead, bit, top, me_ref, own, other, *refs):
    out, *side = refs[-2:] if top else refs[-1:]
    lead_own, lead_other = (own, other) if lay.leads else refs[:2]
    upper = (me_ref[0] >> bit) & 1
    low, high = ordered(
        upper, read_block(lay, own, lead, lead_own), read_block(lay, other, lead, lead_other)
    )
    block = merge(lay, low, high)
    write_block(lay, out, block)
    if top:
        write_side(lay, side[0], block, (me_ref[0] >> (bit + 1)) & 1)


def solve_lines(lay, lead, levels, me, refs):
    owns, gots = refs[:levels], refs[levels : 2 * levels]
    lead_owns, lead_gots = owns, gots
    if not lay.leads:
        lead_owns, lead_gots = refs[2 * levels : 3 * levels], refs[3 * levels : 4 * levels]
    top = levels - 1
    upper = (me >> top) & 1
    own = read_block(lay, owns[top], lead, lead_owns[top])
    met, met_couple, met_edge = read_side(lay, gots[top], lead, lead_gots[top])
    facing = pick(upper, own["last"], own["first"])
    couple = pick(upper, own["far"], own["near"])
    shrink = [1.0 / (1.0 - a * b) for a, b in zip(met_couple, couple)]
    found = []
    for i in range(len(lay.sizes)):
        g = lay.group(i)
        found.append((met[i] + met_couple[g] * facing[i]) * shrink[g])
    zeros = [jnp.zeros_like(v) for v in found]
    blank = [jnp.zeros_like(v) for v in met_edge]
    state = (
        pick(upper, zeros, found), pick(upper, found, zeros),
        pick(upper, blank, met_edge), pick(upper, met_edge, blank),
    )
    partner = None
    for level in reversed(range(top)):
        upper = (me >> level) & 1
        low, high = ordered(
            upper,
            read_block(lay, owns[level], lead, lead_owns[level]),
            read_block(lay, gots[level], lead, lead_gots[level]),
        )
        before, after, behind, ahead = state
        low_last, high_first = inner(lay, low, high, before, after)
        lower = (before, high_first, behind, high["head"])
        higher = (low_last, after, low["tail"], ahead)
        state = tuple(pick(upper, a, b) for a, b in zip(lower, higher))
        partner = tuple(pick(upper, a, b) for a, b in zip(higher, lower))
    return state, partner


def write_answer(lay, ref, state):
    before, after, behind, ahead = state
    write_pieces(lay, ref, before)
    write_pieces(lay, ref, after, lay.total)
    if lay.leads:
        write_rows(ref, 2 * lay.total, behind + ahead, lay.lines)


def solve_kernel(lay, lead, levels, me_ref, *refs):
    state, partner = solve_lines(lay, lead, levels, me_ref[0], refs[:-2])
    write_answer(lay, refs[-2], state)
    write_answer(lay, refs[-1], partner)


def corners(weights):
    one = jnp.ones_like(weights[0])
    value, slope, chain = one, one, [one]
    for weight in weights:
        value, slope = growing_step(value, slope, weight)
        chain.append(value)
    back, fall, backs = one, one, []
    for weight in reversed(weights):
        backs.append(back)
        back, fall = growing_step(back, fall, weight)
    backs.reverse()
    return chain, backs, 1.0 / value


def post(lay, both, row, cells):
    half = cells.shape[0] // 2
    for h in range(2):
        both[pl.ds(h * lay.rows + row, half), :] = cells[h * half : (h + 1) * half]


def z_part(dims, lay, me_ref, cot, phi, psi, w, left, right, arrived, az, both, keep, send):
    nx, ny = dims
    tiles = nx * ny // LANES
    sums = sum_matrix()
    for c in range(len(lay.sizes)):
        arrived(c)
        for t in range(tiles):
            span = pl.ds(t * LANES, LANES)
            cells, up, down = cot[c, span, :], phi[span, :], psi[span, :]
            wide = jnp.concatenate([up * cells, down * cells], axis=1)
            found = sum(
                jnp.dot(part, sums, preferred_element_type=jnp.float32) for part in split3(wide)
            )
            az[c, span, :] = w[span, :] * (down * found[:, :LANES] + up * found[:, LANES:])
        first = jnp.zeros((nx, LANES), jnp.float32)
        last = jnp.zeros((nx, LANES), jnp.float32)
        for y in range(ny):
            cells = az[c, pl.ds(y, nx, stride=ny), :]
            span = pl.ds(y * nx, nx)
            first = first + left[span, :] * cells
            last = last + right[span, :] * cells
        post(lay, both, lay.offsets[c], first)
        post(lay, both, lay.total + lay.offsets[c], last)
    mine = me_ref[0] & 1
    keep[...] = both[pl.ds(pl.multiple_of(mine * lay.rows, TILE), lay.rows), :]
    send[...] = both[pl.ds(pl.multiple_of((1 - mine) * lay.rows, TILE), lay.rows), :]


def lead_z_kernel(
    dims, lay, me_ref, cot_any, diff_any, phase_any, cour_any, upw_any,
    keep, send, az, w, inv, left, right, phi, psi,
    cot, diff, phase, cour, upw, wt, pht, pst, both, in_sems, sems,
):
    nx, ny = dims
    tiles = nx * ny // LANES
    half = nx // 2
    small = [(diff_any, diff), (phase_any, phase), (cour_any.at[1], cour), (upw_any.at[1], upw)]
    for i, (source, target) in enumerate(small):
        pltpu.make_async_copy(source, target, sems.at[i]).start()
    for c in range(len(lay.sizes)):
        pltpu.make_async_copy(cot_any.at[c], cot.at[c], in_sems.at[c]).start()

    for i, (source, target) in enumerate(small[:2]):
        pltpu.make_async_copy(source, target, sems.at[i]).wait()
    w[...] = weight_of(diff[...], phase[...])
    for t in range(tiles):
        span = pl.ds(t * LANES, LANES)
        wt[span, :] = w[span, :].T
    ones = jnp.ones((tiles, LANES), jnp.float32)
    value, slope = ones, ones
    back, fall = ones, ones
    for k in range(LANES):
        here = pl.ds(k, tiles, stride=LANES)
        pht[here, :] = value
        value, slope = growing_step(value, slope, wt[here, :])
        there = pl.ds(LANES - 1 - k, tiles, stride=LANES)
        pst[there, :] = back
        back, fall = growing_step(back, fall, wt[there, :])
    scale = 1.0 / value
    for t in range(tiles):
        span = pl.ds(t * LANES, LANES)
        phi[span, :] = pht[span, :].T
        psi[span, :] = (pst[span, :] * scale[t : t + 1]).T

    chain, backs, total = corners([w[pl.ds(y, nx, stride=ny), :] for y in range(ny)])
    for y in range(ny):
        span = pl.ds(y * nx, nx)
        left[span, :] = backs[y] * total
        right[span, :] = chain[y] * total
        inv[span, :] = chain[y] / chain[y + 1]
    post(lay, both, lay.couple, backs[0] * total)
    post(lay, both, lay.couple + half, total)
    post(lay, both, lay.couple + 2 * half, chain[ny - 1] * total)
    for i, (source, target) in enumerate(small[2:]):
        pltpu.make_async_copy(source, target, sems.at[2 + i]).wait()
    for e, y in enumerate((0, ny - 1)):
        edge = pl.ds(y, nx, stride=ny)
        weight = w[edge, :]
        up = cour[edge, :] * upw[edge, :].astype(jnp.float32)
        flow = up if e == 0 else cour[edge, :] - up
        post(lay, both, lay.edge + 2 * e * half, weight)
        post(lay, both, lay.edge + (2 * e + 1) * half, weight * flow)

    def arrived(c):
        pltpu.make_async_copy(cot_any.at[c], cot.at[c], in_sems.at[c]).wait()

    z_part(dims, lay, me_ref, cot, phi, psi, w, left, right, arrived, az, both, keep, send)


def next_z_kernel(
    dims, lay, start, me_ref, cot_any, phi, psi, w, left, right, keep, send, az, cot, both, in_sems,
):
    def copy(c):
        return pltpu.make_async_copy(cot_any.at[start + c], cot.at[c], in_sems.at[c])

    for c in range(len(lay.sizes)):
        copy(c).start()
    z_part(
        dims, lay, me_ref, cot, phi, psi, w, left, right, lambda c: copy(c).wait(), az, both, keep, send
    )


def coef_kernel(dims, w, courant, upwind, after, block, xinv, left, right, flows):
    del after
    nx, ny = dims
    rows = nx * ny
    one = jnp.ones((ny, LANES), jnp.float32)
    value, slope, back, fall = one, one, one, one
    for k in range(nx):
        low, high = pl.ds(k * ny, ny), pl.ds((nx - 1 - k) * ny, ny)
        right[low, :] = value
        left[high, :] = back
        new_value, slope = growing_step(value, slope, w[low, :])
        xinv[low, :] = value / new_value
        end, value = value, new_value
        corner = back
        back, fall = growing_step(back, fall, w[high, :])
    total = 1.0 / value
    block[pl.ds(0, ny), :] = corner * total
    block[pl.ds(ny, ny), :] = total
    block[pl.ds(2 * ny, ny), :] = end * total

    lane = lax.broadcasted_iota(jnp.int32, (ny, LANES), 1)

    def plane(x, carry):
        span = pl.ds(x * ny, ny)
        left[span, :] = left[span, :] * total
        right[span, :] = right[span, :] * total
        own = one
        for d in range(3):
            flow = courant[d, span, :]
            up = flow * upwind[d, span, :].astype(jnp.float32)
            down = flow - up
            own = own + (down - up)
            if d == 2:
                up = jnp.where(lane == 0, 0.0, up)
                down = jnp.where(lane == LANES - 1, 0.0, down)
            flows[pl.ds((1 + 2 * d) * rows + x * ny, ny), :] = up
            flows[pl.ds((2 + 2 * d) * rows + x * ny, ny), :] = down
        flows[span, :] = own
        return carry

    lax.fori_loop(0, nx, plane, 0, unroll=4)
    first, last = pl.ds(0, ny), pl.ds(rows - ny, ny)
    block[pl.ds(3 * ny, ny), :] = w[first, :] * flows[pl.ds(rows, ny), :]
    block[pl.ds(4 * ny, ny), :] = w[last, :] * flows[pl.ds(2 * rows + rows - ny, ny), :]


def sides(before, after, x):
    return two_sides(before[pl.ds(x, 1), :], after[pl.ds(x, 1), :])


def y_kernel(dims, ylay, xlay, me_ref, az, own, got, w, inv, left, right, *refs):
    nx, ny = dims
    half = nx // 2
    comps = len(ylay.sizes)
    if xlay.leads:
        part, _, block, ay, ghost, ginv, gleft, gright, before, after, joined = refs
    else:
        before, after, gleft, gright, block, ay, ghost, joined = refs
    mine = me_ref[0] & 1
    span = ylay.answer_rows
    joined[pl.ds(pl.multiple_of(mine * span, TILE), span), :] = own[...]
    joined[pl.ds(pl.multiple_of((1 - mine) * span, TILE), span), :] = got[...]
    if xlay.leads:
        for h in range(2):
            for e in range(2):
                where = pl.ds(e * nx + h * half, half)
                row = h * span + 2 * ylay.total + e * half
                before[where, :] = joined[pl.ds(row, half), :]
                after[where, :] = joined[pl.ds(row + 2 * half, half), :]
        one = jnp.ones((TILE, LANES), jnp.float32)
        value, slope, back, fall = one, one, one, one
        for k in range(nx):
            low, high = pl.ds(k * TILE, TILE), pl.ds((nx - 1 - k) * TILE, TILE)
            gright[low, :] = value
            gleft[high, :] = back
            new_value, slope = growing_step(value, slope, sides(before, after, k))
            ginv[low, :] = value / new_value
            end, value = value, new_value
            corner = back
            back, fall = growing_step(back, fall, sides(before, after, nx - 1 - k))
        total = 1.0 / value
        gleft[...] = (gleft[...].reshape(nx, TILE, LANES) * total).reshape(nx * TILE, LANES)
        gright[...] = (gright[...].reshape(nx, TILE, LANES) * total).reshape(nx * TILE, LANES)

    ghost[...] = jnp.zeros(ghost.shape, jnp.float32)
    for c in range(comps):
        for h in range(2):
            piece = pl.ds(h * half, half)
            fb = joined[pl.ds(h * span + c * half, half), :]
            fa = joined[pl.ds(h * span + ylay.total + c * half, half), :]
            ghost[pl.ds(h * half * TILE + c, half, stride=TILE), :] = before[piece, :] * fb
            ghost[pl.ds(h * half * TILE + SIDE + c, half, stride=TILE), :] = after[piece, :] * fa
            swept, chain = fb, []
            for y in range(ny):
                cells = az[c, pl.ds(h * half * ny + y, half, stride=ny), :]
                swept = (cells + swept) * inv[pl.ds(y * nx + h * half, half), :]
                chain.append(swept)
            later = fa
            for y in reversed(range(ny)):
                where = pl.ds(h * half * ny + y, half, stride=ny)
                later = chain[y] + inv[pl.ds(y * nx + h * half, half), :] * later
                ay[c, where, :] = later * w[where, :]

    firsts = [jnp.zeros((n, LANES), jnp.float32) for n in xlay.sizes]
    lasts = list(firsts)
    for x in range(nx):
        here = pl.ds(x * ny, ny)
        near, far = left[here, :], right[here, :]
        for c in range(comps):
            cells = ay[c, here, :]
            firsts[c] = firsts[c] + near * cells
            lasts[c] = lasts[c] + far * cells
        here = pl.ds(x * TILE, TILE)
        cells = ghost[here, :]
        firsts[comps] = firsts[comps] + gleft[here, :] * cells
        lasts[comps] = lasts[comps] + gright[here, :] * cells
    record = {"first": firsts, "last": lasts}
    if xlay.leads:
        pieces = [part[pl.ds(i * ny, ny), :] for i in range(5)]
        record["near"] = [pieces[0], corner * total]
        record["cross"] = [pieces[1], total]
        record["far"] = [pieces[2], end * total]
        record["head"], record["tail"] = pieces[3:4], pieces[4:5]
    write_block(xlay, block, record)


def x_kernel(dims, lay, lead, levels, shift, start, me_ref, *refs):
    nx, ny = dims
    count = (2 if lay.leads else 4) * levels
    state, _ = solve_lines(lay, lead, levels, me_ref[0] >> shift, refs[:count])
    xinv, ginv, ay, ghost, w, lower, higher, flows, *rest = refs[count:]
    out_any, out, field, fluxes, sems = rest[-5:]
    rows = nx * ny
    comps = len(lay.sizes) - 1
    tiles = ny // TILE
    starts, nexts, behind, ahead = state
    near, far = behind[0], ahead[0]

    def sweep(x, carry):
        span, above = pl.ds(x * ny, ny), pl.ds((x + 1) * ny, ny)
        factor = xinv[span, :]
        new = []
        for c in range(comps):
            value = (ay[c, span, :] + carry[c]) * factor
            field[c, above, :] = value
            new.append(value)
        here = pl.ds(x * TILE, TILE)
        edge = (ghost[here, :] + carry[comps]) * ginv[here, :]
        fluxes[here, :] = edge
        return tuple(new) + (edge,)

    lax.fori_loop(0, nx, sweep, tuple(starts), unroll=8)

    def back(step, carry):
        x = nx - 1 - step
        span, above = pl.ds(x * ny, ny), pl.ds((x + 1) * ny, ny)
        factor = xinv[span, :]
        weight = w[span, :]
        new = []
        for c in range(comps):
            value = field[c, above, :] + factor * carry[c]
            field[c, above, :] = value * weight
            new.append(value)
        here = pl.ds(x * TILE, TILE)
        edge = fluxes[here, :] + ginv[here, :] * carry[comps]
        fluxes[here, :] = edge * two_sides(lower[pl.ds(nx + x, 1), :], higher[pl.ds(nx + x, 1), :])
        return tuple(new) + (edge,)

    lax.fori_loop(0, nx, back, tuple(nexts), unroll=8)
    blank = jnp.zeros((comps, ny, LANES), jnp.float32)
    field[:, pl.ds(0, ny), :] = blank
    field[:, pl.ds((nx + 1) * ny, ny), :] = blank

    line = lax.broadcasted_iota(jnp.int32, (TILE, LANES), 0)

    def advect(x, carry):
        before = jnp.maximum(x - 1, 0)
        beyond = jnp.minimum(x + 1, nx - 1)

        def flow(kind, plane, t):
            begin = pl.multiple_of(kind * rows + plane * ny + t * TILE, TILE)
            return flows[pl.ds(begin, TILE), :]

        own = [flow(0, x, t) for t in range(tiles)]
        ahead_x = [flow(1, beyond, t) for t in range(tiles)]
        behind_x = [flow(2, before, t) for t in range(tiles)]
        ahead_y = [flow(3, x, t) for t in range(tiles)]
        behind_y = [flow(4, x, t) for t in range(tiles)]
        ahead_z = [flow(5, x, t) for t in range(tiles)]
        behind_z = [flow(6, x, t) for t in range(tiles)]
        for c in range(comps):

            def cells(plane, t):
                begin = pl.multiple_of((plane + 1) * ny + t * TILE, TILE)
                return field[c, pl.ds(begin, TILE), :]

            grad = [cells(x, t) for t in range(tiles)]
            ups = [pltpu.roll(ahead_y[t] * grad[t], TILE - 1, 0) for t in range(tiles)]
            downs = [pltpu.roll(behind_y[t] * grad[t], 1, 0) for t in range(tiles)]
            lowest = fluxes[pl.ds(x * TILE + c, 1), :]
            highest = fluxes[pl.ds(x * TILE + SIDE + c, 1), :]
            for t in range(tiles):
                part = own[t] * grad[t]
                part = part + ahead_x[t] * cells(x + 1, t) - behind_x[t] * cells(x - 1, t)
                enter = ups[t + 1] if t + 1 < tiles else jnp.broadcast_to(highest, (TILE, LANES))
                part = part + jnp.where(line == TILE - 1, enter, ups[t])
                enter = downs[t - 1] if t > 0 else jnp.broadcast_to(lowest, (TILE, LANES))
                part = part - jnp.where(line == 0, enter, downs[t])
                part = part + pltpu.roll(ahead_z[t] * grad[t], LANES - 1, 1)
                part = part - pltpu.roll(behind_z[t] * grad[t], 1, 1)
                out[c, pl.ds(pl.multiple_of(x * ny + t * TILE, TILE), TILE), :] = part
        return carry

    parts = 4
    share = nx // parts

    def copy(part):
        span = pl.ds(part * share * ny, share * ny)
        target = out_any.at[pl.ds(start, comps), span, :]
        return pltpu.make_async_copy(out.at[:, span, :], target, sems.at[part])

    top, bottom = pl.ds(0, ny), pl.ds(rows - ny, ny)
    for part in range(parts):
        lax.fori_loop(part * share, (part + 1) * share, advect, 0, unroll=2)
        for c in range(comps):
            if part == 0:
                out[c, top, :] = out[c, top, :] - near * starts[c]
            if part == parts - 1:
                out[c, bottom, :] = out[c, bottom, :] + far * nexts[c]
        copy(part).start()
    for part in range(parts):
        copy(part).wait()


def call(
    kernel, name, operands, outs, scratch=(), spaces=None, out_spaces=None, mebibytes=4, aliases=None
):
    params = pltpu.CompilerParams(vmem_limit_bytes=mebibytes * 1024 * 1024)
    memory = {"v": pltpu.VMEM, "k": pltpu.VMEM, "h": pltpu.HBM, "s": pltpu.SMEM}
    held = {"h": pltpu.HBM, "k": pltpu.VMEM}
    spaces = spaces or "s" + "v" * (len(operands) - 1)
    out_spaces = out_spaces or "v" * len(outs)
    operands = [
        pltpu.with_memory_space_constraint(o, held[s]) if s in held else o
        for o, s in zip(operands, spaces)
    ]
    return pl.pallas_call(
        kernel,
        name=name,
        out_shape=[
            held[s](shape, jnp.float32) if s in held else jax.ShapeDtypeStruct(shape, jnp.float32)
            for shape, s in zip(outs, out_spaces)
        ],
        in_specs=[pl.BlockSpec(memory_space=memory[s]) for s in spaces],
        out_specs=[pl.BlockSpec(memory_space=memory[s]) for s in out_spaces],
        scratch_shapes=list(scratch),
        input_output_aliases=aliases or {},
        compiler_params=params,
    )(*operands)


def exchange(rows, axis, bit):
    count = lax.axis_size(axis)
    return lax.ppermute(rows, axis, [(i, i ^ (1 << bit)) for i in range(count)])


class Ladder:
    def __init__(self, lay, axis, shift, me, send, keep, lead=None):
        self.lay, self.axis, self.shift, self.me, self.lead = lay, axis, shift, me, lead
        self.levels = (lax.axis_size(axis) - 1).bit_length()
        self.owns, self.gots, self.outgoing = [keep], [], send

    def send(self):
        self.gots.append(exchange(self.outgoing, self.axis, len(self.gots)))

    def merge(self, beside=()):
        level = len(self.owns) - 1
        top = level == self.levels - 2
        leader = self.lead or self
        coupled = () if self.lay.leads else (leader.owns[level], leader.gots[level])
        shapes = [(self.lay.rows, LANES)] + ([(self.lay.side_rows, LANES)] if top else [])
        merged = call(
            functools.partial(merge_kernel, self.lay, leader.lay, self.shift + level, top),
            "merge_" + self.axis,
            (self.me, self.owns[-1], self.gots[-1]) + coupled + tuple(beside),
            shapes,
        )
        self.owns.append(merged[0])
        self.outgoing = merged[-1]

    def records(self):
        found = (*self.owns, *self.gots)
        return found if self.lay.leads else found + (*self.lead.owns, *self.lead.gots)


def on_device(cotangent, diffusion, phase, courant, upwind):
    comps, nx, ny, nz = cotangent.shape
    shift = (lax.axis_size("gy") - 1).bit_length()
    rows = nx * ny
    half = nx // 2
    size = comps // 2
    starts = (0, size)
    counts = (size, comps - size)
    ylays = [Layout([half] * n, 1, 2, half, g == 0) for g, n in enumerate(counts)]
    xlays = [Layout([ny] * n + [TILE], 2, 1, ny, g == 0) for g, n in enumerate(counts)]
    me = lax.axis_index(("gx", "gy")).astype(jnp.int32).reshape(1)

    def vmem(*shape, dtype=jnp.float32):
        return pltpu.VMEM(shape, dtype)

    flat = (rows, nz)
    cot = cotangent.reshape(comps, rows, nz)
    cour = courant.reshape(3, rows, nz)
    upw = upwind.reshape(3, rows, nz)
    n = counts[0]
    keep, send, az, w, inv, left, right, phi, psi = call(
        functools.partial(lead_z_kernel, (nx, ny), ylays[0]),
        "z_solve_lead",
        (me, cot, diffusion.reshape(flat), phase.reshape(flat), cour, upw),
        [(ylays[0].rows, nz)] * 2 + [(n, rows, nz)] + [flat] * 6,
        [
            vmem(n, rows, nz), vmem(*flat), vmem(*flat, dtype=jnp.int32),
            vmem(*flat), vmem(*flat, dtype=jnp.int32),
            vmem(*flat), vmem(*flat), vmem(*flat), vmem(2 * ylays[0].rows, nz),
            pltpu.SemaphoreType.DMA((n,)), pltpu.SemaphoreType.DMA((4,)),
        ],
        spaces="shhhhh",
        mebibytes=12,
    )
    lead = Ladder(ylays[0], "gy", 0, me, send, keep)
    lead.send()
    azs = [az]
    n = counts[1]
    keep, send, az = call(
        functools.partial(next_z_kernel, (nx, ny), ylays[1], starts[1]),
        "z_solve_next",
        (me, cot, phi, psi, w, left, right),
        [(ylays[1].rows, nz)] * 2 + [(n, rows, nz)],
        [
            vmem(n, rows, nz), vmem(2 * ylays[1].rows, nz), pltpu.SemaphoreType.DMA((n,)),
        ],
        spaces="shvvvvv",
        mebibytes=8,
    )
    azs.append(az)
    follow = Ladder(ylays[1], "gy", 0, me, send, keep, lead)
    follow.send()
    beside = (send,)
    for level in range(lead.levels - 1):
        lead.merge(beside)
        lead.send()
        follow.merge()
        follow.send()
        beside = (follow.outgoing,)
        if level == 0:
            part, xinv, xleft, xright, flows = call(
                functools.partial(coef_kernel, (nx, ny)),
                "x_coefficients",
                (w, cour, upw, lead.owns[1]),
                [(5 * ny, nz), flat, flat, flat, (7 * rows, nz)],
                spaces="vvvv",
                mebibytes=8,
            )
            beside = (part, follow.outgoing)
    ladders, mets, answers = (lead, follow), [], []
    for g, ladder in enumerate(ladders):
        answer, passed = call(
            functools.partial(solve_kernel, ylays[g], ylays[0], ladder.levels),
            "y_reduced",
            (me,) + ladder.records() + (beside if g == 0 else ()),
            [(ylays[g].answer_rows, nz)] * 2,
        )
        answers.append(answer)
        mets.append(exchange(passed, "gy", 0))
    ays, ghosts, climbs = [], [], []
    for g in range(2):
        common = (me, azs[g], answers[g], mets[g], w, inv, xleft, xright)
        outs = [(xlays[g].rows, nz), (counts[g], rows, nz), (nx * TILE, nz)]
        scratch = [vmem(2 * ylays[g].answer_rows, nz)]
        body = functools.partial(y_kernel, (nx, ny), ylays[g], xlays[g])
        if g == 0:
            block, ay, ghost, ginv, gleft, gright, before, after = call(
                body,
                "y_solve_lead",
                common + (part, answers[1]),
                outs + [(nx * TILE, nz)] * 3 + [(2 * nx, nz)] * 2,
                scratch,
                mebibytes=6,
            )
        else:
            block, ay, ghost = call(
                body,
                "y_solve_next",
                common + (before, after, gleft, gright),
                outs,
                scratch,
                mebibytes=6,
            )
        ays.append(ay)
        ghosts.append(ghost)
        climbs.append(Ladder(xlays[g], "gx", shift, me, block, block, climbs[0] if g else None))
        climbs[g].send()
    beside = (block,)
    for level in range(climbs[0].levels - 1):
        for ladder in climbs:
            ladder.merge(beside if ladder.lay.leads else ())
            ladder.send()
        beside = (climbs[1].outgoing,)
    grad = None
    for g, ladder in enumerate(climbs):
        operands = (me,) + ladder.records() + (
            xinv, ginv, ays[g], ghosts[g], w, before, after, flows,
        )
        spaces = "s" + "v" * (len(operands) - 1)
        aliases = None
        if g:
            aliases = {len(operands): 0}
            operands, spaces = operands + (grad,), spaces + "h"
        (grad,) = call(
            functools.partial(
                x_kernel, (nx, ny), xlays[g], xlays[0], ladder.levels, shift, starts[g]
            ),
            "x_solve",
            operands,
            [(comps, rows, nz)],
            [
                vmem(counts[g], rows, nz), vmem(counts[g], rows + 2 * ny, nz), vmem(nx * TILE, nz),
                pltpu.SemaphoreType.DMA((4,)),
            ],
            spaces=spaces,
            out_spaces="h",
            mebibytes=8,
            aliases=aliases,
        )
    return grad.reshape(comps, nx, ny, nz)


def solution(mesh):
    placed = (
        P(None, "gx", "gy", None),
        P("gx", "gy", None),
        P("gx", "gy", None),
        P(None, "gx", "gy", None),
        P(None, "gx", "gy", None),
    )
    return jax.shard_map(
        on_device, mesh=mesh, in_specs=placed, out_specs=P(None, "gx", "gy", None), check_vma=False
    )
```

time: 40.9 us -> 38.9 us (0.951)
  waiting for transfers between devices: 16.3 us -> 9.93 us
  starting transfers between devices: 9.99 us -> 14.8 us
  local copies, waits for them, and re-layouts: 2.55 us -> 0.01 us
  Pallas kernels: 11.9 us -> 13.8 us
    ppermute x6 -> x12, waiting for transfers between devices: 16.3 us -> 9.93 us  [exchange(): return lax.ppermute(rows, axis, [(i, i ^ 1 << bit) for i in range(count)])]
    ppermute x6 -> x12, starting transfers between devices: 9.99 us -> 14.8 us  [exchange(): return lax.ppermute(rows, axis, [(i, i ^ 1 << bit) for i in range(count)])]
    unnamed x8 -> x4, local copies, waits for them, and re-layouts: 2.55 us -> 0.01 us
    pallas_call x8 -> x15, Pallas kernels: 11.9 us -> 13.8 us  [call(): pl.pallas_call(kernel, name=name, out_shape=[held[s](shape, jnp.float32)...]
  transfers between devices with their start and end apart: 6 -> 12, of which waited for: 6 -> 7; matrix products, arithmetic and copies ran while one was open for 0% -> 0% of each run, Pallas kernels for 1% -> 17%
where the time goes in v4:
time: 38.9 us; the launch traced here: 38.7 us
  starting transfers between devices  14.8 us (38%)
  Pallas kernels  13.8 us (35%)
  waiting for transfers between devices  9.93 us (26%)
    ppermute x12, starting transfers between devices, exchange(): return lax.ppermute(rows, axis, [(i, i ^ 1 << bit) for i in range(count)])  14.8 us
    pallas_call x15, Pallas kernels, call(): pl.pallas_call(kernel, name=name, out_shape=[held[s](shape, jnp.float32)...  13.8 us
    ppermute x12, waiting for transfers between devices, exchange(): return lax.ppermute(rows, axis, [(i, i ^ 1 << bit) for i in range(count)])  9.93 us
  transfers between devices with their start and end apart: 12, of which 7 were waited for; matrix products, arithmetic and copies ran while one was open for 0% of the time, Pallas kernels for 17%

profile of v4, /device:TPU:0, one launch (start us, length us, event | category | flops | bytes accessed | tf_op | source)
XLA Modules:
  0.0 38.7 jit_solution(8606740148150903761)
XLA Ops:
  0.0 3.5 %z_solve_lead.1 = (f32[208,128]{1,0:T(8,128)S(1)}, f32[208,128]{1,0:T(8,128)S(1)}, f32[3,512,128]{2,1,0:T(8,128)S(1)}, f32[512,128]{1,0:T(8,128)S(1)}, f32[512,1...) custom-call(s32[1]{0:T(128)} %bitcast.me_ref, ...), custom_call_target="tpu_custom_call" | custom-call | tf_op jit(solution)/shard_map/z_solve_lead/pallas_call | solution.py:633
  3.6 0.5 %collective-permute-start.1 = (f32[208,128]{1,0:T(8,128)S(1)}, f32[208,128]{1,0:T(8,128)S(1)}, u32[]{:S(2)}, u32[]{:S(2)}) collective-permute-start(f32[208,128]{1,0:T(8,128)S(1)} %get-tuple-element.54), channel_id=1, source_target_pairs={{0,1},{1,0},{2,3},{3,2},{4,5},{5,4},{6,7},{7,6},{8,9},{9,8},{10,11... | collective-permute-start | bytes 319496 | tf_op jit(solution)/shard_map/ppermute | solution.py:650
  4.1 2.5 %z_solve_next.1 = (f32[96,128]{1,0:T(8,128)S(1)}, f32[96,128]{1,0:T(8,128)S(1)}, f32[3,512,128]{2,1,0:T(8,128)S(1)}) custom-call(s32[1]{0:T(128)} %bitcast.me_ref, f32[6,512,128]{2,1,0:T(8,128)} %bitcast.12, f32[512,128]{1,0:T(8,128)S(1)} %get-tuple-element.45.phi, f32[512,128]{1,0:T(8,128)S(1)} %get-tuple-element.46.psi, ...), custom_call_target="tpu_custom_call" | custom-call | tf_op jit(solution)/shard_map/z_solve_next/pallas_call | solution.py:633
  6.6 2.6 %collective-permute-start.3 = (f32[208,128]{1,0:T(8,128)S(1)}, f32[208,128]{1,0:T(8,128)S(1)}, u32[]{:S(2)}, u32[]{:S(2)}) collective-permute-start(f32[208,128]{1,0:T(8,128)S(1)} %merge_gy.5.refs_0_.after.own.refs_7_.refs_1_), channel_id=1, source_target_pairs={{0,2},{1,3},{2,0},{3,1},{4,6},{5,7},{6,4},{7,5},{8,10},{9,11},{10,... | collective-permute-start | bytes 319496 | tf_op jit(solution)/shard_map/ppermute | solution.py:650
  9.2 0.2 collective-permute-start
  9.4 0.3 x_coefficients.1
  9.8 0.7 %collective-permute-done.other.refs_3_ = f32[96,128]{1,0:T(8,128)S(1)} collective-permute-done((f32[96,128]{1,0:T(8,128)S(1)}, f32[96,128]{1,0:T(8,128)S(1)}, u32[]{:S(2)}, u32[]{:S(2)}) %collective-permute-start) | collective-permute-done | bytes 49184 | tf_op jit(solution)/shard_map/ppermute | solution.py:650
  10.5 0.3 collective-permute-start.2
  10.8 2.1 %collective-permute-done.3.refs_1_.other.refs_10_.refs_4_ = f32[208,128]{1,0:T(8,128)S(1)} collective-permute-done((f32[208,128]{1,0:T(8,128)S(1)}, f32[208,128]{1,0:T(8,128)S(1)}, u32[]{:S(2)}, u32[]{:S(2)}) %collective-permute-start.3) | collective-permute-done | bytes 106528 | tf_op jit(solution)/shard_map/ppermute | solution.py:650
  12.9 1.8 %collective-permute-start.5 = (f32[96,128]{1,0:T(8,128)S(1)}, f32[96,128]{1,0:T(8,128)S(1)}, u32[]{:S(2)}, u32[]{:S(2)}) collective-permute-start(f32[96,128]{1,0:T(8,128)S(1)} %get-tuple-element.59), channel_id=1, source_target_pairs={{0,4},{1,5},{2,6},{3,7},{4,0},{5,1},{6,2},{7,3},{8,12},{9,13},{10,... | collective-permute-start | bytes 147464 | tf_op jit(solution)/shard_map/ppermute | solution.py:650
  14.8 2.3 %collective-permute-done.5.refs_11_.refs_5_ = f32[96,128]{1,0:T(8,128)S(1)} collective-permute-done((f32[96,128]{1,0:T(8,128)S(1)}, f32[96,128]{1,0:T(8,128)S(1)}, u32[]{:S(2)}, u32[]{:S(2)}) %collective-permute-start.5) | collective-permute-done | bytes 49184 | tf_op jit(solution)/shard_map/ppermute | solution.py:650
  17.2 1.8 %collective-permute-start.4 = (f32[48,128]{1,0:T(8,128)S(1)}, f32[48,128]{1,0:T(8,128)S(1)}, u32[]{:S(2)}, u32[]{:S(2)}) collective-permute-start(f32[48,128]{1,0:T(8,128)S(1)} %get-tuple-element.56.refs_6_), channel_id=1, source_target_pairs={{0,4},{1,5},{2,6},{3,7},{4,0},{5,1},{6,2},{7,3},{8,12},{9,13},{10,... | collective-permute-start | bytes 73736 | tf_op jit(solution)/shard_map/ppermute | solution.py:650
  19.0 2.1 %collective-permute-done.4.refs_5_ = f32[48,128]{1,0:T(8,128)S(1)} collective-permute-done((f32[48,128]{1,0:T(8,128)S(1)}, f32[48,128]{1,0:T(8,128)S(1)}, u32[]{:S(2)}, u32[]{:S(2)}) %collective-permute-start.4) | collective-permute-done | bytes 24608 | tf_op jit(solution)/shard_map/ppermute | solution.py:650
  21.1 0.9 %y_solve_lead.1 = (f32[200,128]{1,0:T(8,128)S(1)}, f32[3,512,128]{2,1,0:T(8,128)S(1)}, f32[256,128]{1,0:T(8,128)S(1)}, f32[256,128]{1,0:T(8,128)S(1)}, f32[256,1...) custom-call(s32[1]{0:T(128)} %bitcast.me_ref, ...), custom_call_target="tpu_custom_call" | custom-call | tf_op jit(solution)/shard_map/y_solve_lead/pallas_call | solution.py:633
  22.1 1.9 %collective-permute-start.9 = (f32[200,128]{1,0:T(8,128)S(1)}, f32[200,128]{1,0:T(8,128)S(1)}, u32[]{:S(2)}, u32[]{:S(2)}) collective-permute-start(f32[200,128]{1,0:T(8,128)S(1)} %get-tuple-element.73.refs_0_.own.refs_4_), channel_id=1, source_target_pairs={{0,8},{8,0},{16,24},{24,16},{1,9},{9,1},{17,25},{25,17},{2,10},{10... | collective-permute-start | bytes 307208 | tf_op jit(solution)/shard_map/ppermute | solution.py:650
  24.0 1.2 %collective-permute-done.6.got = f32[96,128]{1,0:T(8,128)S(1)} collective-permute-done((f32[96,128]{1,0:T(8,128)S(1)}, f32[96,128]{1,0:T(8,128)S(1)}, u32[]{:S(2)}, u32[]{:S(2)}) %collective-permute-start.6) | collective-permute-done | bytes 49184 | tf_op jit(solution)/shard_map/ppermute | solution.py:650
  25.2 0.9 %y_solve_next.1 = (f32[112,128]{1,0:T(8,128)S(1)}, f32[3,512,128]{2,1,0:T(8,128)S(1)}, f32[256,128]{1,0:T(8,128)S(1)}) custom-call(s32[1]{0:T(128)} %bitcast.me_ref, f32[3,512,128]{2,1,0:T(8,128)S(1)} %get-tuple-element.50.az, f32[96,128]{1,0:T(8,128)S(1)} %get-tuple-element.60.refs_1_.own, f32[96,128]{1,0:T(8,128)S(1)} %collective-permute-done.6.got, ...), custom_call_target="tpu_custom_call" | custom-call | tf_op jit(solution)/shard_map/y_solve_next/pallas_call | solution.py:633
  26.1 0.3 collective-permute-start.8
  26.4 0.4 %collective-permute-done.9.refs_1_.other.refs_2_.refs_6_ = f32[200,128]{1,0:T(8,128)S(1)} collective-permute-done((f32[200,128]{1,0:T(8,128)S(1)}, f32[200,128]{1,0:T(8,128)S(1)}, u32[]{:S(2)}, u32[]{:S(2)}) %collective-permute-start.9) | collective-permute-done | bytes 102432 | tf_op jit(solution)/shard_map/ppermute | solution.py:650
  26.9 2.9 %collective-permute-start.11 = (f32[96,128]{1,0:T(8,128)S(1)}, f32[96,128]{1,0:T(8,128)S(1)}, u32[]{:S(2)}, u32[]{:S(2)}) collective-permute-start(f32[96,128]{1,0:T(8,128)S(1)} %get-tuple-element.77), channel_id=1, source_target_pairs={{0,16},{8,24},{16,0},{24,8},{1,17},{9,25},{17,1},{25,9},{2,18},{10... | collective-permute-start | bytes 147464 | tf_op jit(solution)/shard_map/ppermute | solution.py:650
  29.8 1.1 %collective-permute-done.8.other.refs_2_ = f32[112,128]{1,0:T(8,128)S(1)} collective-permute-done((f32[112,128]{1,0:T(8,128)S(1)}, f32[112,128]{1,0:T(8,128)S(1)}, u32[]{:S(2)}, u32[]{:S(2)}) %collective-permute-start.8) | collective-permute-done | bytes 57376 | tf_op jit(solution)/shard_map/ppermute | solution.py:650
  30.9 2.5 %collective-permute-start.10 = (f32[56,128]{1,0:T(8,128)S(1)}, f32[56,128]{1,0:T(8,128)S(1)}, u32[]{:S(2)}, u32[]{:S(2)}) collective-permute-start(f32[56,128]{1,0:T(8,128)S(1)} %get-tuple-element.75), channel_id=1, source_target_pairs={{0,16},{8,24},{16,0},{24,8},{1,17},{9,25},{17,1},{25,9},{2,18},{10... | collective-permute-start | bytes 86024 | tf_op jit(solution)/shard_map/ppermute | solution.py:650
  33.4 2.7 %x_solve.2.refs_16_ = f32[6,512,128]{2,1,0:T(8,128)} custom-call(s32[1]{0:T(128)} %bitcast.me_ref, f32[200,128]{1,0:T(8,128)S(1)} %get-tuple-element.73.refs_0_.own.refs_4_, f32[200,128]{1,0:T(8,128)S(1)} %get-tuple-element.76.refs_1_.refs_5_, f32[200,128]{1,0:T(8,128)S(1)} %collective-permute-done.9.refs_1_.other.refs_2_.refs_6_, ...), custom_call_target="tpu_custom_call" | custom-call | tf_op jit(solution)/shard_map/x_solve/pallas_call | solution.py:633
  36.0 2.7 %x_solve.3 = f32[6,512,128]{2,1,0:T(8,128)} custom-call(s32[1]{0:T(128)} %bitcast.me_ref, f32[112,128]{1,0:T(8,128)S(1)} %get-tuple-element.72.own.refs_0_, f32[112,128]{1,0:T(8,128)S(1)} %get-tuple-element.74.refs_1_, f32[112,128]{1,0:T(8,128)S(1)} %collective-permute-done.8.other.refs_2_, ...), custom_call_target="tpu_custom_call", output_to_operand_aliasing={{}: (17, {})} | custom-call | tf_op jit(solution)/shard_map/x_solve/pallas_call | solution.py:633
  (19 shorter events, 0.4 us)
Async XLA Ops:
  3.6 3.1 %collective-permute-start.1 = (f32[208,128]{1,0:T(8,128)S(1)}, f32[208,128]{1,0:T(8,128)S(1)}, u32[]{:S(2)}, u32[]{:S(2)}) collective-permute-start(f32[208,128]{1,0:T(8,128)S(1)} %get-tuple-element.54), channel_id=1, source_target_pairs={{0,1},{1,0},{2,3},{3,2},{4,5},{5,4},{6,7},{7,6},{8,9},{9,8},{10,11... | collective-permute-start | bytes 319496 | tf_op jit(solution)/shard_map/ppermute | solution.py:650
  4.1 5.4 %copy-start = (f32[3,32,16,128]{3,2,1,0:T(8,128)S(1)}, f32[3,32,16,128]{3,2,1,0:T(8,128)}, u32[]{:S(2)}) copy-start(f32[3,32,16,128]{3,2,1,0:T(8,128)} %param.8) | copy-start | bytes 2359300
  4.1 5.4 %copy-start.1 = (s32[3,32,16,128]{3,2,1,0:T(8,128)S(1)}, s32[3,32,16,128]{3,2,1,0:T(8,128)}, u32[]{:S(2)}) copy-start(s32[3,32,16,128]{3,2,1,0:T(8,128)} %param.9) | copy-start | bytes 2359300
  6.6 6.2 %collective-permute-start.3 = (f32[208,128]{1,0:T(8,128)S(1)}, f32[208,128]{1,0:T(8,128)S(1)}, u32[]{:S(2)}, u32[]{:S(2)}) collective-permute-start(f32[208,128]{1,0:T(8,128)S(1)} %merge_gy.5.refs_0_.after.own.refs_7_.refs_1_), channel_id=1, source_target_pairs={{0,2},{1,3},{2,0},{3,1},{4,6},{5,7},{6,4},{7,5},{8,10},{9,11},{10,... | collective-permute-start | bytes 319496 | tf_op jit(solution)/shard_map/ppermute | solution.py:650
  9.2 1.2 %collective-permute-start = (f32[96,128]{1,0:T(8,128)S(1)}, f32[96,128]{1,0:T(8,128)S(1)}, u32[]{:S(2)}, u32[]{:S(2)}) collective-permute-start(f32[96,128]{1,0:T(8,128)S(1)} %get-tuple-element.52.refs_0_), channel_id=1, source_target_pairs={{0,1},{1,0},{2,3},{3,2},{4,5},{5,4},{6,7},{7,6},{8,9},{9,8},{10,11... | collective-permute-start | bytes 147464 | tf_op jit(solution)/shard_map/ppermute | solution.py:650
  10.5 4.2 %collective-permute-start.2 = (f32[96,128]{1,0:T(8,128)S(1)}, f32[96,128]{1,0:T(8,128)S(1)}, u32[]{:S(2)}, u32[]{:S(2)}) collective-permute-start(f32[96,128]{1,0:T(8,128)S(1)} %merge_gy.4.own.refs_1_), channel_id=1, source_target_pairs={{0,2},{1,3},{2,0},{3,1},{4,6},{5,7},{6,4},{7,5},{8,10},{9,11},{10,... | collective-permute-start | bytes 147464 | tf_op jit(solution)/shard_map/ppermute | solution.py:650
  12.9 4.2 %collective-permute-start.5 = (f32[96,128]{1,0:T(8,128)S(1)}, f32[96,128]{1,0:T(8,128)S(1)}, u32[]{:S(2)}, u32[]{:S(2)}) collective-permute-start(f32[96,128]{1,0:T(8,128)S(1)} %get-tuple-element.59), channel_id=1, source_target_pairs={{0,4},{1,5},{2,6},{3,7},{4,0},{5,1},{6,2},{7,3},{8,12},{9,13},{10,... | collective-permute-start | bytes 147464 | tf_op jit(solution)/shard_map/ppermute | solution.py:650
  17.1 4.0 %collective-permute-start.7 = (f32[160,128]{1,0:T(8,128)S(1)}, f32[160,128]{1,0:T(8,128)S(1)}, u32[]{:S(2)}, u32[]{:S(2)}) collective-permute-start(f32[160,128]{1,0:T(8,128)S(1)} %get-tuple-element.67), channel_id=1, source_target_pairs={{0,1},{1,0},{2,3},{3,2},{4,5},{5,4},{6,7},{7,6},{8,9},{9,8},{10,11... | collective-permute-start | bytes 245768 | tf_op jit(solution)/shard_map/ppermute | solution.py:650
  17.2 3.9 %collective-permute-start.4 = (f32[48,128]{1,0:T(8,128)S(1)}, f32[48,128]{1,0:T(8,128)S(1)}, u32[]{:S(2)}, u32[]{:S(2)}) collective-permute-start(f32[48,128]{1,0:T(8,128)S(1)} %get-tuple-element.56.refs_6_), channel_id=1, source_target_pairs={{0,4},{1,5},{2,6},{3,7},{4,0},{5,1},{6,2},{7,3},{8,12},{9,13},{10,... | collective-permute-start | bytes 73736 | tf_op jit(solution)/shard_map/ppermute | solution.py:650
  22.1 4.7 %collective-permute-start.9 = (f32[200,128]{1,0:T(8,128)S(1)}, f32[200,128]{1,0:T(8,128)S(1)}, u32[]{:S(2)}, u32[]{:S(2)}) collective-permute-start(f32[200,128]{1,0:T(8,128)S(1)} %get-tuple-element.73.refs_0_.own.refs_4_), channel_id=1, source_target_pairs={{0,8},{8,0},{16,24},{24,16},{1,9},{9,1},{17,25},{25,17},{2,10},{10... | collective-permute-start | bytes 307208 | tf_op jit(solution)/shard_map/ppermute | solution.py:650
  24.0 1.2 %collective-permute-start.6 = (f32[96,128]{1,0:T(8,128)S(1)}, f32[96,128]{1,0:T(8,128)S(1)}, u32[]{:S(2)}, u32[]{:S(2)}) collective-permute-start(f32[96,128]{1,0:T(8,128)S(1)} %get-tuple-element.61), channel_id=1, source_target_pairs={{0,1},{1,0},{2,3},{3,2},{4,5},{5,4},{6,7},{7,6},{8,9},{9,8},{10,11... | collective-permute-start | bytes 147464 | tf_op jit(solution)/shard_map/ppermute | solution.py:650
  26.1 4.8 %collective-permute-start.8 = (f32[112,128]{1,0:T(8,128)S(1)}, f32[112,128]{1,0:T(8,128)S(1)}, u32[]{:S(2)}, u32[]{:S(2)}) collective-permute-start(f32[112,128]{1,0:T(8,128)S(1)} %get-tuple-element.72.own.refs_0_), channel_id=1, source_target_pairs={{0,8},{8,0},{16,24},{24,16},{1,9},{9,1},{17,25},{25,17},{2,10},{10... | collective-permute-start | bytes 172040 | tf_op jit(solution)/shard_map/ppermute | solution.py:650
  26.9 6.5 %collective-permute-start.11 = (f32[96,128]{1,0:T(8,128)S(1)}, f32[96,128]{1,0:T(8,128)S(1)}, u32[]{:S(2)}, u32[]{:S(2)}) collective-permute-start(f32[96,128]{1,0:T(8,128)S(1)} %get-tuple-element.77), channel_id=1, source_target_pairs={{0,16},{8,24},{16,0},{24,8},{1,17},{9,25},{17,1},{25,9},{2,18},{10... | collective-permute-start | bytes 147464 | tf_op jit(solution)/shard_map/ppermute | solution.py:650
  30.9 5.1 %collective-permute-start.10 = (f32[56,128]{1,0:T(8,128)S(1)}, f32[56,128]{1,0:T(8,128)S(1)}, u32[]{:S(2)}, u32[]{:S(2)}) collective-permute-start(f32[56,128]{1,0:T(8,128)S(1)} %get-tuple-element.75), channel_id=1, source_target_pairs={{0,16},{8,24},{16,0},{24,8},{1,17},{9,25},{17,1},{25,9},{2,18},{10... | collective-permute-start | bytes 86024 | tf_op jit(solution)/shard_map/ppermute | solution.py:650

commit v5 on v4

--- a/solution.py
+++ b/solution.py
@@ -292,9 +292,10 @@
             span = pl.ds(t * LANES, LANES)
             cells, up, down = cot[c, span, :], phi[span, :], psi[span, :]
             wide = jnp.concatenate([up * cells, down * cells], axis=1)
-            found = sum(
-                jnp.dot(part, sums, preferred_element_type=jnp.float32) for part in split3(wide)
+            found = jnp.dot(
+                jnp.concatenate(split3(wide), axis=0), sums, preferred_element_type=jnp.float32
             )
+            found = found[:LANES] + (found[LANES : 2 * LANES] + found[2 * LANES :])
             az[c, span, :] = w[span, :] * (down * found[:, :LANES] + up * found[:, LANES:])
         first = jnp.zeros((nx, LANES), jnp.float32)
         last = jnp.zeros((nx, LANES), jnp.float32)
@@ -439,7 +440,7 @@
     half = nx // 2
     comps = len(ylay.sizes)
     if xlay.leads:
-        part, _, block, ay, ghost, ginv, gleft, gright, before, after, joined = refs
+        part, block, ay, ghost, ginv, gleft, gright, before, after, joined = refs
     else:
         before, after, gleft, gright, block, ay, ghost, joined = refs
     mine = me_ref[0] & 1
@@ -607,7 +608,7 @@
 
     top, bottom = pl.ds(0, ny), pl.ds(rows - ny, ny)
     for part in range(parts):
-        lax.fori_loop(part * share, (part + 1) * share, advect, 0, unroll=2)
+        lax.fori_loop(part * share, (part + 1) * share, advect, 0, unroll=share)
         for c in range(comps):
             if part == 0:
                 out[c, top, :] = out[c, top, :] - near * starts[c]
@@ -768,7 +769,7 @@
             block, ay, ghost, ginv, gleft, gright, before, after = call(
                 body,
                 "y_solve_lead",
-                common + (part, answers[1]),
+                common + (part,),
                 outs + [(nx * TILE, nz)] * 3 + [(2 * nx, nz)] * 2,
                 scratch,
                 mebibytes=6,

time: 38.9 us -> 34.8 us (0.89)
  waiting for transfers between devices: 9.93 us -> 6.8 us
  Pallas kernels: 13.8 us -> 11.8 us
  starting transfers between devices: 14.8 us -> 16 us
    ppermute x12, waiting for transfers between devices: 9.93 us -> 6.8 us  [exchange(): return lax.ppermute(rows, axis, [(i, i ^ 1 << bit) for i in range(count)])]
    pallas_call x15, Pallas kernels: 13.8 us -> 11.8 us  [call(): pl.pallas_call(kernel, name=name, out_shape=[held[s](shape, jnp.float32)...]
    ppermute x12, starting transfers between devices: 14.8 us -> 16 us  [exchange(): return lax.ppermute(rows, axis, [(i, i ^ 1 << bit) for i in range(count)])]
  transfers between devices with their start and end apart: 12 -> 12, of which waited for: 7 -> 6; matrix products, arithmetic and copies ran while one was open for 0% -> 0% of each run, Pallas kernels for 17% -> 19%
where the time goes in v5:
time: 34.8 us; the launch traced here: 34.7 us
  starting transfers between devices  16 us (46%)
  Pallas kernels  11.8 us (34%)
  waiting for transfers between devices  6.8 us (20%)
    ppermute x12, starting transfers between devices, exchange(): return lax.ppermute(rows, axis, [(i, i ^ 1 << bit) for i in range(count)])  16 us
    pallas_call x15, Pallas kernels, call(): pl.pallas_call(kernel, name=name, out_shape=[held[s](shape, jnp.float32)...  11.8 us
    ppermute x12, waiting for transfers between devices, exchange(): return lax.ppermute(rows, axis, [(i, i ^ 1 << bit) for i in range(count)])  6.8 us
  transfers between devices with their start and end apart: 12, of which 6 were waited for; matrix products, arithmetic and copies ran while one was open for 0% of the time, Pallas kernels for 19%

profile of v5, /device:TPU:0, one launch (start us, length us, event | category | flops | bytes accessed | tf_op | source)
XLA Modules:
  0.0 34.7 jit_solution(17769857994935570147)
XLA Ops:
  0.0 3.6 %z_solve_lead.1 = (f32[208,128]{1,0:T(8,128)S(1)}, f32[208,128]{1,0:T(8,128)S(1)}, f32[3,512,128]{2,1,0:T(8,128)S(1)}, f32[512,128]{1,0:T(8,128)S(1)}, f32[512,1...) custom-call(s32[1]{0:T(128)} %bitcast.me_ref, ...), custom_call_target="tpu_custom_call" | custom-call | tf_op jit(solution)/shard_map/z_solve_lead/pallas_call | solution.py:634
  3.6 0.5 %collective-permute-start.1 = (f32[208,128]{1,0:T(8,128)S(1)}, f32[208,128]{1,0:T(8,128)S(1)}, u32[]{:S(2)}, u32[]{:S(2)}) collective-permute-start(f32[208,128]{1,0:T(8,128)S(1)} %get-tuple-element.54), channel_id=1, source_target_pairs={{0,1},{1,0},{2,3},{3,2},{4,5},{5,4},{6,7},{7,6},{8,9},{9,8},{10,11... | collective-permute-start | bytes 319496 | tf_op jit(solution)/shard_map/ppermute | solution.py:651
  4.1 2.5 %z_solve_next.1 = (f32[96,128]{1,0:T(8,128)S(1)}, f32[96,128]{1,0:T(8,128)S(1)}, f32[3,512,128]{2,1,0:T(8,128)S(1)}) custom-call(s32[1]{0:T(128)} %bitcast.me_ref, f32[6,512,128]{2,1,0:T(8,128)} %bitcast.12, f32[512,128]{1,0:T(8,128)S(1)} %get-tuple-element.45.phi, f32[512,128]{1,0:T(8,128)S(1)} %get-tuple-element.46.psi, ...), custom_call_target="tpu_custom_call" | custom-call | tf_op jit(solution)/shard_map/z_solve_next/pallas_call | solution.py:634
  6.7 2.6 %collective-permute-start.3 = (f32[208,128]{1,0:T(8,128)S(1)}, f32[208,128]{1,0:T(8,128)S(1)}, u32[]{:S(2)}, u32[]{:S(2)}) collective-permute-start(f32[208,128]{1,0:T(8,128)S(1)} %merge_gy.5.refs_0_.after.own.refs_7_.refs_1_), channel_id=1, source_target_pairs={{0,2},{1,3},{2,0},{3,1},{4,6},{5,7},{6,4},{7,5},{8,10},{9,11},{10,... | collective-permute-start | bytes 319496 | tf_op jit(solution)/shard_map/ppermute | solution.py:651
  9.3 0.2 collective-permute-start
  9.5 0.3 x_coefficients.1
  9.8 0.7 %collective-permute-done.other.refs_3_ = f32[96,128]{1,0:T(8,128)S(1)} collective-permute-done((f32[96,128]{1,0:T(8,128)S(1)}, f32[96,128]{1,0:T(8,128)S(1)}, u32[]{:S(2)}, u32[]{:S(2)}) %collective-permute-start) | collective-permute-done | bytes 49184 | tf_op jit(solution)/shard_map/ppermute | solution.py:651
  10.6 0.3 collective-permute-start.2
  10.8 2.1 %collective-permute-done.3.refs_1_.other.refs_10_.refs_4_ = f32[208,128]{1,0:T(8,128)S(1)} collective-permute-done((f32[208,128]{1,0:T(8,128)S(1)}, f32[208,128]{1,0:T(8,128)S(1)}, u32[]{:S(2)}, u32[]{:S(2)}) %collective-permute-start.3) | collective-permute-done | bytes 106528 | tf_op jit(solution)/shard_map/ppermute | solution.py:651
  13.0 1.8 %collective-permute-start.5 = (f32[96,128]{1,0:T(8,128)S(1)}, f32[96,128]{1,0:T(8,128)S(1)}, u32[]{:S(2)}, u32[]{:S(2)}) collective-permute-start(f32[96,128]{1,0:T(8,128)S(1)} %get-tuple-element.59), channel_id=1, source_target_pairs={{0,4},{1,5},{2,6},{3,7},{4,0},{5,1},{6,2},{7,3},{8,12},{9,13},{10,... | collective-permute-start | bytes 147464 | tf_op jit(solution)/shard_map/ppermute | solution.py:651
  14.8 2.3 %collective-permute-done.5.refs_11_.refs_5_ = f32[96,128]{1,0:T(8,128)S(1)} collective-permute-done((f32[96,128]{1,0:T(8,128)S(1)}, f32[96,128]{1,0:T(8,128)S(1)}, u32[]{:S(2)}, u32[]{:S(2)}) %collective-permute-start.5) | collective-permute-done | bytes 49184 | tf_op jit(solution)/shard_map/ppermute | solution.py:651
  17.2 0.1 collective-permute-start.7
  17.2 1.8 %collective-permute-start.4 = (f32[48,128]{1,0:T(8,128)S(1)}, f32[48,128]{1,0:T(8,128)S(1)}, u32[]{:S(2)}, u32[]{:S(2)}) collective-permute-start(f32[48,128]{1,0:T(8,128)S(1)} %get-tuple-element.56.refs_6_), channel_id=1, source_target_pairs={{0,4},{1,5},{2,6},{3,7},{4,0},{5,1},{6,2},{7,3},{8,12},{9,13},{10,... | collective-permute-start | bytes 73736 | tf_op jit(solution)/shard_map/ppermute | solution.py:651
  19.1 0.9 %y_solve_lead.1 = (f32[200,128]{1,0:T(8,128)S(1)}, f32[3,512,128]{2,1,0:T(8,128)S(1)}, f32[256,128]{1,0:T(8,128)S(1)}, f32[256,128]{1,0:T(8,128)S(1)}, f32[256,1...) custom-call(s32[1]{0:T(128)} %bitcast.me_ref, ...), custom_call_target="tpu_custom_call" | custom-call | tf_op jit(solution)/shard_map/y_solve_lead/pallas_call | solution.py:634
  20.0 1.7 %collective-permute-start.9 = (f32[200,128]{1,0:T(8,128)S(1)}, f32[200,128]{1,0:T(8,128)S(1)}, u32[]{:S(2)}, u32[]{:S(2)}) collective-permute-start(f32[200,128]{1,0:T(8,128)S(1)} %get-tuple-element.73.refs_0_.own.refs_4_), channel_id=1, source_target_pairs={{0,8},{8,0},{16,24},{24,16},{1,9},{9,1},{17,25},{25,17},{2,10},{10... | collective-permute-start | bytes 307208 | tf_op jit(solution)/shard_map/ppermute | solution.py:651
  21.8 1.2 %collective-permute-done.6.got = f32[96,128]{1,0:T(8,128)S(1)} collective-permute-done((f32[96,128]{1,0:T(8,128)S(1)}, f32[96,128]{1,0:T(8,128)S(1)}, u32[]{:S(2)}, u32[]{:S(2)}) %collective-permute-start.6) | collective-permute-done | bytes 49184 | tf_op jit(solution)/shard_map/ppermute | solution.py:651
  23.0 0.9 %y_solve_next.1 = (f32[112,128]{1,0:T(8,128)S(1)}, f32[3,512,128]{2,1,0:T(8,128)S(1)}, f32[256,128]{1,0:T(8,128)S(1)}) custom-call(s32[1]{0:T(128)} %bitcast.me_ref, f32[3,512,128]{2,1,0:T(8,128)S(1)} %get-tuple-element.50.az, f32[96,128]{1,0:T(8,128)S(1)} %get-tuple-element.60.own, f32[96,128]{1,0:T(8,128)S(1)} %collective-permute-done.6.got, ...), custom_call_target="tpu_custom_call" | custom-call | tf_op jit(solution)/shard_map/y_solve_next/pallas_call | solution.py:634
  23.9 1.3 %collective-permute-start.8 = (f32[112,128]{1,0:T(8,128)S(1)}, f32[112,128]{1,0:T(8,128)S(1)}, u32[]{:S(2)}, u32[]{:S(2)}) collective-permute-start(f32[112,128]{1,0:T(8,128)S(1)} %get-tuple-element.72.own.refs_0_), channel_id=1, source_target_pairs={{0,8},{8,0},{16,24},{24,16},{1,9},{9,1},{17,25},{25,17},{2,10},{10... | collective-permute-start | bytes 172040 | tf_op jit(solution)/shard_map/ppermute | solution.py:651
  25.3 2.6 %collective-permute-start.11 = (f32[96,128]{1,0:T(8,128)S(1)}, f32[96,128]{1,0:T(8,128)S(1)}, u32[]{:S(2)}, u32[]{:S(2)}) collective-permute-start(f32[96,128]{1,0:T(8,128)S(1)} %get-tuple-element.77), channel_id=1, source_target_pairs={{0,16},{8,24},{16,0},{24,8},{1,17},{9,25},{17,1},{25,9},{2,18},{10... | collective-permute-start | bytes 147464 | tf_op jit(solution)/shard_map/ppermute | solution.py:651
  27.9 0.2 collective-permute-done.8.other.refs_2_
  28.2 3.0 %collective-permute-start.10 = (f32[56,128]{1,0:T(8,128)S(1)}, f32[56,128]{1,0:T(8,128)S(1)}, u32[]{:S(2)}, u32[]{:S(2)}) collective-permute-start(f32[56,128]{1,0:T(8,128)S(1)} %get-tuple-element.75), channel_id=1, source_target_pairs={{0,16},{8,24},{16,0},{24,8},{1,17},{9,25},{17,1},{25,9},{2,18},{10... | collective-permute-start | bytes 86024 | tf_op jit(solution)/shard_map/ppermute | solution.py:651
  31.2 1.6 %x_solve.2.refs_16_ = f32[6,512,128]{2,1,0:T(8,128)} custom-call(s32[1]{0:T(128)} %bitcast.me_ref, f32[200,128]{1,0:T(8,128)S(1)} %get-tuple-element.73.refs_0_.own.refs_4_, f32[200,128]{1,0:T(8,128)S(1)} %get-tuple-element.76.refs_1_.refs_5_, f32[200,128]{1,0:T(8,128)S(1)} %collective-permute-done.9.refs_1_.other.refs_2_.refs_6_, ...), custom_call_target="tpu_custom_call" | custom-call | tf_op jit(solution)/shard_map/x_solve/pallas_call | solution.py:634
  32.8 0.2 collective-permute-done.10.refs_3_
  33.0 1.6 %x_solve.3 = f32[6,512,128]{2,1,0:T(8,128)} custom-call(s32[1]{0:T(128)} %bitcast.me_ref, f32[112,128]{1,0:T(8,128)S(1)} %get-tuple-element.72.own.refs_0_, f32[112,128]{1,0:T(8,128)S(1)} %get-tuple-element.74.refs_1_, f32[112,128]{1,0:T(8,128)S(1)} %collective-permute-done.8.other.refs_2_, ...), custom_call_target="tpu_custom_call", output_to_operand_aliasing={{}: (17, {})} | custom-call | tf_op jit(solution)/shard_map/x_solve/pallas_call | solution.py:634
  (19 shorter events, 0.4 us)
Async XLA Ops:
  3.6 3.0 %collective-permute-start.1 = (f32[208,128]{1,0:T(8,128)S(1)}, f32[208,128]{1,0:T(8,128)S(1)}, u32[]{:S(2)}, u32[]{:S(2)}) collective-permute-start(f32[208,128]{1,0:T(8,128)S(1)} %get-tuple-element.54), channel_id=1, source_target_pairs={{0,1},{1,0},{2,3},{3,2},{4,5},{5,4},{6,7},{7,6},{8,9},{9,8},{10,11... | collective-permute-start | bytes 319496 | tf_op jit(solution)/shard_map/ppermute | solution.py:651
  4.1 5.4 %copy-start = (f32[3,32,16,128]{3,2,1,0:T(8,128)S(1)}, f32[3,32,16,128]{3,2,1,0:T(8,128)}, u32[]{:S(2)}) copy-start(f32[3,32,16,128]{3,2,1,0:T(8,128)} %param.8) | copy-start | bytes 2359300
  4.1 5.4 %copy-start.1 = (s32[3,32,16,128]{3,2,1,0:T(8,128)S(1)}, s32[3,32,16,128]{3,2,1,0:T(8,128)}, u32[]{:S(2)}) copy-start(s32[3,32,16,128]{3,2,1,0:T(8,128)} %param.9) | copy-start | bytes 2359300
  6.7 6.3 %collective-permute-start.3 = (f32[208,128]{1,0:T(8,128)S(1)}, f32[208,128]{1,0:T(8,128)S(1)}, u32[]{:S(2)}, u32[]{:S(2)}) collective-permute-start(f32[208,128]{1,0:T(8,128)S(1)} %merge_gy.5.refs_0_.after.own.refs_7_.refs_1_), channel_id=1, source_target_pairs={{0,2},{1,3},{2,0},{3,1},{4,6},{5,7},{6,4},{7,5},{8,10},{9,11},{10,... | collective-permute-start | bytes 319496 | tf_op jit(solution)/shard_map/ppermute | solution.py:651
  9.3 1.2 %collective-permute-start = (f32[96,128]{1,0:T(8,128)S(1)}, f32[96,128]{1,0:T(8,128)S(1)}, u32[]{:S(2)}, u32[]{:S(2)}) collective-permute-start(f32[96,128]{1,0:T(8,128)S(1)} %get-tuple-element.52.refs_0_), channel_id=1, source_target_pairs={{0,1},{1,0},{2,3},{3,2},{4,5},{5,4},{6,7},{7,6},{8,9},{9,8},{10,11... | collective-permute-start | bytes 147464 | tf_op jit(solution)/shard_map/ppermute | solution.py:651
  10.6 4.2 %collective-permute-start.2 = (f32[96,128]{1,0:T(8,128)S(1)}, f32[96,128]{1,0:T(8,128)S(1)}, u32[]{:S(2)}, u32[]{:S(2)}) collective-permute-start(f32[96,128]{1,0:T(8,128)S(1)} %merge_gy.4.own.refs_1_), channel_id=1, source_target_pairs={{0,2},{1,3},{2,0},{3,1},{4,6},{5,7},{6,4},{7,5},{8,10},{9,11},{10,... | collective-permute-start | bytes 147464 | tf_op jit(solution)/shard_map/ppermute | solution.py:651
  13.0 4.2 %collective-permute-start.5 = (f32[96,128]{1,0:T(8,128)S(1)}, f32[96,128]{1,0:T(8,128)S(1)}, u32[]{:S(2)}, u32[]{:S(2)}) collective-permute-start(f32[96,128]{1,0:T(8,128)S(1)} %get-tuple-element.59), channel_id=1, source_target_pairs={{0,4},{1,5},{2,6},{3,7},{4,0},{5,1},{6,2},{7,3},{8,12},{9,13},{10,... | collective-permute-start | bytes 147464 | tf_op jit(solution)/shard_map/ppermute | solution.py:651
  17.2 1.9 %collective-permute-start.7 = (f32[160,128]{1,0:T(8,128)S(1)}, f32[160,128]{1,0:T(8,128)S(1)}, u32[]{:S(2)}, u32[]{:S(2)}) collective-permute-start(f32[160,128]{1,0:T(8,128)S(1)} %get-tuple-element.67), channel_id=1, source_target_pairs={{0,1},{1,0},{2,3},{3,2},{4,5},{5,4},{6,7},{7,6},{8,9},{9,8},{10,11... | collective-permute-start | bytes 245768 | tf_op jit(solution)/shard_map/ppermute | solution.py:651
  17.2 4.4 %collective-permute-start.4 = (f32[48,128]{1,0:T(8,128)S(1)}, f32[48,128]{1,0:T(8,128)S(1)}, u32[]{:S(2)}, u32[]{:S(2)}) collective-permute-start(f32[48,128]{1,0:T(8,128)S(1)} %get-tuple-element.56.refs_6_), channel_id=1, source_target_pairs={{0,4},{1,5},{2,6},{3,7},{4,0},{5,1},{6,2},{7,3},{8,12},{9,13},{10,... | collective-permute-start | bytes 73736 | tf_op jit(solution)/shard_map/ppermute | solution.py:651
  20.0 5.2 %collective-permute-start.9 = (f32[200,128]{1,0:T(8,128)S(1)}, f32[200,128]{1,0:T(8,128)S(1)}, u32[]{:S(2)}, u32[]{:S(2)}) collective-permute-start(f32[200,128]{1,0:T(8,128)S(1)} %get-tuple-element.73.refs_0_.own.refs_4_), channel_id=1, source_target_pairs={{0,8},{8,0},{16,24},{24,16},{1,9},{9,1},{17,25},{25,17},{2,10},{10... | collective-permute-start | bytes 307208 | tf_op jit(solution)/shard_map/ppermute | solution.py:651
  21.7 1.3 %collective-permute-start.6 = (f32[96,128]{1,0:T(8,128)S(1)}, f32[96,128]{1,0:T(8,128)S(1)}, u32[]{:S(2)}, u32[]{:S(2)}) collective-permute-start(f32[96,128]{1,0:T(8,128)S(1)} %get-tuple-element.61), channel_id=1, source_target_pairs={{0,1},{1,0},{2,3},{3,2},{4,5},{5,4},{6,7},{7,6},{8,9},{9,8},{10,11... | collective-permute-start | bytes 147464 | tf_op jit(solution)/shard_map/ppermute | solution.py:651
  23.9 4.2 %collective-permute-start.8 = (f32[112,128]{1,0:T(8,128)S(1)}, f32[112,128]{1,0:T(8,128)S(1)}, u32[]{:S(2)}, u32[]{:S(2)}) collective-permute-start(f32[112,128]{1,0:T(8,128)S(1)} %get-tuple-element.72.own.refs_0_), channel_id=1, source_target_pairs={{0,8},{8,0},{16,24},{24,16},{1,9},{9,1},{17,25},{25,17},{2,10},{10... | collective-permute-start | bytes 172040 | tf_op jit(solution)/shard_map/ppermute | solution.py:651
  25.3 5.9 %collective-permute-start.11 = (f32[96,128]{1,0:T(8,128)S(1)}, f32[96,128]{1,0:T(8,128)S(1)}, u32[]{:S(2)}, u32[]{:S(2)}) collective-permute-start(f32[96,128]{1,0:T(8,128)S(1)} %get-tuple-element.77), channel_id=1, source_target_pairs={{0,16},{8,24},{16,0},{24,8},{1,17},{9,25},{17,1},{25,9},{2,18},{10... | collective-permute-start | bytes 147464 | tf_op jit(solution)/shard_map/ppermute | solution.py:651
  28.2 4.8 %collective-permute-start.10 = (f32[56,128]{1,0:T(8,128)S(1)}, f32[56,128]{1,0:T(8,128)S(1)}, u32[]{:S(2)}, u32[]{:S(2)}) collective-permute-start(f32[56,128]{1,0:T(8,128)S(1)} %get-tuple-element.75), channel_id=1, source_target_pairs={{0,16},{8,24},{16,0},{24,8},{1,17},{9,25},{17,1},{25,9},{2,18},{10... | collective-permute-start | bytes 86024 | tf_op jit(solution)/shard_map/ppermute | solution.py:651

commit v6 on v5

--- a/solution.py
+++ b/solution.py
@@ -313,17 +313,20 @@
 
 def lead_z_kernel(
     dims, lay, me_ref, cot_any, diff_any, phase_any, cour_any, upw_any,
-    keep, send, az, w, inv, left, right, phi, psi,
+    keep, send, az, w, inv, left, right, phi, psi, later,
     cot, diff, phase, cour, upw, wt, pht, pst, both, in_sems, sems,
 ):
     nx, ny = dims
     tiles = nx * ny // LANES
     half = nx // 2
+    count = len(lay.sizes)
+    ahead = pltpu.make_async_copy(cot_any.at[pl.ds(count, later.shape[0])], later, sems.at[4])
     small = [(diff_any, diff), (phase_any, phase), (cour_any.at[1], cour), (upw_any.at[1], upw)]
     for i, (source, target) in enumerate(small):
         pltpu.make_async_copy(source, target, sems.at[i]).start()
-    for c in range(len(lay.sizes)):
+    for c in range(count):
         pltpu.make_async_copy(cot_any.at[c], cot.at[c], in_sems.at[c]).start()
+    ahead.start()
 
     for i, (source, target) in enumerate(small[:2]):
         pltpu.make_async_copy(source, target, sems.at[i]).wait()
@@ -370,18 +373,12 @@
         pltpu.make_async_copy(cot_any.at[c], cot.at[c], in_sems.at[c]).wait()
 
     z_part(dims, lay, me_ref, cot, phi, psi, w, left, right, arrived, az, both, keep, send)
-
-
-def next_z_kernel(
-    dims, lay, start, me_ref, cot_any, phi, psi, w, left, right, keep, send, az, cot, both, in_sems,
-):
-    def copy(c):
-        return pltpu.make_async_copy(cot_any.at[start + c], cot.at[c], in_sems.at[c])
-
-    for c in range(len(lay.sizes)):
-        copy(c).start()
+    ahead.wait()
+
+
+def next_z_kernel(dims, lay, me_ref, cot, phi, psi, w, left, right, keep, send, az, both):
     z_part(
-        dims, lay, me_ref, cot, phi, psi, w, left, right, lambda c: copy(c).wait(), az, both, keep, send
+        dims, lay, me_ref, cot, phi, psi, w, left, right, lambda c: None, az, both, keep, send
     )
 
 
@@ -536,7 +533,7 @@
         fluxes[here, :] = edge
         return tuple(new) + (edge,)
 
-    lax.fori_loop(0, nx, sweep, tuple(starts), unroll=8)
+    lax.fori_loop(0, nx, sweep, tuple(starts), unroll=16)
 
     def back(step, carry):
         x = nx - 1 - step
@@ -553,7 +550,7 @@
         fluxes[here, :] = edge * two_sides(lower[pl.ds(nx + x, 1), :], higher[pl.ds(nx + x, 1), :])
         return tuple(new) + (edge,)
 
-    lax.fori_loop(0, nx, back, tuple(nexts), unroll=8)
+    lax.fori_loop(0, nx, back, tuple(nexts), unroll=16)
     blank = jnp.zeros((comps, ny, LANES), jnp.float32)
     field[:, pl.ds(0, ny), :] = blank
     field[:, pl.ds((nx + 1) * ny, ny), :] = blank
@@ -643,6 +640,7 @@
         scratch_shapes=list(scratch),
         input_output_aliases=aliases or {},
         compiler_params=params,
+        cost_estimate=pl.CostEstimate(flops=1024, bytes_accessed=1024, transcendentals=0),
     )(*operands)
 
 
@@ -700,16 +698,16 @@
     cour = courant.reshape(3, rows, nz)
     upw = upwind.reshape(3, rows, nz)
     n = counts[0]
-    keep, send, az, w, inv, left, right, phi, psi = call(
+    keep, send, az, w, inv, left, right, phi, psi, cot_next = call(
         functools.partial(lead_z_kernel, (nx, ny), ylays[0]),
         "z_solve_lead",
         (me, cot, diffusion.reshape(flat), phase.reshape(flat), cour, upw),
-        [(ylays[0].rows, nz)] * 2 + [(n, rows, nz)] + [flat] * 6,
+        [(ylays[0].rows, nz)] * 2 + [(n, rows, nz)] + [flat] * 6 + [(counts[1], rows, nz)],
         [
             vmem(n, rows, nz), vmem(*flat), vmem(*flat, dtype=jnp.int32),
             vmem(*flat), vmem(*flat, dtype=jnp.int32),
             vmem(*flat), vmem(*flat), vmem(*flat), vmem(2 * ylays[0].rows, nz),
-            pltpu.SemaphoreType.DMA((n,)), pltpu.SemaphoreType.DMA((4,)),
+            pltpu.SemaphoreType.DMA((n,)), pltpu.SemaphoreType.DMA((5,)),
         ],
         spaces="shhhhh",
         mebibytes=12,
@@ -719,14 +717,11 @@
     azs = [az]
     n = counts[1]
     keep, send, az = call(
-        functools.partial(next_z_kernel, (nx, ny), ylays[1], starts[1]),
+        functools.partial(next_z_kernel, (nx, ny), ylays[1]),
         "z_solve_next",
-        (me, cot, phi, psi, w, left, right),
+        (me, cot_next, phi, psi, w, left, right),
         [(ylays[1].rows, nz)] * 2 + [(n, rows, nz)],
-        [
-            vmem(n, rows, nz), vmem(2 * ylays[1].rows, nz), pltpu.SemaphoreType.DMA((n,)),
-        ],
-        spaces="shvvvvv",
+        [vmem(2 * ylays[1].rows, nz)],
         mebibytes=8,
     )
     azs.append(az)

time: 34.8 us -> 33.5 us (0.963)
  Pallas kernels: 11.8 us -> 10.4 us
    pallas_call x15, Pallas kernels: 11.8 us -> 10.4 us  [call(): pl.pallas_call(kernel, name=name, out_shape=[held[s](shape, jnp.float32)...]
  transfers between devices with their start and end apart: 12 -> 12, of which waited for: 6 -> 6; matrix products, arithmetic and copies ran while one was open for 0% -> 0% of each run, Pallas kernels for 19% -> 16%
where the time goes in v6:
time: 33.5 us; the launch traced here: 33.3 us
  starting transfers between devices  16 us (48%)
  Pallas kernels  10.4 us (31%)
  waiting for transfers between devices  6.78 us (20%)
    ppermute x12, starting transfers between devices, exchange(): return lax.ppermute(rows, axis, [(i, i ^ 1 << bit) for i in range(count)])  16 us
    pallas_call x15, Pallas kernels, call(): pl.pallas_call(kernel, name=name, out_shape=[held[s](shape, jnp.float32)...  10.4 us
    ppermute x12, waiting for transfers between devices, exchange(): return lax.ppermute(rows, axis, [(i, i ^ 1 << bit) for i in range(count)])  6.78 us
  transfers between devices with their start and end apart: 12, of which 6 were waited for; matrix products, arithmetic and copies ran while one was open for 0% of the time, Pallas kernels for 16%

profile of v6, /device:TPU:0, one launch (start us, length us, event | category | flops | bytes accessed | tf_op | source)
XLA Modules:
  0.0 33.3 jit_solution(16683783689940761591)
XLA Ops:
  0.0 3.5 %z_solve_lead.1 = (f32[208,128]{1,0:T(8,128)S(1)}, f32[208,128]{1,0:T(8,128)S(1)}, f32[3,512,128]{2,1,0:T(8,128)S(1)}, f32[512,128]{1,0:T(8,128)S(1)}, f32[512,1...) custom-call(s32[1]{0:T(128)} %bitcast.me_ref, ...), custom_call_target="tpu_custom_call" | custom-call | flops 1024 | bytes 1024 | tf_op jit(solution)/shard_map/z_solve_lead/pallas_call | solution.py:631
  3.6 0.5 %collective-permute-start.1 = (f32[208,128]{1,0:T(8,128)S(1)}, f32[208,128]{1,0:T(8,128)S(1)}, u32[]{:S(2)}, u32[]{:S(2)}) collective-permute-start(f32[208,128]{1,0:T(8,128)S(1)} %get-tuple-element.56), channel_id=1, source_target_pairs={{0,1},{1,0},{2,3},{3,2},{4,5},{5,4},{6,7},{7,6},{8,9},{9,8},{10,11... | collective-permute-start | bytes 319496 | tf_op jit(solution)/shard_map/ppermute | solution.py:649
  4.1 1.2 %z_solve_next.1 = (f32[96,128]{1,0:T(8,128)S(1)}, f32[96,128]{1,0:T(8,128)S(1)}, f32[3,512,128]{2,1,0:T(8,128)S(1)}) custom-call(s32[1]{0:T(128)} %bitcast.me_ref, f32[3,512,128]{2,1,0:T(8,128)S(1)} %get-tuple-element.46.cot, f32[512,128]{1,0:T(8,128)S(1)} %get-tuple-element.47.phi, f32[512,128]{1,0:T(8,128)S(1)} %get-tuple-element.48.psi, ...), custom_call_target="tpu_custom_call" | custom-call | flops 1024 | bytes 1024 | tf_op jit(solution)/shard_map/z_solve_next/pallas_call | solution.py:631
  5.4 2.6 %collective-permute-start.3 = (f32[208,128]{1,0:T(8,128)S(1)}, f32[208,128]{1,0:T(8,128)S(1)}, u32[]{:S(2)}, u32[]{:S(2)}) collective-permute-start(f32[208,128]{1,0:T(8,128)S(1)} %merge_gy.5.refs_0_.after.own.refs_7_.refs_1_), channel_id=1, source_target_pairs={{0,2},{1,3},{2,0},{3,1},{4,6},{5,7},{6,4},{7,5},{8,10},{9,11},{10,... | collective-permute-start | bytes 319496 | tf_op jit(solution)/shard_map/ppermute | solution.py:649
  8.0 0.2 collective-permute-start
  8.2 0.3 %x_coefficients.1 = (f32[80,128]{1,0:T(8,128)S(1)}, f32[512,128]{1,0:T(8,128)S(1)}, f32[512,128]{1,0:T(8,128)S(1)}, f32[512,128]{1,0:T(8,128)S(1)}, f32[3584,128]{1,0:T(8,128)S(1)}) custom-call(f32[512,128]{1,0:T(8,128)S(1)} %get-tuple-element.49.w.refs_8_.refs_12_, f32[3,512,128]{2,1,0:T(8,128)S(1)} %bitcast.8, s32[3,512,128]{2,1,0:T(8,128)S(1)} %bitcast.10, ...), custom_call_target="tpu_custom_call" | custom-call | flops 1024 | bytes 1024 | tf_op jit(solution)/shard_map/x_coefficients/pallas_call | solution.py:631
  8.5 0.7 %collective-permute-done.other.refs_3_ = f32[96,128]{1,0:T(8,128)S(1)} collective-permute-done((f32[96,128]{1,0:T(8,128)S(1)}, f32[96,128]{1,0:T(8,128)S(1)}, u32[]{:S(2)}, u32[]{:S(2)}) %collective-permute-start) | collective-permute-done | bytes 49184 | tf_op jit(solution)/shard_map/ppermute | solution.py:649
  9.2 0.2 collective-permute-start.2
  9.5 2.1 %collective-permute-done.3.refs_1_.other.refs_10_.refs_4_ = f32[208,128]{1,0:T(8,128)S(1)} collective-permute-done((f32[208,128]{1,0:T(8,128)S(1)}, f32[208,128]{1,0:T(8,128)S(1)}, u32[]{:S(2)}, u32[]{:S(2)}) %collective-permute-start.3) | collective-permute-done | bytes 106528 | tf_op jit(solution)/shard_map/ppermute | solution.py:649
  11.6 1.8 %collective-permute-start.5 = (f32[96,128]{1,0:T(8,128)S(1)}, f32[96,128]{1,0:T(8,128)S(1)}, u32[]{:S(2)}, u32[]{:S(2)}) collective-permute-start(f32[96,128]{1,0:T(8,128)S(1)} %get-tuple-element.61), channel_id=1, source_target_pairs={{0,4},{1,5},{2,6},{3,7},{4,0},{5,1},{6,2},{7,3},{8,12},{9,13},{10,... | collective-permute-start | bytes 147464 | tf_op jit(solution)/shard_map/ppermute | solution.py:649
  13.5 2.3 %collective-permute-done.5.refs_11_.refs_5_ = f32[96,128]{1,0:T(8,128)S(1)} collective-permute-done((f32[96,128]{1,0:T(8,128)S(1)}, f32[96,128]{1,0:T(8,128)S(1)}, u32[]{:S(2)}, u32[]{:S(2)}) %collective-permute-start.5) | collective-permute-done | bytes 49184 | tf_op jit(solution)/shard_map/ppermute | solution.py:649
  15.9 1.8 %collective-permute-start.4 = (f32[48,128]{1,0:T(8,128)S(1)}, f32[48,128]{1,0:T(8,128)S(1)}, u32[]{:S(2)}, u32[]{:S(2)}) collective-permute-start(f32[48,128]{1,0:T(8,128)S(1)} %get-tuple-element.58.refs_6_), channel_id=1, source_target_pairs={{0,4},{1,5},{2,6},{3,7},{4,0},{5,1},{6,2},{7,3},{8,12},{9,13},{10,... | collective-permute-start | bytes 73736 | tf_op jit(solution)/shard_map/ppermute | solution.py:649
  17.7 0.9 %y_solve_lead.1 = (f32[200,128]{1,0:T(8,128)S(1)}, f32[3,512,128]{2,1,0:T(8,128)S(1)}, f32[256,128]{1,0:T(8,128)S(1)}, f32[256,128]{1,0:T(8,128)S(1)}, f32[256,1...) custom-call(s32[1]{0:T(128)} %bitcast.me_ref, ...), custom_call_target="tpu_custom_call" | custom-call | flops 1024 | bytes 1024 | tf_op jit(solution)/shard_map/y_solve_lead/pallas_call | solution.py:631
  18.7 1.7 %collective-permute-start.9 = (f32[200,128]{1,0:T(8,128)S(1)}, f32[200,128]{1,0:T(8,128)S(1)}, u32[]{:S(2)}, u32[]{:S(2)}) collective-permute-start(f32[200,128]{1,0:T(8,128)S(1)} %get-tuple-element.75.refs_0_.own.refs_4_), channel_id=1, source_target_pairs={{0,8},{8,0},{16,24},{24,16},{1,9},{9,1},{17,25},{25,17},{2,10},{10... | collective-permute-start | bytes 307208 | tf_op jit(solution)/shard_map/ppermute | solution.py:649
  20.4 0.1 collective-permute-start.6
  20.5 1.2 %collective-permute-done.6.got = f32[96,128]{1,0:T(8,128)S(1)} collective-permute-done((f32[96,128]{1,0:T(8,128)S(1)}, f32[96,128]{1,0:T(8,128)S(1)}, u32[]{:S(2)}, u32[]{:S(2)}) %collective-permute-start.6) | collective-permute-done | bytes 49184 | tf_op jit(solution)/shard_map/ppermute | solution.py:649
  21.7 0.9 %y_solve_next.1 = (f32[112,128]{1,0:T(8,128)S(1)}, f32[3,512,128]{2,1,0:T(8,128)S(1)}, f32[256,128]{1,0:T(8,128)S(1)}) custom-call(s32[1]{0:T(128)} %bitcast.me_ref, f32[3,512,128]{2,1,0:T(8,128)S(1)} %get-tuple-element.52.az, f32[96,128]{1,0:T(8,128)S(1)} %get-tuple-element.62.own, f32[96,128]{1,0:T(8,128)S(1)} %collective-permute-done.6.got, ...), custom_call_target="tpu_custom_call" | custom-call | flops 1024 | bytes 1024 | tf_op jit(solution)/shard_map/y_solve_next/pallas_call | solution.py:631
  22.6 1.4 %collective-permute-start.8 = (f32[112,128]{1,0:T(8,128)S(1)}, f32[112,128]{1,0:T(8,128)S(1)}, u32[]{:S(2)}, u32[]{:S(2)}) collective-permute-start(f32[112,128]{1,0:T(8,128)S(1)} %get-tuple-element.74.own.refs_0_), channel_id=1, source_target_pairs={{0,8},{8,0},{16,24},{24,16},{1,9},{9,1},{17,25},{25,17},{2,10},{10... | collective-permute-start | bytes 172040 | tf_op jit(solution)/shard_map/ppermute | solution.py:649
  24.0 2.6 %collective-permute-start.11 = (f32[96,128]{1,0:T(8,128)S(1)}, f32[96,128]{1,0:T(8,128)S(1)}, u32[]{:S(2)}, u32[]{:S(2)}) collective-permute-start(f32[96,128]{1,0:T(8,128)S(1)} %get-tuple-element.79), channel_id=1, source_target_pairs={{0,16},{8,24},{16,0},{24,8},{1,17},{9,25},{17,1},{25,9},{2,18},{10... | collective-permute-start | bytes 147464 | tf_op jit(solution)/shard_map/ppermute | solution.py:649
  26.6 0.2 collective-permute-done.8.other.refs_2_
  26.9 3.0 %collective-permute-start.10 = (f32[56,128]{1,0:T(8,128)S(1)}, f32[56,128]{1,0:T(8,128)S(1)}, u32[]{:S(2)}, u32[]{:S(2)}) collective-permute-start(f32[56,128]{1,0:T(8,128)S(1)} %get-tuple-element.77), channel_id=1, source_target_pairs={{0,16},{8,24},{16,0},{24,8},{1,17},{9,25},{17,1},{25,9},{2,18},{10... | collective-permute-start | bytes 86024 | tf_op jit(solution)/shard_map/ppermute | solution.py:649
  29.8 1.6 %x_solve.2.refs_16_ = f32[6,512,128]{2,1,0:T(8,128)} custom-call(s32[1]{0:T(128)} %bitcast.me_ref, f32[200,128]{1,0:T(8,128)S(1)} %get-tuple-element.75.refs_0_.own.refs_4_, f32[200,128]{1,0:T(8,128)S(1)} %get-tuple-element.78.refs_1_.refs_5_, f32[200,128]{1,0:T(8,128)S(1)} %collective-permute-done.9.refs_1_.other.refs_2_.refs_6_, ...), custom_call_target="tpu_custom_call" | custom-call | flops 1024 | bytes 1024 | tf_op jit(solution)/shard_map/x_solve/pallas_call | solution.py:631
  31.5 0.2 collective-permute-done.10.refs_3_
  31.7 1.6 %x_solve.3 = f32[6,512,128]{2,1,0:T(8,128)} custom-call(s32[1]{0:T(128)} %bitcast.me_ref, f32[112,128]{1,0:T(8,128)S(1)} %get-tuple-element.74.own.refs_0_, f32[112,128]{1,0:T(8,128)S(1)} %get-tuple-element.76.refs_1_, f32[112,128]{1,0:T(8,128)S(1)} %collective-permute-done.8.other.refs_2_, ...), custom_call_target="tpu_custom_call", output_to_operand_aliasing={{}: (17, {})} | custom-call | flops 1024 | bytes 1024 | tf_op jit(solution)/shard_map/x_solve/pallas_call | solution.py:631
  (19 shorter events, 0.3 us)
Async XLA Ops:
  3.6 4.6 %copy-start = (f32[3,32,16,128]{3,2,1,0:T(8,128)S(1)}, f32[3,32,16,128]{3,2,1,0:T(8,128)}, u32[]{:S(2)}) copy-start(f32[3,32,16,128]{3,2,1,0:T(8,128)} %param.8) | copy-start | bytes 2359300
  3.6 4.6 %copy-start.1 = (s32[3,32,16,128]{3,2,1,0:T(8,128)S(1)}, s32[3,32,16,128]{3,2,1,0:T(8,128)}, u32[]{:S(2)}) copy-start(s32[3,32,16,128]{3,2,1,0:T(8,128)} %param.9) | copy-start | bytes 2359300
  3.6 1.7 %collective-permute-start.1 = (f32[208,128]{1,0:T(8,128)S(1)}, f32[208,128]{1,0:T(8,128)S(1)}, u32[]{:S(2)}, u32[]{:S(2)}) collective-permute-start(f32[208,128]{1,0:T(8,128)S(1)} %get-tuple-element.56), channel_id=1, source_target_pairs={{0,1},{1,0},{2,3},{3,2},{4,5},{5,4},{6,7},{7,6},{8,9},{9,8},{10,11... | collective-permute-start | bytes 319496 | tf_op jit(solution)/shard_map/ppermute | solution.py:649
  5.4 6.2 %collective-permute-start.3 = (f32[208,128]{1,0:T(8,128)S(1)}, f32[208,128]{1,0:T(8,128)S(1)}, u32[]{:S(2)}, u32[]{:S(2)}) collective-permute-start(f32[208,128]{1,0:T(8,128)S(1)} %merge_gy.5.refs_0_.after.own.refs_7_.refs_1_), channel_id=1, source_target_pairs={{0,2},{1,3},{2,0},{3,1},{4,6},{5,7},{6,4},{7,5},{8,10},{9,11},{10,... | collective-permute-start | bytes 319496 | tf_op jit(solution)/shard_map/ppermute | solution.py:649
  8.0 1.2 %collective-permute-start = (f32[96,128]{1,0:T(8,128)S(1)}, f32[96,128]{1,0:T(8,128)S(1)}, u32[]{:S(2)}, u32[]{:S(2)}) collective-permute-start(f32[96,128]{1,0:T(8,128)S(1)} %get-tuple-element.54.refs_0_), channel_id=1, source_target_pairs={{0,1},{1,0},{2,3},{3,2},{4,5},{5,4},{6,7},{7,6},{8,9},{9,8},{10,11... | collective-permute-start | bytes 147464 | tf_op jit(solution)/shard_map/ppermute | solution.py:649
  9.2 4.2 %collective-permute-start.2 = (f32[96,128]{1,0:T(8,128)S(1)}, f32[96,128]{1,0:T(8,128)S(1)}, u32[]{:S(2)}, u32[]{:S(2)}) collective-permute-start(f32[96,128]{1,0:T(8,128)S(1)} %merge_gy.4.own.refs_1_), channel_id=1, source_target_pairs={{0,2},{1,3},{2,0},{3,1},{4,6},{5,7},{6,4},{7,5},{8,10},{9,11},{10,... | collective-permute-start | bytes 147464 | tf_op jit(solution)/shard_map/ppermute | solution.py:649
  11.6 4.2 %collective-permute-start.5 = (f32[96,128]{1,0:T(8,128)S(1)}, f32[96,128]{1,0:T(8,128)S(1)}, u32[]{:S(2)}, u32[]{:S(2)}) collective-permute-start(f32[96,128]{1,0:T(8,128)S(1)} %get-tuple-element.61), channel_id=1, source_target_pairs={{0,4},{1,5},{2,6},{3,7},{4,0},{5,1},{6,2},{7,3},{8,12},{9,13},{10,... | collective-permute-start | bytes 147464 | tf_op jit(solution)/shard_map/ppermute | solution.py:649
  15.8 1.9 %collective-permute-start.7 = (f32[160,128]{1,0:T(8,128)S(1)}, f32[160,128]{1,0:T(8,128)S(1)}, u32[]{:S(2)}, u32[]{:S(2)}) collective-permute-start(f32[160,128]{1,0:T(8,128)S(1)} %get-tuple-element.69), channel_id=1, source_target_pairs={{0,1},{1,0},{2,3},{3,2},{4,5},{5,4},{6,7},{7,6},{8,9},{9,8},{10,11... | collective-permute-start | bytes 245768 | tf_op jit(solution)/shard_map/ppermute | solution.py:649
  15.9 4.5 %collective-permute-start.4 = (f32[48,128]{1,0:T(8,128)S(1)}, f32[48,128]{1,0:T(8,128)S(1)}, u32[]{:S(2)}, u32[]{:S(2)}) collective-permute-start(f32[48,128]{1,0:T(8,128)S(1)} %get-tuple-element.58.refs_6_), channel_id=1, source_target_pairs={{0,4},{1,5},{2,6},{3,7},{4,0},{5,1},{6,2},{7,3},{8,12},{9,13},{10,... | collective-permute-start | bytes 73736 | tf_op jit(solution)/shard_map/ppermute | solution.py:649
  18.7 5.3 %collective-permute-start.9 = (f32[200,128]{1,0:T(8,128)S(1)}, f32[200,128]{1,0:T(8,128)S(1)}, u32[]{:S(2)}, u32[]{:S(2)}) collective-permute-start(f32[200,128]{1,0:T(8,128)S(1)} %get-tuple-element.75.refs_0_.own.refs_4_), channel_id=1, source_target_pairs={{0,8},{8,0},{16,24},{24,16},{1,9},{9,1},{17,25},{25,17},{2,10},{10... | collective-permute-start | bytes 307208 | tf_op jit(solution)/shard_map/ppermute | solution.py:649
  20.4 1.3 %collective-permute-start.6 = (f32[96,128]{1,0:T(8,128)S(1)}, f32[96,128]{1,0:T(8,128)S(1)}, u32[]{:S(2)}, u32[]{:S(2)}) collective-permute-start(f32[96,128]{1,0:T(8,128)S(1)} %get-tuple-element.63), channel_id=1, source_target_pairs={{0,1},{1,0},{2,3},{3,2},{4,5},{5,4},{6,7},{7,6},{8,9},{9,8},{10,11... | collective-permute-start | bytes 147464 | tf_op jit(solution)/shard_map/ppermute | solution.py:649
  22.6 4.2 %collective-permute-start.8 = (f32[112,128]{1,0:T(8,128)S(1)}, f32[112,128]{1,0:T(8,128)S(1)}, u32[]{:S(2)}, u32[]{:S(2)}) collective-permute-start(f32[112,128]{1,0:T(8,128)S(1)} %get-tuple-element.74.own.refs_0_), channel_id=1, source_target_pairs={{0,8},{8,0},{16,24},{24,16},{1,9},{9,1},{17,25},{25,17},{2,10},{10... | collective-permute-start | bytes 172040 | tf_op jit(solution)/shard_map/ppermute | solution.py:649
  24.0 5.9 %collective-permute-start.11 = (f32[96,128]{1,0:T(8,128)S(1)}, f32[96,128]{1,0:T(8,128)S(1)}, u32[]{:S(2)}, u32[]{:S(2)}) collective-permute-start(f32[96,128]{1,0:T(8,128)S(1)} %get-tuple-element.79), channel_id=1, source_target_pairs={{0,16},{8,24},{16,0},{24,8},{1,17},{9,25},{17,1},{25,9},{2,18},{10... | collective-permute-start | bytes 147464 | tf_op jit(solution)/shard_map/ppermute | solution.py:649
  26.9 4.8 %collective-permute-start.10 = (f32[56,128]{1,0:T(8,128)S(1)}, f32[56,128]{1,0:T(8,128)S(1)}, u32[]{:S(2)}, u32[]{:S(2)}) collective-permute-start(f32[56,128]{1,0:T(8,128)S(1)} %get-tuple-element.77), channel_id=1, source_target_pairs={{0,16},{8,24},{16,0},{24,8},{1,17},{9,25},{17,1},{25,9},{2,18},{10... | collective-permute-start | bytes 86024 | tf_op jit(solution)/shard_map/ppermute | solution.py:649

commit v7 on v6

--- a/solution.py
+++ b/solution.py
@@ -207,6 +207,16 @@
     write_block(lay, out, block)
     if top:
         write_side(lay, side[0], block, (me_ref[0] >> (bit + 1)) & 1)
+
+
+def first_merge_kernel(lay, bit, top, me_ref, own, slim, apart, *refs):
+    out, joined, *side = refs[-3:] if top else refs[-2:]
+    joined[pl.ds(0, lay.couple), :] = slim[pl.ds(0, lay.couple), :]
+    joined[pl.ds(lay.packed, TILE), :] = slim[pl.ds(lay.couple, TILE), :]
+    joined[pl.ds(lay.couple, 3 * lay.lines), :] = apart[pl.ds(0, 3 * lay.lines), :]
+    edges = 2 * lay.edges * lay.lines
+    joined[pl.ds(lay.edge, edges), :] = apart[pl.ds(3 * lay.lines, edges), :]
+    merge_kernel(lay, lay, bit, top, me_ref, own, joined, out, *side)
 
 
 def solve_lines(lay, lead, levels, me, refs):
@@ -437,7 +447,7 @@
     half = nx // 2
     comps = len(ylay.sizes)
     if xlay.leads:
-        part, block, ay, ghost, ginv, gleft, gright, before, after, joined = refs
+        part, block, slim, ay, ghost, ginv, gleft, gright, before, after, joined = refs
     else:
         before, after, gleft, gright, block, ay, ghost, joined = refs
     mine = me_ref[0] & 1
@@ -506,6 +516,9 @@
         record["far"] = [pieces[2], end * total]
         record["head"], record["tail"] = pieces[3:4], pieces[4:5]
     write_block(xlay, block, record)
+    if xlay.leads:
+        slim[pl.ds(0, xlay.couple), :] = block[pl.ds(0, xlay.couple), :]
+        slim[pl.ds(xlay.couple, TILE), :] = block[pl.ds(xlay.packed, TILE), :]
 
 
 def x_kernel(dims, lay, lead, levels, shift, start, me_ref, *refs):
@@ -640,7 +653,7 @@
         scratch_shapes=list(scratch),
         input_output_aliases=aliases or {},
         compiler_params=params,
-        cost_estimate=pl.CostEstimate(flops=1024, bytes_accessed=1024, transcendentals=0),
+        cost_estimate=pl.CostEstimate(flops=10**9, bytes_accessed=10**7, transcendentals=0),
     )(*operands)
 
 
@@ -658,12 +671,22 @@
     def send(self):
         self.gots.append(exchange(self.outgoing, self.axis, len(self.gots)))
 
-    def merge(self, beside=()):
+    def merge(self, beside=(), apart=None):
         level = len(self.owns) - 1
         top = level == self.levels - 2
         leader = self.lead or self
         coupled = () if self.lay.leads else (leader.owns[level], leader.gots[level])
         shapes = [(self.lay.rows, LANES)] + ([(self.lay.side_rows, LANES)] if top else [])
+        if apart is not None:
+            merged, self.gots[0], *side = call(
+                functools.partial(first_merge_kernel, self.lay, self.shift, top),
+                "merge_" + self.axis,
+                (self.me, self.owns[0], self.gots[0], apart) + tuple(beside),
+                shapes[:1] + shapes,
+            )
+            self.owns.append(merged)
+            self.outgoing = side[-1] if top else merged
+            return
         merged = call(
             functools.partial(merge_kernel, self.lay, leader.lay, self.shift + level, top),
             "merge_" + self.axis,
@@ -744,12 +767,13 @@
                 mebibytes=8,
             )
             beside = (part, follow.outgoing)
+            apart = exchange(part, "gx", 0)
     ladders, mets, answers = (lead, follow), [], []
     for g, ladder in enumerate(ladders):
         answer, passed = call(
             functools.partial(solve_kernel, ylays[g], ylays[0], ladder.levels),
             "y_reduced",
-            (me,) + ladder.records() + (beside if g == 0 else ()),
+            (me,) + ladder.records() + (beside + (apart,) if g == 0 else ()),
             [(ylays[g].answer_rows, nz)] * 2,
         )
         answers.append(answer)
@@ -757,15 +781,16 @@
     ays, ghosts, climbs = [], [], []
     for g in range(2):
         common = (me, azs[g], answers[g], mets[g], w, inv, xleft, xright)
-        outs = [(xlays[g].rows, nz), (counts[g], rows, nz), (nx * TILE, nz)]
+        outs = [(counts[g], rows, nz), (nx * TILE, nz)]
         scratch = [vmem(2 * ylays[g].answer_rows, nz)]
         body = functools.partial(y_kernel, (nx, ny), ylays[g], xlays[g])
         if g == 0:
-            block, ay, ghost, ginv, gleft, gright, before, after = call(
+            block, slim, ay, ghost, ginv, gleft, gright, before, after = call(
                 body,
                 "y_solve_lead",
                 common + (part,),
-                outs + [(nx * TILE, nz)] * 3 + [(2 * nx, nz)] * 2,
+                [(xlays[0].rows, nz), (xlays[0].couple + TILE, nz)]
+                + outs + [(nx * TILE, nz)] * 3 + [(2 * nx, nz)] * 2,
                 scratch,
                 mebibytes=6,
             )
@@ -774,18 +799,20 @@
                 body,
                 "y_solve_next",
                 common + (before, after, gleft, gright),
-                outs,
+                [(xlays[1].rows, nz)] + outs,
                 scratch,
                 mebibytes=6,
             )
         ays.append(ay)
         ghosts.append(ghost)
-        climbs.append(Ladder(xlays[g], "gx", shift, me, block, block, climbs[0] if g else None))
+        outgoing, leader = (block, climbs[0]) if g else (slim, None)
+        climbs.append(Ladder(xlays[g], "gx", shift, me, outgoing, block, leader))
         climbs[g].send()
     beside = (block,)
     for level in range(climbs[0].levels - 1):
         for ladder in climbs:
-            ladder.merge(beside if ladder.lay.leads else ())
+            leads = ladder.lay.leads
+            ladder.merge(beside if leads else (), apart if leads and level == 0 else None)
             ladder.send()
         beside = (climbs[1].outgoing,)
     grad = None

time: 33.5 us -> 32.8 us (0.979)
  waiting for transfers between devices: 6.78 us -> 5.79 us
  local copies, waits for them, and re-layouts: 0.01 us -> 0.5 us
    ppermute x12 -> x13, waiting for transfers between devices: 6.78 us -> 5.79 us  [exchange(): return lax.ppermute(rows, axis, [(i, i ^ 1 << bit) for i in range(count)])]
    unnamed x4, local copies, waits for them, and re-layouts: 0.01 us -> 0.5 us
    ppermute x12 -> x13, starting transfers between devices: 16 us -> 15.8 us  [exchange(): return lax.ppermute(rows, axis, [(i, i ^ 1 << bit) for i in range(count)])]
  transfers between devices with their start and end apart: 12 -> 13, of which waited for: 6 -> 6; matrix products, arithmetic and copies ran while one was open for 0% -> 0% of each run, Pallas kernels for 16% -> 16%
where the time goes in v7:
time: 32.8 us; the launch traced here: 32.7 us
  starting transfers between devices  15.8 us (48%)
  Pallas kernels  10.5 us (32%)
  waiting for transfers between devices  5.79 us (18%)
  local copies, waits for them, and re-layouts  0.5 us (2%)
    ppermute x13, starting transfers between devices, exchange(): return lax.ppermute(rows, axis, [(i, i ^ 1 << bit) for i in range(count)])  15.8 us
    pallas_call x15, Pallas kernels, call(): pl.pallas_call(kernel, name=name, out_shape=[held[s](shape, jnp.float32)...  10.5 us
    ppermute x13, waiting for transfers between devices, exchange(): return lax.ppermute(rows, axis, [(i, i ^ 1 << bit) for i in range(count)])  5.79 us
  transfers between devices with their start and end apart: 13, of which 6 were waited for; matrix products, arithmetic and copies ran while one was open for 0% of the time, Pallas kernels for 16%

profile of v7, /device:TPU:0, one launch (start us, length us, event | category | flops | bytes accessed | tf_op | source)
XLA Modules:
  0.0 32.7 jit_solution(4702342804618682406)
XLA Ops:
  0.0 3.5 %z_solve_lead.1 = (f32[208,128]{1,0:T(8,128)S(1)}, f32[208,128]{1,0:T(8,128)S(1)}, f32[3,512,128]{2,1,0:T(8,128)S(1)}, f32[512,128]{1,0:T(8,128)S(1)}, f32[512,1...) custom-call(s32[1]{0:T(128)} %bitcast.me_ref, ...), custom_call_target="tpu_custom_call" | custom-call | flops 1000000000 | bytes 10000000 | tf_op jit(solution)/shard_map/z_solve_lead/pallas_call | solution.py:644
  3.6 0.6 %collective-permute-start.1 = (f32[208,128]{1,0:T(8,128)S(1)}, f32[208,128]{1,0:T(8,128)S(1)}, u32[]{:S(2)}, u32[]{:S(2)}) collective-permute-start(f32[208,128]{1,0:T(8,128)S(1)} %get-tuple-element.58), channel_id=1, source_target_pairs={{0,1},{1,0},{2,3},{3,2},{4,5},{5,4},{6,7},{7,6},{8,9},{9,8},{10,11... | collective-permute-start | bytes 319496 | tf_op jit(solution)/shard_map/ppermute | solution.py:662
  4.1 1.2 %z_solve_next.1 = (f32[96,128]{1,0:T(8,128)S(1)}, f32[96,128]{1,0:T(8,128)S(1)}, f32[3,512,128]{2,1,0:T(8,128)S(1)}) custom-call(s32[1]{0:T(128)} %bitcast.me_ref, f32[3,512,128]{2,1,0:T(8,128)S(1)} %get-tuple-element.48.cot, f32[512,128]{1,0:T(8,128)S(1)} %get-tuple-element.49.phi, f32[512,128]{1,0:T(8,128)S(1)} %get-tuple-element.50.psi, ...), custom_call_target="tpu_custom_call" | custom-call | flops 1000000000 | bytes 10000000 | tf_op jit(solution)/shard_map/z_solve_next/pallas_call | solution.py:644
  5.4 3.0 %collective-permute-start.3 = (f32[208,128]{1,0:T(8,128)S(1)}, f32[208,128]{1,0:T(8,128)S(1)}, u32[]{:S(2)}, u32[]{:S(2)}) collective-permute-start(f32[208,128]{1,0:T(8,128)S(1)} %merge_gy.5.refs_0_.after.own.refs_7_.refs_1_), channel_id=1, source_target_pairs={{0,2},{1,3},{2,0},{3,1},{4,6},{5,7},{6,4},{7,5},{8,10},{9,11},{10,... | collective-permute-start | bytes 319496 | tf_op jit(solution)/shard_map/ppermute | solution.py:662
  8.5 0.8 %collective-permute-start.2 = (f32[96,128]{1,0:T(8,128)S(1)}, f32[96,128]{1,0:T(8,128)S(1)}, u32[]{:S(2)}, u32[]{:S(2)}) collective-permute-start(f32[96,128]{1,0:T(8,128)S(1)} %merge_gy.4.own.refs_1_), channel_id=1, source_target_pairs={{0,2},{1,3},{2,0},{3,1},{4,6},{5,7},{6,4},{7,5},{8,10},{9,11},{10,... | collective-permute-start | bytes 147464 | tf_op jit(solution)/shard_map/ppermute | solution.py:662
  9.3 0.3 copy-done
  9.8 0.4 %x_coefficients.1 = (f32[80,128]{1,0:T(8,128)S(1)}, f32[512,128]{1,0:T(8,128)S(1)}, f32[512,128]{1,0:T(8,128)S(1)}, f32[512,128]{1,0:T(8,128)S(1)}, f32[3584,128]{1,0:T(8,128)S(1)}) custom-call(f32[512,128]{1,0:T(8,128)S(1)} %get-tuple-element.51.w.refs_8_.refs_12_, f32[3,512,128]{2,1,0:T(8,128)S(1)} %bitcast.8, s32[3,512,128]{2,1,0:T(8,128)S(1)} %bitcast.10, ...), custom_call_target="tpu_custom_call" | custom-call | flops 1000000000 | bytes 10000000 | tf_op jit(solution)/shard_map/x_coefficients/pallas_call | solution.py:644
  10.2 1.6 %collective-permute-start.7 = (f32[80,128]{1,0:T(8,128)S(1)}, f32[80,128]{1,0:T(8,128)S(1)}, u32[]{:S(2)}, u32[]{:S(2)}) collective-permute-start(f32[80,128]{1,0:T(8,128)S(1)} %get-tuple-element.61.refs_0_), channel_id=1, source_target_pairs={{0,8},{8,0},{16,24},{24,16},{1,9},{9,1},{17,25},{25,17},{2,10},{10... | collective-permute-start | bytes 122888 | tf_op jit(solution)/shard_map/ppermute | solution.py:662
  11.8 0.4 %collective-permute-done.3.refs_1_.other.refs_10_.refs_4_ = f32[208,128]{1,0:T(8,128)S(1)} collective-permute-done((f32[208,128]{1,0:T(8,128)S(1)}, f32[208,128]{1,0:T(8,128)S(1)}, u32[]{:S(2)}, u32[]{:S(2)}) %collective-permute-start.3) | collective-permute-done | bytes 106528 | tf_op jit(solution)/shard_map/ppermute | solution.py:662
  12.2 1.8 %collective-permute-start.5 = (f32[96,128]{1,0:T(8,128)S(1)}, f32[96,128]{1,0:T(8,128)S(1)}, u32[]{:S(2)}, u32[]{:S(2)}) collective-permute-start(f32[96,128]{1,0:T(8,128)S(1)} %get-tuple-element.63), channel_id=1, source_target_pairs={{0,4},{1,5},{2,6},{3,7},{4,0},{5,1},{6,2},{7,3},{8,12},{9,13},{10,... | collective-permute-start | bytes 147464 | tf_op jit(solution)/shard_map/ppermute | solution.py:662
  14.0 0.5 %collective-permute-start.4 = (f32[48,128]{1,0:T(8,128)S(1)}, f32[48,128]{1,0:T(8,128)S(1)}, u32[]{:S(2)}, u32[]{:S(2)}) collective-permute-start(f32[48,128]{1,0:T(8,128)S(1)} %get-tuple-element.60.refs_6_), channel_id=1, source_target_pairs={{0,4},{1,5},{2,6},{3,7},{4,0},{5,1},{6,2},{7,3},{8,12},{9,13},{10,... | collective-permute-start | bytes 73736 | tf_op jit(solution)/shard_map/ppermute | solution.py:662
  14.5 1.8 %collective-permute-done.5.refs_11_.refs_5_ = f32[96,128]{1,0:T(8,128)S(1)} collective-permute-done((f32[96,128]{1,0:T(8,128)S(1)}, f32[96,128]{1,0:T(8,128)S(1)}, u32[]{:S(2)}, u32[]{:S(2)}) %collective-permute-start.5) | collective-permute-done | bytes 49184 | tf_op jit(solution)/shard_map/ppermute | solution.py:662
  16.5 1.4 %collective-permute-done.4.refs_5_ = f32[48,128]{1,0:T(8,128)S(1)} collective-permute-done((f32[48,128]{1,0:T(8,128)S(1)}, f32[48,128]{1,0:T(8,128)S(1)}, u32[]{:S(2)}, u32[]{:S(2)}) %collective-permute-start.4) | collective-permute-done | bytes 24608 | tf_op jit(solution)/shard_map/ppermute | solution.py:662
  18.0 1.0 %y_solve_lead.1 = (f32[200,128]{1,0:T(8,128)S(1)}, f32[120,128]{1,0:T(8,128)S(1)}, f32[3,512,128]{2,1,0:T(8,128)S(1)}, f32[256,128]{1,0:T(8,128)S(1)}, f32[256,1...) custom-call(s32[1]{0:T(128)} %bitcast.me_ref, ...), custom_call_target="tpu_custom_call" | custom-call | flops 1000000000 | bytes 10000000 | tf_op jit(solution)/shard_map/y_solve_lead/pallas_call | solution.py:644
  19.0 1.6 %collective-permute-start.10 = (f32[120,128]{1,0:T(8,128)S(1)}, f32[120,128]{1,0:T(8,128)S(1)}, u32[]{:S(2)}, u32[]{:S(2)}) collective-permute-start(f32[120,128]{1,0:T(8,128)S(1)} %get-tuple-element.78), channel_id=1, source_target_pairs={{0,8},{8,0},{16,24},{24,16},{1,9},{9,1},{17,25},{25,17},{2,10},{10... | collective-permute-start | bytes 184328 | tf_op jit(solution)/shard_map/ppermute | solution.py:662
  20.7 0.9 %y_solve_next.1 = (f32[112,128]{1,0:T(8,128)S(1)}, f32[3,512,128]{2,1,0:T(8,128)S(1)}, f32[256,128]{1,0:T(8,128)S(1)}) custom-call(s32[1]{0:T(128)} %bitcast.me_ref, f32[3,512,128]{2,1,0:T(8,128)S(1)} %get-tuple-element.54.az, f32[96,128]{1,0:T(8,128)S(1)} %get-tuple-element.64.own, f32[96,128]{1,0:T(8,128)S(1)} %collective-permute-done.6.got, ...), custom_call_target="tpu_custom_call" | custom-call | flops 1000000000 | bytes 10000000 | tf_op jit(solution)/shard_map/y_solve_next/pallas_call | solution.py:644
  21.6 0.5 %collective-permute-start.9 = (f32[112,128]{1,0:T(8,128)S(1)}, f32[112,128]{1,0:T(8,128)S(1)}, u32[]{:S(2)}, u32[]{:S(2)}) collective-permute-start(f32[112,128]{1,0:T(8,128)S(1)} %get-tuple-element.76.refs_0_.own), channel_id=1, source_target_pairs={{0,8},{8,0},{16,24},{24,16},{1,9},{9,1},{17,25},{25,17},{2,10},{10... | collective-permute-start | bytes 172040 | tf_op jit(solution)/shard_map/ppermute | solution.py:662
  22.1 1.4 %collective-permute-done.10.slim = f32[120,128]{1,0:T(8,128)S(1)} collective-permute-done((f32[120,128]{1,0:T(8,128)S(1)}, f32[120,128]{1,0:T(8,128)S(1)}, u32[]{:S(2)}, u32[]{:S(2)}) %collective-permute-start.10) | collective-permute-done | bytes 61472 | tf_op jit(solution)/shard_map/ppermute | solution.py:662
  23.5 2.7 %collective-permute-start.12 = (f32[96,128]{1,0:T(8,128)S(1)}, f32[96,128]{1,0:T(8,128)S(1)}, u32[]{:S(2)}, u32[]{:S(2)}) collective-permute-start(f32[96,128]{1,0:T(8,128)S(1)} %get-tuple-element.83), channel_id=1, source_target_pairs={{0,16},{8,24},{16,0},{24,8},{1,17},{9,25},{17,1},{25,9},{2,18},{10... | collective-permute-start | bytes 147464 | tf_op jit(solution)/shard_map/ppermute | solution.py:662
  26.2 2.4 %collective-permute-start.11 = (f32[56,128]{1,0:T(8,128)S(1)}, f32[56,128]{1,0:T(8,128)S(1)}, u32[]{:S(2)}, u32[]{:S(2)}) collective-permute-start(f32[56,128]{1,0:T(8,128)S(1)} %get-tuple-element.81), channel_id=1, source_target_pairs={{0,16},{8,24},{16,0},{24,8},{1,17},{9,25},{17,1},{25,9},{2,18},{10... | collective-permute-start | bytes 86024 | tf_op jit(solution)/shard_map/ppermute | solution.py:662
  28.6 0.3 collective-permute-done.12.refs_3_.refs_7_
  28.9 1.6 %x_solve.2.refs_16_ = f32[6,512,128]{2,1,0:T(8,128)} custom-call(s32[1]{0:T(128)} %bitcast.me_ref, f32[200,128]{1,0:T(8,128)S(1)} %get-tuple-element.77.own.refs_0_.refs_4_, f32[200,128]{1,0:T(8,128)S(1)} %get-tuple-element.82.refs_1_.refs_5_, f32[200,128]{1,0:T(8,128)S(1)} %get-tuple-element.79.refs_1_.refs_2_.refs_6_, ...), custom_call_target="tpu_custom_call" | custom-call | flops 1000000000 | bytes 10000000 | tf_op jit(solution)/shard_map/x_solve/pallas_call | solution.py:644
  30.5 0.5 %collective-permute-done.11.refs_3_ = f32[56,128]{1,0:T(8,128)S(1)} collective-permute-done((f32[56,128]{1,0:T(8,128)S(1)}, f32[56,128]{1,0:T(8,128)S(1)}, u32[]{:S(2)}, u32[]{:S(2)}) %collective-permute-start.11) | collective-permute-done | bytes 28704 | tf_op jit(solution)/shard_map/ppermute | solution.py:662
  31.0 1.6 %x_solve.3 = f32[6,512,128]{2,1,0:T(8,128)} custom-call(s32[1]{0:T(128)} %bitcast.me_ref, f32[112,128]{1,0:T(8,128)S(1)} %get-tuple-element.76.refs_0_.own, f32[112,128]{1,0:T(8,128)S(1)} %get-tuple-element.80.refs_1_, f32[112,128]{1,0:T(8,128)S(1)} %collective-permute-done.9.other.refs_2_, ...), custom_call_target="tpu_custom_call", output_to_operand_aliasing={{}: (17, {})} | custom-call | flops 1000000000 | bytes 10000000 | tf_op jit(solution)/shard_map/x_solve/pallas_call | solution.py:644
  (21 shorter events, 0.8 us)
Async XLA Ops:
  3.6 1.8 %collective-permute-start.1 = (f32[208,128]{1,0:T(8,128)S(1)}, f32[208,128]{1,0:T(8,128)S(1)}, u32[]{:S(2)}, u32[]{:S(2)}) collective-permute-start(f32[208,128]{1,0:T(8,128)S(1)} %get-tuple-element.58), channel_id=1, source_target_pairs={{0,1},{1,0},{2,3},{3,2},{4,5},{5,4},{6,7},{7,6},{8,9},{9,8},{10,11... | collective-permute-start | bytes 319496 | tf_op jit(solution)/shard_map/ppermute | solution.py:662
  5.3 3.2 %collective-permute-start = (f32[96,128]{1,0:T(8,128)S(1)}, f32[96,128]{1,0:T(8,128)S(1)}, u32[]{:S(2)}, u32[]{:S(2)}) collective-permute-start(f32[96,128]{1,0:T(8,128)S(1)} %get-tuple-element.56.refs_0_), channel_id=1, source_target_pairs={{0,1},{1,0},{2,3},{3,2},{4,5},{5,4},{6,7},{7,6},{8,9},{9,8},{10,11... | collective-permute-start | bytes 147464 | tf_op jit(solution)/shard_map/ppermute | solution.py:662
  5.4 6.7 %collective-permute-start.3 = (f32[208,128]{1,0:T(8,128)S(1)}, f32[208,128]{1,0:T(8,128)S(1)}, u32[]{:S(2)}, u32[]{:S(2)}) collective-permute-start(f32[208,128]{1,0:T(8,128)S(1)} %merge_gy.5.refs_0_.after.own.refs_7_.refs_1_), channel_id=1, source_target_pairs={{0,2},{1,3},{2,0},{3,1},{4,6},{5,7},{6,4},{7,5},{8,10},{9,11},{10,... | collective-permute-start | bytes 319496 | tf_op jit(solution)/shard_map/ppermute | solution.py:662
  8.5 1.1 %copy-start = (f32[3,32,16,128]{3,2,1,0:T(8,128)S(1)}, f32[3,32,16,128]{3,2,1,0:T(8,128)}, u32[]{:S(2)}) copy-start(f32[3,32,16,128]{3,2,1,0:T(8,128)} %param.8) | copy-start | bytes 2359300
  8.5 1.4 %copy-start.1 = (s32[3,32,16,128]{3,2,1,0:T(8,128)S(1)}, s32[3,32,16,128]{3,2,1,0:T(8,128)}, u32[]{:S(2)}) copy-start(s32[3,32,16,128]{3,2,1,0:T(8,128)} %param.9) | copy-start | bytes 2359300
  8.5 5.5 %collective-permute-start.2 = (f32[96,128]{1,0:T(8,128)S(1)}, f32[96,128]{1,0:T(8,128)S(1)}, u32[]{:S(2)}, u32[]{:S(2)}) collective-permute-start(f32[96,128]{1,0:T(8,128)S(1)} %merge_gy.4.own.refs_1_), channel_id=1, source_target_pairs={{0,2},{1,3},{2,0},{3,1},{4,6},{5,7},{6,4},{7,5},{8,10},{9,11},{10,... | collective-permute-start | bytes 147464 | tf_op jit(solution)/shard_map/ppermute | solution.py:662
  10.2 4.3 %collective-permute-start.7 = (f32[80,128]{1,0:T(8,128)S(1)}, f32[80,128]{1,0:T(8,128)S(1)}, u32[]{:S(2)}, u32[]{:S(2)}) collective-permute-start(f32[80,128]{1,0:T(8,128)S(1)} %get-tuple-element.61.refs_0_), channel_id=1, source_target_pairs={{0,8},{8,0},{16,24},{24,16},{1,9},{9,1},{17,25},{25,17},{2,10},{10... | collective-permute-start | bytes 122888 | tf_op jit(solution)/shard_map/ppermute | solution.py:662
  12.2 4.2 %collective-permute-start.5 = (f32[96,128]{1,0:T(8,128)S(1)}, f32[96,128]{1,0:T(8,128)S(1)}, u32[]{:S(2)}, u32[]{:S(2)}) collective-permute-start(f32[96,128]{1,0:T(8,128)S(1)} %get-tuple-element.63), channel_id=1, source_target_pairs={{0,4},{1,5},{2,6},{3,7},{4,0},{5,1},{6,2},{7,3},{8,12},{9,13},{10,... | collective-permute-start | bytes 147464 | tf_op jit(solution)/shard_map/ppermute | solution.py:662
  14.0 3.9 %collective-permute-start.4 = (f32[48,128]{1,0:T(8,128)S(1)}, f32[48,128]{1,0:T(8,128)S(1)}, u32[]{:S(2)}, u32[]{:S(2)}) collective-permute-start(f32[48,128]{1,0:T(8,128)S(1)} %get-tuple-element.60.refs_6_), channel_id=1, source_target_pairs={{0,4},{1,5},{2,6},{3,7},{4,0},{5,1},{6,2},{7,3},{8,12},{9,13},{10,... | collective-permute-start | bytes 73736 | tf_op jit(solution)/shard_map/ppermute | solution.py:662
  16.4 1.6 %collective-permute-start.8 = (f32[160,128]{1,0:T(8,128)S(1)}, f32[160,128]{1,0:T(8,128)S(1)}, u32[]{:S(2)}, u32[]{:S(2)}) collective-permute-start(f32[160,128]{1,0:T(8,128)S(1)} %get-tuple-element.71), channel_id=1, source_target_pairs={{0,1},{1,0},{2,3},{3,2},{4,5},{5,4},{6,7},{7,6},{8,9},{9,8},{10,11... | collective-permute-start | bytes 245768 | tf_op jit(solution)/shard_map/ppermute | solution.py:662
  18.0 2.7 %collective-permute-start.6 = (f32[96,128]{1,0:T(8,128)S(1)}, f32[96,128]{1,0:T(8,128)S(1)}, u32[]{:S(2)}, u32[]{:S(2)}) collective-permute-start(f32[96,128]{1,0:T(8,128)S(1)} %get-tuple-element.65), channel_id=1, source_target_pairs={{0,1},{1,0},{2,3},{3,2},{4,5},{5,4},{6,7},{7,6},{8,9},{9,8},{10,11... | collective-permute-start | bytes 147464 | tf_op jit(solution)/shard_map/ppermute | solution.py:662
  19.0 4.5 %collective-permute-start.10 = (f32[120,128]{1,0:T(8,128)S(1)}, f32[120,128]{1,0:T(8,128)S(1)}, u32[]{:S(2)}, u32[]{:S(2)}) collective-permute-start(f32[120,128]{1,0:T(8,128)S(1)} %get-tuple-element.78), channel_id=1, source_target_pairs={{0,8},{8,0},{16,24},{24,16},{1,9},{9,1},{17,25},{25,17},{2,10},{10... | collective-permute-start | bytes 184328 | tf_op jit(solution)/shard_map/ppermute | solution.py:662
  21.6 4.6 %collective-permute-start.9 = (f32[112,128]{1,0:T(8,128)S(1)}, f32[112,128]{1,0:T(8,128)S(1)}, u32[]{:S(2)}, u32[]{:S(2)}) collective-permute-start(f32[112,128]{1,0:T(8,128)S(1)} %get-tuple-element.76.refs_0_.own), channel_id=1, source_target_pairs={{0,8},{8,0},{16,24},{24,16},{1,9},{9,1},{17,25},{25,17},{2,10},{10... | collective-permute-start | bytes 172040 | tf_op jit(solution)/shard_map/ppermute | solution.py:662
  23.5 5.4 %collective-permute-start.12 = (f32[96,128]{1,0:T(8,128)S(1)}, f32[96,128]{1,0:T(8,128)S(1)}, u32[]{:S(2)}, u32[]{:S(2)}) collective-permute-start(f32[96,128]{1,0:T(8,128)S(1)} %get-tuple-element.83), channel_id=1, source_target_pairs={{0,16},{8,24},{16,0},{24,8},{1,17},{9,25},{17,1},{25,9},{2,18},{10... | collective-permute-start | bytes 147464 | tf_op jit(solution)/shard_map/ppermute | solution.py:662
  26.2 4.8 %collective-permute-start.11 = (f32[56,128]{1,0:T(8,128)S(1)}, f32[56,128]{1,0:T(8,128)S(1)}, u32[]{:S(2)}, u32[]{:S(2)}) collective-permute-start(f32[56,128]{1,0:T(8,128)S(1)} %get-tuple-element.81), channel_id=1, source_target_pairs={{0,16},{8,24},{16,0},{24,8},{1,17},{9,25},{17,1},{25,9},{2,18},{10... | collective-permute-start | bytes 86024 | tf_op jit(solution)/shard_map/ppermute | solution.py:662

commit v8 on v7

--- a/solution.py
+++ b/solution.py
@@ -207,6 +207,17 @@
     write_block(lay, out, block)
     if top:
         write_side(lay, side[0], block, (me_ref[0] >> (bit + 1)) & 1)
+
+
+def relay_merge_kernel(lay, bit, me_ref, own, other, held, out, passed):
+    passed[...] = held[...]
+    merge_kernel(lay, lay, bit, False, me_ref, own, other, out)
+
+
+def joint_merge_kernel(lay, lead, bit, me_ref, own, other, lead_own, lead_other, side, out, joint):
+    joint[pl.ds(0, lead.side_rows), :] = side[...]
+    rest = joint.at[pl.ds(lead.side_rows, lay.side_rows)]
+    merge_kernel(lay, lead, bit, True, me_ref, own, other, lead_own, lead_other, out, rest)
 
 
 def first_merge_kernel(lay, bit, top, me_ref, own, slim, apart, *refs):
@@ -323,7 +334,7 @@
 
 def lead_z_kernel(
     dims, lay, me_ref, cot_any, diff_any, phase_any, cour_any, upw_any,
-    keep, send, az, w, inv, left, right, phi, psi, later,
+    keep, send, az, w, left, right, phi, psi, later,
     cot, diff, phase, cour, upw, wt, pht, pst, both, in_sems, sems,
 ):
     nx, ny = dims
@@ -365,7 +376,6 @@
         span = pl.ds(y * nx, nx)
         left[span, :] = backs[y] * total
         right[span, :] = chain[y] * total
-        inv[span, :] = chain[y] / chain[y + 1]
     post(lay, both, lay.couple, backs[0] * total)
     post(lay, both, lay.couple + half, total)
     post(lay, both, lay.couple + 2 * half, chain[ny - 1] * total)
@@ -392,7 +402,7 @@
     )
 
 
-def coef_kernel(dims, w, courant, upwind, after, block, xinv, left, right, flows):
+def coef_kernel(dims, w, courant, upwind, after, block, inv, xinv, left, right, flows):
     del after
     nx, ny = dims
     rows = nx * ny
@@ -411,13 +421,20 @@
     block[pl.ds(0, ny), :] = corner * total
     block[pl.ds(ny, ny), :] = total
     block[pl.ds(2 * ny, ny), :] = end * total
+    value = jnp.ones((nx, LANES), jnp.float32)
+    slope = value
+    for y in range(ny):
+        new_value, slope = growing_step(value, slope, w[pl.ds(y, nx, stride=ny), :])
+        inv[pl.ds(y * nx, nx), :] = value / new_value
+        value = new_value
 
     lane = lax.broadcasted_iota(jnp.int32, (ny, LANES), 1)
 
     def plane(x, carry):
         span = pl.ds(x * ny, ny)
-        left[span, :] = left[span, :] * total
-        right[span, :] = right[span, :] * total
+        scale = w[span, :] * total
+        left[span, :] = left[span, :] * scale
+        right[span, :] = right[span, :] * scale
         own = one
         for d in range(3):
             flow = courant[d, span, :]
@@ -442,14 +459,14 @@
     return two_sides(before[pl.ds(x, 1), :], after[pl.ds(x, 1), :])
 
 
-def y_kernel(dims, ylay, xlay, me_ref, az, own, got, w, inv, left, right, *refs):
+def y_kernel(dims, ylay, xlay, me_ref, az, own, got, w, inv, xinv, *refs):
     nx, ny = dims
     half = nx // 2
     comps = len(ylay.sizes)
     if xlay.leads:
-        part, block, slim, ay, ghost, ginv, gleft, gright, before, after, joined = refs
+        part, block, slim, field, ghost, ginv, gleft, gright, before, after, ay, joined = refs
     else:
-        before, after, gleft, gright, block, ay, ghost, joined = refs
+        before, after, ginv, block, field, ghost, ay, joined = refs
     mine = me_ref[0] & 1
     span = ylay.answer_rows
     joined[pl.ds(pl.multiple_of(mine * span, TILE), span), :] = own[...]
@@ -473,8 +490,11 @@
             corner = back
             back, fall = growing_step(back, fall, sides(before, after, nx - 1 - k))
         total = 1.0 / value
-        gleft[...] = (gleft[...].reshape(nx, TILE, LANES) * total).reshape(nx * TILE, LANES)
-        gright[...] = (gright[...].reshape(nx, TILE, LANES) * total).reshape(nx * TILE, LANES)
+        for x in range(nx):
+            here = pl.ds(x * TILE, TILE)
+            scale = sides(before, after, nx + x) * total
+            gleft[here, :] = gleft[here, :] * scale
+            gright[here, :] = gright[here, :] * scale
 
     ghost[...] = jnp.zeros(ghost.shape, jnp.float32)
     for c in range(comps):
@@ -495,20 +515,25 @@
                 later = chain[y] + inv[pl.ds(y * nx + h * half, half), :] * later
                 ay[c, where, :] = later * w[where, :]
 
-    firsts = [jnp.zeros((n, LANES), jnp.float32) for n in xlay.sizes]
-    lasts = list(firsts)
+    swept = [jnp.zeros((n, LANES), jnp.float32) for n in xlay.sizes]
     for x in range(nx):
-        here = pl.ds(x * ny, ny)
-        near, far = left[here, :], right[here, :]
+        here, there = pl.ds(x * ny, ny), pl.ds(x * TILE, TILE)
         for c in range(comps):
-            cells = ay[c, here, :]
-            firsts[c] = firsts[c] + near * cells
-            lasts[c] = lasts[c] + far * cells
-        here = pl.ds(x * TILE, TILE)
-        cells = ghost[here, :]
-        firsts[comps] = firsts[comps] + gleft[here, :] * cells
-        lasts[comps] = lasts[comps] + gright[here, :] * cells
-    record = {"first": firsts, "last": lasts}
+            swept[c] = (ay[c, here, :] + swept[c]) * xinv[here, :]
+            ay[c, here, :] = swept[c]
+        swept[comps] = (ghost[there, :] + swept[comps]) * ginv[there, :]
+        ghost[there, :] = swept[comps]
+    lasts, solved = list(swept), list(swept)
+    for x in reversed(range(nx)):
+        here, there = pl.ds(x * ny, ny), pl.ds(x * TILE, TILE)
+        for c in range(comps):
+            if x + 1 < nx:
+                solved[c] = ay[c, here, :] + xinv[here, :] * solved[c]
+            field[c, here, :] = solved[c] * w[here, :]
+        if x + 1 < nx:
+            solved[comps] = ghost[there, :] + ginv[there, :] * solved[comps]
+        ghost[there, :] = solved[comps] * sides(before, after, nx + x)
+    record = {"first": solved, "last": lasts}
     if xlay.leads:
         pieces = [part[pl.ds(i * ny, ny), :] for i in range(5)]
         record["near"] = [pieces[0], corner * total]
@@ -521,49 +546,41 @@
         slim[pl.ds(xlay.couple, TILE), :] = block[pl.ds(xlay.packed, TILE), :]
 
 
-def x_kernel(dims, lay, lead, levels, shift, start, me_ref, *refs):
+def x_kernel(dims, lays, levels, shift, me_ref, *refs):
     nx, ny = dims
-    count = (2 if lay.leads else 4) * levels
-    state, _ = solve_lines(lay, lead, levels, me_ref[0] >> shift, refs[:count])
-    xinv, ginv, ay, ghost, w, lower, higher, flows, *rest = refs[count:]
-    out_any, out, field, fluxes, sems = rest[-5:]
+    lead, follow = lays
+    owns, gots, later_owns, later_gots = (refs[i * levels : (i + 1) * levels] for i in range(4))
+    later_gots = later_gots[:-1]
+    (left, right, gleft, gright, flows, *rest) = refs[4 * levels - 1 :]
+    inputs, ghosts = rest[:2], rest[2:4]
+    out_any, out, field, fluxes, sems = rest[4:]
     rows = nx * ny
-    comps = len(lay.sizes) - 1
     tiles = ny // TILE
-    starts, nexts, behind, ahead = state
-    near, far = behind[0], ahead[0]
-
-    def sweep(x, carry):
+    me = me_ref[0] >> shift
+    joint = gots[-1]
+    gots = gots[:-1] + (joint.at[pl.ds(0, lead.side_rows)],)
+    later_gots = later_gots + (joint.at[pl.ds(lead.side_rows, follow.side_rows)],)
+    first, _ = solve_lines(lead, lead, levels, me, owns + gots)
+    second, _ = solve_lines(follow, lead, levels, me, later_owns + later_gots + owns + gots)
+    near, far = first[2][0], first[3][0]
+    groups = (first, second)
+    place = [(g, c) for g, lay in enumerate(lays) for c in range(len(lay.sizes) - 1)]
+    starts = [groups[g][0][c] for g, c in place]
+    nexts = [groups[g][1][c] for g, c in place]
+    comps = len(place)
+
+    def fill(x, carry):
         span, above = pl.ds(x * ny, ny), pl.ds((x + 1) * ny, ny)
-        factor = xinv[span, :]
-        new = []
-        for c in range(comps):
-            value = (ay[c, span, :] + carry[c]) * factor
-            field[c, above, :] = value
-            new.append(value)
+        lower, upper = left[span, :], right[span, :]
+        for i, (g, c) in enumerate(place):
+            field[i, above, :] = inputs[g][c, span, :] + lower * starts[i] + upper * nexts[i]
         here = pl.ds(x * TILE, TILE)
-        edge = (ghost[here, :] + carry[comps]) * ginv[here, :]
-        fluxes[here, :] = edge
-        return tuple(new) + (edge,)
-
-    lax.fori_loop(0, nx, sweep, tuple(starts), unroll=16)
-
-    def back(step, carry):
-        x = nx - 1 - step
-        span, above = pl.ds(x * ny, ny), pl.ds((x + 1) * ny, ny)
-        factor = xinv[span, :]
-        weight = w[span, :]
-        new = []
-        for c in range(comps):
-            value = field[c, above, :] + factor * carry[c]
-            field[c, above, :] = value * weight
-            new.append(value)
-        here = pl.ds(x * TILE, TILE)
-        edge = fluxes[here, :] + ginv[here, :] * carry[comps]
-        fluxes[here, :] = edge * two_sides(lower[pl.ds(nx + x, 1), :], higher[pl.ds(nx + x, 1), :])
-        return tuple(new) + (edge,)
-
-    lax.fori_loop(0, nx, back, tuple(nexts), unroll=16)
+        lower, upper = gleft[here, :], gright[here, :]
+        for g in range(2):
+            fluxes[g, here, :] = ghosts[g][here, :] + lower * groups[g][0][-1] + upper * groups[g][1][-1]
+        return carry
+
+    lax.fori_loop(0, nx, fill, 0, unroll=8)
     blank = jnp.zeros((comps, ny, LANES), jnp.float32)
     field[:, pl.ds(0, ny), :] = blank
     field[:, pl.ds((nx + 1) * ny, ny), :] = blank
@@ -585,17 +602,17 @@
         behind_y = [flow(4, x, t) for t in range(tiles)]
         ahead_z = [flow(5, x, t) for t in range(tiles)]
         behind_z = [flow(6, x, t) for t in range(tiles)]
-        for c in range(comps):
+        for i, (g, c) in enumerate(place):
 
             def cells(plane, t):
                 begin = pl.multiple_of((plane + 1) * ny + t * TILE, TILE)
-                return field[c, pl.ds(begin, TILE), :]
+                return field[i, pl.ds(begin, TILE), :]
 
             grad = [cells(x, t) for t in range(tiles)]
             ups = [pltpu.roll(ahead_y[t] * grad[t], TILE - 1, 0) for t in range(tiles)]
             downs = [pltpu.roll(behind_y[t] * grad[t], 1, 0) for t in range(tiles)]
-            lowest = fluxes[pl.ds(x * TILE + c, 1), :]
-            highest = fluxes[pl.ds(x * TILE + SIDE + c, 1), :]
+            lowest = fluxes[g, pl.ds(x * TILE + c, 1), :]
+            highest = fluxes[g, pl.ds(x * TILE + SIDE + c, 1), :]
             for t in range(tiles):
                 part = own[t] * grad[t]
                 part = part + ahead_x[t] * cells(x + 1, t) - behind_x[t] * cells(x - 1, t)
@@ -605,25 +622,24 @@
                 part = part - jnp.where(line == 0, enter, downs[t])
                 part = part + pltpu.roll(ahead_z[t] * grad[t], LANES - 1, 1)
                 part = part - pltpu.roll(behind_z[t] * grad[t], 1, 1)
-                out[c, pl.ds(pl.multiple_of(x * ny + t * TILE, TILE), TILE), :] = part
+                out[i, pl.ds(pl.multiple_of(x * ny + t * TILE, TILE), TILE), :] = part
         return carry
 
-    parts = 4
+    parts = 8
     share = nx // parts
 
     def copy(part):
         span = pl.ds(part * share * ny, share * ny)
-        target = out_any.at[pl.ds(start, comps), span, :]
-        return pltpu.make_async_copy(out.at[:, span, :], target, sems.at[part])
+        return pltpu.make_async_copy(out.at[:, span, :], out_any.at[:, span, :], sems.at[part])
 
     top, bottom = pl.ds(0, ny), pl.ds(rows - ny, ny)
     for part in range(parts):
         lax.fori_loop(part * share, (part + 1) * share, advect, 0, unroll=share)
-        for c in range(comps):
+        for i in range(comps):
             if part == 0:
-                out[c, top, :] = out[c, top, :] - near * starts[c]
+                out[i, top, :] = out[i, top, :] - near * starts[i]
             if part == parts - 1:
-                out[c, bottom, :] = out[c, bottom, :] + far * nexts[c]
+                out[i, bottom, :] = out[i, bottom, :] + far * nexts[i]
         copy(part).start()
     for part in range(parts):
         copy(part).wait()
@@ -671,30 +687,34 @@
     def send(self):
         self.gots.append(exchange(self.outgoing, self.axis, len(self.gots)))
 
-    def merge(self, beside=(), apart=None):
+    def merge(self, beside=(), apart=None, held=None, joint=False):
         level = len(self.owns) - 1
         top = level == self.levels - 2
+        lay, bit = self.lay, self.shift + level
         leader = self.lead or self
-        coupled = () if self.lay.leads else (leader.owns[level], leader.gots[level])
-        shapes = [(self.lay.rows, LANES)] + ([(self.lay.side_rows, LANES)] if top else [])
+        operands = (self.me, self.owns[-1], self.gots[-1])
+        if not lay.leads:
+            operands += (leader.owns[level], leader.gots[level])
+        shapes = [(lay.rows, LANES)] + ([(lay.side_rows, LANES)] if top else [])
+        kernel = functools.partial(merge_kernel, lay, leader.lay, bit, top)
         if apart is not None:
-            merged, self.gots[0], *side = call(
-                functools.partial(first_merge_kernel, self.lay, self.shift, top),
-                "merge_" + self.axis,
-                (self.me, self.owns[0], self.gots[0], apart) + tuple(beside),
-                shapes[:1] + shapes,
-            )
-            self.owns.append(merged)
-            self.outgoing = side[-1] if top else merged
-            return
-        merged = call(
-            functools.partial(merge_kernel, self.lay, leader.lay, self.shift + level, top),
-            "merge_" + self.axis,
-            (self.me, self.owns[-1], self.gots[-1]) + coupled + tuple(beside),
-            shapes,
-        )
-        self.owns.append(merged[0])
-        self.outgoing = merged[-1]
+            kernel = functools.partial(first_merge_kernel, lay, bit, top)
+            operands += (apart,)
+            shapes = shapes[:1] + shapes
+        elif held is not None:
+            kernel = functools.partial(relay_merge_kernel, lay, bit)
+            operands += (held,)
+            shapes.append(held.shape)
+        elif joint and top:
+            kernel = functools.partial(joint_merge_kernel, lay, leader.lay, bit)
+            operands += (leader.outgoing,)
+            shapes = [shapes[0], (leader.lay.side_rows + lay.side_rows, LANES)]
+        found = call(kernel, "merge_" + self.axis, operands + tuple(beside), shapes)
+        self.owns.append(found[0])
+        self.outgoing = found[-1] if top else found[0]
+        if apart is not None:
+            self.gots[0] = found[1]
+        return found[-1]
 
     def records(self):
         found = (*self.owns, *self.gots)
@@ -721,11 +741,11 @@
     cour = courant.reshape(3, rows, nz)
     upw = upwind.reshape(3, rows, nz)
     n = counts[0]
-    keep, send, az, w, inv, left, right, phi, psi, cot_next = call(
+    keep, send, az, w, left, right, phi, psi, cot_next = call(
         functools.partial(lead_z_kernel, (nx, ny), ylays[0]),
         "z_solve_lead",
         (me, cot, diffusion.reshape(flat), phase.reshape(flat), cour, upw),
-        [(ylays[0].rows, nz)] * 2 + [(n, rows, nz)] + [flat] * 6 + [(counts[1], rows, nz)],
+        [(ylays[0].rows, nz)] * 2 + [(n, rows, nz)] + [flat] * 5 + [(counts[1], rows, nz)],
         [
             vmem(n, rows, nz), vmem(*flat), vmem(*flat, dtype=jnp.int32),
             vmem(*flat), vmem(*flat, dtype=jnp.int32),
@@ -748,21 +768,23 @@
         mebibytes=8,
     )
     azs.append(az)
+    send = lead.merge(held=send)
+    lead.send()
     follow = Ladder(ylays[1], "gy", 0, me, send, keep, lead)
     follow.send()
-    beside = (send,)
     for level in range(lead.levels - 1):
-        lead.merge(beside)
-        lead.send()
+        if level:
+            lead.merge(beside)
+            lead.send()
         follow.merge()
         follow.send()
         beside = (follow.outgoing,)
         if level == 0:
-            part, xinv, xleft, xright, flows = call(
+            part, inv, xinv, xleft, xright, flows = call(
                 functools.partial(coef_kernel, (nx, ny)),
                 "x_coefficients",
                 (w, cour, upw, lead.owns[1]),
-                [(5 * ny, nz), flat, flat, flat, (7 * rows, nz)],
+                [(5 * ny, nz), flat, flat, flat, flat, (7 * rows, nz)],
                 spaces="vvvv",
                 mebibytes=8,
             )
@@ -778,69 +800,61 @@
         )
         answers.append(answer)
         mets.append(exchange(passed, "gy", 0))
-    ays, ghosts, climbs = [], [], []
+    fields, ghosts, climbs = [], [], []
     for g in range(2):
-        common = (me, azs[g], answers[g], mets[g], w, inv, xleft, xright)
-        outs = [(counts[g], rows, nz), (nx * TILE, nz)]
-        scratch = [vmem(2 * ylays[g].answer_rows, nz)]
+        common = (me, azs[g], answers[g], mets[g], w, inv, xinv)
+        edge = (nx * TILE, nz)
+        outs = [(counts[g], rows, nz), edge]
+        scratch = [vmem(counts[g], rows, nz), vmem(2 * ylays[g].answer_rows, nz)]
         body = functools.partial(y_kernel, (nx, ny), ylays[g], xlays[g])
         if g == 0:
-            block, slim, ay, ghost, ginv, gleft, gright, before, after = call(
+            block, slim, field, ghost, ginv, gleft, gright, before, after = call(
                 body,
                 "y_solve_lead",
                 common + (part,),
                 [(xlays[0].rows, nz), (xlays[0].couple + TILE, nz)]
-                + outs + [(nx * TILE, nz)] * 3 + [(2 * nx, nz)] * 2,
+                + outs + [edge] * 3 + [(2 * nx, nz)] * 2,
                 scratch,
                 mebibytes=6,
             )
+            climbs.append(Ladder(xlays[0], "gx", shift, me, slim, block))
         else:
-            block, ay, ghost = call(
+            block, field, ghost = call(
                 body,
                 "y_solve_next",
-                common + (before, after, gleft, gright),
+                common + (before, after, ginv),
                 [(xlays[1].rows, nz)] + outs,
                 scratch,
                 mebibytes=6,
             )
-        ays.append(ay)
+            climbs.append(Ladder(xlays[1], "gx", shift, me, block, block, climbs[0]))
+        fields.append(field)
         ghosts.append(ghost)
-        outgoing, leader = (block, climbs[0]) if g else (slim, None)
-        climbs.append(Ladder(xlays[g], "gx", shift, me, outgoing, block, leader))
         climbs[g].send()
     beside = (block,)
-    for level in range(climbs[0].levels - 1):
-        for ladder in climbs:
-            leads = ladder.lay.leads
-            ladder.merge(beside if leads else (), apart if leads and level == 0 else None)
-            ladder.send()
-        beside = (climbs[1].outgoing,)
-    grad = None
-    for g, ladder in enumerate(climbs):
-        operands = (me,) + ladder.records() + (
-            xinv, ginv, ays[g], ghosts[g], w, before, after, flows,
-        )
-        spaces = "s" + "v" * (len(operands) - 1)
-        aliases = None
-        if g:
-            aliases = {len(operands): 0}
-            operands, spaces = operands + (grad,), spaces + "h"
-        (grad,) = call(
-            functools.partial(
-                x_kernel, (nx, ny), xlays[g], xlays[0], ladder.levels, shift, starts[g]
-            ),
-            "x_solve",
-            operands,
-            [(comps, rows, nz)],
-            [
-                vmem(counts[g], rows, nz), vmem(counts[g], rows + 2 * ny, nz), vmem(nx * TILE, nz),
-                pltpu.SemaphoreType.DMA((4,)),
-            ],
-            spaces=spaces,
-            out_spaces="h",
-            mebibytes=8,
-            aliases=aliases,
-        )
+    first, second = climbs
+    for level in range(first.levels - 1):
+        top = level == first.levels - 2
+        first.merge(beside, apart if level == 0 else None)
+        if not top:
+            first.send()
+        second.merge(joint=True)
+        second.send()
+        beside = (second.outgoing,)
+    joint = second.gots.pop()
+    (grad,) = call(
+        functools.partial(x_kernel, (nx, ny), xlays, first.levels, shift),
+        "x_solve",
+        (me, *first.owns, *first.gots, joint, *second.owns, *second.gots)
+        + (xleft, xright, gleft, gright, flows, *fields, *ghosts),
+        [(comps, rows, nz)],
+        [
+            vmem(comps, rows, nz), vmem(comps, rows + 2 * ny, nz), vmem(2, nx * TILE, nz),
+            pltpu.SemaphoreType.DMA((8,)),
+        ],
+        out_spaces="h",
+        mebibytes=12,
+    )
     return grad.reshape(comps, nx, ny, nz)
 
 

time: 32.8 us -> 34.4 us (1.049)
  waiting for transfers between devices: 5.79 us -> 10.1 us
  starting transfers between devices: 15.8 us -> 14.4 us
  Pallas kernels: 10.5 us -> 9.63 us
  local copies, waits for them, and re-layouts: 0.5 us -> 0.01 us
    ppermute x13 -> x12, waiting for transfers between devices: 5.79 us -> 10.1 us  [exchange(): return lax.ppermute(rows, axis, [(i, i ^ 1 << bit) for i in range(count)])]
    ppermute x13 -> x12, starting transfers between devices: 15.8 us -> 14.4 us  [exchange(): return lax.ppermute(rows, axis, [(i, i ^ 1 << bit) for i in range(count)])]
    pallas_call x15 -> x14, Pallas kernels: 10.5 us -> 9.63 us  [call(): pl.pallas_call(kernel, name=name, out_shape=[held[s](shape, jnp.float32)...]
    unnamed x4, local copies, waits for them, and re-layouts: 0.5 us -> 0.01 us
  transfers between devices with their start and end apart: 13 -> 12, of which waited for: 6 -> 6; matrix products, arithmetic and copies ran while one was open for 0% -> 0% of each run, Pallas kernels for 16% -> 11%
where the time goes in v8:
time: 34.4 us; the launch traced here: 34.2 us
  starting transfers between devices  14.4 us (42%)
  waiting for transfers between devices  10.1 us (29%)
  Pallas kernels  9.63 us (28%)
    ppermute x12, starting transfers between devices, exchange(): return lax.ppermute(rows, axis, [(i, i ^ 1 << bit) for i in range(count)])  14.4 us
    ppermute x12, waiting for transfers between devices, exchange(): return lax.ppermute(rows, axis, [(i, i ^ 1 << bit) for i in range(count)])  10.1 us
    pallas_call x14, Pallas kernels, call(): pl.pallas_call(kernel, name=name, out_shape=[held[s](shape, jnp.float32)...  9.63 us
  transfers between devices with their start and end apart: 12, of which 6 were waited for; matrix products, arithmetic and copies ran while one was open for 0% of the time, Pallas kernels for 11%

profile of v8, /device:TPU:0, one launch (start us, length us, event | category | flops | bytes accessed | tf_op | source)
XLA Modules:
  0.0 34.2 jit_solution(4045025173865021880)
XLA Ops:
  0.0 3.6 %z_solve_lead.1 = (f32[208,128]{1,0:T(8,128)S(1)}, f32[208,128]{1,0:T(8,128)S(1)}, f32[3,512,128]{2,1,0:T(8,128)S(1)}, f32[512,128]{1,0:T(8,128)S(1)}, f32[512,1...) custom-call(s32[1]{0:T(128)} %bitcast.me_ref, ...), custom_call_target="tpu_custom_call" | custom-call | flops 1000000000 | bytes 10000000 | tf_op jit(solution)/shard_map/z_solve_lead/pallas_call | solution.py:660
  3.6 0.5 %collective-permute-start = (f32[208,128]{1,0:T(8,128)S(1)}, f32[208,128]{1,0:T(8,128)S(1)}, u32[]{:S(2)}, u32[]{:S(2)}) collective-permute-start(f32[208,128]{1,0:T(8,128)S(1)} %get-tuple-element.52), channel_id=1, source_target_pairs={{0,1},{1,0},{2,3},{3,2},{4,5},{5,4},{6,7},{7,6},{8,9},{9,8},{10,11... | collective-permute-start | bytes 319496 | tf_op jit(solution)/shard_map/ppermute | solution.py:678
  4.1 1.3 %z_solve_next.1 = (f32[96,128]{1,0:T(8,128)S(1)}, f32[96,128]{1,0:T(8,128)S(1)}, f32[3,512,128]{2,1,0:T(8,128)S(1)}) custom-call(s32[1]{0:T(128)} %bitcast.me_ref, f32[3,512,128]{2,1,0:T(8,128)S(1)} %get-tuple-element.53.cot, f32[512,128]{1,0:T(8,128)S(1)} %get-tuple-element.54.phi, f32[512,128]{1,0:T(8,128)S(1)} %get-tuple-element.55.psi, ...), custom_call_target="tpu_custom_call" | custom-call | flops 1000000000 | bytes 10000000 | tf_op jit(solution)/shard_map/z_solve_next/pallas_call | solution.py:660
  5.4 0.1 collective-permute-start.2
  5.6 2.9 %collective-permute-start.1 = (f32[208,128]{1,0:T(8,128)S(1)}, f32[208,128]{1,0:T(8,128)S(1)}, u32[]{:S(2)}, u32[]{:S(2)}) collective-permute-start(f32[208,128]{1,0:T(8,128)S(1)} %get-tuple-element.60.after.own.refs_0_.refs_1_.refs_7_), channel_id=1, source_target_pairs={{0,2},{1,3},{2,0},{3,1},{4,6},{5,7},{6,4},{7,5},{8,10},{9,11},{10,... | collective-permute-start | bytes 319496 | tf_op jit(solution)/shard_map/ppermute | solution.py:678
  8.5 0.4 %x_coefficients.1 = (f32[80,128]{1,0:T(8,128)S(1)}, f32[512,128]{1,0:T(8,128)S(1)}, f32[512,128]{1,0:T(8,128)S(1)}, f32[512,128]{1,0:T(8,128)S(1)}, f32[512,128]{1,0:T(8,128)S(1)}, /*index=5*/f32[3584,128]{1,0:T(8,128)S(1)}) custom-call(f32[512,128]{1,0:T(8,128)S(1)} %get-tuple-element.56.w, f32[3,512,128]{2,1,0:T(8,128)S(1)} %bitcast.8, ...), custom_call_target="tpu_custom_call" | custom-call | flops 1000000000 | bytes 10000000 | tf_op jit(solution)/shard_map/x_coefficients/pallas_call | solution.py:660
  8.9 1.6 %collective-permute-start.5 = (f32[80,128]{1,0:T(8,128)S(1)}, f32[80,128]{1,0:T(8,128)S(1)}, u32[]{:S(2)}, u32[]{:S(2)}) collective-permute-start(f32[80,128]{1,0:T(8,128)S(1)} %get-tuple-element.61.refs_0_), channel_id=1, source_target_pairs={{0,8},{8,0},{16,24},{24,16},{1,9},{9,1},{17,25},{25,17},{2,10},{10... | collective-permute-start | bytes 122888 | tf_op jit(solution)/shard_map/ppermute | solution.py:678
  10.6 0.8 %collective-permute-start.4 = (f32[96,128]{1,0:T(8,128)S(1)}, f32[96,128]{1,0:T(8,128)S(1)}, u32[]{:S(2)}, u32[]{:S(2)}) collective-permute-start(f32[96,128]{1,0:T(8,128)S(1)} %merge_gy.5.refs_1_.own), channel_id=1, source_target_pairs={{0,2},{1,3},{2,0},{3,1},{4,6},{5,7},{6,4},{7,5},{8,10},{9,11},{10,... | collective-permute-start | bytes 147464 | tf_op jit(solution)/shard_map/ppermute | solution.py:678
  11.4 0.3 collective-permute-done.1.other.refs_1_.refs_4_.refs_10_
  11.7 1.8 %collective-permute-start.3 = (f32[96,128]{1,0:T(8,128)S(1)}, f32[96,128]{1,0:T(8,128)S(1)}, u32[]{:S(2)}, u32[]{:S(2)}) collective-permute-start(f32[96,128]{1,0:T(8,128)S(1)} %get-tuple-element.65), channel_id=1, source_target_pairs={{0,4},{1,5},{2,6},{3,7},{4,0},{5,1},{6,2},{7,3},{8,12},{9,13},{10,... | collective-permute-start | bytes 147464 | tf_op jit(solution)/shard_map/ppermute | solution.py:678
  13.6 1.2 %collective-permute-done.4.other.refs_4_ = f32[96,128]{1,0:T(8,128)S(1)} collective-permute-done((f32[96,128]{1,0:T(8,128)S(1)}, f32[96,128]{1,0:T(8,128)S(1)}, u32[]{:S(2)}, u32[]{:S(2)}) %collective-permute-start.4) | collective-permute-done | bytes 49184 | tf_op jit(solution)/shard_map/ppermute | solution.py:678
  14.8 1.6 %collective-permute-start.8 = (f32[48,128]{1,0:T(8,128)S(1)}, f32[48,128]{1,0:T(8,128)S(1)}, u32[]{:S(2)}, u32[]{:S(2)}) collective-permute-start(f32[48,128]{1,0:T(8,128)S(1)} %get-tuple-element.66.refs_6_), channel_id=1, source_target_pairs={{0,4},{1,5},{2,6},{3,7},{4,0},{5,1},{6,2},{7,3},{8,12},{9,13},{10,... | collective-permute-start | bytes 73736 | tf_op jit(solution)/shard_map/ppermute | solution.py:678
  16.4 0.1 collective-permute-start.6
  16.5 2.2 %collective-permute-done.8.refs_5_ = f32[48,128]{1,0:T(8,128)S(1)} collective-permute-done((f32[48,128]{1,0:T(8,128)S(1)}, f32[48,128]{1,0:T(8,128)S(1)}, u32[]{:S(2)}, u32[]{:S(2)}) %collective-permute-start.8) | collective-permute-done | bytes 24608 | tf_op jit(solution)/shard_map/ppermute | solution.py:678
  18.7 0.1 collective-permute-start.9
  18.8 1.1 %y_solve_lead.1 = (f32[200,128]{1,0:T(8,128)S(1)}, f32[120,128]{1,0:T(8,128)S(1)}, f32[3,512,128]{2,1,0:T(8,128)S(1)}, f32[256,128]{1,0:T(8,128)S(1)}, f32[256,1...) custom-call(s32[1]{0:T(128)} %bitcast.me_ref, ...), custom_call_target="tpu_custom_call" | custom-call | flops 1000000000 | bytes 10000000 | tf_op jit(solution)/shard_map/y_solve_lead/pallas_call | solution.py:660
  19.9 0.8 %collective-permute-start.7 = (f32[120,128]{1,0:T(8,128)S(1)}, f32[120,128]{1,0:T(8,128)S(1)}, u32[]{:S(2)}, u32[]{:S(2)}) collective-permute-start(f32[120,128]{1,0:T(8,128)S(1)} %get-tuple-element.72), channel_id=1, source_target_pairs={{0,8},{8,0},{16,24},{24,16},{1,9},{9,1},{17,25},{25,17},{2,10},{10... | collective-permute-start | bytes 184328 | tf_op jit(solution)/shard_map/ppermute | solution.py:678
  20.7 1.0 %y_solve_next.1 = (f32[112,128]{1,0:T(8,128)S(1)}, f32[3,512,128]{2,1,0:T(8,128)S(1)}, f32[256,128]{1,0:T(8,128)S(1)}) custom-call(s32[1]{0:T(128)} %bitcast.me_ref, f32[3,512,128]{2,1,0:T(8,128)S(1)} %get-tuple-element.73.az, f32[96,128]{1,0:T(8,128)S(1)} %get-tuple-element.75.own, f32[96,128]{1,0:T(8,128)S(1)} %collective-permute-done.9.got, ...), custom_call_target="tpu_custom_call" | custom-call | flops 1000000000 | bytes 10000000 | tf_op jit(solution)/shard_map/y_solve_next/pallas_call | solution.py:660
  21.7 1.3 %collective-permute-start.10 = (f32[112,128]{1,0:T(8,128)S(1)}, f32[112,128]{1,0:T(8,128)S(1)}, u32[]{:S(2)}, u32[]{:S(2)}) collective-permute-start(f32[112,128]{1,0:T(8,128)S(1)} %get-tuple-element.80.refs_0_.own.refs_4_), channel_id=1, source_target_pairs={{0,8},{8,0},{16,24},{24,16},{1,9},{9,1},{17,25},{25,17},{2,10},{10... | collective-permute-start | bytes 172040 | tf_op jit(solution)/shard_map/ppermute | solution.py:678
  23.0 1.3 %collective-permute-done.7.slim = f32[120,128]{1,0:T(8,128)S(1)} collective-permute-done((f32[120,128]{1,0:T(8,128)S(1)}, f32[120,128]{1,0:T(8,128)S(1)}, u32[]{:S(2)}, u32[]{:S(2)}) %collective-permute-start.7) | collective-permute-done | bytes 61472 | tf_op jit(solution)/shard_map/ppermute | solution.py:678
  24.4 1.6 %collective-permute-done.10.other.refs_6_ = f32[112,128]{1,0:T(8,128)S(1)} collective-permute-done((f32[112,128]{1,0:T(8,128)S(1)}, f32[112,128]{1,0:T(8,128)S(1)}, u32[]{:S(2)}, u32[]{:S(2)}) %collective-permute-start.10) | collective-permute-done | bytes 57376 | tf_op jit(solution)/shard_map/ppermute | solution.py:678
  26.0 2.7 %collective-permute-start.11 = (f32[152,128]{1,0:T(8,128)S(1)}, f32[152,128]{1,0:T(8,128)S(1)}, u32[]{:S(2)}, u32[]{:S(2)}) collective-permute-start(f32[152,128]{1,0:T(8,128)S(1)} %get-tuple-element.84), channel_id=1, source_target_pairs={{0,16},{8,24},{16,0},{24,8},{1,17},{9,25},{17,1},{25,9},{2,18},{10... | collective-permute-start | bytes 233480 | tf_op jit(solution)/shard_map/ppermute | solution.py:678
  28.6 3.5 %collective-permute-done.11.refs_3_ = f32[152,128]{1,0:T(8,128)S(1)} collective-permute-done((f32[152,128]{1,0:T(8,128)S(1)}, f32[152,128]{1,0:T(8,128)S(1)}, u32[]{:S(2)}, u32[]{:S(2)}) %collective-permute-start.11) | collective-permute-done | bytes 77856 | tf_op jit(solution)/shard_map/ppermute | solution.py:678
  32.1 2.1 %x_solve.1 = f32[6,512,128]{2,1,0:T(8,128)} custom-call(s32[1]{0:T(128)} %bitcast.me_ref, f32[200,128]{1,0:T(8,128)S(1)} %get-tuple-element.71.own.lead_own.refs_0_, f32[200,128]{1,0:T(8,128)S(1)} %get-tuple-element.81.refs_1_, f32[200,128]{1,0:T(8,128)S(1)} %get-tuple-element.82.lead_other.refs_2_, f32[152,128]{1,0:T(8,128)S(1)} %collective-permute-done.11.refs_3_, ...), custom_call_target="tpu_custom_call" | custom-call | flops 1000000000 | bytes 10000000 | tf_op jit(solution)/shard_map/x_solve/pallas_call | solution.py:660
  (18 shorter events, 0.3 us)
Async XLA Ops:
  3.6 1.8 %collective-permute-start = (f32[208,128]{1,0:T(8,128)S(1)}, f32[208,128]{1,0:T(8,128)S(1)}, u32[]{:S(2)}, u32[]{:S(2)}) collective-permute-start(f32[208,128]{1,0:T(8,128)S(1)} %get-tuple-element.52), channel_id=1, source_target_pairs={{0,1},{1,0},{2,3},{3,2},{4,5},{5,4},{6,7},{7,6},{8,9},{9,8},{10,11... | collective-permute-start | bytes 319496 | tf_op jit(solution)/shard_map/ppermute | solution.py:678
  5.4 3.1 %copy-start = (f32[3,32,16,128]{3,2,1,0:T(8,128)S(1)}, f32[3,32,16,128]{3,2,1,0:T(8,128)}, u32[]{:S(2)}) copy-start(f32[3,32,16,128]{3,2,1,0:T(8,128)} %param.8) | copy-start | bytes 2359300
  5.4 3.1 %copy-start.1 = (s32[3,32,16,128]{3,2,1,0:T(8,128)S(1)}, s32[3,32,16,128]{3,2,1,0:T(8,128)}, u32[]{:S(2)}) copy-start(s32[3,32,16,128]{3,2,1,0:T(8,128)} %param.9) | copy-start | bytes 2359300
  5.4 5.1 %collective-permute-start.2 = (f32[96,128]{1,0:T(8,128)S(1)}, f32[96,128]{1,0:T(8,128)S(1)}, u32[]{:S(2)}, u32[]{:S(2)}) collective-permute-start(f32[96,128]{1,0:T(8,128)S(1)} %get-tuple-element.63), channel_id=1, source_target_pairs={{0,1},{1,0},{2,3},{3,2},{4,5},{5,4},{6,7},{7,6},{8,9},{9,8},{10,11... | collective-permute-start | bytes 147464 | tf_op jit(solution)/shard_map/ppermute | solution.py:678
  5.6 6.2 %collective-permute-start.1 = (f32[208,128]{1,0:T(8,128)S(1)}, f32[208,128]{1,0:T(8,128)S(1)}, u32[]{:S(2)}, u32[]{:S(2)}) collective-permute-start(f32[208,128]{1,0:T(8,128)S(1)} %get-tuple-element.60.after.own.refs_0_.refs_1_.refs_7_), channel_id=1, source_target_pairs={{0,2},{1,3},{2,0},{3,1},{4,6},{5,7},{6,4},{7,5},{8,10},{9,11},{10,... | collective-permute-start | bytes 319496 | tf_op jit(solution)/shard_map/ppermute | solution.py:678
  8.9 7.4 %collective-permute-start.5 = (f32[80,128]{1,0:T(8,128)S(1)}, f32[80,128]{1,0:T(8,128)S(1)}, u32[]{:S(2)}, u32[]{:S(2)}) collective-permute-start(f32[80,128]{1,0:T(8,128)S(1)} %get-tuple-element.61.refs_0_), channel_id=1, source_target_pairs={{0,8},{8,0},{16,24},{24,16},{1,9},{9,1},{17,25},{25,17},{2,10},{10... | collective-permute-start | bytes 122888 | tf_op jit(solution)/shard_map/ppermute | solution.py:678
  10.6 4.2 %collective-permute-start.4 = (f32[96,128]{1,0:T(8,128)S(1)}, f32[96,128]{1,0:T(8,128)S(1)}, u32[]{:S(2)}, u32[]{:S(2)}) collective-permute-start(f32[96,128]{1,0:T(8,128)S(1)} %merge_gy.5.refs_1_.own), channel_id=1, source_target_pairs={{0,2},{1,3},{2,0},{3,1},{4,6},{5,7},{6,4},{7,5},{8,10},{9,11},{10,... | collective-permute-start | bytes 147464 | tf_op jit(solution)/shard_map/ppermute | solution.py:678
  11.7 4.6 %collective-permute-start.3 = (f32[96,128]{1,0:T(8,128)S(1)}, f32[96,128]{1,0:T(8,128)S(1)}, u32[]{:S(2)}, u32[]{:S(2)}) collective-permute-start(f32[96,128]{1,0:T(8,128)S(1)} %get-tuple-element.65), channel_id=1, source_target_pairs={{0,4},{1,5},{2,6},{3,7},{4,0},{5,1},{6,2},{7,3},{8,12},{9,13},{10,... | collective-permute-start | bytes 147464 | tf_op jit(solution)/shard_map/ppermute | solution.py:678
  14.8 3.9 %collective-permute-start.8 = (f32[48,128]{1,0:T(8,128)S(1)}, f32[48,128]{1,0:T(8,128)S(1)}, u32[]{:S(2)}, u32[]{:S(2)}) collective-permute-start(f32[48,128]{1,0:T(8,128)S(1)} %get-tuple-element.66.refs_6_), channel_id=1, source_target_pairs={{0,4},{1,5},{2,6},{3,7},{4,0},{5,1},{6,2},{7,3},{8,12},{9,13},{10,... | collective-permute-start | bytes 73736 | tf_op jit(solution)/shard_map/ppermute | solution.py:678
  16.4 2.4 %collective-permute-start.6 = (f32[160,128]{1,0:T(8,128)S(1)}, f32[160,128]{1,0:T(8,128)S(1)}, u32[]{:S(2)}, u32[]{:S(2)}) collective-permute-start(f32[160,128]{1,0:T(8,128)S(1)} %get-tuple-element.68), channel_id=1, source_target_pairs={{0,1},{1,0},{2,3},{3,2},{4,5},{5,4},{6,7},{7,6},{8,9},{9,8},{10,11... | collective-permute-start | bytes 245768 | tf_op jit(solution)/shard_map/ppermute | solution.py:678
  18.7 2.0 %collective-permute-start.9 = (f32[96,128]{1,0:T(8,128)S(1)}, f32[96,128]{1,0:T(8,128)S(1)}, u32[]{:S(2)}, u32[]{:S(2)}) collective-permute-start(f32[96,128]{1,0:T(8,128)S(1)} %get-tuple-element.76), channel_id=1, source_target_pairs={{0,1},{1,0},{2,3},{3,2},{4,5},{5,4},{6,7},{7,6},{8,9},{9,8},{10,11... | collective-permute-start | bytes 147464 | tf_op jit(solution)/shard_map/ppermute | solution.py:678
  19.9 4.5 %collective-permute-start.7 = (f32[120,128]{1,0:T(8,128)S(1)}, f32[120,128]{1,0:T(8,128)S(1)}, u32[]{:S(2)}, u32[]{:S(2)}) collective-permute-start(f32[120,128]{1,0:T(8,128)S(1)} %get-tuple-element.72), channel_id=1, source_target_pairs={{0,8},{8,0},{16,24},{24,16},{1,9},{9,1},{17,25},{25,17},{2,10},{10... | collective-permute-start | bytes 184328 | tf_op jit(solution)/shard_map/ppermute | solution.py:678
  21.7 4.2 %collective-permute-start.10 = (f32[112,128]{1,0:T(8,128)S(1)}, f32[112,128]{1,0:T(8,128)S(1)}, u32[]{:S(2)}, u32[]{:S(2)}) collective-permute-start(f32[112,128]{1,0:T(8,128)S(1)} %get-tuple-element.80.refs_0_.own.refs_4_), channel_id=1, source_target_pairs={{0,8},{8,0},{16,24},{24,16},{1,9},{9,1},{17,25},{25,17},{2,10},{10... | collective-permute-start | bytes 172040 | tf_op jit(solution)/shard_map/ppermute | solution.py:678
  26.0 6.2 %collective-permute-start.11 = (f32[152,128]{1,0:T(8,128)S(1)}, f32[152,128]{1,0:T(8,128)S(1)}, u32[]{:S(2)}, u32[]{:S(2)}) collective-permute-start(f32[152,128]{1,0:T(8,128)S(1)} %get-tuple-element.84), channel_id=1, source_target_pairs={{0,16},{8,24},{16,0},{24,8},{1,17},{9,25},{17,1},{25,9},{2,18},{10... | collective-permute-start | bytes 233480 | tf_op jit(solution)/shard_map/ppermute | solution.py:678

commit v9 on v8

--- a/solution.py
+++ b/solution.py
@@ -207,17 +207,6 @@
     write_block(lay, out, block)
     if top:
         write_side(lay, side[0], block, (me_ref[0] >> (bit + 1)) & 1)
-
-
-def relay_merge_kernel(lay, bit, me_ref, own, other, held, out, passed):
-    passed[...] = held[...]
-    merge_kernel(lay, lay, bit, False, me_ref, own, other, out)
-
-
-def joint_merge_kernel(lay, lead, bit, me_ref, own, other, lead_own, lead_other, side, out, joint):
-    joint[pl.ds(0, lead.side_rows), :] = side[...]
-    rest = joint.at[pl.ds(lead.side_rows, lay.side_rows)]
-    merge_kernel(lay, lead, bit, True, me_ref, own, other, lead_own, lead_other, out, rest)
 
 
 def first_merge_kernel(lay, bit, top, me_ref, own, slim, apart, *refs):
@@ -343,14 +332,15 @@
     count = len(lay.sizes)
     ahead = pltpu.make_async_copy(cot_any.at[pl.ds(count, later.shape[0])], later, sems.at[4])
     small = [(diff_any, diff), (phase_any, phase), (cour_any.at[1], cour), (upw_any.at[1], upw)]
-    for i, (source, target) in enumerate(small):
+    for i, (source, target) in enumerate(small[:2]):
         pltpu.make_async_copy(source, target, sems.at[i]).start()
+    for i, (source, target) in enumerate(small[:2]):
+        pltpu.make_async_copy(source, target, sems.at[i]).wait()
     for c in range(count):
         pltpu.make_async_copy(cot_any.at[c], cot.at[c], in_sems.at[c]).start()
+    for i, (source, target) in enumerate(small[2:]):
+        pltpu.make_async_copy(source, target, sems.at[2 + i]).start()
     ahead.start()
-
-    for i, (source, target) in enumerate(small[:2]):
-        pltpu.make_async_copy(source, target, sems.at[i]).wait()
     w[...] = weight_of(diff[...], phase[...])
     for t in range(tiles):
         span = pl.ds(t * LANES, LANES)
@@ -546,38 +536,24 @@
         slim[pl.ds(xlay.couple, TILE), :] = block[pl.ds(xlay.packed, TILE), :]
 
 
-def x_kernel(dims, lays, levels, shift, me_ref, *refs):
+def x_kernel(dims, lay, lead, levels, shift, start, me_ref, *refs):
     nx, ny = dims
-    lead, follow = lays
-    owns, gots, later_owns, later_gots = (refs[i * levels : (i + 1) * levels] for i in range(4))
-    later_gots = later_gots[:-1]
-    (left, right, gleft, gright, flows, *rest) = refs[4 * levels - 1 :]
-    inputs, ghosts = rest[:2], rest[2:4]
-    out_any, out, field, fluxes, sems = rest[4:]
+    count = (2 if lay.leads else 4) * levels
+    state, _ = solve_lines(lay, lead, levels, me_ref[0] >> shift, refs[:count])
+    left, right, gleft, gright, flows, inputs, ghost, *rest = refs[count:]
+    out_any, out, field, fluxes, sems = rest[-5:]
     rows = nx * ny
     tiles = ny // TILE
-    me = me_ref[0] >> shift
-    joint = gots[-1]
-    gots = gots[:-1] + (joint.at[pl.ds(0, lead.side_rows)],)
-    later_gots = later_gots + (joint.at[pl.ds(lead.side_rows, follow.side_rows)],)
-    first, _ = solve_lines(lead, lead, levels, me, owns + gots)
-    second, _ = solve_lines(follow, lead, levels, me, later_owns + later_gots + owns + gots)
-    near, far = first[2][0], first[3][0]
-    groups = (first, second)
-    place = [(g, c) for g, lay in enumerate(lays) for c in range(len(lay.sizes) - 1)]
-    starts = [groups[g][0][c] for g, c in place]
-    nexts = [groups[g][1][c] for g, c in place]
-    comps = len(place)
+    comps = len(lay.sizes) - 1
+    starts, nexts, (near,), (far,) = state
 
     def fill(x, carry):
         span, above = pl.ds(x * ny, ny), pl.ds((x + 1) * ny, ny)
         lower, upper = left[span, :], right[span, :]
-        for i, (g, c) in enumerate(place):
-            field[i, above, :] = inputs[g][c, span, :] + lower * starts[i] + upper * nexts[i]
+        for c in range(comps):
+            field[c, above, :] = inputs[c, span, :] + lower * starts[c] + upper * nexts[c]
         here = pl.ds(x * TILE, TILE)
-        lower, upper = gleft[here, :], gright[here, :]
-        for g in range(2):
-            fluxes[g, here, :] = ghosts[g][here, :] + lower * groups[g][0][-1] + upper * groups[g][1][-1]
+        fluxes[here, :] = ghost[here, :] + gleft[here, :] * starts[comps] + gright[here, :] * nexts[comps]
         return carry
 
     lax.fori_loop(0, nx, fill, 0, unroll=8)
@@ -602,17 +578,17 @@
         behind_y = [flow(4, x, t) for t in range(tiles)]
         ahead_z = [flow(5, x, t) for t in range(tiles)]
         behind_z = [flow(6, x, t) for t in range(tiles)]
-        for i, (g, c) in enumerate(place):
+        for c in range(comps):
 
             def cells(plane, t):
                 begin = pl.multiple_of((plane + 1) * ny + t * TILE, TILE)
-                return field[i, pl.ds(begin, TILE), :]
+                return field[c, pl.ds(begin, TILE), :]
 
             grad = [cells(x, t) for t in range(tiles)]
             ups = [pltpu.roll(ahead_y[t] * grad[t], TILE - 1, 0) for t in range(tiles)]
             downs = [pltpu.roll(behind_y[t] * grad[t], 1, 0) for t in range(tiles)]
-            lowest = fluxes[g, pl.ds(x * TILE + c, 1), :]
-            highest = fluxes[g, pl.ds(x * TILE + SIDE + c, 1), :]
+            lowest = fluxes[pl.ds(x * TILE + c, 1), :]
+            highest = fluxes[pl.ds(x * TILE + SIDE + c, 1), :]
             for t in range(tiles):
                 part = own[t] * grad[t]
                 part = part + ahead_x[t] * cells(x + 1, t) - behind_x[t] * cells(x - 1, t)
@@ -622,7 +598,7 @@
                 part = part - jnp.where(line == 0, enter, downs[t])
                 part = part + pltpu.roll(ahead_z[t] * grad[t], LANES - 1, 1)
                 part = part - pltpu.roll(behind_z[t] * grad[t], 1, 1)
-                out[i, pl.ds(pl.multiple_of(x * ny + t * TILE, TILE), TILE), :] = part
+                out[c, pl.ds(pl.multiple_of(x * ny + t * TILE, TILE), TILE), :] = part
         return carry
 
     parts = 8
@@ -630,16 +606,17 @@
 
     def copy(part):
         span = pl.ds(part * share * ny, share * ny)
-        return pltpu.make_async_copy(out.at[:, span, :], out_any.at[:, span, :], sems.at[part])
+        target = out_any.at[pl.ds(start, comps), span, :]
+        return pltpu.make_async_copy(out.at[:, span, :], target, sems.at[part])
 
     top, bottom = pl.ds(0, ny), pl.ds(rows - ny, ny)
     for part in range(parts):
         lax.fori_loop(part * share, (part + 1) * share, advect, 0, unroll=share)
-        for i in range(comps):
+        for c in range(comps):
             if part == 0:
-                out[i, top, :] = out[i, top, :] - near * starts[i]
+                out[c, top, :] = out[c, top, :] - near * starts[c]
             if part == parts - 1:
-                out[i, bottom, :] = out[i, bottom, :] + far * nexts[i]
+                out[c, bottom, :] = out[c, bottom, :] + far * nexts[c]
         copy(part).start()
     for part in range(parts):
         copy(part).wait()
@@ -687,7 +664,7 @@
     def send(self):
         self.gots.append(exchange(self.outgoing, self.axis, len(self.gots)))
 
-    def merge(self, beside=(), apart=None, held=None, joint=False):
+    def merge(self, beside=(), apart=None):
         level = len(self.owns) - 1
         top = level == self.levels - 2
         lay, bit = self.lay, self.shift + level
@@ -701,20 +678,11 @@
             kernel = functools.partial(first_merge_kernel, lay, bit, top)
             operands += (apart,)
             shapes = shapes[:1] + shapes
-        elif held is not None:
-            kernel = functools.partial(relay_merge_kernel, lay, bit)
-            operands += (held,)
-            shapes.append(held.shape)
-        elif joint and top:
-            kernel = functools.partial(joint_merge_kernel, lay, leader.lay, bit)
-            operands += (leader.outgoing,)
-            shapes = [shapes[0], (leader.lay.side_rows + lay.side_rows, LANES)]
         found = call(kernel, "merge_" + self.axis, operands + tuple(beside), shapes)
         self.owns.append(found[0])
         self.outgoing = found[-1] if top else found[0]
         if apart is not None:
             self.gots[0] = found[1]
-        return found[-1]
 
     def records(self):
         found = (*self.owns, *self.gots)
@@ -768,14 +736,12 @@
         mebibytes=8,
     )
     azs.append(az)
-    send = lead.merge(held=send)
-    lead.send()
     follow = Ladder(ylays[1], "gy", 0, me, send, keep, lead)
     follow.send()
+    beside = (send,)
     for level in range(lead.levels - 1):
-        if level:
-            lead.merge(beside)
-            lead.send()
+        lead.merge(beside)
+        lead.send()
         follow.merge()
         follow.send()
         beside = (follow.outgoing,)
@@ -832,29 +798,36 @@
         ghosts.append(ghost)
         climbs[g].send()
     beside = (block,)
-    first, second = climbs
-    for level in range(first.levels - 1):
-        top = level == first.levels - 2
-        first.merge(beside, apart if level == 0 else None)
-        if not top:
-            first.send()
-        second.merge(joint=True)
-        second.send()
-        beside = (second.outgoing,)
-    joint = second.gots.pop()
-    (grad,) = call(
-        functools.partial(x_kernel, (nx, ny), xlays, first.levels, shift),
-        "x_solve",
-        (me, *first.owns, *first.gots, joint, *second.owns, *second.gots)
-        + (xleft, xright, gleft, gright, flows, *fields, *ghosts),
-        [(comps, rows, nz)],
-        [
-            vmem(comps, rows, nz), vmem(comps, rows + 2 * ny, nz), vmem(2, nx * TILE, nz),
-            pltpu.SemaphoreType.DMA((8,)),
-        ],
-        out_spaces="h",
-        mebibytes=12,
-    )
+    for level in range(climbs[0].levels - 1):
+        for ladder in climbs:
+            leads = ladder.lay.leads
+            ladder.merge(beside if leads else (), apart if leads and level == 0 else None)
+            ladder.send()
+        beside = (climbs[1].outgoing,)
+    grad = None
+    for g, ladder in enumerate(climbs):
+        operands = (me, *ladder.records(), xleft, xright, gleft, gright, flows, fields[g], ghosts[g])
+        spaces = "s" + "v" * (len(operands) - 1)
+        aliases = None
+        if g:
+            aliases = {len(operands): 0}
+            operands, spaces = operands + (grad,), spaces + "h"
+        (grad,) = call(
+            functools.partial(
+                x_kernel, (nx, ny), xlays[g], xlays[0], ladder.levels, shift, starts[g]
+            ),
+            "x_solve",
+            operands,
+            [(comps, rows, nz)],
+            [
+                vmem(counts[g], rows, nz), vmem(counts[g], rows + 2 * ny, nz), vmem(nx * TILE, nz),
+                pltpu.SemaphoreType.DMA((8,)),
+            ],
+            spaces=spaces,
+            out_spaces="h",
+            mebibytes=8,
+            aliases=aliases,
+        )
     return grad.reshape(comps, nx, ny, nz)
 
 

time: 34.4 us -> 33.1 us (0.962)
  waiting for transfers between devices: 10.1 us -> 5.67 us
  starting transfers between devices: 14.4 us -> 16 us
  Pallas kernels: 9.63 us -> 10.7 us
  local copies, waits for them, and re-layouts: 0.01 us -> 0.5 us
    ppermute x12 -> x13, waiting for transfers between devices: 10.1 us -> 5.67 us  [exchange(): return lax.ppermute(rows, axis, [(i, i ^ 1 << bit) for i in range(count)])]
    ppermute x12 -> x13, starting transfers between devices: 14.4 us -> 16 us  [exchange(): return lax.ppermute(rows, axis, [(i, i ^ 1 << bit) for i in range(count)])]
    pallas_call x14 -> x15, Pallas kernels: 9.63 us -> 10.7 us  [call(): pl.pallas_call(kernel, name=name, out_shape=[held[s](shape, jnp.float32)...]
    unnamed x4, local copies, waits for them, and re-layouts: 0.01 us -> 0.5 us
  transfers between devices with their start and end apart: 12 -> 13, of which waited for: 6 -> 6; matrix products, arithmetic and copies ran while one was open for 0% -> 0% of each run, Pallas kernels for 11% -> 16%
where the time goes in v9:
time: 33.1 us; the launch traced here: 32.9 us
  starting transfers between devices  16 us (48%)
  Pallas kernels  10.7 us (32%)
  waiting for transfers between devices  5.67 us (17%)
  local copies, waits for them, and re-layouts  0.5 us (2%)
    ppermute x13, starting transfers between devices, exchange(): return lax.ppermute(rows, axis, [(i, i ^ 1 << bit) for i in range(count)])  16 us
    pallas_call x15, Pallas kernels, call(): pl.pallas_call(kernel, name=name, out_shape=[held[s](shape, jnp.float32)...  10.7 us
    ppermute x13, waiting for transfers between devices, exchange(): return lax.ppermute(rows, axis, [(i, i ^ 1 << bit) for i in range(count)])  5.67 us
  transfers between devices with their start and end apart: 13, of which 6 were waited for; matrix products, arithmetic and copies ran while one was open for 0% of the time, Pallas kernels for 16%

profile of v9, /device:TPU:0, one launch (start us, length us, event | category | flops | bytes accessed | tf_op | source)
XLA Modules:
  0.0 32.9 jit_solution(9601735789269185159)
XLA Ops:
  0.0 3.8 %z_solve_lead.1 = (f32[208,128]{1,0:T(8,128)S(1)}, f32[208,128]{1,0:T(8,128)S(1)}, f32[3,512,128]{2,1,0:T(8,128)S(1)}, f32[512,128]{1,0:T(8,128)S(1)}, f32[512,1...) custom-call(s32[1]{0:T(128)} %bitcast.me_ref, ...), custom_call_target="tpu_custom_call" | custom-call | flops 1000000000 | bytes 10000000 | tf_op jit(solution)/shard_map/z_solve_lead/pallas_call | solution.py:637
  3.8 0.5 %collective-permute-start.1 = (f32[208,128]{1,0:T(8,128)S(1)}, f32[208,128]{1,0:T(8,128)S(1)}, u32[]{:S(2)}, u32[]{:S(2)}) collective-permute-start(f32[208,128]{1,0:T(8,128)S(1)} %get-tuple-element.58), channel_id=1, source_target_pairs={{0,1},{1,0},{2,3},{3,2},{4,5},{5,4},{6,7},{7,6},{8,9},{9,8},{10,11... | collective-permute-start | bytes 319496 | tf_op jit(solution)/shard_map/ppermute | solution.py:655
  4.3 1.2 %z_solve_next.1 = (f32[96,128]{1,0:T(8,128)S(1)}, f32[96,128]{1,0:T(8,128)S(1)}, f32[3,512,128]{2,1,0:T(8,128)S(1)}) custom-call(s32[1]{0:T(128)} %bitcast.me_ref, f32[3,512,128]{2,1,0:T(8,128)S(1)} %get-tuple-element.48.cot, f32[512,128]{1,0:T(8,128)S(1)} %get-tuple-element.49.phi, f32[512,128]{1,0:T(8,128)S(1)} %get-tuple-element.50.psi, ...), custom_call_target="tpu_custom_call" | custom-call | flops 1000000000 | bytes 10000000 | tf_op jit(solution)/shard_map/z_solve_next/pallas_call | solution.py:637
  5.6 3.0 %collective-permute-start.3 = (f32[208,128]{1,0:T(8,128)S(1)}, f32[208,128]{1,0:T(8,128)S(1)}, u32[]{:S(2)}, u32[]{:S(2)}) collective-permute-start(f32[208,128]{1,0:T(8,128)S(1)} %merge_gy.5.refs_0_.after.own.refs_7_.refs_1_), channel_id=1, source_target_pairs={{0,2},{1,3},{2,0},{3,1},{4,6},{5,7},{6,4},{7,5},{8,10},{9,11},{10,... | collective-permute-start | bytes 319496 | tf_op jit(solution)/shard_map/ppermute | solution.py:655
  8.6 0.8 %collective-permute-start.2 = (f32[96,128]{1,0:T(8,128)S(1)}, f32[96,128]{1,0:T(8,128)S(1)}, u32[]{:S(2)}, u32[]{:S(2)}) collective-permute-start(f32[96,128]{1,0:T(8,128)S(1)} %merge_gy.4.own.refs_1_), channel_id=1, source_target_pairs={{0,2},{1,3},{2,0},{3,1},{4,6},{5,7},{6,4},{7,5},{8,10},{9,11},{10,... | collective-permute-start | bytes 147464 | tf_op jit(solution)/shard_map/ppermute | solution.py:655
  9.5 0.3 copy-done
  9.7 0.2 copy-done.1
  10.0 0.4 %x_coefficients.1 = (f32[80,128]{1,0:T(8,128)S(1)}, f32[512,128]{1,0:T(8,128)S(1)}, f32[512,128]{1,0:T(8,128)S(1)}, f32[512,128]{1,0:T(8,128)S(1)}, f32[512,128]{1,0:T(8,128)S(1)}, /*index=5*/f32[3584,128]{1,0:T(8,128)S(1)}) custom-call(f32[512,128]{1,0:T(8,128)S(1)} %get-tuple-element.51.w, f32[3,512,128]{2,1,0:T(8,128)S(1)} %bitcast.8, ...), custom_call_target="tpu_custom_call" | custom-call | flops 1000000000 | bytes 10000000 | tf_op jit(solution)/shard_map/x_coefficients/pallas_call | solution.py:637
  10.4 1.7 %collective-permute-start.7 = (f32[80,128]{1,0:T(8,128)S(1)}, f32[80,128]{1,0:T(8,128)S(1)}, u32[]{:S(2)}, u32[]{:S(2)}) collective-permute-start(f32[80,128]{1,0:T(8,128)S(1)} %get-tuple-element.61.refs_0_), channel_id=1, source_target_pairs={{0,8},{8,0},{16,24},{24,16},{1,9},{9,1},{17,25},{25,17},{2,10},{10... | collective-permute-start | bytes 122888 | tf_op jit(solution)/shard_map/ppermute | solution.py:655
  12.0 0.3 collective-permute-done.3.refs_1_.other.refs_10_.refs_4_
  12.3 1.9 %collective-permute-start.5 = (f32[96,128]{1,0:T(8,128)S(1)}, f32[96,128]{1,0:T(8,128)S(1)}, u32[]{:S(2)}, u32[]{:S(2)}) collective-permute-start(f32[96,128]{1,0:T(8,128)S(1)} %get-tuple-element.63), channel_id=1, source_target_pairs={{0,4},{1,5},{2,6},{3,7},{4,0},{5,1},{6,2},{7,3},{8,12},{9,13},{10,... | collective-permute-start | bytes 147464 | tf_op jit(solution)/shard_map/ppermute | solution.py:655
  14.2 0.5 %collective-permute-start.4 = (f32[48,128]{1,0:T(8,128)S(1)}, f32[48,128]{1,0:T(8,128)S(1)}, u32[]{:S(2)}, u32[]{:S(2)}) collective-permute-start(f32[48,128]{1,0:T(8,128)S(1)} %get-tuple-element.60.refs_6_), channel_id=1, source_target_pairs={{0,4},{1,5},{2,6},{3,7},{4,0},{5,1},{6,2},{7,3},{8,12},{9,13},{10,... | collective-permute-start | bytes 73736 | tf_op jit(solution)/shard_map/ppermute | solution.py:655
  14.7 1.8 %collective-permute-done.5.refs_11_.refs_5_ = f32[96,128]{1,0:T(8,128)S(1)} collective-permute-done((f32[96,128]{1,0:T(8,128)S(1)}, f32[96,128]{1,0:T(8,128)S(1)}, u32[]{:S(2)}, u32[]{:S(2)}) %collective-permute-start.5) | collective-permute-done | bytes 49184 | tf_op jit(solution)/shard_map/ppermute | solution.py:655
  16.6 1.5 %collective-permute-done.4.refs_5_ = f32[48,128]{1,0:T(8,128)S(1)} collective-permute-done((f32[48,128]{1,0:T(8,128)S(1)}, f32[48,128]{1,0:T(8,128)S(1)}, u32[]{:S(2)}, u32[]{:S(2)}) %collective-permute-start.4) | collective-permute-done | bytes 24608 | tf_op jit(solution)/shard_map/ppermute | solution.py:655
  18.2 1.1 %y_solve_lead.1 = (f32[200,128]{1,0:T(8,128)S(1)}, f32[120,128]{1,0:T(8,128)S(1)}, f32[3,512,128]{2,1,0:T(8,128)S(1)}, f32[256,128]{1,0:T(8,128)S(1)}, f32[256,1...) custom-call(s32[1]{0:T(128)} %bitcast.me_ref, ...), custom_call_target="tpu_custom_call" | custom-call | flops 1000000000 | bytes 10000000 | tf_op jit(solution)/shard_map/y_solve_lead/pallas_call | solution.py:637
  19.4 1.6 %collective-permute-start.10 = (f32[120,128]{1,0:T(8,128)S(1)}, f32[120,128]{1,0:T(8,128)S(1)}, u32[]{:S(2)}, u32[]{:S(2)}) collective-permute-start(f32[120,128]{1,0:T(8,128)S(1)} %get-tuple-element.76), channel_id=1, source_target_pairs={{0,8},{8,0},{16,24},{24,16},{1,9},{9,1},{17,25},{25,17},{2,10},{10... | collective-permute-start | bytes 184328 | tf_op jit(solution)/shard_map/ppermute | solution.py:655
  21.0 1.0 %y_solve_next.1 = (f32[112,128]{1,0:T(8,128)S(1)}, f32[3,512,128]{2,1,0:T(8,128)S(1)}, f32[256,128]{1,0:T(8,128)S(1)}) custom-call(s32[1]{0:T(128)} %bitcast.me_ref, f32[3,512,128]{2,1,0:T(8,128)S(1)} %get-tuple-element.54.az, f32[96,128]{1,0:T(8,128)S(1)} %get-tuple-element.64.own, f32[96,128]{1,0:T(8,128)S(1)} %collective-permute-done.6.got, ...), custom_call_target="tpu_custom_call" | custom-call | flops 1000000000 | bytes 10000000 | tf_op jit(solution)/shard_map/y_solve_next/pallas_call | solution.py:637
  22.0 0.5 %collective-permute-start.9 = (f32[112,128]{1,0:T(8,128)S(1)}, f32[112,128]{1,0:T(8,128)S(1)}, u32[]{:S(2)}, u32[]{:S(2)}) collective-permute-start(f32[112,128]{1,0:T(8,128)S(1)} %get-tuple-element.74.refs_0_.own), channel_id=1, source_target_pairs={{0,8},{8,0},{16,24},{24,16},{1,9},{9,1},{17,25},{25,17},{2,10},{10... | collective-permute-start | bytes 172040 | tf_op jit(solution)/shard_map/ppermute | solution.py:655
  22.5 1.3 %collective-permute-done.10.slim = f32[120,128]{1,0:T(8,128)S(1)} collective-permute-done((f32[120,128]{1,0:T(8,128)S(1)}, f32[120,128]{1,0:T(8,128)S(1)}, u32[]{:S(2)}, u32[]{:S(2)}) %collective-permute-start.10) | collective-permute-done | bytes 61472 | tf_op jit(solution)/shard_map/ppermute | solution.py:655
  23.9 2.6 %collective-permute-start.12 = (f32[96,128]{1,0:T(8,128)S(1)}, f32[96,128]{1,0:T(8,128)S(1)}, u32[]{:S(2)}, u32[]{:S(2)}) collective-permute-start(f32[96,128]{1,0:T(8,128)S(1)} %get-tuple-element.81), channel_id=1, source_target_pairs={{0,16},{8,24},{16,0},{24,8},{1,17},{9,25},{17,1},{25,9},{2,18},{10... | collective-permute-start | bytes 147464 | tf_op jit(solution)/shard_map/ppermute | solution.py:655
  26.6 2.5 %collective-permute-start.11 = (f32[56,128]{1,0:T(8,128)S(1)}, f32[56,128]{1,0:T(8,128)S(1)}, u32[]{:S(2)}, u32[]{:S(2)}) collective-permute-start(f32[56,128]{1,0:T(8,128)S(1)} %get-tuple-element.79), channel_id=1, source_target_pairs={{0,16},{8,24},{16,0},{24,8},{1,17},{9,25},{17,1},{25,9},{2,18},{10... | collective-permute-start | bytes 86024 | tf_op jit(solution)/shard_map/ppermute | solution.py:655
  29.3 1.5 %x_solve.2.refs_15_ = f32[6,512,128]{2,1,0:T(8,128)} custom-call(s32[1]{0:T(128)} %bitcast.me_ref, f32[200,128]{1,0:T(8,128)S(1)} %get-tuple-element.75.own.refs_0_.refs_4_, f32[200,128]{1,0:T(8,128)S(1)} %get-tuple-element.80.refs_1_.refs_5_, f32[200,128]{1,0:T(8,128)S(1)} %get-tuple-element.77.refs_1_.refs_2_.refs_6_, ...), custom_call_target="tpu_custom_call" | custom-call | flops 1000000000 | bytes 10000000 | tf_op jit(solution)/shard_map/x_solve/pallas_call | solution.py:637
  30.8 0.6 %collective-permute-done.11.refs_3_ = f32[56,128]{1,0:T(8,128)S(1)} collective-permute-done((f32[56,128]{1,0:T(8,128)S(1)}, f32[56,128]{1,0:T(8,128)S(1)}, u32[]{:S(2)}, u32[]{:S(2)}) %collective-permute-start.11) | collective-permute-done | bytes 28704 | tf_op jit(solution)/shard_map/ppermute | solution.py:655
  31.4 1.5 %x_solve.3 = f32[6,512,128]{2,1,0:T(8,128)} custom-call(s32[1]{0:T(128)} %bitcast.me_ref, f32[112,128]{1,0:T(8,128)S(1)} %get-tuple-element.74.refs_0_.own, f32[112,128]{1,0:T(8,128)S(1)} %get-tuple-element.78.refs_1_, f32[112,128]{1,0:T(8,128)S(1)} %collective-permute-done.9.other.refs_2_, ...), custom_call_target="tpu_custom_call", output_to_operand_aliasing={{}: (16, {})} | custom-call | flops 1000000000 | bytes 10000000 | tf_op jit(solution)/shard_map/x_solve/pallas_call | solution.py:637
  (21 shorter events, 0.8 us)
Async XLA Ops:
  3.8 1.8 %collective-permute-start.1 = (f32[208,128]{1,0:T(8,128)S(1)}, f32[208,128]{1,0:T(8,128)S(1)}, u32[]{:S(2)}, u32[]{:S(2)}) collective-permute-start(f32[208,128]{1,0:T(8,128)S(1)} %get-tuple-element.58), channel_id=1, source_target_pairs={{0,1},{1,0},{2,3},{3,2},{4,5},{5,4},{6,7},{7,6},{8,9},{9,8},{10,11... | collective-permute-start | bytes 319496 | tf_op jit(solution)/shard_map/ppermute | solution.py:655
  5.4 3.2 %collective-permute-start = (f32[96,128]{1,0:T(8,128)S(1)}, f32[96,128]{1,0:T(8,128)S(1)}, u32[]{:S(2)}, u32[]{:S(2)}) collective-permute-start(f32[96,128]{1,0:T(8,128)S(1)} %get-tuple-element.56.refs_0_), channel_id=1, source_target_pairs={{0,1},{1,0},{2,3},{3,2},{4,5},{5,4},{6,7},{7,6},{8,9},{9,8},{10,11... | collective-permute-start | bytes 147464 | tf_op jit(solution)/shard_map/ppermute | solution.py:655
  5.6 6.7 %collective-permute-start.3 = (f32[208,128]{1,0:T(8,128)S(1)}, f32[208,128]{1,0:T(8,128)S(1)}, u32[]{:S(2)}, u32[]{:S(2)}) collective-permute-start(f32[208,128]{1,0:T(8,128)S(1)} %merge_gy.5.refs_0_.after.own.refs_7_.refs_1_), channel_id=1, source_target_pairs={{0,2},{1,3},{2,0},{3,1},{4,6},{5,7},{6,4},{7,5},{8,10},{9,11},{10,... | collective-permute-start | bytes 319496 | tf_op jit(solution)/shard_map/ppermute | solution.py:655
  8.6 1.1 %copy-start = (f32[3,32,16,128]{3,2,1,0:T(8,128)S(1)}, f32[3,32,16,128]{3,2,1,0:T(8,128)}, u32[]{:S(2)}) copy-start(f32[3,32,16,128]{3,2,1,0:T(8,128)} %param.8) | copy-start | bytes 2359300
  8.6 1.4 %copy-start.1 = (s32[3,32,16,128]{3,2,1,0:T(8,128)S(1)}, s32[3,32,16,128]{3,2,1,0:T(8,128)}, u32[]{:S(2)}) copy-start(s32[3,32,16,128]{3,2,1,0:T(8,128)} %param.9) | copy-start | bytes 2359300
  8.6 5.5 %collective-permute-start.2 = (f32[96,128]{1,0:T(8,128)S(1)}, f32[96,128]{1,0:T(8,128)S(1)}, u32[]{:S(2)}, u32[]{:S(2)}) collective-permute-start(f32[96,128]{1,0:T(8,128)S(1)} %merge_gy.4.own.refs_1_), channel_id=1, source_target_pairs={{0,2},{1,3},{2,0},{3,1},{4,6},{5,7},{6,4},{7,5},{8,10},{9,11},{10,... | collective-permute-start | bytes 147464 | tf_op jit(solution)/shard_map/ppermute | solution.py:655
  10.4 4.3 %collective-permute-start.7 = (f32[80,128]{1,0:T(8,128)S(1)}, f32[80,128]{1,0:T(8,128)S(1)}, u32[]{:S(2)}, u32[]{:S(2)}) collective-permute-start(f32[80,128]{1,0:T(8,128)S(1)} %get-tuple-element.61.refs_0_), channel_id=1, source_target_pairs={{0,8},{8,0},{16,24},{24,16},{1,9},{9,1},{17,25},{25,17},{2,10},{10... | collective-permute-start | bytes 122888 | tf_op jit(solution)/shard_map/ppermute | solution.py:655
  12.3 4.2 %collective-permute-start.5 = (f32[96,128]{1,0:T(8,128)S(1)}, f32[96,128]{1,0:T(8,128)S(1)}, u32[]{:S(2)}, u32[]{:S(2)}) collective-permute-start(f32[96,128]{1,0:T(8,128)S(1)} %get-tuple-element.63), channel_id=1, source_target_pairs={{0,4},{1,5},{2,6},{3,7},{4,0},{5,1},{6,2},{7,3},{8,12},{9,13},{10,... | collective-permute-start | bytes 147464 | tf_op jit(solution)/shard_map/ppermute | solution.py:655
  14.2 3.9 %collective-permute-start.4 = (f32[48,128]{1,0:T(8,128)S(1)}, f32[48,128]{1,0:T(8,128)S(1)}, u32[]{:S(2)}, u32[]{:S(2)}) collective-permute-start(f32[48,128]{1,0:T(8,128)S(1)} %get-tuple-element.60.refs_6_), channel_id=1, source_target_pairs={{0,4},{1,5},{2,6},{3,7},{4,0},{5,1},{6,2},{7,3},{8,12},{9,13},{10,... | collective-permute-start | bytes 73736 | tf_op jit(solution)/shard_map/ppermute | solution.py:655
  16.5 1.7 %collective-permute-start.8 = (f32[160,128]{1,0:T(8,128)S(1)}, f32[160,128]{1,0:T(8,128)S(1)}, u32[]{:S(2)}, u32[]{:S(2)}) collective-permute-start(f32[160,128]{1,0:T(8,128)S(1)} %get-tuple-element.70), channel_id=1, source_target_pairs={{0,1},{1,0},{2,3},{3,2},{4,5},{5,4},{6,7},{7,6},{8,9},{9,8},{10,11... | collective-permute-start | bytes 245768 | tf_op jit(solution)/shard_map/ppermute | solution.py:655
  18.2 2.9 %collective-permute-start.6 = (f32[96,128]{1,0:T(8,128)S(1)}, f32[96,128]{1,0:T(8,128)S(1)}, u32[]{:S(2)}, u32[]{:S(2)}) collective-permute-start(f32[96,128]{1,0:T(8,128)S(1)} %get-tuple-element.65), channel_id=1, source_target_pairs={{0,1},{1,0},{2,3},{3,2},{4,5},{5,4},{6,7},{7,6},{8,9},{9,8},{10,11... | collective-permute-start | bytes 147464 | tf_op jit(solution)/shard_map/ppermute | solution.py:655
  19.4 4.5 %collective-permute-start.10 = (f32[120,128]{1,0:T(8,128)S(1)}, f32[120,128]{1,0:T(8,128)S(1)}, u32[]{:S(2)}, u32[]{:S(2)}) collective-permute-start(f32[120,128]{1,0:T(8,128)S(1)} %get-tuple-element.76), channel_id=1, source_target_pairs={{0,8},{8,0},{16,24},{24,16},{1,9},{9,1},{17,25},{25,17},{2,10},{10... | collective-permute-start | bytes 184328 | tf_op jit(solution)/shard_map/ppermute | solution.py:655
  22.0 4.5 %collective-permute-start.9 = (f32[112,128]{1,0:T(8,128)S(1)}, f32[112,128]{1,0:T(8,128)S(1)}, u32[]{:S(2)}, u32[]{:S(2)}) collective-permute-start(f32[112,128]{1,0:T(8,128)S(1)} %get-tuple-element.74.refs_0_.own), channel_id=1, source_target_pairs={{0,8},{8,0},{16,24},{24,16},{1,9},{9,1},{17,25},{25,17},{2,10},{10... | collective-permute-start | bytes 172040 | tf_op jit(solution)/shard_map/ppermute | solution.py:655
  23.9 5.4 %collective-permute-start.12 = (f32[96,128]{1,0:T(8,128)S(1)}, f32[96,128]{1,0:T(8,128)S(1)}, u32[]{:S(2)}, u32[]{:S(2)}) collective-permute-start(f32[96,128]{1,0:T(8,128)S(1)} %get-tuple-element.81), channel_id=1, source_target_pairs={{0,16},{8,24},{16,0},{24,8},{1,17},{9,25},{17,1},{25,9},{2,18},{10... | collective-permute-start | bytes 147464 | tf_op jit(solution)/shard_map/ppermute | solution.py:655
  26.6 4.8 %collective-permute-start.11 = (f32[56,128]{1,0:T(8,128)S(1)}, f32[56,128]{1,0:T(8,128)S(1)}, u32[]{:S(2)}, u32[]{:S(2)}) collective-permute-start(f32[56,128]{1,0:T(8,128)S(1)} %get-tuple-element.79), channel_id=1, source_target_pairs={{0,16},{8,24},{16,0},{24,8},{1,17},{9,25},{17,1},{25,9},{2,18},{10... | collective-permute-start | bytes 86024 | tf_op jit(solution)/shard_map/ppermute | solution.py:655

commit v10 on v9

--- a/solution.py
+++ b/solution.py
@@ -321,10 +321,53 @@
     send[...] = both[pl.ds(pl.multiple_of((1 - mine) * lay.rows, TILE), lay.rows), :]
 
 
+def carried(maps, state):
+    return maps[0] * state[0] + maps[1] * state[1], maps[2] * state[0] + maps[3] * state[1]
+
+
+def z_continuants(tiles, wt, pht, pst, maps, ends):
+    deep = LANES // TILE
+    lines = tiles * TILE
+    one = jnp.ones((lines, LANES), jnp.float32)
+    zero = jnp.zeros((lines, LANES), jnp.float32)
+
+    def at(k, t):
+        return pl.ds(t * LANES + k, TILE, stride=deep)
+
+    weights = [
+        jnp.concatenate([wt[at(k, t), :] for t in range(tiles)], axis=0) for k in range(deep)
+    ]
+    found = []
+    for order in (range(deep), reversed(range(deep))):
+        pair = [(one, zero), (zero, one)]
+        values = {}
+        for k in order:
+            values[k] = (pair[0][0], pair[1][0])
+            pair = [growing_step(*state, weights[k]) for state in pair]
+        base = len(found) * 4 * lines
+        found.append(values)
+        for i, entry in enumerate((pair[0][0], pair[1][0], pair[0][1], pair[1][1])):
+            maps[pl.ds(base + i * lines, lines), :] = entry
+    state = (jnp.ones((tiles, LANES), jnp.float32),) * 2
+    for side, order in enumerate((range(TILE), reversed(range(TILE)))):
+        for s in order:
+            for i in range(2):
+                ends[pl.ds((2 * side + i) * lines + s, tiles, stride=TILE), :] = state[i]
+            rows = [pl.ds((4 * side + i) * lines + s, tiles, stride=TILE) for i in range(4)]
+            state = carried([maps[row, :] for row in rows], state)
+        state = (1.0 / state[0],) * 2
+    for values, target, side in ((found[0], pht, 0), (found[1], pst, 1)):
+        first, second = (ends[pl.ds((2 * side + i) * lines, lines), :] for i in range(2))
+        for k in range(deep):
+            cells = values[k][0] * first + values[k][1] * second
+            for t in range(tiles):
+                target[at(k, t), :] = cells[t * TILE : (t + 1) * TILE]
+
+
 def lead_z_kernel(
     dims, lay, me_ref, cot_any, diff_any, phase_any, cour_any, upw_any,
     keep, send, az, w, left, right, phi, psi, later,
-    cot, diff, phase, cour, upw, wt, pht, pst, both, in_sems, sems,
+    cot, diff, phase, cour, upw, wt, pht, pst, maps, ends, both, in_sems, sems,
 ):
     nx, ny = dims
     tiles = nx * ny // LANES
@@ -332,34 +375,23 @@
     count = len(lay.sizes)
     ahead = pltpu.make_async_copy(cot_any.at[pl.ds(count, later.shape[0])], later, sems.at[4])
     small = [(diff_any, diff), (phase_any, phase), (cour_any.at[1], cour), (upw_any.at[1], upw)]
-    for i, (source, target) in enumerate(small[:2]):
+    for i, (source, target) in enumerate(small):
         pltpu.make_async_copy(source, target, sems.at[i]).start()
+    for c in range(count):
+        pltpu.make_async_copy(cot_any.at[c], cot.at[c], in_sems.at[c]).start()
+    ahead.start()
+
     for i, (source, target) in enumerate(small[:2]):
         pltpu.make_async_copy(source, target, sems.at[i]).wait()
-    for c in range(count):
-        pltpu.make_async_copy(cot_any.at[c], cot.at[c], in_sems.at[c]).start()
-    for i, (source, target) in enumerate(small[2:]):
-        pltpu.make_async_copy(source, target, sems.at[2 + i]).start()
-    ahead.start()
     w[...] = weight_of(diff[...], phase[...])
     for t in range(tiles):
         span = pl.ds(t * LANES, LANES)
         wt[span, :] = w[span, :].T
-    ones = jnp.ones((tiles, LANES), jnp.float32)
-    value, slope = ones, ones
-    back, fall = ones, ones
-    for k in range(LANES):
-        here = pl.ds(k, tiles, stride=LANES)
-        pht[here, :] = value
-        value, slope = growing_step(value, slope, wt[here, :])
-        there = pl.ds(LANES - 1 - k, tiles, stride=LANES)
-        pst[there, :] = back
-        back, fall = growing_step(back, fall, wt[there, :])
-    scale = 1.0 / value
+    z_continuants(tiles, wt, pht, pst, maps, ends)
     for t in range(tiles):
         span = pl.ds(t * LANES, LANES)
         phi[span, :] = pht[span, :].T
-        psi[span, :] = (pst[span, :] * scale[t : t + 1]).T
+        psi[span, :] = pst[span, :].T
 
     chain, backs, total = corners([w[pl.ds(y, nx, stride=ny), :] for y in range(ny)])
     for y in range(ny):
@@ -456,7 +488,12 @@
     if xlay.leads:
         part, block, slim, field, ghost, ginv, gleft, gright, before, after, ay, joined = refs
     else:
-        before, after, ginv, block, field, ghost, ay, joined = refs
+        before, after, ginv, gleft, gright, block, field, ghost, fleft, fright, ay, joined = refs
+        for x in range(nx):
+            here = pl.ds(x * TILE, TILE)
+            scale = sides(before, after, nx + x)
+            fleft[here, :] = gleft[here, :] * scale
+            fright[here, :] = gright[here, :] * scale
     mine = me_ref[0] & 1
     span = ylay.answer_rows
     joined[pl.ds(pl.multiple_of(mine * span, TILE), span), :] = own[...]
@@ -482,9 +519,8 @@
         total = 1.0 / value
         for x in range(nx):
             here = pl.ds(x * TILE, TILE)
-            scale = sides(before, after, nx + x) * total
-            gleft[here, :] = gleft[here, :] * scale
-            gright[here, :] = gright[here, :] * scale
+            gleft[here, :] = gleft[here, :] * total
+            gright[here, :] = gright[here, :] * total
 
     ghost[...] = jnp.zeros(ghost.shape, jnp.float32)
     for c in range(comps):
@@ -717,7 +753,9 @@
         [
             vmem(n, rows, nz), vmem(*flat), vmem(*flat, dtype=jnp.int32),
             vmem(*flat), vmem(*flat, dtype=jnp.int32),
-            vmem(*flat), vmem(*flat), vmem(*flat), vmem(2 * ylays[0].rows, nz),
+            vmem(*flat), vmem(*flat), vmem(*flat),
+            vmem(rows // LANES * 8 * TILE, nz), vmem(rows // LANES * 4 * TILE, nz),
+            vmem(2 * ylays[0].rows, nz),
             pltpu.SemaphoreType.DMA((n,)), pltpu.SemaphoreType.DMA((5,)),
         ],
         spaces="shhhhh",
@@ -785,11 +823,11 @@
             )
             climbs.append(Ladder(xlays[0], "gx", shift, me, slim, block))
         else:
-            block, field, ghost = call(
+            block, field, ghost, gleft, gright = call(
                 body,
                 "y_solve_next",
-                common + (before, after, ginv),
-                [(xlays[1].rows, nz)] + outs,
+                common + (before, after, ginv, gleft, gright),
+                [(xlays[1].rows, nz)] + outs + [edge] * 2,
                 scratch,
                 mebibytes=6,
             )

time: 33.1 us -> 32.5 us (0.982)
  Pallas kernels: 10.7 us -> 10.2 us
    pallas_call x15, Pallas kernels: 10.7 us -> 10.2 us  [call(): pl.pallas_call(kernel, name=name, out_shape=[held[s](shape, jnp.float32)...]
  transfers between devices with their start and end apart: 13 -> 13, of which waited for: 6 -> 6; matrix products, arithmetic and copies ran while one was open for 0% -> 0% of each run, Pallas kernels for 16% -> 17%
where the time goes in v10:
time: 32.5 us; the launch traced here: 32.4 us
  starting transfers between devices  16 us (49%)
  Pallas kernels  10.2 us (31%)
  waiting for transfers between devices  5.59 us (17%)
  local copies, waits for them, and re-layouts  0.5 us (2%)
    ppermute x13, starting transfers between devices, exchange(): return lax.ppermute(rows, axis, [(i, i ^ 1 << bit) for i in range(count)])  16 us
    pallas_call x15, Pallas kernels, call(): pl.pallas_call(kernel, name=name, out_shape=[held[s](shape, jnp.float32)...  10.2 us
    ppermute x13, waiting for transfers between devices, exchange(): return lax.ppermute(rows, axis, [(i, i ^ 1 << bit) for i in range(count)])  5.59 us
  transfers between devices with their start and end apart: 13, of which 6 were waited for; matrix products, arithmetic and copies ran while one was open for 0% of the time, Pallas kernels for 17%

profile of v10, /device:TPU:0, one launch (start us, length us, event | category | flops | bytes accessed | tf_op | source)
XLA Modules:
  0.0 32.4 jit_solution(6557541764957000095)
XLA Ops:
  0.0 3.4 %z_solve_lead.1 = (f32[208,128]{1,0:T(8,128)S(1)}, f32[208,128]{1,0:T(8,128)S(1)}, f32[3,512,128]{2,1,0:T(8,128)S(1)}, f32[512,128]{1,0:T(8,128)S(1)}, f32[512,1...) custom-call(s32[1]{0:T(128)} %bitcast.me_ref, ...), custom_call_target="tpu_custom_call" | custom-call | flops 1000000000 | bytes 10000000 | tf_op jit(solution)/shard_map/z_solve_lead/pallas_call | solution.py:673
  3.4 0.5 %collective-permute-start.1 = (f32[208,128]{1,0:T(8,128)S(1)}, f32[208,128]{1,0:T(8,128)S(1)}, u32[]{:S(2)}, u32[]{:S(2)}) collective-permute-start(f32[208,128]{1,0:T(8,128)S(1)} %get-tuple-element.60), channel_id=1, source_target_pairs={{0,1},{1,0},{2,3},{3,2},{4,5},{5,4},{6,7},{7,6},{8,9},{9,8},{10,11... | collective-permute-start | bytes 319496 | tf_op jit(solution)/shard_map/ppermute | solution.py:691
  3.9 1.2 %z_solve_next.1 = (f32[96,128]{1,0:T(8,128)S(1)}, f32[96,128]{1,0:T(8,128)S(1)}, f32[3,512,128]{2,1,0:T(8,128)S(1)}) custom-call(s32[1]{0:T(128)} %bitcast.me_ref, f32[3,512,128]{2,1,0:T(8,128)S(1)} %get-tuple-element.50.cot, f32[512,128]{1,0:T(8,128)S(1)} %get-tuple-element.51.phi, f32[512,128]{1,0:T(8,128)S(1)} %get-tuple-element.52.psi, ...), custom_call_target="tpu_custom_call" | custom-call | flops 1000000000 | bytes 10000000 | tf_op jit(solution)/shard_map/z_solve_next/pallas_call | solution.py:673
  5.2 3.0 %collective-permute-start.3 = (f32[208,128]{1,0:T(8,128)S(1)}, f32[208,128]{1,0:T(8,128)S(1)}, u32[]{:S(2)}, u32[]{:S(2)}) collective-permute-start(f32[208,128]{1,0:T(8,128)S(1)} %merge_gy.5.refs_0_.after.own.refs_7_.refs_1_), channel_id=1, source_target_pairs={{0,2},{1,3},{2,0},{3,1},{4,6},{5,7},{6,4},{7,5},{8,10},{9,11},{10,... | collective-permute-start | bytes 319496 | tf_op jit(solution)/shard_map/ppermute | solution.py:691
  8.2 0.8 %collective-permute-start.2 = (f32[96,128]{1,0:T(8,128)S(1)}, f32[96,128]{1,0:T(8,128)S(1)}, u32[]{:S(2)}, u32[]{:S(2)}) collective-permute-start(f32[96,128]{1,0:T(8,128)S(1)} %merge_gy.4.own.refs_1_), channel_id=1, source_target_pairs={{0,2},{1,3},{2,0},{3,1},{4,6},{5,7},{6,4},{7,5},{8,10},{9,11},{10,... | collective-permute-start | bytes 147464 | tf_op jit(solution)/shard_map/ppermute | solution.py:691
  9.1 0.3 copy-done
  9.3 0.2 copy-done.1
  9.6 0.4 %x_coefficients.1 = (f32[80,128]{1,0:T(8,128)S(1)}, f32[512,128]{1,0:T(8,128)S(1)}, f32[512,128]{1,0:T(8,128)S(1)}, f32[512,128]{1,0:T(8,128)S(1)}, f32[512,128]{1,0:T(8,128)S(1)}, /*index=5*/f32[3584,128]{1,0:T(8,128)S(1)}) custom-call(f32[512,128]{1,0:T(8,128)S(1)} %get-tuple-element.53.w, f32[3,512,128]{2,1,0:T(8,128)S(1)} %bitcast.8, ...), custom_call_target="tpu_custom_call" | custom-call | flops 1000000000 | bytes 10000000 | tf_op jit(solution)/shard_map/x_coefficients/pallas_call | solution.py:673
  10.0 1.7 %collective-permute-start.7 = (f32[80,128]{1,0:T(8,128)S(1)}, f32[80,128]{1,0:T(8,128)S(1)}, u32[]{:S(2)}, u32[]{:S(2)}) collective-permute-start(f32[80,128]{1,0:T(8,128)S(1)} %get-tuple-element.63.refs_0_), channel_id=1, source_target_pairs={{0,8},{8,0},{16,24},{24,16},{1,9},{9,1},{17,25},{25,17},{2,10},{10... | collective-permute-start | bytes 122888 | tf_op jit(solution)/shard_map/ppermute | solution.py:691
  11.6 0.3 collective-permute-done.3.refs_1_.other.refs_10_.refs_4_
  11.9 1.9 %collective-permute-start.5 = (f32[96,128]{1,0:T(8,128)S(1)}, f32[96,128]{1,0:T(8,128)S(1)}, u32[]{:S(2)}, u32[]{:S(2)}) collective-permute-start(f32[96,128]{1,0:T(8,128)S(1)} %get-tuple-element.65), channel_id=1, source_target_pairs={{0,4},{1,5},{2,6},{3,7},{4,0},{5,1},{6,2},{7,3},{8,12},{9,13},{10,... | collective-permute-start | bytes 147464 | tf_op jit(solution)/shard_map/ppermute | solution.py:691
  13.8 0.5 %collective-permute-start.4 = (f32[48,128]{1,0:T(8,128)S(1)}, f32[48,128]{1,0:T(8,128)S(1)}, u32[]{:S(2)}, u32[]{:S(2)}) collective-permute-start(f32[48,128]{1,0:T(8,128)S(1)} %get-tuple-element.62.refs_6_), channel_id=1, source_target_pairs={{0,4},{1,5},{2,6},{3,7},{4,0},{5,1},{6,2},{7,3},{8,12},{9,13},{10,... | collective-permute-start | bytes 73736 | tf_op jit(solution)/shard_map/ppermute | solution.py:691
  14.3 1.8 %collective-permute-done.5.refs_11_.refs_5_ = f32[96,128]{1,0:T(8,128)S(1)} collective-permute-done((f32[96,128]{1,0:T(8,128)S(1)}, f32[96,128]{1,0:T(8,128)S(1)}, u32[]{:S(2)}, u32[]{:S(2)}) %collective-permute-start.5) | collective-permute-done | bytes 49184 | tf_op jit(solution)/shard_map/ppermute | solution.py:691
  16.2 1.5 %collective-permute-done.4.refs_5_ = f32[48,128]{1,0:T(8,128)S(1)} collective-permute-done((f32[48,128]{1,0:T(8,128)S(1)}, f32[48,128]{1,0:T(8,128)S(1)}, u32[]{:S(2)}, u32[]{:S(2)}) %collective-permute-start.4) | collective-permute-done | bytes 24608 | tf_op jit(solution)/shard_map/ppermute | solution.py:691
  17.8 1.1 %y_solve_lead.1 = (f32[200,128]{1,0:T(8,128)S(1)}, f32[120,128]{1,0:T(8,128)S(1)}, f32[3,512,128]{2,1,0:T(8,128)S(1)}, f32[256,128]{1,0:T(8,128)S(1)}, f32[256,1...) custom-call(s32[1]{0:T(128)} %bitcast.me_ref, ...), custom_call_target="tpu_custom_call" | custom-call | flops 1000000000 | bytes 10000000 | tf_op jit(solution)/shard_map/y_solve_lead/pallas_call | solution.py:673
  18.9 1.6 %collective-permute-start.10 = (f32[120,128]{1,0:T(8,128)S(1)}, f32[120,128]{1,0:T(8,128)S(1)}, u32[]{:S(2)}, u32[]{:S(2)}) collective-permute-start(f32[120,128]{1,0:T(8,128)S(1)} %get-tuple-element.80), channel_id=1, source_target_pairs={{0,8},{8,0},{16,24},{24,16},{1,9},{9,1},{17,25},{25,17},{2,10},{10... | collective-permute-start | bytes 184328 | tf_op jit(solution)/shard_map/ppermute | solution.py:691
  20.6 1.0 %y_solve_next.1 = (f32[112,128]{1,0:T(8,128)S(1)}, f32[3,512,128]{2,1,0:T(8,128)S(1)}, f32[256,128]{1,0:T(8,128)S(1)}, f32[256,128]{1,0:T(8,128)S(1)}, f32[256,128]{1,0:T(8,128)S(1)}) custom-call(s32[1]{0:T(128)} %bitcast.me_ref, f32[3,512,128]{2,1,0:T(8,128)S(1)} %get-tuple-element.56.az, f32[96,128]{1,0:T(8,128)S(1)} %get-tuple-element.66.own, ...), custom_call_target="tpu_custom_call" | custom-call | flops 1000000000 | bytes 10000000 | tf_op jit(solution)/shard_map/y_solve_next/pallas_call | solution.py:673
  21.6 0.5 %collective-permute-start.9 = (f32[112,128]{1,0:T(8,128)S(1)}, f32[112,128]{1,0:T(8,128)S(1)}, u32[]{:S(2)}, u32[]{:S(2)}) collective-permute-start(f32[112,128]{1,0:T(8,128)S(1)} %get-tuple-element.78.refs_0_.own), channel_id=1, source_target_pairs={{0,8},{8,0},{16,24},{24,16},{1,9},{9,1},{17,25},{25,17},{2,10},{10... | collective-permute-start | bytes 172040 | tf_op jit(solution)/shard_map/ppermute | solution.py:691
  22.1 1.3 %collective-permute-done.10.slim = f32[120,128]{1,0:T(8,128)S(1)} collective-permute-done((f32[120,128]{1,0:T(8,128)S(1)}, f32[120,128]{1,0:T(8,128)S(1)}, u32[]{:S(2)}, u32[]{:S(2)}) %collective-permute-start.10) | collective-permute-done | bytes 61472 | tf_op jit(solution)/shard_map/ppermute | solution.py:691
  23.4 2.6 %collective-permute-start.12 = (f32[96,128]{1,0:T(8,128)S(1)}, f32[96,128]{1,0:T(8,128)S(1)}, u32[]{:S(2)}, u32[]{:S(2)}) collective-permute-start(f32[96,128]{1,0:T(8,128)S(1)} %get-tuple-element.85), channel_id=1, source_target_pairs={{0,16},{8,24},{16,0},{24,8},{1,17},{9,25},{17,1},{25,9},{2,18},{10... | collective-permute-start | bytes 147464 | tf_op jit(solution)/shard_map/ppermute | solution.py:691
  26.1 2.6 %collective-permute-start.11 = (f32[56,128]{1,0:T(8,128)S(1)}, f32[56,128]{1,0:T(8,128)S(1)}, u32[]{:S(2)}, u32[]{:S(2)}) collective-permute-start(f32[56,128]{1,0:T(8,128)S(1)} %get-tuple-element.83), channel_id=1, source_target_pairs={{0,16},{8,24},{16,0},{24,8},{1,17},{9,25},{17,1},{25,9},{2,18},{10... | collective-permute-start | bytes 86024 | tf_op jit(solution)/shard_map/ppermute | solution.py:691
  28.8 1.5 %x_solve.2.refs_15_ = f32[6,512,128]{2,1,0:T(8,128)} custom-call(s32[1]{0:T(128)} %bitcast.me_ref, f32[200,128]{1,0:T(8,128)S(1)} %get-tuple-element.79.own.refs_0_.refs_4_, f32[200,128]{1,0:T(8,128)S(1)} %get-tuple-element.84.refs_1_.refs_5_, f32[200,128]{1,0:T(8,128)S(1)} %get-tuple-element.81.refs_1_.refs_2_.refs_6_, ...), custom_call_target="tpu_custom_call" | custom-call | flops 1000000000 | bytes 10000000 | tf_op jit(solution)/shard_map/x_solve/pallas_call | solution.py:673
  30.3 0.6 %collective-permute-done.11.refs_3_ = f32[56,128]{1,0:T(8,128)S(1)} collective-permute-done((f32[56,128]{1,0:T(8,128)S(1)}, f32[56,128]{1,0:T(8,128)S(1)}, u32[]{:S(2)}, u32[]{:S(2)}) %collective-permute-start.11) | collective-permute-done | bytes 28704 | tf_op jit(solution)/shard_map/ppermute | solution.py:691
  30.9 1.5 %x_solve.3 = f32[6,512,128]{2,1,0:T(8,128)} custom-call(s32[1]{0:T(128)} %bitcast.me_ref, f32[112,128]{1,0:T(8,128)S(1)} %get-tuple-element.78.refs_0_.own, f32[112,128]{1,0:T(8,128)S(1)} %get-tuple-element.82.refs_1_, f32[112,128]{1,0:T(8,128)S(1)} %collective-permute-done.9.other.refs_2_, ...), custom_call_target="tpu_custom_call", output_to_operand_aliasing={{}: (16, {})} | custom-call | flops 1000000000 | bytes 10000000 | tf_op jit(solution)/shard_map/x_solve/pallas_call | solution.py:673
  (21 shorter events, 0.7 us)
Async XLA Ops:
  3.4 1.8 %collective-permute-start.1 = (f32[208,128]{1,0:T(8,128)S(1)}, f32[208,128]{1,0:T(8,128)S(1)}, u32[]{:S(2)}, u32[]{:S(2)}) collective-permute-start(f32[208,128]{1,0:T(8,128)S(1)} %get-tuple-element.60), channel_id=1, source_target_pairs={{0,1},{1,0},{2,3},{3,2},{4,5},{5,4},{6,7},{7,6},{8,9},{9,8},{10,11... | collective-permute-start | bytes 319496 | tf_op jit(solution)/shard_map/ppermute | solution.py:691
  5.0 3.1 %collective-permute-start = (f32[96,128]{1,0:T(8,128)S(1)}, f32[96,128]{1,0:T(8,128)S(1)}, u32[]{:S(2)}, u32[]{:S(2)}) collective-permute-start(f32[96,128]{1,0:T(8,128)S(1)} %get-tuple-element.58.refs_0_), channel_id=1, source_target_pairs={{0,1},{1,0},{2,3},{3,2},{4,5},{5,4},{6,7},{7,6},{8,9},{9,8},{10,11... | collective-permute-start | bytes 147464 | tf_op jit(solution)/shard_map/ppermute | solution.py:691
  5.2 6.7 %collective-permute-start.3 = (f32[208,128]{1,0:T(8,128)S(1)}, f32[208,128]{1,0:T(8,128)S(1)}, u32[]{:S(2)}, u32[]{:S(2)}) collective-permute-start(f32[208,128]{1,0:T(8,128)S(1)} %merge_gy.5.refs_0_.after.own.refs_7_.refs_1_), channel_id=1, source_target_pairs={{0,2},{1,3},{2,0},{3,1},{4,6},{5,7},{6,4},{7,5},{8,10},{9,11},{10,... | collective-permute-start | bytes 319496 | tf_op jit(solution)/shard_map/ppermute | solution.py:691
  8.2 1.1 %copy-start = (f32[3,32,16,128]{3,2,1,0:T(8,128)S(1)}, f32[3,32,16,128]{3,2,1,0:T(8,128)}, u32[]{:S(2)}) copy-start(f32[3,32,16,128]{3,2,1,0:T(8,128)} %param.8) | copy-start | bytes 2359300
  8.2 1.4 %copy-start.1 = (s32[3,32,16,128]{3,2,1,0:T(8,128)S(1)}, s32[3,32,16,128]{3,2,1,0:T(8,128)}, u32[]{:S(2)}) copy-start(s32[3,32,16,128]{3,2,1,0:T(8,128)} %param.9) | copy-start | bytes 2359300
  8.2 5.6 %collective-permute-start.2 = (f32[96,128]{1,0:T(8,128)S(1)}, f32[96,128]{1,0:T(8,128)S(1)}, u32[]{:S(2)}, u32[]{:S(2)}) collective-permute-start(f32[96,128]{1,0:T(8,128)S(1)} %merge_gy.4.own.refs_1_), channel_id=1, source_target_pairs={{0,2},{1,3},{2,0},{3,1},{4,6},{5,7},{6,4},{7,5},{8,10},{9,11},{10,... | collective-permute-start | bytes 147464 | tf_op jit(solution)/shard_map/ppermute | solution.py:691
  10.0 4.3 %collective-permute-start.7 = (f32[80,128]{1,0:T(8,128)S(1)}, f32[80,128]{1,0:T(8,128)S(1)}, u32[]{:S(2)}, u32[]{:S(2)}) collective-permute-start(f32[80,128]{1,0:T(8,128)S(1)} %get-tuple-element.63.refs_0_), channel_id=1, source_target_pairs={{0,8},{8,0},{16,24},{24,16},{1,9},{9,1},{17,25},{25,17},{2,10},{10... | collective-permute-start | bytes 122888 | tf_op jit(solution)/shard_map/ppermute | solution.py:691
  11.9 4.2 %collective-permute-start.5 = (f32[96,128]{1,0:T(8,128)S(1)}, f32[96,128]{1,0:T(8,128)S(1)}, u32[]{:S(2)}, u32[]{:S(2)}) collective-permute-start(f32[96,128]{1,0:T(8,128)S(1)} %get-tuple-element.65), channel_id=1, source_target_pairs={{0,4},{1,5},{2,6},{3,7},{4,0},{5,1},{6,2},{7,3},{8,12},{9,13},{10,... | collective-permute-start | bytes 147464 | tf_op jit(solution)/shard_map/ppermute | solution.py:691
  13.8 3.9 %collective-permute-start.4 = (f32[48,128]{1,0:T(8,128)S(1)}, f32[48,128]{1,0:T(8,128)S(1)}, u32[]{:S(2)}, u32[]{:S(2)}) collective-permute-start(f32[48,128]{1,0:T(8,128)S(1)} %get-tuple-element.62.refs_6_), channel_id=1, source_target_pairs={{0,4},{1,5},{2,6},{3,7},{4,0},{5,1},{6,2},{7,3},{8,12},{9,13},{10,... | collective-permute-start | bytes 73736 | tf_op jit(solution)/shard_map/ppermute | solution.py:691
  16.1 1.7 %collective-permute-start.8 = (f32[160,128]{1,0:T(8,128)S(1)}, f32[160,128]{1,0:T(8,128)S(1)}, u32[]{:S(2)}, u32[]{:S(2)}) collective-permute-start(f32[160,128]{1,0:T(8,128)S(1)} %get-tuple-element.72), channel_id=1, source_target_pairs={{0,1},{1,0},{2,3},{3,2},{4,5},{5,4},{6,7},{7,6},{8,9},{9,8},{10,11... | collective-permute-start | bytes 245768 | tf_op jit(solution)/shard_map/ppermute | solution.py:691
  17.7 2.8 %collective-permute-start.6 = (f32[96,128]{1,0:T(8,128)S(1)}, f32[96,128]{1,0:T(8,128)S(1)}, u32[]{:S(2)}, u32[]{:S(2)}) collective-permute-start(f32[96,128]{1,0:T(8,128)S(1)} %get-tuple-element.67), channel_id=1, source_target_pairs={{0,1},{1,0},{2,3},{3,2},{4,5},{5,4},{6,7},{7,6},{8,9},{9,8},{10,11... | collective-permute-start | bytes 147464 | tf_op jit(solution)/shard_map/ppermute | solution.py:691
  18.9 4.5 %collective-permute-start.10 = (f32[120,128]{1,0:T(8,128)S(1)}, f32[120,128]{1,0:T(8,128)S(1)}, u32[]{:S(2)}, u32[]{:S(2)}) collective-permute-start(f32[120,128]{1,0:T(8,128)S(1)} %get-tuple-element.80), channel_id=1, source_target_pairs={{0,8},{8,0},{16,24},{24,16},{1,9},{9,1},{17,25},{25,17},{2,10},{10... | collective-permute-start | bytes 184328 | tf_op jit(solution)/shard_map/ppermute | solution.py:691
  21.6 4.5 %collective-permute-start.9 = (f32[112,128]{1,0:T(8,128)S(1)}, f32[112,128]{1,0:T(8,128)S(1)}, u32[]{:S(2)}, u32[]{:S(2)}) collective-permute-start(f32[112,128]{1,0:T(8,128)S(1)} %get-tuple-element.78.refs_0_.own), channel_id=1, source_target_pairs={{0,8},{8,0},{16,24},{24,16},{1,9},{9,1},{17,25},{25,17},{2,10},{10... | collective-permute-start | bytes 172040 | tf_op jit(solution)/shard_map/ppermute | solution.py:691
  23.4 5.4 %collective-permute-start.12 = (f32[96,128]{1,0:T(8,128)S(1)}, f32[96,128]{1,0:T(8,128)S(1)}, u32[]{:S(2)}, u32[]{:S(2)}) collective-permute-start(f32[96,128]{1,0:T(8,128)S(1)} %get-tuple-element.85), channel_id=1, source_target_pairs={{0,16},{8,24},{16,0},{24,8},{1,17},{9,25},{17,1},{25,9},{2,18},{10... | collective-permute-start | bytes 147464 | tf_op jit(solution)/shard_map/ppermute | solution.py:691
  26.1 4.8 %collective-permute-start.11 = (f32[56,128]{1,0:T(8,128)S(1)}, f32[56,128]{1,0:T(8,128)S(1)}, u32[]{:S(2)}, u32[]{:S(2)}) collective-permute-start(f32[56,128]{1,0:T(8,128)S(1)} %get-tuple-element.83), channel_id=1, source_target_pairs={{0,16},{8,24},{16,0},{24,8},{1,17},{9,25},{17,1},{25,9},{2,18},{10... | collective-permute-start | bytes 86024 | tf_op jit(solution)/shard_map/ppermute | solution.py:691

commit v11 on v10

--- a/solution.py
+++ b/solution.py
@@ -292,7 +292,7 @@
         both[pl.ds(h * lay.rows + row, half), :] = cells[h * half : (h + 1) * half]
 
 
-def z_part(dims, lay, me_ref, cot, phi, psi, w, left, right, arrived, az, both, keep, send):
+def z_part(dims, lay, me_ref, cot, phi, psi, w, left, right, arrived, turned, az, both, keep, send):
     nx, ny = dims
     tiles = nx * ny // LANES
     sums = sum_matrix()
@@ -312,6 +312,7 @@
         for y in range(ny):
             cells = az[c, pl.ds(y, nx, stride=ny), :]
             span = pl.ds(y * nx, nx)
+            turned[c, span, :] = cells
             first = first + left[span, :] * cells
             last = last + right[span, :] * cells
         post(lay, both, lay.offsets[c], first)
@@ -366,8 +367,8 @@
 
 def lead_z_kernel(
     dims, lay, me_ref, cot_any, diff_any, phase_any, cour_any, upw_any,
-    keep, send, az, w, left, right, phi, psi, later,
-    cot, diff, phase, cour, upw, wt, pht, pst, maps, ends, both, in_sems, sems,
+    keep, send, turned, w, left, right, phi, psi, later,
+    az, cot, diff, phase, cour, upw, wt, pht, pst, maps, ends, both, in_sems, sems,
 ):
     nx, ny = dims
     tiles = nx * ny // LANES
@@ -414,17 +415,17 @@
     def arrived(c):
         pltpu.make_async_copy(cot_any.at[c], cot.at[c], in_sems.at[c]).wait()
 
-    z_part(dims, lay, me_ref, cot, phi, psi, w, left, right, arrived, az, both, keep, send)
+    z_part(dims, lay, me_ref, cot, phi, psi, w, left, right, arrived, turned, az, both, keep, send)
     ahead.wait()
 
 
-def next_z_kernel(dims, lay, me_ref, cot, phi, psi, w, left, right, keep, send, az, both):
+def next_z_kernel(dims, lay, me_ref, cot, phi, psi, w, left, right, keep, send, turned, az, both):
     z_part(
-        dims, lay, me_ref, cot, phi, psi, w, left, right, lambda c: None, az, both, keep, send
+        dims, lay, me_ref, cot, phi, psi, w, left, right, lambda c: None, turned, az, both, keep, send
     )
 
 
-def coef_kernel(dims, w, courant, upwind, after, block, inv, xinv, left, right, flows):
+def coef_kernel(dims, w, courant, upwind, after, block, inv, wy, xinv, seam, left, right, flows):
     del after
     nx, ny = dims
     rows = nx * ny
@@ -435,10 +436,14 @@
         right[low, :] = value
         left[high, :] = back
         new_value, slope = growing_step(value, slope, w[low, :])
-        xinv[low, :] = value / new_value
+        new_back, fall = growing_step(back, fall, w[high, :])
+        if k < nx // 2:
+            up, down = value / new_value, back / new_back
+            xinv[low, :] = up
+            xinv[high, :] = down
         end, value = value, new_value
-        corner = back
-        back, fall = growing_step(back, fall, w[high, :])
+        corner, back = back, new_back
+    seam[...] = 1.0 / (1.0 - up * down)
     total = 1.0 / value
     block[pl.ds(0, ny), :] = corner * total
     block[pl.ds(ny, ny), :] = total
@@ -446,7 +451,9 @@
     value = jnp.ones((nx, LANES), jnp.float32)
     slope = value
     for y in range(ny):
-        new_value, slope = growing_step(value, slope, w[pl.ds(y, nx, stride=ny), :])
+        weight = w[pl.ds(y, nx, stride=ny), :]
+        wy[pl.ds(y * nx, nx), :] = weight
+        new_value, slope = growing_step(value, slope, weight)
         inv[pl.ds(y * nx, nx), :] = value / new_value
         value = new_value
 
@@ -481,14 +488,14 @@
     return two_sides(before[pl.ds(x, 1), :], after[pl.ds(x, 1), :])
 
 
-def y_kernel(dims, ylay, xlay, me_ref, az, own, got, w, inv, xinv, *refs):
+def y_kernel(dims, ylay, xlay, me_ref, az, own, got, w, wy, inv, xinv, seam, *refs):
     nx, ny = dims
     half = nx // 2
     comps = len(ylay.sizes)
     if xlay.leads:
-        part, block, slim, field, ghost, ginv, gleft, gright, before, after, ay, joined = refs
+        part, block, slim, field, ghost, ginv, gseam, gleft, gright, before, after, ay, joined = refs
     else:
-        before, after, ginv, gleft, gright, block, field, ghost, fleft, fright, ay, joined = refs
+        before, after, ginv, gseam, gleft, gright, block, field, ghost, fleft, fright, ay, joined = refs
         for x in range(nx):
             here = pl.ds(x * TILE, TILE)
             scale = sides(before, after, nx + x)
@@ -512,10 +519,14 @@
             gright[low, :] = value
             gleft[high, :] = back
             new_value, slope = growing_step(value, slope, sides(before, after, k))
-            ginv[low, :] = value / new_value
+            new_back, fall = growing_step(back, fall, sides(before, after, nx - 1 - k))
+            if k < nx // 2:
+                up, down = value / new_value, back / new_back
+                ginv[low, :] = up
+                ginv[high, :] = down
             end, value = value, new_value
-            corner = back
-            back, fall = growing_step(back, fall, sides(before, after, nx - 1 - k))
+            corner, back = back, new_back
+        gseam[...] = 1.0 / (1.0 - up * down)
         total = 1.0 / value
         for x in range(nx):
             here = pl.ds(x * TILE, TILE)
@@ -532,33 +543,60 @@
             ghost[pl.ds(h * half * TILE + SIDE + c, half, stride=TILE), :] = after[piece, :] * fa
             swept, chain = fb, []
             for y in range(ny):
-                cells = az[c, pl.ds(h * half * ny + y, half, stride=ny), :]
+                cells = az[c, pl.ds(y * nx + h * half, half), :]
                 swept = (cells + swept) * inv[pl.ds(y * nx + h * half, half), :]
                 chain.append(swept)
             later = fa
             for y in reversed(range(ny)):
-                where = pl.ds(h * half * ny + y, half, stride=ny)
-                later = chain[y] + inv[pl.ds(y * nx + h * half, half), :] * later
-                ay[c, where, :] = later * w[where, :]
-
-    swept = [jnp.zeros((n, LANES), jnp.float32) for n in xlay.sizes]
-    for x in range(nx):
-        here, there = pl.ds(x * ny, ny), pl.ds(x * TILE, TILE)
-        for c in range(comps):
-            swept[c] = (ay[c, here, :] + swept[c]) * xinv[here, :]
-            ay[c, here, :] = swept[c]
-        swept[comps] = (ghost[there, :] + swept[comps]) * ginv[there, :]
-        ghost[there, :] = swept[comps]
-    lasts, solved = list(swept), list(swept)
-    for x in reversed(range(nx)):
-        here, there = pl.ds(x * ny, ny), pl.ds(x * TILE, TILE)
-        for c in range(comps):
-            if x + 1 < nx:
-                solved[c] = ay[c, here, :] + xinv[here, :] * solved[c]
-            field[c, here, :] = solved[c] * w[here, :]
-        if x + 1 < nx:
-            solved[comps] = ghost[there, :] + ginv[there, :] * solved[comps]
-        ghost[there, :] = solved[comps] * sides(before, after, nx + x)
+                row = pl.ds(y * nx + h * half, half)
+                later = chain[y] + inv[row, :] * later
+                ay[c, pl.ds(h * half * ny + y, half, stride=ny), :] = later * wy[row, :]
+
+    def load(i, x):
+        return ghost[pl.ds(x * TILE, TILE), :] if i == comps else ay[i, pl.ds(x * ny, ny), :]
+
+    def keep(i, x, cells):
+        if i == comps:
+            ghost[pl.ds(x * TILE, TILE), :] = cells
+        else:
+            ay[i, pl.ds(x * ny, ny), :] = cells
+
+    def pivot(i, x):
+        return ginv[pl.ds(x * TILE, TILE), :] if i == comps else xinv[pl.ds(x * ny, ny), :]
+
+    def finish(i, x, cells):
+        if i == comps:
+            ghost[pl.ds(x * TILE, TILE), :] = cells * sides(before, after, nx + x)
+        else:
+            here = pl.ds(x * ny, ny)
+            field[i, here, :] = cells * w[here, :]
+
+    pieces = range(comps + 1)
+    middle = nx // 2
+    lows = [jnp.zeros((n, LANES), jnp.float32) for n in xlay.sizes]
+    highs = list(lows)
+    for k in range(middle):
+        x, mirror = k, nx - 1 - k
+        for i in pieces:
+            lows[i] = (load(i, x) + lows[i]) * pivot(i, x)
+            highs[i] = (load(i, mirror) + highs[i]) * pivot(i, mirror)
+            if k + 1 < middle:
+                keep(i, x, lows[i])
+                keep(i, mirror, highs[i])
+    for i in pieces:
+        joint_scale = gseam[...] if i == comps else seam[...]
+        highs[i] = (highs[i] + pivot(i, middle) * lows[i]) * joint_scale
+        lows[i] = lows[i] + pivot(i, middle - 1) * highs[i]
+        finish(i, middle - 1, lows[i])
+        finish(i, middle, highs[i])
+    for k in range(1, middle):
+        x, mirror = middle - 1 - k, middle + k
+        for i in pieces:
+            lows[i] = load(i, x) + pivot(i, x) * lows[i]
+            highs[i] = load(i, mirror) + pivot(i, mirror) * highs[i]
+            finish(i, x, lows[i])
+            finish(i, mirror, highs[i])
+    solved, lasts = lows, highs
     record = {"first": solved, "last": lasts}
     if xlay.leads:
         pieces = [part[pl.ds(i * ny, ny), :] for i in range(5)]
@@ -751,7 +789,7 @@
         (me, cot, diffusion.reshape(flat), phase.reshape(flat), cour, upw),
         [(ylays[0].rows, nz)] * 2 + [(n, rows, nz)] + [flat] * 5 + [(counts[1], rows, nz)],
         [
-            vmem(n, rows, nz), vmem(*flat), vmem(*flat, dtype=jnp.int32),
+            vmem(n, rows, nz), vmem(n, rows, nz), vmem(*flat), vmem(*flat, dtype=jnp.int32),
             vmem(*flat), vmem(*flat, dtype=jnp.int32),
             vmem(*flat), vmem(*flat), vmem(*flat),
             vmem(rows // LANES * 8 * TILE, nz), vmem(rows // LANES * 4 * TILE, nz),
@@ -770,7 +808,7 @@
         "z_solve_next",
         (me, cot_next, phi, psi, w, left, right),
         [(ylays[1].rows, nz)] * 2 + [(n, rows, nz)],
-        [vmem(2 * ylays[1].rows, nz)],
+        [vmem(n, rows, nz), vmem(2 * ylays[1].rows, nz)],
         mebibytes=8,
     )
     azs.append(az)
@@ -784,11 +822,11 @@
         follow.send()
         beside = (follow.outgoing,)
         if level == 0:
-            part, inv, xinv, xleft, xright, flows = call(
+            part, inv, wy, xinv, seam, xleft, xright, flows = call(
                 functools.partial(coef_kernel, (nx, ny)),
                 "x_coefficients",
                 (w, cour, upw, lead.owns[1]),
-                [(5 * ny, nz), flat, flat, flat, flat, (7 * rows, nz)],
+                [(5 * ny, nz), flat, flat, flat, (ny, nz), flat, flat, (7 * rows, nz)],
                 spaces="vvvv",
                 mebibytes=8,
             )
@@ -806,18 +844,18 @@
         mets.append(exchange(passed, "gy", 0))
     fields, ghosts, climbs = [], [], []
     for g in range(2):
-        common = (me, azs[g], answers[g], mets[g], w, inv, xinv)
+        common = (me, azs[g], answers[g], mets[g], w, wy, inv, xinv, seam)
         edge = (nx * TILE, nz)
         outs = [(counts[g], rows, nz), edge]
         scratch = [vmem(counts[g], rows, nz), vmem(2 * ylays[g].answer_rows, nz)]
         body = functools.partial(y_kernel, (nx, ny), ylays[g], xlays[g])
         if g == 0:
-            block, slim, field, ghost, ginv, gleft, gright, before, after = call(
+            block, slim, field, ghost, ginv, gseam, gleft, gright, before, after = call(
                 body,
                 "y_solve_lead",
                 common + (part,),
                 [(xlays[0].rows, nz), (xlays[0].couple + TILE, nz)]
-                + outs + [edge] * 3 + [(2 * nx, nz)] * 2,
+                + outs + [edge, (TILE, nz), edge, edge] + [(2 * nx, nz)] * 2,
                 scratch,
                 mebibytes=6,
             )
@@ -826,7 +864,7 @@
             block, field, ghost, gleft, gright = call(
                 body,
                 "y_solve_next",
-                common + (before, after, ginv, gleft, gright),
+                common + (before, after, ginv, gseam, gleft, gright),
                 [(xlays[1].rows, nz)] + outs + [edge] * 2,
                 scratch,
                 mebibytes=6,

time: 32.5 us -> 32.3 us (level)
  waiting for transfers between devices: 5.59 us -> 6.42 us
  Pallas kernels: 10.2 us -> 9.61 us
  starting transfers between devices: 16 us -> 15.5 us
    ppermute x13, waiting for transfers between devices: 5.59 us -> 6.42 us  [exchange(): return lax.ppermute(rows, axis, [(i, i ^ 1 << bit) for i in range(count)])]
    pallas_call x15, Pallas kernels: 10.2 us -> 9.61 us  [call(): pl.pallas_call(kernel, name=name, out_shape=[held[s](shape, jnp.float32)...]
    ppermute x13, starting transfers between devices: 16 us -> 15.5 us  [exchange(): return lax.ppermute(rows, axis, [(i, i ^ 1 << bit) for i in range(count)])]
  transfers between devices with their start and end apart: 13 -> 13, of which waited for: 6 -> 6; matrix products, arithmetic and copies ran while one was open for 0% -> 0% of each run, Pallas kernels for 17% -> 15%
where the time goes in v11:
time: 32.3 us; the launch traced here: 32.1 us
  starting transfers between devices  15.5 us (48%)
  Pallas kernels  9.61 us (30%)
  waiting for transfers between devices  6.42 us (20%)
  local copies, waits for them, and re-layouts  0.5 us (2%)
    ppermute x13, starting transfers between devices, exchange(): return lax.ppermute(rows, axis, [(i, i ^ 1 << bit) for i in range(count)])  15.5 us
    pallas_call x15, Pallas kernels, call(): pl.pallas_call(kernel, name=name, out_shape=[held[s](shape, jnp.float32)...  9.61 us
    ppermute x13, waiting for transfers between devices, exchange(): return lax.ppermute(rows, axis, [(i, i ^ 1 << bit) for i in range(count)])  6.42 us
  transfers between devices with their start and end apart: 13, of which 6 were waited for; matrix products, arithmetic and copies ran while one was open for 0% of the time, Pallas kernels for 15%

profile of v11, /device:TPU:0, one launch (start us, length us, event | category | flops | bytes accessed | tf_op | source)
XLA Modules:
  0.0 32.1 jit_solution(4289817946950540712)
XLA Ops:
  0.0 3.4 %z_solve_lead.1 = (f32[208,128]{1,0:T(8,128)S(1)}, f32[208,128]{1,0:T(8,128)S(1)}, f32[3,512,128]{2,1,0:T(8,128)S(1)}, f32[512,128]{1,0:T(8,128)S(1)}, f32[512,1...) custom-call(s32[1]{0:T(128)} %bitcast.me_ref, ...), custom_call_target="tpu_custom_call" | custom-call | flops 1000000000 | bytes 10000000 | tf_op jit(solution)/shard_map/z_solve_lead/pallas_call | solution.py:711
  3.4 0.5 %collective-permute-start.1 = (f32[208,128]{1,0:T(8,128)S(1)}, f32[208,128]{1,0:T(8,128)S(1)}, u32[]{:S(2)}, u32[]{:S(2)}) collective-permute-start(f32[208,128]{1,0:T(8,128)S(1)} %get-tuple-element.63), channel_id=1, source_target_pairs={{0,1},{1,0},{2,3},{3,2},{4,5},{5,4},{6,7},{7,6},{8,9},{9,8},{10,11... | collective-permute-start | bytes 319496 | tf_op jit(solution)/shard_map/ppermute | solution.py:729
  3.9 1.2 %z_solve_next.1 = (f32[96,128]{1,0:T(8,128)S(1)}, f32[96,128]{1,0:T(8,128)S(1)}, f32[3,512,128]{2,1,0:T(8,128)S(1)}) custom-call(s32[1]{0:T(128)} %bitcast.me_ref, f32[3,512,128]{2,1,0:T(8,128)S(1)} %get-tuple-element.53.cot, f32[512,128]{1,0:T(8,128)S(1)} %get-tuple-element.54.phi, f32[512,128]{1,0:T(8,128)S(1)} %get-tuple-element.55.psi, ...), custom_call_target="tpu_custom_call" | custom-call | flops 1000000000 | bytes 10000000 | tf_op jit(solution)/shard_map/z_solve_next/pallas_call | solution.py:711
  5.3 3.0 %collective-permute-start.3 = (f32[208,128]{1,0:T(8,128)S(1)}, f32[208,128]{1,0:T(8,128)S(1)}, u32[]{:S(2)}, u32[]{:S(2)}) collective-permute-start(f32[208,128]{1,0:T(8,128)S(1)} %merge_gy.5.refs_0_.after.own.refs_7_.refs_1_), channel_id=1, source_target_pairs={{0,2},{1,3},{2,0},{3,1},{4,6},{5,7},{6,4},{7,5},{8,10},{9,11},{10,... | collective-permute-start | bytes 319496 | tf_op jit(solution)/shard_map/ppermute | solution.py:729
  8.3 0.8 %collective-permute-start.2 = (f32[96,128]{1,0:T(8,128)S(1)}, f32[96,128]{1,0:T(8,128)S(1)}, u32[]{:S(2)}, u32[]{:S(2)}) collective-permute-start(f32[96,128]{1,0:T(8,128)S(1)} %merge_gy.4.own.refs_1_), channel_id=1, source_target_pairs={{0,2},{1,3},{2,0},{3,1},{4,6},{5,7},{6,4},{7,5},{8,10},{9,11},{10,... | collective-permute-start | bytes 147464 | tf_op jit(solution)/shard_map/ppermute | solution.py:729
  9.1 0.3 copy-done
  9.6 0.4 %x_coefficients.1 = (f32[80,128]{1,0:T(8,128)S(1)}, f32[512,128]{1,0:T(8,128)S(1)}, f32[512,128]{1,0:T(8,128)S(1)}, f32[512,128]{1,0:T(8,128)S(1)}, f32[16,128]{...) custom-call(f32[512,128]{1,0:T(8,128)S(1)} %get-tuple-element.56.w, ...), custom_call_target="tpu_custom_call" | custom-call | flops 1000000000 | bytes 10000000 | tf_op jit(solution)/shard_map/x_coefficients/pallas_call | solution.py:711
  10.0 1.7 %collective-permute-start.7 = (f32[80,128]{1,0:T(8,128)S(1)}, f32[80,128]{1,0:T(8,128)S(1)}, u32[]{:S(2)}, u32[]{:S(2)}) collective-permute-start(f32[80,128]{1,0:T(8,128)S(1)} %get-tuple-element.66.refs_0_), channel_id=1, source_target_pairs={{0,8},{8,0},{16,24},{24,16},{1,9},{9,1},{17,25},{25,17},{2,10},{10... | collective-permute-start | bytes 122888 | tf_op jit(solution)/shard_map/ppermute | solution.py:729
  11.7 0.2 collective-permute-done.3.refs_1_.other.refs_10_.refs_4_
  12.0 1.9 %collective-permute-start.5 = (f32[96,128]{1,0:T(8,128)S(1)}, f32[96,128]{1,0:T(8,128)S(1)}, u32[]{:S(2)}, u32[]{:S(2)}) collective-permute-start(f32[96,128]{1,0:T(8,128)S(1)} %get-tuple-element.68), channel_id=1, source_target_pairs={{0,4},{1,5},{2,6},{3,7},{4,0},{5,1},{6,2},{7,3},{8,12},{9,13},{10,... | collective-permute-start | bytes 147464 | tf_op jit(solution)/shard_map/ppermute | solution.py:729
  13.9 0.5 %collective-permute-start.4 = (f32[48,128]{1,0:T(8,128)S(1)}, f32[48,128]{1,0:T(8,128)S(1)}, u32[]{:S(2)}, u32[]{:S(2)}) collective-permute-start(f32[48,128]{1,0:T(8,128)S(1)} %get-tuple-element.65.refs_6_), channel_id=1, source_target_pairs={{0,4},{1,5},{2,6},{3,7},{4,0},{5,1},{6,2},{7,3},{8,12},{9,13},{10,... | collective-permute-start | bytes 73736 | tf_op jit(solution)/shard_map/ppermute | solution.py:729
  14.3 1.8 %collective-permute-done.5.refs_11_.refs_5_ = f32[96,128]{1,0:T(8,128)S(1)} collective-permute-done((f32[96,128]{1,0:T(8,128)S(1)}, f32[96,128]{1,0:T(8,128)S(1)}, u32[]{:S(2)}, u32[]{:S(2)}) %collective-permute-start.5) | collective-permute-done | bytes 49184 | tf_op jit(solution)/shard_map/ppermute | solution.py:729
  16.3 1.5 %collective-permute-done.4.refs_5_ = f32[48,128]{1,0:T(8,128)S(1)} collective-permute-done((f32[48,128]{1,0:T(8,128)S(1)}, f32[48,128]{1,0:T(8,128)S(1)}, u32[]{:S(2)}, u32[]{:S(2)}) %collective-permute-start.4) | collective-permute-done | bytes 24608 | tf_op jit(solution)/shard_map/ppermute | solution.py:729
  17.9 0.7 %y_solve_lead.1 = (f32[200,128]{1,0:T(8,128)S(1)}, f32[120,128]{1,0:T(8,128)S(1)}, f32[3,512,128]{2,1,0:T(8,128)S(1)}, f32[256,128]{1,0:T(8,128)S(1)}, f32[256,1...) custom-call(s32[1]{0:T(128)} %bitcast.me_ref, ...), custom_call_target="tpu_custom_call" | custom-call | flops 1000000000 | bytes 10000000 | tf_op jit(solution)/shard_map/y_solve_lead/pallas_call | solution.py:711
  18.6 1.6 %collective-permute-start.10 = (f32[120,128]{1,0:T(8,128)S(1)}, f32[120,128]{1,0:T(8,128)S(1)}, u32[]{:S(2)}, u32[]{:S(2)}) collective-permute-start(f32[120,128]{1,0:T(8,128)S(1)} %get-tuple-element.86), channel_id=1, source_target_pairs={{0,8},{8,0},{16,24},{24,16},{1,9},{9,1},{17,25},{25,17},{2,10},{10... | collective-permute-start | bytes 184328 | tf_op jit(solution)/shard_map/ppermute | solution.py:729
  20.3 0.7 %y_solve_next.1 = (f32[112,128]{1,0:T(8,128)S(1)}, f32[3,512,128]{2,1,0:T(8,128)S(1)}, f32[256,128]{1,0:T(8,128)S(1)}, f32[256,128]{1,0:T(8,128)S(1)}, f32[256,128]{1,0:T(8,128)S(1)}) custom-call(s32[1]{0:T(128)} %bitcast.me_ref, f32[3,512,128]{2,1,0:T(8,128)S(1)} %get-tuple-element.59.az, f32[96,128]{1,0:T(8,128)S(1)} %get-tuple-element.69.own, ...), custom_call_target="tpu_custom_call" | custom-call | flops 1000000000 | bytes 10000000 | tf_op jit(solution)/shard_map/y_solve_next/pallas_call | solution.py:711
  21.0 0.5 %collective-permute-start.9 = (f32[112,128]{1,0:T(8,128)S(1)}, f32[112,128]{1,0:T(8,128)S(1)}, u32[]{:S(2)}, u32[]{:S(2)}) collective-permute-start(f32[112,128]{1,0:T(8,128)S(1)} %get-tuple-element.84.refs_0_.own), channel_id=1, source_target_pairs={{0,8},{8,0},{16,24},{24,16},{1,9},{9,1},{17,25},{25,17},{2,10},{10... | collective-permute-start | bytes 172040 | tf_op jit(solution)/shard_map/ppermute | solution.py:729
  21.5 1.6 %collective-permute-done.10.slim = f32[120,128]{1,0:T(8,128)S(1)} collective-permute-done((f32[120,128]{1,0:T(8,128)S(1)}, f32[120,128]{1,0:T(8,128)S(1)}, u32[]{:S(2)}, u32[]{:S(2)}) %collective-permute-start.10) | collective-permute-done | bytes 61472 | tf_op jit(solution)/shard_map/ppermute | solution.py:729
  23.1 2.6 %collective-permute-start.12 = (f32[96,128]{1,0:T(8,128)S(1)}, f32[96,128]{1,0:T(8,128)S(1)}, u32[]{:S(2)}, u32[]{:S(2)}) collective-permute-start(f32[96,128]{1,0:T(8,128)S(1)} %get-tuple-element.91), channel_id=1, source_target_pairs={{0,16},{8,24},{16,0},{24,8},{1,17},{9,25},{17,1},{25,9},{2,18},{10... | collective-permute-start | bytes 147464 | tf_op jit(solution)/shard_map/ppermute | solution.py:729
  25.8 2.1 %collective-permute-start.11 = (f32[56,128]{1,0:T(8,128)S(1)}, f32[56,128]{1,0:T(8,128)S(1)}, u32[]{:S(2)}, u32[]{:S(2)}) collective-permute-start(f32[56,128]{1,0:T(8,128)S(1)} %get-tuple-element.89), channel_id=1, source_target_pairs={{0,16},{8,24},{16,0},{24,8},{1,17},{9,25},{17,1},{25,9},{2,18},{10... | collective-permute-start | bytes 86024 | tf_op jit(solution)/shard_map/ppermute | solution.py:729
  27.9 0.6 %collective-permute-done.12.refs_3_.refs_7_ = f32[96,128]{1,0:T(8,128)S(1)} collective-permute-done((f32[96,128]{1,0:T(8,128)S(1)}, f32[96,128]{1,0:T(8,128)S(1)}, u32[]{:S(2)}, u32[]{:S(2)}) %collective-permute-start.12) | collective-permute-done | bytes 49184 | tf_op jit(solution)/shard_map/ppermute | solution.py:729
  28.5 1.5 %x_solve.2.refs_15_ = f32[6,512,128]{2,1,0:T(8,128)} custom-call(s32[1]{0:T(128)} %bitcast.me_ref, f32[200,128]{1,0:T(8,128)S(1)} %get-tuple-element.85.own.refs_0_.refs_4_, f32[200,128]{1,0:T(8,128)S(1)} %get-tuple-element.90.refs_1_.refs_5_, f32[200,128]{1,0:T(8,128)S(1)} %get-tuple-element.87.refs_1_.refs_2_.refs_6_, ...), custom_call_target="tpu_custom_call" | custom-call | flops 1000000000 | bytes 10000000 | tf_op jit(solution)/shard_map/x_solve/pallas_call | solution.py:711
  29.9 0.7 %collective-permute-done.11.refs_3_ = f32[56,128]{1,0:T(8,128)S(1)} collective-permute-done((f32[56,128]{1,0:T(8,128)S(1)}, f32[56,128]{1,0:T(8,128)S(1)}, u32[]{:S(2)}, u32[]{:S(2)}) %collective-permute-start.11) | collective-permute-done | bytes 28704 | tf_op jit(solution)/shard_map/ppermute | solution.py:729
  30.6 1.5 %x_solve.3 = f32[6,512,128]{2,1,0:T(8,128)} custom-call(s32[1]{0:T(128)} %bitcast.me_ref, f32[112,128]{1,0:T(8,128)S(1)} %get-tuple-element.84.refs_0_.own, f32[112,128]{1,0:T(8,128)S(1)} %get-tuple-element.88.refs_1_, f32[112,128]{1,0:T(8,128)S(1)} %collective-permute-done.9.other.refs_2_, ...), custom_call_target="tpu_custom_call", output_to_operand_aliasing={{}: (16, {})} | custom-call | flops 1000000000 | bytes 10000000 | tf_op jit(solution)/shard_map/x_solve/pallas_call | solution.py:711
  (21 shorter events, 0.8 us)
Async XLA Ops:
  3.4 1.8 %collective-permute-start.1 = (f32[208,128]{1,0:T(8,128)S(1)}, f32[208,128]{1,0:T(8,128)S(1)}, u32[]{:S(2)}, u32[]{:S(2)}) collective-permute-start(f32[208,128]{1,0:T(8,128)S(1)} %get-tuple-element.63), channel_id=1, source_target_pairs={{0,1},{1,0},{2,3},{3,2},{4,5},{5,4},{6,7},{7,6},{8,9},{9,8},{10,11... | collective-permute-start | bytes 319496 | tf_op jit(solution)/shard_map/ppermute | solution.py:729
  5.1 3.2 %collective-permute-start = (f32[96,128]{1,0:T(8,128)S(1)}, f32[96,128]{1,0:T(8,128)S(1)}, u32[]{:S(2)}, u32[]{:S(2)}) collective-permute-start(f32[96,128]{1,0:T(8,128)S(1)} %get-tuple-element.61.refs_0_), channel_id=1, source_target_pairs={{0,1},{1,0},{2,3},{3,2},{4,5},{5,4},{6,7},{7,6},{8,9},{9,8},{10,11... | collective-permute-start | bytes 147464 | tf_op jit(solution)/shard_map/ppermute | solution.py:729
  5.3 6.7 %collective-permute-start.3 = (f32[208,128]{1,0:T(8,128)S(1)}, f32[208,128]{1,0:T(8,128)S(1)}, u32[]{:S(2)}, u32[]{:S(2)}) collective-permute-start(f32[208,128]{1,0:T(8,128)S(1)} %merge_gy.5.refs_0_.after.own.refs_7_.refs_1_), channel_id=1, source_target_pairs={{0,2},{1,3},{2,0},{3,1},{4,6},{5,7},{6,4},{7,5},{8,10},{9,11},{10,... | collective-permute-start | bytes 319496 | tf_op jit(solution)/shard_map/ppermute | solution.py:729
  8.2 1.1 %copy-start = (f32[3,32,16,128]{3,2,1,0:T(8,128)S(1)}, f32[3,32,16,128]{3,2,1,0:T(8,128)}, u32[]{:S(2)}) copy-start(f32[3,32,16,128]{3,2,1,0:T(8,128)} %param.8) | copy-start | bytes 2359300
  8.2 1.4 %copy-start.1 = (s32[3,32,16,128]{3,2,1,0:T(8,128)S(1)}, s32[3,32,16,128]{3,2,1,0:T(8,128)}, u32[]{:S(2)}) copy-start(s32[3,32,16,128]{3,2,1,0:T(8,128)} %param.9) | copy-start | bytes 2359300
  8.3 5.6 %collective-permute-start.2 = (f32[96,128]{1,0:T(8,128)S(1)}, f32[96,128]{1,0:T(8,128)S(1)}, u32[]{:S(2)}, u32[]{:S(2)}) collective-permute-start(f32[96,128]{1,0:T(8,128)S(1)} %merge_gy.4.own.refs_1_), channel_id=1, source_target_pairs={{0,2},{1,3},{2,0},{3,1},{4,6},{5,7},{6,4},{7,5},{8,10},{9,11},{10,... | collective-permute-start | bytes 147464 | tf_op jit(solution)/shard_map/ppermute | solution.py:729
  10.0 4.3 %collective-permute-start.7 = (f32[80,128]{1,0:T(8,128)S(1)}, f32[80,128]{1,0:T(8,128)S(1)}, u32[]{:S(2)}, u32[]{:S(2)}) collective-permute-start(f32[80,128]{1,0:T(8,128)S(1)} %get-tuple-element.66.refs_0_), channel_id=1, source_target_pairs={{0,8},{8,0},{16,24},{24,16},{1,9},{9,1},{17,25},{25,17},{2,10},{10... | collective-permute-start | bytes 122888 | tf_op jit(solution)/shard_map/ppermute | solution.py:729
  12.0 4.2 %collective-permute-start.5 = (f32[96,128]{1,0:T(8,128)S(1)}, f32[96,128]{1,0:T(8,128)S(1)}, u32[]{:S(2)}, u32[]{:S(2)}) collective-permute-start(f32[96,128]{1,0:T(8,128)S(1)} %get-tuple-element.68), channel_id=1, source_target_pairs={{0,4},{1,5},{2,6},{3,7},{4,0},{5,1},{6,2},{7,3},{8,12},{9,13},{10,... | collective-permute-start | bytes 147464 | tf_op jit(solution)/shard_map/ppermute | solution.py:729
  13.9 3.9 %collective-permute-start.4 = (f32[48,128]{1,0:T(8,128)S(1)}, f32[48,128]{1,0:T(8,128)S(1)}, u32[]{:S(2)}, u32[]{:S(2)}) collective-permute-start(f32[48,128]{1,0:T(8,128)S(1)} %get-tuple-element.65.refs_6_), channel_id=1, source_target_pairs={{0,4},{1,5},{2,6},{3,7},{4,0},{5,1},{6,2},{7,3},{8,12},{9,13},{10,... | collective-permute-start | bytes 73736 | tf_op jit(solution)/shard_map/ppermute | solution.py:729
  16.2 1.7 %collective-permute-start.8 = (f32[160,128]{1,0:T(8,128)S(1)}, f32[160,128]{1,0:T(8,128)S(1)}, u32[]{:S(2)}, u32[]{:S(2)}) collective-permute-start(f32[160,128]{1,0:T(8,128)S(1)} %get-tuple-element.77), channel_id=1, source_target_pairs={{0,1},{1,0},{2,3},{3,2},{4,5},{5,4},{6,7},{7,6},{8,9},{9,8},{10,11... | collective-permute-start | bytes 245768 | tf_op jit(solution)/shard_map/ppermute | solution.py:729
  17.8 2.5 %collective-permute-start.6 = (f32[96,128]{1,0:T(8,128)S(1)}, f32[96,128]{1,0:T(8,128)S(1)}, u32[]{:S(2)}, u32[]{:S(2)}) collective-permute-start(f32[96,128]{1,0:T(8,128)S(1)} %get-tuple-element.70), channel_id=1, source_target_pairs={{0,1},{1,0},{2,3},{3,2},{4,5},{5,4},{6,7},{7,6},{8,9},{9,8},{10,11... | collective-permute-start | bytes 147464 | tf_op jit(solution)/shard_map/ppermute | solution.py:729
  18.6 4.5 %collective-permute-start.10 = (f32[120,128]{1,0:T(8,128)S(1)}, f32[120,128]{1,0:T(8,128)S(1)}, u32[]{:S(2)}, u32[]{:S(2)}) collective-permute-start(f32[120,128]{1,0:T(8,128)S(1)} %get-tuple-element.86), channel_id=1, source_target_pairs={{0,8},{8,0},{16,24},{24,16},{1,9},{9,1},{17,25},{25,17},{2,10},{10... | collective-permute-start | bytes 184328 | tf_op jit(solution)/shard_map/ppermute | solution.py:729
  21.0 4.8 %collective-permute-start.9 = (f32[112,128]{1,0:T(8,128)S(1)}, f32[112,128]{1,0:T(8,128)S(1)}, u32[]{:S(2)}, u32[]{:S(2)}) collective-permute-start(f32[112,128]{1,0:T(8,128)S(1)} %get-tuple-element.84.refs_0_.own), channel_id=1, source_target_pairs={{0,8},{8,0},{16,24},{24,16},{1,9},{9,1},{17,25},{25,17},{2,10},{10... | collective-permute-start | bytes 172040 | tf_op jit(solution)/shard_map/ppermute | solution.py:729
  23.1 5.3 %collective-permute-start.12 = (f32[96,128]{1,0:T(8,128)S(1)}, f32[96,128]{1,0:T(8,128)S(1)}, u32[]{:S(2)}, u32[]{:S(2)}) collective-permute-start(f32[96,128]{1,0:T(8,128)S(1)} %get-tuple-element.91), channel_id=1, source_target_pairs={{0,16},{8,24},{16,0},{24,8},{1,17},{9,25},{17,1},{25,9},{2,18},{10... | collective-permute-start | bytes 147464 | tf_op jit(solution)/shard_map/ppermute | solution.py:729
  25.8 4.8 %collective-permute-start.11 = (f32[56,128]{1,0:T(8,128)S(1)}, f32[56,128]{1,0:T(8,128)S(1)}, u32[]{:S(2)}, u32[]{:S(2)}) collective-permute-start(f32[56,128]{1,0:T(8,128)S(1)} %get-tuple-element.89), channel_id=1, source_target_pairs={{0,16},{8,24},{16,0},{24,8},{1,17},{9,25},{17,1},{25,9},{2,18},{10... | collective-permute-start | bytes 86024 | tf_op jit(solution)/shard_map/ppermute | solution.py:729

commit v12 on v11

--- a/solution.py
+++ b/solution.py
@@ -286,13 +286,7 @@
     return chain, backs, 1.0 / value
 
 
-def post(lay, both, row, cells):
-    half = cells.shape[0] // 2
-    for h in range(2):
-        both[pl.ds(h * lay.rows + row, half), :] = cells[h * half : (h + 1) * half]
-
-
-def z_part(dims, lay, me_ref, cot, phi, psi, w, left, right, arrived, turned, az, both, keep, send):
+def z_part(dims, lay, cot, phi, psi, w, left, right, arrived, record, turned, az):
     nx, ny = dims
     tiles = nx * ny // LANES
     sums = sum_matrix()
@@ -315,11 +309,8 @@
             turned[c, span, :] = cells
             first = first + left[span, :] * cells
             last = last + right[span, :] * cells
-        post(lay, both, lay.offsets[c], first)
-        post(lay, both, lay.total + lay.offsets[c], last)
-    mine = me_ref[0] & 1
-    keep[...] = both[pl.ds(pl.multiple_of(mine * lay.rows, TILE), lay.rows), :]
-    send[...] = both[pl.ds(pl.multiple_of((1 - mine) * lay.rows, TILE), lay.rows), :]
+        record[pl.ds(lay.offsets[c], nx), :] = first
+        record[pl.ds(lay.total + lay.offsets[c], nx), :] = last
 
 
 def carried(maps, state):
@@ -366,13 +357,12 @@
 
 
 def lead_z_kernel(
-    dims, lay, me_ref, cot_any, diff_any, phase_any, cour_any, upw_any,
-    keep, send, turned, w, left, right, phi, psi, later,
-    az, cot, diff, phase, cour, upw, wt, pht, pst, maps, ends, both, in_sems, sems,
+    dims, lay, cot_any, diff_any, phase_any, cour_any, upw_any,
+    record, turned, w, left, right, phi, psi, later,
+    az, cot, diff, phase, cour, upw, wt, pht, pst, maps, ends, in_sems, sems,
 ):
     nx, ny = dims
     tiles = nx * ny // LANES
-    half = nx // 2
     count = len(lay.sizes)
     ahead = pltpu.make_async_copy(cot_any.at[pl.ds(count, later.shape[0])], later, sems.at[4])
     small = [(diff_any, diff), (phase_any, phase), (cour_any.at[1], cour), (upw_any.at[1], upw)]
@@ -399,9 +389,7 @@
         span = pl.ds(y * nx, nx)
         left[span, :] = backs[y] * total
         right[span, :] = chain[y] * total
-    post(lay, both, lay.couple, backs[0] * total)
-    post(lay, both, lay.couple + half, total)
-    post(lay, both, lay.couple + 2 * half, chain[ny - 1] * total)
+    write_rows(record, lay.couple, [backs[0] * total, total, chain[ny - 1] * total], nx)
     for i, (source, target) in enumerate(small[2:]):
         pltpu.make_async_copy(source, target, sems.at[2 + i]).wait()
     for e, y in enumerate((0, ny - 1)):
@@ -409,20 +397,17 @@
         weight = w[edge, :]
         up = cour[edge, :] * upw[edge, :].astype(jnp.float32)
         flow = up if e == 0 else cour[edge, :] - up
-        post(lay, both, lay.edge + 2 * e * half, weight)
-        post(lay, both, lay.edge + (2 * e + 1) * half, weight * flow)
+        write_rows(record, lay.edge + 2 * e * nx, [weight, weight * flow], nx)
 
     def arrived(c):
         pltpu.make_async_copy(cot_any.at[c], cot.at[c], in_sems.at[c]).wait()
 
-    z_part(dims, lay, me_ref, cot, phi, psi, w, left, right, arrived, turned, az, both, keep, send)
+    z_part(dims, lay, cot, phi, psi, w, left, right, arrived, record, turned, az)
     ahead.wait()
 
 
-def next_z_kernel(dims, lay, me_ref, cot, phi, psi, w, left, right, keep, send, turned, az, both):
-    z_part(
-        dims, lay, me_ref, cot, phi, psi, w, left, right, lambda c: None, turned, az, both, keep, send
-    )
+def next_z_kernel(dims, lay, cot, phi, psi, w, left, right, record, turned, az):
+    z_part(dims, lay, cot, phi, psi, w, left, right, lambda c: None, record, turned, az)
 
 
 def coef_kernel(dims, w, courant, upwind, after, block, inv, wy, xinv, seam, left, right, flows):
@@ -490,7 +475,6 @@
 
 def y_kernel(dims, ylay, xlay, me_ref, az, own, got, w, wy, inv, xinv, seam, *refs):
     nx, ny = dims
-    half = nx // 2
     comps = len(ylay.sizes)
     if xlay.leads:
         part, block, slim, field, ghost, ginv, gseam, gleft, gright, before, after, ay, joined = refs
@@ -501,17 +485,10 @@
             scale = sides(before, after, nx + x)
             fleft[here, :] = gleft[here, :] * scale
             fright[here, :] = gright[here, :] * scale
-    mine = me_ref[0] & 1
-    span = ylay.answer_rows
-    joined[pl.ds(pl.multiple_of(mine * span, TILE), span), :] = own[...]
-    joined[pl.ds(pl.multiple_of((1 - mine) * span, TILE), span), :] = got[...]
+    joined[...] = pick(me_ref[0] & 1, got[...], own[...])
     if xlay.leads:
-        for h in range(2):
-            for e in range(2):
-                where = pl.ds(e * nx + h * half, half)
-                row = h * span + 2 * ylay.total + e * half
-                before[where, :] = joined[pl.ds(row, half), :]
-                after[where, :] = joined[pl.ds(row + 2 * half, half), :]
+        before[...] = joined[pl.ds(2 * ylay.total, 2 * nx), :]
+        after[...] = joined[pl.ds(2 * ylay.total + 2 * nx, 2 * nx), :]
         one = jnp.ones((TILE, LANES), jnp.float32)
         value, slope, back, fall = one, one, one, one
         for k in range(nx):
@@ -535,22 +512,20 @@
 
     ghost[...] = jnp.zeros(ghost.shape, jnp.float32)
     for c in range(comps):
-        for h in range(2):
-            piece = pl.ds(h * half, half)
-            fb = joined[pl.ds(h * span + c * half, half), :]
-            fa = joined[pl.ds(h * span + ylay.total + c * half, half), :]
-            ghost[pl.ds(h * half * TILE + c, half, stride=TILE), :] = before[piece, :] * fb
-            ghost[pl.ds(h * half * TILE + SIDE + c, half, stride=TILE), :] = after[piece, :] * fa
-            swept, chain = fb, []
-            for y in range(ny):
-                cells = az[c, pl.ds(y * nx + h * half, half), :]
-                swept = (cells + swept) * inv[pl.ds(y * nx + h * half, half), :]
-                chain.append(swept)
-            later = fa
-            for y in reversed(range(ny)):
-                row = pl.ds(y * nx + h * half, half)
-                later = chain[y] + inv[row, :] * later
-                ay[c, pl.ds(h * half * ny + y, half, stride=ny), :] = later * wy[row, :]
+        fb = joined[pl.ds(c * nx, nx), :]
+        fa = joined[pl.ds(ylay.total + c * nx, nx), :]
+        ghost[pl.ds(c, nx, stride=TILE), :] = before[pl.ds(0, nx), :] * fb
+        ghost[pl.ds(SIDE + c, nx, stride=TILE), :] = after[pl.ds(0, nx), :] * fa
+        swept, chain = fb, []
+        for y in range(ny):
+            row = pl.ds(y * nx, nx)
+            swept = (az[c, row, :] + swept) * inv[row, :]
+            chain.append(swept)
+        later = fa
+        for y in reversed(range(ny)):
+            row = pl.ds(y * nx, nx)
+            later = chain[y] + inv[row, :] * later
+            ay[c, pl.ds(y, nx, stride=ny), :] = later * wy[row, :]
 
     def load(i, x):
         return ghost[pl.ds(x * TILE, TILE), :] if i == comps else ay[i, pl.ds(x * ny, ny), :]
@@ -724,19 +699,23 @@
     )(*operands)
 
 
-def exchange(rows, axis, bit):
+def exchange(rows, axis, bit, odd=False):
     count = lax.axis_size(axis)
-    return lax.ppermute(rows, axis, [(i, i ^ (1 << bit)) for i in range(count)])
+    pairs = [(i, i ^ (1 << bit)) for i in range(count)]
+    if odd:
+        pairs = [(i, j) for i, j in pairs if (j if bit == 0 else i) % 2]
+    return lax.ppermute(rows, axis, pairs)
 
 
 class Ladder:
-    def __init__(self, lay, axis, shift, me, send, keep, lead=None):
+    def __init__(self, lay, axis, shift, me, send, keep, lead=None, odd=False):
+        self.odd = odd
         self.lay, self.axis, self.shift, self.me, self.lead = lay, axis, shift, me, lead
         self.levels = (lax.axis_size(axis) - 1).bit_length()
         self.owns, self.gots, self.outgoing = [keep], [], send
 
     def send(self):
-        self.gots.append(exchange(self.outgoing, self.axis, len(self.gots)))
+        self.gots.append(exchange(self.outgoing, self.axis, len(self.gots), self.odd))
 
     def merge(self, beside=(), apart=None):
         level = len(self.owns) - 1
@@ -767,11 +746,10 @@
     comps, nx, ny, nz = cotangent.shape
     shift = (lax.axis_size("gy") - 1).bit_length()
     rows = nx * ny
-    half = nx // 2
     size = comps // 2
     starts = (0, size)
     counts = (size, comps - size)
-    ylays = [Layout([half] * n, 1, 2, half, g == 0) for g, n in enumerate(counts)]
+    ylays = [Layout([nx] * n, 1, 2, nx, g == 0) for g, n in enumerate(counts)]
     xlays = [Layout([ny] * n + [TILE], 2, 1, ny, g == 0) for g, n in enumerate(counts)]
     me = lax.axis_index(("gx", "gy")).astype(jnp.int32).reshape(1)
 
@@ -783,42 +761,42 @@
     cour = courant.reshape(3, rows, nz)
     upw = upwind.reshape(3, rows, nz)
     n = counts[0]
-    keep, send, az, w, left, right, phi, psi, cot_next = call(
+    record, az, w, left, right, phi, psi, cot_next = call(
         functools.partial(lead_z_kernel, (nx, ny), ylays[0]),
         "z_solve_lead",
-        (me, cot, diffusion.reshape(flat), phase.reshape(flat), cour, upw),
-        [(ylays[0].rows, nz)] * 2 + [(n, rows, nz)] + [flat] * 5 + [(counts[1], rows, nz)],
+        (cot, diffusion.reshape(flat), phase.reshape(flat), cour, upw),
+        [(ylays[0].rows, nz), (n, rows, nz)] + [flat] * 5 + [(counts[1], rows, nz)],
         [
             vmem(n, rows, nz), vmem(n, rows, nz), vmem(*flat), vmem(*flat, dtype=jnp.int32),
             vmem(*flat), vmem(*flat, dtype=jnp.int32),
             vmem(*flat), vmem(*flat), vmem(*flat),
             vmem(rows // LANES * 8 * TILE, nz), vmem(rows // LANES * 4 * TILE, nz),
-            vmem(2 * ylays[0].rows, nz),
             pltpu.SemaphoreType.DMA((n,)), pltpu.SemaphoreType.DMA((5,)),
         ],
-        spaces="shhhhh",
+        spaces="hhhhh",
         mebibytes=12,
     )
-    lead = Ladder(ylays[0], "gy", 0, me, send, keep)
+    lead = Ladder(ylays[0], "gy", 0, me, record, record, odd=True)
     lead.send()
     azs = [az]
     n = counts[1]
-    keep, send, az = call(
+    record, az = call(
         functools.partial(next_z_kernel, (nx, ny), ylays[1]),
         "z_solve_next",
-        (me, cot_next, phi, psi, w, left, right),
-        [(ylays[1].rows, nz)] * 2 + [(n, rows, nz)],
-        [vmem(n, rows, nz), vmem(2 * ylays[1].rows, nz)],
+        (cot_next, phi, psi, w, left, right),
+        [(ylays[1].rows, nz), (n, rows, nz)],
+        [vmem(n, rows, nz)],
+        spaces="vvvvvv",
         mebibytes=8,
     )
     azs.append(az)
-    follow = Ladder(ylays[1], "gy", 0, me, send, keep, lead)
+    follow = Ladder(ylays[1], "gy", 0, me, record, record, lead, odd=True)
     follow.send()
-    beside = (send,)
+    beside = (record,)
     for level in range(lead.levels - 1):
         lead.merge(beside)
         lead.send()
-        follow.merge()
+        follow.merge((apart,) if level == 1 else ())
         follow.send()
         beside = (follow.outgoing,)
         if level == 0:
@@ -837,17 +815,18 @@
         answer, passed = call(
             functools.partial(solve_kernel, ylays[g], ylays[0], ladder.levels),
             "y_reduced",
-            (me,) + ladder.records() + (beside + (apart,) if g == 0 else ()),
+            (me,) + ladder.records() + ((follow.gots[-1],) if g == 0 else ()),
             [(ylays[g].answer_rows, nz)] * 2,
         )
         answers.append(answer)
-        mets.append(exchange(passed, "gy", 0))
+        count = lax.axis_size("gy")
+        mets.append(lax.ppermute(passed, "gy", [(i, i - 1) for i in range(1, count, 2)]))
     fields, ghosts, climbs = [], [], []
     for g in range(2):
         common = (me, azs[g], answers[g], mets[g], w, wy, inv, xinv, seam)
         edge = (nx * TILE, nz)
         outs = [(counts[g], rows, nz), edge]
-        scratch = [vmem(counts[g], rows, nz), vmem(2 * ylays[g].answer_rows, nz)]
+        scratch = [vmem(counts[g], rows, nz), vmem(ylays[g].answer_rows, nz)]
         body = functools.partial(y_kernel, (nx, ny), ylays[g], xlays[g])
         if g == 0:
             block, slim, field, ghost, ginv, gseam, gleft, gright, before, after = call(

time: 32.3 us -> 40.7 us (1.26)
  waiting for transfers between devices: 6.42 us -> 12.5 us
  starting transfers between devices: 15.5 us -> 17.9 us
  local copies, waits for them, and re-layouts: 0.5 us -> 0.01 us
    ppermute x13, waiting for transfers between devices: 6.42 us -> 12.5 us  [the longest x2 7.9 us: on_device(): lax.ppermute(passed, 'gy', [(i, i - 1) for i in range(1, count, 2)])]
    ppermute x13, starting transfers between devices: 15.5 us -> 17.9 us  [the longest x11 15.3 us: exchange(): return lax.ppermute(rows, axis, pairs)]
    unnamed x4, local copies, waits for them, and re-layouts: 0.5 us -> 0.01 us
  transfers between devices with their start and end apart: 13 -> 13, of which waited for: 6 -> 5; matrix products, arithmetic and copies ran while one was open for 0% -> 0% of each run, Pallas kernels for 15% -> 12%
where the time goes in v12:
time: 40.7 us; the launch traced here: 40.4 us
  starting transfers between devices  17.9 us (44%)
  waiting for transfers between devices  12.5 us (31%)
  Pallas kernels  9.72 us (24%)
    ppermute x11, starting transfers between devices, exchange(): return lax.ppermute(rows, axis, pairs)  15.3 us
    pallas_call x15, Pallas kernels, call(): pl.pallas_call(kernel, name=name, out_shape=[held[s](shape, jnp.float32)...  9.72 us
    ppermute x2, waiting for transfers between devices, on_device(): lax.ppermute(passed, 'gy', [(i, i - 1) for i in range(1, count, 2)])  7.9 us
    ppermute x11, waiting for transfers between devices, exchange(): return lax.ppermute(rows, axis, pairs)  4.63 us
    ppermute x2, starting transfers between devices, on_device(): lax.ppermute(passed, 'gy', [(i, i - 1) for i in range(1, count, 2)])  2.58 us
  transfers between devices with their start and end apart: 13, of which 5 were waited for; matrix products, arithmetic and copies ran while one was open for 0% of the time, Pallas kernels for 12%

profile of v12, /device:TPU:0, one launch (start us, length us, event | category | flops | bytes accessed | tf_op | source)
XLA Modules:
  0.0 40.4 jit_solution(3194079963160369824)
XLA Ops:
  0.0 3.2 %z_solve_lead.1 = (f32[416,128]{1,0:T(8,128)S(1)}, f32[3,512,128]{2,1,0:T(8,128)S(1)}, f32[512,128]{1,0:T(8,128)S(1)}, f32[512,128]{1,0:T(8,128)S(1)}, f32[512,1...) custom-call(f32[6,512,128]{2,1,0:T(8,128)} %bitcast.11, ...), custom_call_target="tpu_custom_call" | custom-call | flops 1000000000 | bytes 10000000 | tf_op jit(solution)/shard_map/z_solve_lead/pallas_call | solution.py:686
  3.2 2.4 %collective-permute-start.1 = (f32[416,128]{1,0:T(8,128)S(1)}, f32[416,128]{1,0:T(8,128)S(1)}, u32[]{:S(2)}, u32[]{:S(2)}) collective-permute-start(f32[416,128]{1,0:T(8,128)S(1)} %get-tuple-element.59.refs_0_.own.refs_6_), channel_id=1, source_target_pairs={{0,1},{2,3},{4,5},{6,7},{8,9},{10,11},{12,13},{14,15},{16,17},{18,... | collective-permute-start | bytes 638984 | tf_op jit(solution)/shard_map/ppermute | solution.py:707
  5.6 1.1 %z_solve_next.1 = (f32[192,128]{1,0:T(8,128)S(1)}, f32[3,512,128]{2,1,0:T(8,128)S(1)}) custom-call(f32[3,512,128]{2,1,0:T(8,128)S(1)} %get-tuple-element.51.cot, f32[512,128]{1,0:T(8,128)S(1)} %get-tuple-element.52.phi, f32[512,128]{1,0:T(8,128)S(1)} %get-tuple-element.53.psi, f32[512,128]{1,0:T(8,128)S(1)} %get-tuple-element.54.w, ...), custom_call_target="tpu_custom_call" | custom-call | flops 1000000000 | bytes 10000000 | tf_op jit(solution)/shard_map/z_solve_next/pallas_call | solution.py:686
  6.7 1.3 %collective-permute-start = (f32[192,128]{1,0:T(8,128)S(1)}, f32[192,128]{1,0:T(8,128)S(1)}, u32[]{:S(2)}, u32[]{:S(2)}) collective-permute-start(f32[192,128]{1,0:T(8,128)S(1)} %get-tuple-element.58.own.refs_0_), channel_id=1, source_target_pairs={{0,1},{2,3},{4,5},{6,7},{8,9},{10,11},{12,13},{14,15},{16,17},{18,... | collective-permute-start | bytes 294920 | tf_op jit(solution)/shard_map/ppermute | solution.py:707
  8.1 0.8 %collective-permute-start.3 = (f32[416,128]{1,0:T(8,128)S(1)}, f32[416,128]{1,0:T(8,128)S(1)}, u32[]{:S(2)}, u32[]{:S(2)}) collective-permute-start(f32[416,128]{1,0:T(8,128)S(1)} %merge_gy.5.after.refs_0_.own.refs_7_.refs_1_), channel_id=1, source_target_pairs={{1,3},{3,1},{5,7},{7,5},{9,11},{11,9},{13,15},{15,13},{17,19},{19,... | collective-permute-start | bytes 638984 | tf_op jit(solution)/shard_map/ppermute | solution.py:707
  9.0 0.7 %collective-permute-start.2 = (f32[192,128]{1,0:T(8,128)S(1)}, f32[192,128]{1,0:T(8,128)S(1)}, u32[]{:S(2)}, u32[]{:S(2)}) collective-permute-start(f32[192,128]{1,0:T(8,128)S(1)} %merge_gy.4.own.refs_1_), channel_id=1, source_target_pairs={{1,3},{3,1},{5,7},{7,5},{9,11},{11,9},{13,15},{15,13},{17,19},{19,... | collective-permute-start | bytes 294920 | tf_op jit(solution)/shard_map/ppermute | solution.py:707
  10.1 2.5 %collective-permute-start.4 = (f32[80,128]{1,0:T(8,128)S(1)}, f32[80,128]{1,0:T(8,128)S(1)}, u32[]{:S(2)}, u32[]{:S(2)}) collective-permute-start(f32[80,128]{1,0:T(8,128)S(1)} %get-tuple-element.60.refs_0_), channel_id=1, source_target_pairs={{0,8},{8,0},{16,24},{24,16},{1,9},{9,1},{17,25},{25,17},{2,10},{10... | collective-permute-start | bytes 122888 | tf_op jit(solution)/shard_map/ppermute | solution.py:707
  12.6 0.7 %collective-permute-start.6 = (f32[192,128]{1,0:T(8,128)S(1)}, f32[192,128]{1,0:T(8,128)S(1)}, u32[]{:S(2)}, u32[]{:S(2)}) collective-permute-start(f32[192,128]{1,0:T(8,128)S(1)} %get-tuple-element.64), channel_id=1, source_target_pairs={{1,5},{3,7},{5,1},{7,3},{9,13},{11,15},{13,9},{15,11},{17,21},{19,... | collective-permute-start | bytes 294920 | tf_op jit(solution)/shard_map/ppermute | solution.py:707
  13.3 1.2 %collective-permute-done.4.refs_2_.apart = f32[80,128]{1,0:T(8,128)S(1)} collective-permute-done((f32[80,128]{1,0:T(8,128)S(1)}, f32[80,128]{1,0:T(8,128)S(1)}, u32[]{:S(2)}, u32[]{:S(2)}) %collective-permute-start.4) | collective-permute-done | bytes 40992 | tf_op jit(solution)/shard_map/ppermute | solution.py:707
  14.6 0.7 %collective-permute-start.5 = (f32[96,128]{1,0:T(8,128)S(1)}, f32[96,128]{1,0:T(8,128)S(1)}, u32[]{:S(2)}, u32[]{:S(2)}) collective-permute-start(f32[96,128]{1,0:T(8,128)S(1)} %get-tuple-element.62), channel_id=1, source_target_pairs={{1,5},{3,7},{5,1},{7,3},{9,13},{11,15},{13,9},{15,11},{17,21},{19,... | collective-permute-start | bytes 147464 | tf_op jit(solution)/shard_map/ppermute | solution.py:707
  15.4 1.3 %collective-permute-start.8 = (f32[320,128]{1,0:T(8,128)S(1)}, f32[320,128]{1,0:T(8,128)S(1)}, u32[]{:S(2)}, u32[]{:S(2)}) collective-permute-start(f32[320,128]{1,0:T(8,128)S(1)} %get-tuple-element.73), channel_id=1, source_target_pairs={{1,0},{3,2},{5,4},{7,6},{9,8},{11,10},{13,12},{15,14},{17,16},{19,... | collective-permute-start | bytes 491528 | tf_op jit(solution)/shard_map/ppermute | solution.py:823
  16.8 1.3 %collective-permute-start.7 = (f32[192,128]{1,0:T(8,128)S(1)}, f32[192,128]{1,0:T(8,128)S(1)}, u32[]{:S(2)}, u32[]{:S(2)}) collective-permute-start(f32[192,128]{1,0:T(8,128)S(1)} %get-tuple-element.66), channel_id=1, source_target_pairs={{1,0},{3,2},{5,4},{7,6},{9,8},{11,10},{13,12},{15,14},{17,16},{19,... | collective-permute-start | bytes 294920 | tf_op jit(solution)/shard_map/ppermute | solution.py:823
  18.1 7.9 %collective-permute-done.8.got = f32[320,128]{1,0:T(8,128)S(1)} collective-permute-done((f32[320,128]{1,0:T(8,128)S(1)}, f32[320,128]{1,0:T(8,128)S(1)}, u32[]{:S(2)}, u32[]{:S(2)}) %collective-permute-start.8) | collective-permute-done | bytes 163872 | tf_op jit(solution)/shard_map/ppermute | solution.py:823
  26.0 0.8 %y_solve_lead.1 = (f32[200,128]{1,0:T(8,128)S(1)}, f32[120,128]{1,0:T(8,128)S(1)}, f32[3,512,128]{2,1,0:T(8,128)S(1)}, f32[256,128]{1,0:T(8,128)S(1)}, f32[256,1...) custom-call(s32[1]{0:T(128)} %bitcast.me_ref, ...), custom_call_target="tpu_custom_call" | custom-call | flops 1000000000 | bytes 10000000 | tf_op jit(solution)/shard_map/y_solve_lead/pallas_call | solution.py:686
  26.8 1.1 %collective-permute-start.10 = (f32[120,128]{1,0:T(8,128)S(1)}, f32[120,128]{1,0:T(8,128)S(1)}, u32[]{:S(2)}, u32[]{:S(2)}) collective-permute-start(f32[120,128]{1,0:T(8,128)S(1)} %get-tuple-element.82), channel_id=1, source_target_pairs={{0,8},{8,0},{16,24},{24,16},{1,9},{9,1},{17,25},{25,17},{2,10},{10... | collective-permute-start | bytes 184328 | tf_op jit(solution)/shard_map/ppermute | solution.py:707
  28.0 0.8 %y_solve_next.1 = (f32[112,128]{1,0:T(8,128)S(1)}, f32[3,512,128]{2,1,0:T(8,128)S(1)}, f32[256,128]{1,0:T(8,128)S(1)}, f32[256,128]{1,0:T(8,128)S(1)}, f32[256,128]{1,0:T(8,128)S(1)}) custom-call(s32[1]{0:T(128)} %bitcast.me_ref, f32[3,512,128]{2,1,0:T(8,128)S(1)} %get-tuple-element.57.az, f32[192,128]{1,0:T(8,128)S(1)} %get-tuple-element.65.own, ...), custom_call_target="tpu_custom_call" | custom-call | flops 1000000000 | bytes 10000000 | tf_op jit(solution)/shard_map/y_solve_next/pallas_call | solution.py:686
  28.8 1.0 %collective-permute-start.9 = (f32[112,128]{1,0:T(8,128)S(1)}, f32[112,128]{1,0:T(8,128)S(1)}, u32[]{:S(2)}, u32[]{:S(2)}) collective-permute-start(f32[112,128]{1,0:T(8,128)S(1)} %get-tuple-element.80.refs_0_.own), channel_id=1, source_target_pairs={{0,8},{8,0},{16,24},{24,16},{1,9},{9,1},{17,25},{25,17},{2,10},{10... | collective-permute-start | bytes 172040 | tf_op jit(solution)/shard_map/ppermute | solution.py:707
  29.8 1.6 %collective-permute-done.10.slim = f32[120,128]{1,0:T(8,128)S(1)} collective-permute-done((f32[120,128]{1,0:T(8,128)S(1)}, f32[120,128]{1,0:T(8,128)S(1)}, u32[]{:S(2)}, u32[]{:S(2)}) %collective-permute-start.10) | collective-permute-done | bytes 61472 | tf_op jit(solution)/shard_map/ppermute | solution.py:707
  31.4 2.7 %collective-permute-start.12 = (f32[96,128]{1,0:T(8,128)S(1)}, f32[96,128]{1,0:T(8,128)S(1)}, u32[]{:S(2)}, u32[]{:S(2)}) collective-permute-start(f32[96,128]{1,0:T(8,128)S(1)} %get-tuple-element.87), channel_id=1, source_target_pairs={{0,16},{8,24},{16,0},{24,8},{1,17},{9,25},{17,1},{25,9},{2,18},{10... | collective-permute-start | bytes 147464 | tf_op jit(solution)/shard_map/ppermute | solution.py:707
  34.1 1.6 %collective-permute-start.11 = (f32[56,128]{1,0:T(8,128)S(1)}, f32[56,128]{1,0:T(8,128)S(1)}, u32[]{:S(2)}, u32[]{:S(2)}) collective-permute-start(f32[56,128]{1,0:T(8,128)S(1)} %get-tuple-element.85), channel_id=1, source_target_pairs={{0,16},{8,24},{16,0},{24,8},{1,17},{9,25},{17,1},{25,9},{2,18},{10... | collective-permute-start | bytes 86024 | tf_op jit(solution)/shard_map/ppermute | solution.py:707
  35.7 0.8 %collective-permute-done.12.refs_3_.refs_7_ = f32[96,128]{1,0:T(8,128)S(1)} collective-permute-done((f32[96,128]{1,0:T(8,128)S(1)}, f32[96,128]{1,0:T(8,128)S(1)}, u32[]{:S(2)}, u32[]{:S(2)}) %collective-permute-start.12) | collective-permute-done | bytes 49184 | tf_op jit(solution)/shard_map/ppermute | solution.py:707
  36.5 1.5 %x_solve.2.refs_15_ = f32[6,512,128]{2,1,0:T(8,128)} custom-call(s32[1]{0:T(128)} %bitcast.me_ref, f32[200,128]{1,0:T(8,128)S(1)} %get-tuple-element.81.own.refs_0_.refs_4_, f32[200,128]{1,0:T(8,128)S(1)} %get-tuple-element.86.refs_1_.refs_5_, f32[200,128]{1,0:T(8,128)S(1)} %get-tuple-element.83.refs_1_.refs_2_.refs_6_, ...), custom_call_target="tpu_custom_call" | custom-call | flops 1000000000 | bytes 10000000 | tf_op jit(solution)/shard_map/x_solve/pallas_call | solution.py:686
  37.9 1.0 %collective-permute-done.11.refs_3_ = f32[56,128]{1,0:T(8,128)S(1)} collective-permute-done((f32[56,128]{1,0:T(8,128)S(1)}, f32[56,128]{1,0:T(8,128)S(1)}, u32[]{:S(2)}, u32[]{:S(2)}) %collective-permute-start.11) | collective-permute-done | bytes 28704 | tf_op jit(solution)/shard_map/ppermute | solution.py:707
  38.9 1.5 %x_solve.3 = f32[6,512,128]{2,1,0:T(8,128)} custom-call(s32[1]{0:T(128)} %bitcast.me_ref, f32[112,128]{1,0:T(8,128)S(1)} %get-tuple-element.80.refs_0_.own, f32[112,128]{1,0:T(8,128)S(1)} %get-tuple-element.84.refs_1_, f32[112,128]{1,0:T(8,128)S(1)} %collective-permute-done.9.other.refs_2_, ...), custom_call_target="tpu_custom_call", output_to_operand_aliasing={{}: (16, {})} | custom-call | flops 1000000000 | bytes 10000000 | tf_op jit(solution)/shard_map/x_solve/pallas_call | solution.py:686
  (21 shorter events, 0.9 us)
Async XLA Ops:
  3.2 4.8 %collective-permute-start.1 = (f32[416,128]{1,0:T(8,128)S(1)}, f32[416,128]{1,0:T(8,128)S(1)}, u32[]{:S(2)}, u32[]{:S(2)}) collective-permute-start(f32[416,128]{1,0:T(8,128)S(1)} %get-tuple-element.59.refs_0_.own.refs_6_), channel_id=1, source_target_pairs={{0,1},{2,3},{4,5},{6,7},{8,9},{10,11},{12,13},{14,15},{16,17},{18,... | collective-permute-start | bytes 638984 | tf_op jit(solution)/shard_map/ppermute | solution.py:707
  6.7 2.2 %collective-permute-start = (f32[192,128]{1,0:T(8,128)S(1)}, f32[192,128]{1,0:T(8,128)S(1)}, u32[]{:S(2)}, u32[]{:S(2)}) collective-permute-start(f32[192,128]{1,0:T(8,128)S(1)} %get-tuple-element.58.own.refs_0_), channel_id=1, source_target_pairs={{0,1},{2,3},{4,5},{6,7},{8,9},{10,11},{12,13},{14,15},{16,17},{18,... | collective-permute-start | bytes 294920 | tf_op jit(solution)/shard_map/ppermute | solution.py:707
  8.1 1.6 %copy-start = (f32[3,32,16,128]{3,2,1,0:T(8,128)S(1)}, f32[3,32,16,128]{3,2,1,0:T(8,128)}, u32[]{:S(2)}) copy-start(f32[3,32,16,128]{3,2,1,0:T(8,128)} %param.8) | copy-start | bytes 2359300
  8.1 1.6 %copy-start.1 = (s32[3,32,16,128]{3,2,1,0:T(8,128)S(1)}, s32[3,32,16,128]{3,2,1,0:T(8,128)}, u32[]{:S(2)}) copy-start(s32[3,32,16,128]{3,2,1,0:T(8,128)} %param.9) | copy-start | bytes 2359300
  8.1 4.4 %collective-permute-start.3 = (f32[416,128]{1,0:T(8,128)S(1)}, f32[416,128]{1,0:T(8,128)S(1)}, u32[]{:S(2)}, u32[]{:S(2)}) collective-permute-start(f32[416,128]{1,0:T(8,128)S(1)} %merge_gy.5.after.refs_0_.own.refs_7_.refs_1_), channel_id=1, source_target_pairs={{1,3},{3,1},{5,7},{7,5},{9,11},{11,9},{13,15},{15,13},{17,19},{19,... | collective-permute-start | bytes 638984 | tf_op jit(solution)/shard_map/ppermute | solution.py:707
  9.0 5.6 %collective-permute-start.2 = (f32[192,128]{1,0:T(8,128)S(1)}, f32[192,128]{1,0:T(8,128)S(1)}, u32[]{:S(2)}, u32[]{:S(2)}) collective-permute-start(f32[192,128]{1,0:T(8,128)S(1)} %merge_gy.4.own.refs_1_), channel_id=1, source_target_pairs={{1,3},{3,1},{5,7},{7,5},{9,11},{11,9},{13,15},{15,13},{17,19},{19,... | collective-permute-start | bytes 294920 | tf_op jit(solution)/shard_map/ppermute | solution.py:707
  10.1 4.5 %collective-permute-start.4 = (f32[80,128]{1,0:T(8,128)S(1)}, f32[80,128]{1,0:T(8,128)S(1)}, u32[]{:S(2)}, u32[]{:S(2)}) collective-permute-start(f32[80,128]{1,0:T(8,128)S(1)} %get-tuple-element.60.refs_0_), channel_id=1, source_target_pairs={{0,8},{8,0},{16,24},{24,16},{1,9},{9,1},{17,25},{25,17},{2,10},{10... | collective-permute-start | bytes 122888 | tf_op jit(solution)/shard_map/ppermute | solution.py:707
  12.6 2.7 %collective-permute-start.6 = (f32[192,128]{1,0:T(8,128)S(1)}, f32[192,128]{1,0:T(8,128)S(1)}, u32[]{:S(2)}, u32[]{:S(2)}) collective-permute-start(f32[192,128]{1,0:T(8,128)S(1)} %get-tuple-element.64), channel_id=1, source_target_pairs={{1,5},{3,7},{5,1},{7,3},{9,13},{11,15},{13,9},{15,11},{17,21},{19,... | collective-permute-start | bytes 294920 | tf_op jit(solution)/shard_map/ppermute | solution.py:707
  14.6 0.7 %collective-permute-start.5 = (f32[96,128]{1,0:T(8,128)S(1)}, f32[96,128]{1,0:T(8,128)S(1)}, u32[]{:S(2)}, u32[]{:S(2)}) collective-permute-start(f32[96,128]{1,0:T(8,128)S(1)} %get-tuple-element.62), channel_id=1, source_target_pairs={{1,5},{3,7},{5,1},{7,3},{9,13},{11,15},{13,9},{15,11},{17,21},{19,... | collective-permute-start | bytes 147464 | tf_op jit(solution)/shard_map/ppermute | solution.py:707
  15.4 10.6 %collective-permute-start.8 = (f32[320,128]{1,0:T(8,128)S(1)}, f32[320,128]{1,0:T(8,128)S(1)}, u32[]{:S(2)}, u32[]{:S(2)}) collective-permute-start(f32[320,128]{1,0:T(8,128)S(1)} %get-tuple-element.73), channel_id=1, source_target_pairs={{1,0},{3,2},{5,4},{7,6},{9,8},{11,10},{13,12},{15,14},{17,16},{19,... | collective-permute-start | bytes 491528 | tf_op jit(solution)/shard_map/ppermute | solution.py:823
  16.8 11.2 %collective-permute-start.7 = (f32[192,128]{1,0:T(8,128)S(1)}, f32[192,128]{1,0:T(8,128)S(1)}, u32[]{:S(2)}, u32[]{:S(2)}) collective-permute-start(f32[192,128]{1,0:T(8,128)S(1)} %get-tuple-element.66), channel_id=1, source_target_pairs={{1,0},{3,2},{5,4},{7,6},{9,8},{11,10},{13,12},{15,14},{17,16},{19,... | collective-permute-start | bytes 294920 | tf_op jit(solution)/shard_map/ppermute | solution.py:823
  26.8 4.5 %collective-permute-start.10 = (f32[120,128]{1,0:T(8,128)S(1)}, f32[120,128]{1,0:T(8,128)S(1)}, u32[]{:S(2)}, u32[]{:S(2)}) collective-permute-start(f32[120,128]{1,0:T(8,128)S(1)} %get-tuple-element.82), channel_id=1, source_target_pairs={{0,8},{8,0},{16,24},{24,16},{1,9},{9,1},{17,25},{25,17},{2,10},{10... | collective-permute-start | bytes 184328 | tf_op jit(solution)/shard_map/ppermute | solution.py:707
  28.8 5.3 %collective-permute-start.9 = (f32[112,128]{1,0:T(8,128)S(1)}, f32[112,128]{1,0:T(8,128)S(1)}, u32[]{:S(2)}, u32[]{:S(2)}) collective-permute-start(f32[112,128]{1,0:T(8,128)S(1)} %get-tuple-element.80.refs_0_.own), channel_id=1, source_target_pairs={{0,8},{8,0},{16,24},{24,16},{1,9},{9,1},{17,25},{25,17},{2,10},{10... | collective-permute-start | bytes 172040 | tf_op jit(solution)/shard_map/ppermute | solution.py:707
  31.4 5.1 %collective-permute-start.12 = (f32[96,128]{1,0:T(8,128)S(1)}, f32[96,128]{1,0:T(8,128)S(1)}, u32[]{:S(2)}, u32[]{:S(2)}) collective-permute-start(f32[96,128]{1,0:T(8,128)S(1)} %get-tuple-element.87), channel_id=1, source_target_pairs={{0,16},{8,24},{16,0},{24,8},{1,17},{9,25},{17,1},{25,9},{2,18},{10... | collective-permute-start | bytes 147464 | tf_op jit(solution)/shard_map/ppermute | solution.py:707
  34.1 4.8 %collective-permute-start.11 = (f32[56,128]{1,0:T(8,128)S(1)}, f32[56,128]{1,0:T(8,128)S(1)}, u32[]{:S(2)}, u32[]{:S(2)}) collective-permute-start(f32[56,128]{1,0:T(8,128)S(1)} %get-tuple-element.85), channel_id=1, source_target_pairs={{0,16},{8,24},{16,0},{24,8},{1,17},{9,25},{17,1},{25,9},{2,18},{10... | collective-permute-start | bytes 86024 | tf_op jit(solution)/shard_map/ppermute | solution.py:707

commit v13 on v11

--- a/solution.py
+++ b/solution.py
@@ -286,16 +286,18 @@
     return chain, backs, 1.0 / value
 
 
-def post(lay, both, row, cells):
+def post(mine, keep, send, row, cells):
     half = cells.shape[0] // 2
-    for h in range(2):
-        both[pl.ds(h * lay.rows + row, half), :] = cells[h * half : (h + 1) * half]
-
-
-def z_part(dims, lay, me_ref, cot, phi, psi, w, left, right, arrived, turned, az, both, keep, send):
+    low, high = cells[:half], cells[half:]
+    keep[pl.ds(row, half), :] = pick(mine, low, high)
+    send[pl.ds(row, half), :] = pick(mine, high, low)
+
+
+def z_part(dims, lay, me_ref, cot, phi, psi, w, left, right, arrived, turned, az, keep, send):
     nx, ny = dims
     tiles = nx * ny // LANES
     sums = sum_matrix()
+    mine = me_ref[0] & 1
     for c in range(len(lay.sizes)):
         arrived(c)
         for t in range(tiles):
@@ -315,11 +317,8 @@
             turned[c, span, :] = cells
             first = first + left[span, :] * cells
             last = last + right[span, :] * cells
-        post(lay, both, lay.offsets[c], first)
-        post(lay, both, lay.total + lay.offsets[c], last)
-    mine = me_ref[0] & 1
-    keep[...] = both[pl.ds(pl.multiple_of(mine * lay.rows, TILE), lay.rows), :]
-    send[...] = both[pl.ds(pl.multiple_of((1 - mine) * lay.rows, TILE), lay.rows), :]
+        post(mine, keep, send, lay.offsets[c], first)
+        post(mine, keep, send, lay.total + lay.offsets[c], last)
 
 
 def carried(maps, state):
@@ -368,7 +367,7 @@
 def lead_z_kernel(
     dims, lay, me_ref, cot_any, diff_any, phase_any, cour_any, upw_any,
     keep, send, turned, w, left, right, phi, psi, later,
-    az, cot, diff, phase, cour, upw, wt, pht, pst, maps, ends, both, in_sems, sems,
+    az, cot, diff, phase, cour, upw, wt, pht, pst, maps, ends, in_sems, sems,
 ):
     nx, ny = dims
     tiles = nx * ny // LANES
@@ -399,9 +398,10 @@
         span = pl.ds(y * nx, nx)
         left[span, :] = backs[y] * total
         right[span, :] = chain[y] * total
-    post(lay, both, lay.couple, backs[0] * total)
-    post(lay, both, lay.couple + half, total)
-    post(lay, both, lay.couple + 2 * half, chain[ny - 1] * total)
+    mine = me_ref[0] & 1
+    post(mine, keep, send, lay.couple, backs[0] * total)
+    post(mine, keep, send, lay.couple + half, total)
+    post(mine, keep, send, lay.couple + 2 * half, chain[ny - 1] * total)
     for i, (source, target) in enumerate(small[2:]):
         pltpu.make_async_copy(source, target, sems.at[2 + i]).wait()
     for e, y in enumerate((0, ny - 1)):
@@ -409,19 +409,19 @@
         weight = w[edge, :]
         up = cour[edge, :] * upw[edge, :].astype(jnp.float32)
         flow = up if e == 0 else cour[edge, :] - up
-        post(lay, both, lay.edge + 2 * e * half, weight)
-        post(lay, both, lay.edge + (2 * e + 1) * half, weight * flow)
+        post(mine, keep, send, lay.edge + 2 * e * half, weight)
+        post(mine, keep, send, lay.edge + (2 * e + 1) * half, weight * flow)
 
     def arrived(c):
         pltpu.make_async_copy(cot_any.at[c], cot.at[c], in_sems.at[c]).wait()
 
-    z_part(dims, lay, me_ref, cot, phi, psi, w, left, right, arrived, turned, az, both, keep, send)
+    z_part(dims, lay, me_ref, cot, phi, psi, w, left, right, arrived, turned, az, keep, send)
     ahead.wait()
 
 
-def next_z_kernel(dims, lay, me_ref, cot, phi, psi, w, left, right, keep, send, turned, az, both):
+def next_z_kernel(dims, lay, me_ref, cot, phi, psi, w, left, right, keep, send, turned, az):
     z_part(
-        dims, lay, me_ref, cot, phi, psi, w, left, right, lambda c: None, turned, az, both, keep, send
+        dims, lay, me_ref, cot, phi, psi, w, left, right, lambda c: None, turned, az, keep, send
     )
 
 
@@ -793,7 +793,6 @@
             vmem(*flat), vmem(*flat, dtype=jnp.int32),
             vmem(*flat), vmem(*flat), vmem(*flat),
             vmem(rows // LANES * 8 * TILE, nz), vmem(rows // LANES * 4 * TILE, nz),
-            vmem(2 * ylays[0].rows, nz),
             pltpu.SemaphoreType.DMA((n,)), pltpu.SemaphoreType.DMA((5,)),
         ],
         spaces="shhhhh",
@@ -808,7 +807,7 @@
         "z_solve_next",
         (me, cot_next, phi, psi, w, left, right),
         [(ylays[1].rows, nz)] * 2 + [(n, rows, nz)],
-        [vmem(n, rows, nz), vmem(2 * ylays[1].rows, nz)],
+        [vmem(n, rows, nz)],
         mebibytes=8,
     )
     azs.append(az)

time: 32.3 us -> 32.3 us (level)
  no operation moved by 1% of the time
where the time goes in v13:
time: 32.3 us; the launch traced here: 32.1 us
  starting transfers between devices  15.5 us (48%)
  Pallas kernels  9.58 us (30%)
  waiting for transfers between devices  6.44 us (20%)
  local copies, waits for them, and re-layouts  0.5 us (2%)
    ppermute x13, starting transfers between devices, exchange(): return lax.ppermute(rows, axis, [(i, i ^ 1 << bit) for i in range(count)])  15.5 us
    pallas_call x15, Pallas kernels, call(): pl.pallas_call(kernel, name=name, out_shape=[held[s](shape, jnp.float32)...  9.58 us
    ppermute x13, waiting for transfers between devices, exchange(): return lax.ppermute(rows, axis, [(i, i ^ 1 << bit) for i in range(count)])  6.44 us
  transfers between devices with their start and end apart: 13, of which 6 were waited for; matrix products, arithmetic and copies ran while one was open for 0% of the time, Pallas kernels for 15%

profile of v13, /device:TPU:0, one launch (start us, length us, event | category | flops | bytes accessed | tf_op | source)
XLA Modules:
  0.0 32.1 jit_solution(3575558151346552019)
XLA Ops:
  0.0 3.4 %z_solve_lead.1 = (f32[208,128]{1,0:T(8,128)S(1)}, f32[208,128]{1,0:T(8,128)S(1)}, f32[3,512,128]{2,1,0:T(8,128)S(1)}, f32[512,128]{1,0:T(8,128)S(1)}, f32[512,1...) custom-call(s32[1]{0:T(128)} %bitcast.me_ref, ...), custom_call_target="tpu_custom_call" | custom-call | flops 1000000000 | bytes 10000000 | tf_op jit(solution)/shard_map/z_solve_lead/pallas_call | solution.py:711
  3.4 0.5 %collective-permute-start.1 = (f32[208,128]{1,0:T(8,128)S(1)}, f32[208,128]{1,0:T(8,128)S(1)}, u32[]{:S(2)}, u32[]{:S(2)}) collective-permute-start(f32[208,128]{1,0:T(8,128)S(1)} %get-tuple-element.63), channel_id=1, source_target_pairs={{0,1},{1,0},{2,3},{3,2},{4,5},{5,4},{6,7},{7,6},{8,9},{9,8},{10,11... | collective-permute-start | bytes 319496 | tf_op jit(solution)/shard_map/ppermute | solution.py:729
  3.9 1.2 %z_solve_next.1 = (f32[96,128]{1,0:T(8,128)S(1)}, f32[96,128]{1,0:T(8,128)S(1)}, f32[3,512,128]{2,1,0:T(8,128)S(1)}) custom-call(s32[1]{0:T(128)} %bitcast.me_ref, f32[3,512,128]{2,1,0:T(8,128)S(1)} %get-tuple-element.53.cot, f32[512,128]{1,0:T(8,128)S(1)} %get-tuple-element.54.phi, f32[512,128]{1,0:T(8,128)S(1)} %get-tuple-element.55.psi, ...), custom_call_target="tpu_custom_call" | custom-call | flops 1000000000 | bytes 10000000 | tf_op jit(solution)/shard_map/z_solve_next/pallas_call | solution.py:711
  5.2 3.0 %collective-permute-start.3 = (f32[208,128]{1,0:T(8,128)S(1)}, f32[208,128]{1,0:T(8,128)S(1)}, u32[]{:S(2)}, u32[]{:S(2)}) collective-permute-start(f32[208,128]{1,0:T(8,128)S(1)} %merge_gy.5.refs_0_.after.own.refs_7_.refs_1_), channel_id=1, source_target_pairs={{0,2},{1,3},{2,0},{3,1},{4,6},{5,7},{6,4},{7,5},{8,10},{9,11},{10,... | collective-permute-start | bytes 319496 | tf_op jit(solution)/shard_map/ppermute | solution.py:729
  8.3 0.8 %collective-permute-start.2 = (f32[96,128]{1,0:T(8,128)S(1)}, f32[96,128]{1,0:T(8,128)S(1)}, u32[]{:S(2)}, u32[]{:S(2)}) collective-permute-start(f32[96,128]{1,0:T(8,128)S(1)} %merge_gy.4.own.refs_1_), channel_id=1, source_target_pairs={{0,2},{1,3},{2,0},{3,1},{4,6},{5,7},{6,4},{7,5},{8,10},{9,11},{10,... | collective-permute-start | bytes 147464 | tf_op jit(solution)/shard_map/ppermute | solution.py:729
  9.1 0.3 copy-done
  9.6 0.4 %x_coefficients.1 = (f32[80,128]{1,0:T(8,128)S(1)}, f32[512,128]{1,0:T(8,128)S(1)}, f32[512,128]{1,0:T(8,128)S(1)}, f32[512,128]{1,0:T(8,128)S(1)}, f32[16,128]{...) custom-call(f32[512,128]{1,0:T(8,128)S(1)} %get-tuple-element.56.w, ...), custom_call_target="tpu_custom_call" | custom-call | flops 1000000000 | bytes 10000000 | tf_op jit(solution)/shard_map/x_coefficients/pallas_call | solution.py:711
  10.0 1.6 %collective-permute-start.7 = (f32[80,128]{1,0:T(8,128)S(1)}, f32[80,128]{1,0:T(8,128)S(1)}, u32[]{:S(2)}, u32[]{:S(2)}) collective-permute-start(f32[80,128]{1,0:T(8,128)S(1)} %get-tuple-element.66.refs_0_), channel_id=1, source_target_pairs={{0,8},{8,0},{16,24},{24,16},{1,9},{9,1},{17,25},{25,17},{2,10},{10... | collective-permute-start | bytes 122888 | tf_op jit(solution)/shard_map/ppermute | solution.py:729
  11.7 0.3 collective-permute-done.3.refs_1_.other.refs_10_.refs_4_
  12.0 1.8 %collective-permute-start.5 = (f32[96,128]{1,0:T(8,128)S(1)}, f32[96,128]{1,0:T(8,128)S(1)}, u32[]{:S(2)}, u32[]{:S(2)}) collective-permute-start(f32[96,128]{1,0:T(8,128)S(1)} %get-tuple-element.68), channel_id=1, source_target_pairs={{0,4},{1,5},{2,6},{3,7},{4,0},{5,1},{6,2},{7,3},{8,12},{9,13},{10,... | collective-permute-start | bytes 147464 | tf_op jit(solution)/shard_map/ppermute | solution.py:729
  13.8 0.5 %collective-permute-start.4 = (f32[48,128]{1,0:T(8,128)S(1)}, f32[48,128]{1,0:T(8,128)S(1)}, u32[]{:S(2)}, u32[]{:S(2)}) collective-permute-start(f32[48,128]{1,0:T(8,128)S(1)} %get-tuple-element.65.refs_6_), channel_id=1, source_target_pairs={{0,4},{1,5},{2,6},{3,7},{4,0},{5,1},{6,2},{7,3},{8,12},{9,13},{10,... | collective-permute-start | bytes 73736 | tf_op jit(solution)/shard_map/ppermute | solution.py:729
  14.3 1.8 %collective-permute-done.5.refs_11_.refs_5_ = f32[96,128]{1,0:T(8,128)S(1)} collective-permute-done((f32[96,128]{1,0:T(8,128)S(1)}, f32[96,128]{1,0:T(8,128)S(1)}, u32[]{:S(2)}, u32[]{:S(2)}) %collective-permute-start.5) | collective-permute-done | bytes 49184 | tf_op jit(solution)/shard_map/ppermute | solution.py:729
  16.3 1.5 %collective-permute-done.4.refs_5_ = f32[48,128]{1,0:T(8,128)S(1)} collective-permute-done((f32[48,128]{1,0:T(8,128)S(1)}, f32[48,128]{1,0:T(8,128)S(1)}, u32[]{:S(2)}, u32[]{:S(2)}) %collective-permute-start.4) | collective-permute-done | bytes 24608 | tf_op jit(solution)/shard_map/ppermute | solution.py:729
  17.9 0.7 %y_solve_lead.1 = (f32[200,128]{1,0:T(8,128)S(1)}, f32[120,128]{1,0:T(8,128)S(1)}, f32[3,512,128]{2,1,0:T(8,128)S(1)}, f32[256,128]{1,0:T(8,128)S(1)}, f32[256,1...) custom-call(s32[1]{0:T(128)} %bitcast.me_ref, ...), custom_call_target="tpu_custom_call" | custom-call | flops 1000000000 | bytes 10000000 | tf_op jit(solution)/shard_map/y_solve_lead/pallas_call | solution.py:711
  18.6 1.6 %collective-permute-start.10 = (f32[120,128]{1,0:T(8,128)S(1)}, f32[120,128]{1,0:T(8,128)S(1)}, u32[]{:S(2)}, u32[]{:S(2)}) collective-permute-start(f32[120,128]{1,0:T(8,128)S(1)} %get-tuple-element.86), channel_id=1, source_target_pairs={{0,8},{8,0},{16,24},{24,16},{1,9},{9,1},{17,25},{25,17},{2,10},{10... | collective-permute-start | bytes 184328 | tf_op jit(solution)/shard_map/ppermute | solution.py:729
  20.2 0.7 %y_solve_next.1 = (f32[112,128]{1,0:T(8,128)S(1)}, f32[3,512,128]{2,1,0:T(8,128)S(1)}, f32[256,128]{1,0:T(8,128)S(1)}, f32[256,128]{1,0:T(8,128)S(1)}, f32[256,128]{1,0:T(8,128)S(1)}) custom-call(s32[1]{0:T(128)} %bitcast.me_ref, f32[3,512,128]{2,1,0:T(8,128)S(1)} %get-tuple-element.59.az, f32[96,128]{1,0:T(8,128)S(1)} %get-tuple-element.69.own, ...), custom_call_target="tpu_custom_call" | custom-call | flops 1000000000 | bytes 10000000 | tf_op jit(solution)/shard_map/y_solve_next/pallas_call | solution.py:711
  20.9 0.5 %collective-permute-start.9 = (f32[112,128]{1,0:T(8,128)S(1)}, f32[112,128]{1,0:T(8,128)S(1)}, u32[]{:S(2)}, u32[]{:S(2)}) collective-permute-start(f32[112,128]{1,0:T(8,128)S(1)} %get-tuple-element.84.refs_0_.own), channel_id=1, source_target_pairs={{0,8},{8,0},{16,24},{24,16},{1,9},{9,1},{17,25},{25,17},{2,10},{10... | collective-permute-start | bytes 172040 | tf_op jit(solution)/shard_map/ppermute | solution.py:729
  21.5 1.6 %collective-permute-done.10.slim = f32[120,128]{1,0:T(8,128)S(1)} collective-permute-done((f32[120,128]{1,0:T(8,128)S(1)}, f32[120,128]{1,0:T(8,128)S(1)}, u32[]{:S(2)}, u32[]{:S(2)}) %collective-permute-start.10) | collective-permute-done | bytes 61472 | tf_op jit(solution)/shard_map/ppermute | solution.py:729
  23.1 2.7 %collective-permute-start.12 = (f32[96,128]{1,0:T(8,128)S(1)}, f32[96,128]{1,0:T(8,128)S(1)}, u32[]{:S(2)}, u32[]{:S(2)}) collective-permute-start(f32[96,128]{1,0:T(8,128)S(1)} %get-tuple-element.91), channel_id=1, source_target_pairs={{0,16},{8,24},{16,0},{24,8},{1,17},{9,25},{17,1},{25,9},{2,18},{10... | collective-permute-start | bytes 147464 | tf_op jit(solution)/shard_map/ppermute | solution.py:729
  25.8 2.1 %collective-permute-start.11 = (f32[56,128]{1,0:T(8,128)S(1)}, f32[56,128]{1,0:T(8,128)S(1)}, u32[]{:S(2)}, u32[]{:S(2)}) collective-permute-start(f32[56,128]{1,0:T(8,128)S(1)} %get-tuple-element.89), channel_id=1, source_target_pairs={{0,16},{8,24},{16,0},{24,8},{1,17},{9,25},{17,1},{25,9},{2,18},{10... | collective-permute-start | bytes 86024 | tf_op jit(solution)/shard_map/ppermute | solution.py:729
  27.9 0.6 %collective-permute-done.12.refs_3_.refs_7_ = f32[96,128]{1,0:T(8,128)S(1)} collective-permute-done((f32[96,128]{1,0:T(8,128)S(1)}, f32[96,128]{1,0:T(8,128)S(1)}, u32[]{:S(2)}, u32[]{:S(2)}) %collective-permute-start.12) | collective-permute-done | bytes 49184 | tf_op jit(solution)/shard_map/ppermute | solution.py:729
  28.4 1.5 %x_solve.2.refs_15_ = f32[6,512,128]{2,1,0:T(8,128)} custom-call(s32[1]{0:T(128)} %bitcast.me_ref, f32[200,128]{1,0:T(8,128)S(1)} %get-tuple-element.85.own.refs_0_.refs_4_, f32[200,128]{1,0:T(8,128)S(1)} %get-tuple-element.90.refs_1_.refs_5_, f32[200,128]{1,0:T(8,128)S(1)} %get-tuple-element.87.refs_1_.refs_2_.refs_6_, ...), custom_call_target="tpu_custom_call" | custom-call | flops 1000000000 | bytes 10000000 | tf_op jit(solution)/shard_map/x_solve/pallas_call | solution.py:711
  29.9 0.7 %collective-permute-done.11.refs_3_ = f32[56,128]{1,0:T(8,128)S(1)} collective-permute-done((f32[56,128]{1,0:T(8,128)S(1)}, f32[56,128]{1,0:T(8,128)S(1)}, u32[]{:S(2)}, u32[]{:S(2)}) %collective-permute-start.11) | collective-permute-done | bytes 28704 | tf_op jit(solution)/shard_map/ppermute | solution.py:729
  30.6 1.5 %x_solve.3 = f32[6,512,128]{2,1,0:T(8,128)} custom-call(s32[1]{0:T(128)} %bitcast.me_ref, f32[112,128]{1,0:T(8,128)S(1)} %get-tuple-element.84.refs_0_.own, f32[112,128]{1,0:T(8,128)S(1)} %get-tuple-element.88.refs_1_, f32[112,128]{1,0:T(8,128)S(1)} %collective-permute-done.9.other.refs_2_, ...), custom_call_target="tpu_custom_call", output_to_operand_aliasing={{}: (16, {})} | custom-call | flops 1000000000 | bytes 10000000 | tf_op jit(solution)/shard_map/x_solve/pallas_call | solution.py:711
  (21 shorter events, 0.8 us)
Async XLA Ops:
  3.4 1.8 %collective-permute-start.1 = (f32[208,128]{1,0:T(8,128)S(1)}, f32[208,128]{1,0:T(8,128)S(1)}, u32[]{:S(2)}, u32[]{:S(2)}) collective-permute-start(f32[208,128]{1,0:T(8,128)S(1)} %get-tuple-element.63), channel_id=1, source_target_pairs={{0,1},{1,0},{2,3},{3,2},{4,5},{5,4},{6,7},{7,6},{8,9},{9,8},{10,11... | collective-permute-start | bytes 319496 | tf_op jit(solution)/shard_map/ppermute | solution.py:729
  5.1 3.2 %collective-permute-start = (f32[96,128]{1,0:T(8,128)S(1)}, f32[96,128]{1,0:T(8,128)S(1)}, u32[]{:S(2)}, u32[]{:S(2)}) collective-permute-start(f32[96,128]{1,0:T(8,128)S(1)} %get-tuple-element.61.refs_0_), channel_id=1, source_target_pairs={{0,1},{1,0},{2,3},{3,2},{4,5},{5,4},{6,7},{7,6},{8,9},{9,8},{10,11... | collective-permute-start | bytes 147464 | tf_op jit(solution)/shard_map/ppermute | solution.py:729
  5.2 6.7 %collective-permute-start.3 = (f32[208,128]{1,0:T(8,128)S(1)}, f32[208,128]{1,0:T(8,128)S(1)}, u32[]{:S(2)}, u32[]{:S(2)}) collective-permute-start(f32[208,128]{1,0:T(8,128)S(1)} %merge_gy.5.refs_0_.after.own.refs_7_.refs_1_), channel_id=1, source_target_pairs={{0,2},{1,3},{2,0},{3,1},{4,6},{5,7},{6,4},{7,5},{8,10},{9,11},{10,... | collective-permute-start | bytes 319496 | tf_op jit(solution)/shard_map/ppermute | solution.py:729
  8.2 1.1 %copy-start = (f32[3,32,16,128]{3,2,1,0:T(8,128)S(1)}, f32[3,32,16,128]{3,2,1,0:T(8,128)}, u32[]{:S(2)}) copy-start(f32[3,32,16,128]{3,2,1,0:T(8,128)} %param.8) | copy-start | bytes 2359300
  8.2 1.4 %copy-start.1 = (s32[3,32,16,128]{3,2,1,0:T(8,128)S(1)}, s32[3,32,16,128]{3,2,1,0:T(8,128)}, u32[]{:S(2)}) copy-start(s32[3,32,16,128]{3,2,1,0:T(8,128)} %param.9) | copy-start | bytes 2359300
  8.3 5.5 %collective-permute-start.2 = (f32[96,128]{1,0:T(8,128)S(1)}, f32[96,128]{1,0:T(8,128)S(1)}, u32[]{:S(2)}, u32[]{:S(2)}) collective-permute-start(f32[96,128]{1,0:T(8,128)S(1)} %merge_gy.4.own.refs_1_), channel_id=1, source_target_pairs={{0,2},{1,3},{2,0},{3,1},{4,6},{5,7},{6,4},{7,5},{8,10},{9,11},{10,... | collective-permute-start | bytes 147464 | tf_op jit(solution)/shard_map/ppermute | solution.py:729
  10.0 4.3 %collective-permute-start.7 = (f32[80,128]{1,0:T(8,128)S(1)}, f32[80,128]{1,0:T(8,128)S(1)}, u32[]{:S(2)}, u32[]{:S(2)}) collective-permute-start(f32[80,128]{1,0:T(8,128)S(1)} %get-tuple-element.66.refs_0_), channel_id=1, source_target_pairs={{0,8},{8,0},{16,24},{24,16},{1,9},{9,1},{17,25},{25,17},{2,10},{10... | collective-permute-start | bytes 122888 | tf_op jit(solution)/shard_map/ppermute | solution.py:729
  12.0 4.2 %collective-permute-start.5 = (f32[96,128]{1,0:T(8,128)S(1)}, f32[96,128]{1,0:T(8,128)S(1)}, u32[]{:S(2)}, u32[]{:S(2)}) collective-permute-start(f32[96,128]{1,0:T(8,128)S(1)} %get-tuple-element.68), channel_id=1, source_target_pairs={{0,4},{1,5},{2,6},{3,7},{4,0},{5,1},{6,2},{7,3},{8,12},{9,13},{10,... | collective-permute-start | bytes 147464 | tf_op jit(solution)/shard_map/ppermute | solution.py:729
  13.8 3.9 %collective-permute-start.4 = (f32[48,128]{1,0:T(8,128)S(1)}, f32[48,128]{1,0:T(8,128)S(1)}, u32[]{:S(2)}, u32[]{:S(2)}) collective-permute-start(f32[48,128]{1,0:T(8,128)S(1)} %get-tuple-element.65.refs_6_), channel_id=1, source_target_pairs={{0,4},{1,5},{2,6},{3,7},{4,0},{5,1},{6,2},{7,3},{8,12},{9,13},{10,... | collective-permute-start | bytes 73736 | tf_op jit(solution)/shard_map/ppermute | solution.py:729
  16.2 1.7 %collective-permute-start.8 = (f32[160,128]{1,0:T(8,128)S(1)}, f32[160,128]{1,0:T(8,128)S(1)}, u32[]{:S(2)}, u32[]{:S(2)}) collective-permute-start(f32[160,128]{1,0:T(8,128)S(1)} %get-tuple-element.77), channel_id=1, source_target_pairs={{0,1},{1,0},{2,3},{3,2},{4,5},{5,4},{6,7},{7,6},{8,9},{9,8},{10,11... | collective-permute-start | bytes 245768 | tf_op jit(solution)/shard_map/ppermute | solution.py:729
  17.8 2.5 %collective-permute-start.6 = (f32[96,128]{1,0:T(8,128)S(1)}, f32[96,128]{1,0:T(8,128)S(1)}, u32[]{:S(2)}, u32[]{:S(2)}) collective-permute-start(f32[96,128]{1,0:T(8,128)S(1)} %get-tuple-element.70), channel_id=1, source_target_pairs={{0,1},{1,0},{2,3},{3,2},{4,5},{5,4},{6,7},{7,6},{8,9},{9,8},{10,11... | collective-permute-start | bytes 147464 | tf_op jit(solution)/shard_map/ppermute | solution.py:729
  18.6 4.5 %collective-permute-start.10 = (f32[120,128]{1,0:T(8,128)S(1)}, f32[120,128]{1,0:T(8,128)S(1)}, u32[]{:S(2)}, u32[]{:S(2)}) collective-permute-start(f32[120,128]{1,0:T(8,128)S(1)} %get-tuple-element.86), channel_id=1, source_target_pairs={{0,8},{8,0},{16,24},{24,16},{1,9},{9,1},{17,25},{25,17},{2,10},{10... | collective-permute-start | bytes 184328 | tf_op jit(solution)/shard_map/ppermute | solution.py:729
  20.9 4.8 %collective-permute-start.9 = (f32[112,128]{1,0:T(8,128)S(1)}, f32[112,128]{1,0:T(8,128)S(1)}, u32[]{:S(2)}, u32[]{:S(2)}) collective-permute-start(f32[112,128]{1,0:T(8,128)S(1)} %get-tuple-element.84.refs_0_.own), channel_id=1, source_target_pairs={{0,8},{8,0},{16,24},{24,16},{1,9},{9,1},{17,25},{25,17},{2,10},{10... | collective-permute-start | bytes 172040 | tf_op jit(solution)/shard_map/ppermute | solution.py:729
  23.1 5.3 %collective-permute-start.12 = (f32[96,128]{1,0:T(8,128)S(1)}, f32[96,128]{1,0:T(8,128)S(1)}, u32[]{:S(2)}, u32[]{:S(2)}) collective-permute-start(f32[96,128]{1,0:T(8,128)S(1)} %get-tuple-element.91), channel_id=1, source_target_pairs={{0,16},{8,24},{16,0},{24,8},{1,17},{9,25},{17,1},{25,9},{2,18},{10... | collective-permute-start | bytes 147464 | tf_op jit(solution)/shard_map/ppermute | solution.py:729
  25.8 4.8 %collective-permute-start.11 = (f32[56,128]{1,0:T(8,128)S(1)}, f32[56,128]{1,0:T(8,128)S(1)}, u32[]{:S(2)}, u32[]{:S(2)}) collective-permute-start(f32[56,128]{1,0:T(8,128)S(1)} %get-tuple-element.89), channel_id=1, source_target_pairs={{0,16},{8,24},{16,0},{24,8},{1,17},{9,25},{17,1},{25,9},{2,18},{10... | collective-permute-start | bytes 86024 | tf_op jit(solution)/shard_map/ppermute | solution.py:729

commit v14 on v13

--- a/solution.py
+++ b/solution.py
@@ -768,7 +768,7 @@
     shift = (lax.axis_size("gy") - 1).bit_length()
     rows = nx * ny
     half = nx // 2
-    size = comps // 2
+    size = comps // 3
     starts = (0, size)
     counts = (size, comps - size)
     ylays = [Layout([half] * n, 1, 2, half, g == 0) for g, n in enumerate(counts)]
@@ -817,7 +817,7 @@
     for level in range(lead.levels - 1):
         lead.merge(beside)
         lead.send()
-        follow.merge()
+        follow.merge((lead.outgoing,))
         follow.send()
         beside = (follow.outgoing,)
         if level == 0:

time: 32.3 us -> 32 us (level)
  waiting for transfers between devices: 6.44 us -> 4.8 us
  starting transfers between devices: 15.5 us -> 17.1 us
    ppermute x13, waiting for transfers between devices: 6.44 us -> 4.8 us  [exchange(): return lax.ppermute(rows, axis, [(i, i ^ 1 << bit) for i in range(count)])]
    ppermute x13, starting transfers between devices: 15.5 us -> 17.1 us  [exchange(): return lax.ppermute(rows, axis, [(i, i ^ 1 << bit) for i in range(count)])]
  transfers between devices with their start and end apart: 13 -> 13, of which waited for: 6 -> 5; matrix products, arithmetic and copies ran while one was open for 0% -> 0% of each run, Pallas kernels for 15% -> 15%
where the time goes in v14:
time: 32 us; the launch traced here: 31.9 us
  starting transfers between devices  17.1 us (53%)
  Pallas kernels  9.41 us (29%)
  waiting for transfers between devices  4.8 us (15%)
  local copies, waits for them, and re-layouts  0.47 us (1%)
    ppermute x13, starting transfers between devices, exchange(): return lax.ppermute(rows, axis, [(i, i ^ 1 << bit) for i in range(count)])  17.1 us
    pallas_call x15, Pallas kernels, call(): pl.pallas_call(kernel, name=name, out_shape=[held[s](shape, jnp.float32)...  9.41 us
    ppermute x13, waiting for transfers between devices, exchange(): return lax.ppermute(rows, axis, [(i, i ^ 1 << bit) for i in range(count)])  4.8 us
  transfers between devices with their start and end apart: 13, of which 5 were waited for; matrix products, arithmetic and copies ran while one was open for 0% of the time, Pallas kernels for 15%

profile of v14, /device:TPU:0, one launch (start us, length us, event | category | flops | bytes accessed | tf_op | source)
XLA Modules:
  0.0 31.9 jit_solution(12004387089604644101)
XLA Ops:
  0.0 2.9 %z_solve_lead.1 = (f32[176,128]{1,0:T(8,128)S(1)}, f32[176,128]{1,0:T(8,128)S(1)}, f32[2,512,128]{2,1,0:T(8,128)S(1)}, f32[512,128]{1,0:T(8,128)S(1)}, f32[512,1...) custom-call(s32[1]{0:T(128)} %bitcast.me_ref, ...), custom_call_target="tpu_custom_call" | custom-call | flops 1000000000 | bytes 10000000 | tf_op jit(solution)/shard_map/z_solve_lead/pallas_call | solution.py:711
  2.9 0.5 %collective-permute-start.1 = (f32[176,128]{1,0:T(8,128)S(1)}, f32[176,128]{1,0:T(8,128)S(1)}, u32[]{:S(2)}, u32[]{:S(2)}) collective-permute-start(f32[176,128]{1,0:T(8,128)S(1)} %get-tuple-element.63), channel_id=1, source_target_pairs={{0,1},{1,0},{2,3},{3,2},{4,5},{5,4},{6,7},{7,6},{8,9},{9,8},{10,11... | collective-permute-start | bytes 270344 | tf_op jit(solution)/shard_map/ppermute | solution.py:729
  3.4 1.5 %z_solve_next.1 = (f32[128,128]{1,0:T(8,128)S(1)}, f32[128,128]{1,0:T(8,128)S(1)}, f32[4,512,128]{2,1,0:T(8,128)S(1)}) custom-call(s32[1]{0:T(128)} %bitcast.me_ref, f32[4,512,128]{2,1,0:T(8,128)S(1)} %get-tuple-element.53.cot, f32[512,128]{1,0:T(8,128)S(1)} %get-tuple-element.54.phi, f32[512,128]{1,0:T(8,128)S(1)} %get-tuple-element.55.psi, ...), custom_call_target="tpu_custom_call" | custom-call | flops 1000000000 | bytes 10000000 | tf_op jit(solution)/shard_map/z_solve_next/pallas_call | solution.py:711
  4.9 0.1 collective-permute-start
  5.1 3.0 %collective-permute-start.3 = (f32[176,128]{1,0:T(8,128)S(1)}, f32[176,128]{1,0:T(8,128)S(1)}, u32[]{:S(2)}, u32[]{:S(2)}) collective-permute-start(f32[176,128]{1,0:T(8,128)S(1)} %merge_gy.4.refs_2_.after.own.refs_0_.refs_7_.refs_1_), channel_id=1, source_target_pairs={{0,2},{1,3},{2,0},{3,1},{4,6},{5,7},{6,4},{7,5},{8,10},{9,11},{10,... | collective-permute-start | bytes 270344 | tf_op jit(solution)/shard_map/ppermute | solution.py:729
  8.1 0.9 %collective-permute-start.2 = (f32[128,128]{1,0:T(8,128)S(1)}, f32[128,128]{1,0:T(8,128)S(1)}, u32[]{:S(2)}, u32[]{:S(2)}) collective-permute-start(f32[128,128]{1,0:T(8,128)S(1)} %merge_gy.5.refs_1_.own), channel_id=1, source_target_pairs={{0,2},{1,3},{2,0},{3,1},{4,6},{5,7},{6,4},{7,5},{8,10},{9,11},{10,... | collective-permute-start | bytes 196616 | tf_op jit(solution)/shard_map/ppermute | solution.py:729
  9.0 0.2 copy-done
  9.2 0.2 copy-done.1
  9.5 0.4 %x_coefficients.1 = (f32[80,128]{1,0:T(8,128)S(1)}, f32[512,128]{1,0:T(8,128)S(1)}, f32[512,128]{1,0:T(8,128)S(1)}, f32[512,128]{1,0:T(8,128)S(1)}, f32[16,128]{...) custom-call(f32[512,128]{1,0:T(8,128)S(1)} %get-tuple-element.56.w, ...), custom_call_target="tpu_custom_call" | custom-call | flops 1000000000 | bytes 10000000 | tf_op jit(solution)/shard_map/x_coefficients/pallas_call | solution.py:711
  9.9 1.6 %collective-permute-start.7 = (f32[80,128]{1,0:T(8,128)S(1)}, f32[80,128]{1,0:T(8,128)S(1)}, u32[]{:S(2)}, u32[]{:S(2)}) collective-permute-start(f32[80,128]{1,0:T(8,128)S(1)} %get-tuple-element.64.refs_0_), channel_id=1, source_target_pairs={{0,8},{8,0},{16,24},{24,16},{1,9},{9,1},{17,25},{25,17},{2,10},{10... | collective-permute-start | bytes 122888 | tf_op jit(solution)/shard_map/ppermute | solution.py:729
  11.5 1.8 %collective-permute-start.5 = (f32[80,128]{1,0:T(8,128)S(1)}, f32[80,128]{1,0:T(8,128)S(1)}, u32[]{:S(2)}, u32[]{:S(2)}) collective-permute-start(f32[80,128]{1,0:T(8,128)S(1)} %get-tuple-element.65.refs_2_), channel_id=1, source_target_pairs={{0,4},{1,5},{2,6},{3,7},{4,0},{5,1},{6,2},{7,3},{8,12},{9,13},{10,... | collective-permute-start | bytes 122888 | tf_op jit(solution)/shard_map/ppermute | solution.py:729
  13.4 0.8 %collective-permute-start.4 = (f32[64,128]{1,0:T(8,128)S(1)}, f32[64,128]{1,0:T(8,128)S(1)}, u32[]{:S(2)}, u32[]{:S(2)}) collective-permute-start(f32[64,128]{1,0:T(8,128)S(1)} %get-tuple-element.67.refs_6_), channel_id=1, source_target_pairs={{0,4},{1,5},{2,6},{3,7},{4,0},{5,1},{6,2},{7,3},{8,12},{9,13},{10,... | collective-permute-start | bytes 98312 | tf_op jit(solution)/shard_map/ppermute | solution.py:729
  14.2 1.6 %collective-permute-done.5.refs_11_.refs_5_ = f32[80,128]{1,0:T(8,128)S(1)} collective-permute-done((f32[80,128]{1,0:T(8,128)S(1)}, f32[80,128]{1,0:T(8,128)S(1)}, u32[]{:S(2)}, u32[]{:S(2)}) %collective-permute-start.5) | collective-permute-done | bytes 40992 | tf_op jit(solution)/shard_map/ppermute | solution.py:729
  15.9 1.5 %collective-permute-done.4.refs_5_ = f32[64,128]{1,0:T(8,128)S(1)} collective-permute-done((f32[64,128]{1,0:T(8,128)S(1)}, f32[64,128]{1,0:T(8,128)S(1)}, u32[]{:S(2)}, u32[]{:S(2)}) %collective-permute-start.4) | collective-permute-done | bytes 32800 | tf_op jit(solution)/shard_map/ppermute | solution.py:729
  17.6 0.6 %y_solve_lead.1 = (f32[168,128]{1,0:T(8,128)S(1)}, f32[88,128]{1,0:T(8,128)S(1)}, f32[2,512,128]{2,1,0:T(8,128)S(1)}, f32[256,128]{1,0:T(8,128)S(1)}, f32[256,12...) custom-call(s32[1]{0:T(128)} %bitcast.me_ref, ...), custom_call_target="tpu_custom_call" | custom-call | flops 1000000000 | bytes 10000000 | tf_op jit(solution)/shard_map/y_solve_lead/pallas_call | solution.py:711
  18.1 1.7 %collective-permute-start.10 = (f32[88,128]{1,0:T(8,128)S(1)}, f32[88,128]{1,0:T(8,128)S(1)}, u32[]{:S(2)}, u32[]{:S(2)}) collective-permute-start(f32[88,128]{1,0:T(8,128)S(1)} %get-tuple-element.86), channel_id=1, source_target_pairs={{0,8},{8,0},{16,24},{24,16},{1,9},{9,1},{17,25},{25,17},{2,10},{10... | collective-permute-start | bytes 135176 | tf_op jit(solution)/shard_map/ppermute | solution.py:729
  19.8 0.8 %y_solve_next.1 = (f32[144,128]{1,0:T(8,128)S(1)}, f32[4,512,128]{2,1,0:T(8,128)S(1)}, f32[256,128]{1,0:T(8,128)S(1)}, f32[256,128]{1,0:T(8,128)S(1)}, f32[256,128]{1,0:T(8,128)S(1)}) custom-call(s32[1]{0:T(128)} %bitcast.me_ref, f32[4,512,128]{2,1,0:T(8,128)S(1)} %get-tuple-element.59.az, f32[128,128]{1,0:T(8,128)S(1)} %get-tuple-element.69.own, ...), custom_call_target="tpu_custom_call" | custom-call | flops 1000000000 | bytes 10000000 | tf_op jit(solution)/shard_map/y_solve_next/pallas_call | solution.py:711
  20.6 0.7 %collective-permute-start.9 = (f32[144,128]{1,0:T(8,128)S(1)}, f32[144,128]{1,0:T(8,128)S(1)}, u32[]{:S(2)}, u32[]{:S(2)}) collective-permute-start(f32[144,128]{1,0:T(8,128)S(1)} %get-tuple-element.84.refs_0_.own), channel_id=1, source_target_pairs={{0,8},{8,0},{16,24},{24,16},{1,9},{9,1},{17,25},{25,17},{2,10},{10... | collective-permute-start | bytes 221192 | tf_op jit(solution)/shard_map/ppermute | solution.py:729
  21.3 0.9 %collective-permute-done.10.slim = f32[88,128]{1,0:T(8,128)S(1)} collective-permute-done((f32[88,128]{1,0:T(8,128)S(1)}, f32[88,128]{1,0:T(8,128)S(1)}, u32[]{:S(2)}, u32[]{:S(2)}) %collective-permute-start.10) | collective-permute-done | bytes 45088 | tf_op jit(solution)/shard_map/ppermute | solution.py:729
  22.3 2.7 %collective-permute-start.12 = (f32[80,128]{1,0:T(8,128)S(1)}, f32[80,128]{1,0:T(8,128)S(1)}, u32[]{:S(2)}, u32[]{:S(2)}) collective-permute-start(f32[80,128]{1,0:T(8,128)S(1)} %get-tuple-element.91), channel_id=1, source_target_pairs={{0,16},{8,24},{16,0},{24,8},{1,17},{9,25},{17,1},{25,9},{2,18},{10... | collective-permute-start | bytes 122888 | tf_op jit(solution)/shard_map/ppermute | solution.py:729
  25.1 3.2 %collective-permute-start.11 = (f32[72,128]{1,0:T(8,128)S(1)}, f32[72,128]{1,0:T(8,128)S(1)}, u32[]{:S(2)}, u32[]{:S(2)}) collective-permute-start(f32[72,128]{1,0:T(8,128)S(1)} %get-tuple-element.89), channel_id=1, source_target_pairs={{0,16},{8,24},{16,0},{24,8},{1,17},{9,25},{17,1},{25,9},{2,18},{10... | collective-permute-start | bytes 110600 | tf_op jit(solution)/shard_map/ppermute | solution.py:729
  28.3 1.3 %x_solve.2.refs_15_ = f32[6,512,128]{2,1,0:T(8,128)} custom-call(s32[1]{0:T(128)} %bitcast.me_ref, f32[168,128]{1,0:T(8,128)S(1)} %get-tuple-element.85.own.refs_0_.refs_4_, f32[168,128]{1,0:T(8,128)S(1)} %get-tuple-element.90.refs_1_.refs_5_, f32[168,128]{1,0:T(8,128)S(1)} %get-tuple-element.87.refs_1_.refs_2_.refs_6_, ...), custom_call_target="tpu_custom_call" | custom-call | flops 1000000000 | bytes 10000000 | tf_op jit(solution)/shard_map/x_solve/pallas_call | solution.py:711
  29.5 0.7 %collective-permute-done.11.refs_3_ = f32[72,128]{1,0:T(8,128)S(1)} collective-permute-done((f32[72,128]{1,0:T(8,128)S(1)}, f32[72,128]{1,0:T(8,128)S(1)}, u32[]{:S(2)}, u32[]{:S(2)}) %collective-permute-start.11) | collective-permute-done | bytes 36896 | tf_op jit(solution)/shard_map/ppermute | solution.py:729
  30.2 1.7 %x_solve.3 = f32[6,512,128]{2,1,0:T(8,128)} custom-call(s32[1]{0:T(128)} %bitcast.me_ref, f32[144,128]{1,0:T(8,128)S(1)} %get-tuple-element.84.refs_0_.own, f32[144,128]{1,0:T(8,128)S(1)} %get-tuple-element.88.refs_1_, f32[144,128]{1,0:T(8,128)S(1)} %collective-permute-done.9.other.refs_2_, ...), custom_call_target="tpu_custom_call", output_to_operand_aliasing={{}: (16, {})} | custom-call | flops 1000000000 | bytes 10000000 | tf_op jit(solution)/shard_map/x_solve/pallas_call | solution.py:711
  (21 shorter events, 0.5 us)
Async XLA Ops:
  2.9 2.2 %collective-permute-start.1 = (f32[176,128]{1,0:T(8,128)S(1)}, f32[176,128]{1,0:T(8,128)S(1)}, u32[]{:S(2)}, u32[]{:S(2)}) collective-permute-start(f32[176,128]{1,0:T(8,128)S(1)} %get-tuple-element.63), channel_id=1, source_target_pairs={{0,1},{1,0},{2,3},{3,2},{4,5},{5,4},{6,7},{7,6},{8,9},{9,8},{10,11... | collective-permute-start | bytes 270344 | tf_op jit(solution)/shard_map/ppermute | solution.py:729
  4.9 3.2 %collective-permute-start = (f32[128,128]{1,0:T(8,128)S(1)}, f32[128,128]{1,0:T(8,128)S(1)}, u32[]{:S(2)}, u32[]{:S(2)}) collective-permute-start(f32[128,128]{1,0:T(8,128)S(1)} %get-tuple-element.61.refs_0_), channel_id=1, source_target_pairs={{0,1},{1,0},{2,3},{3,2},{4,5},{5,4},{6,7},{7,6},{8,9},{9,8},{10,11... | collective-permute-start | bytes 196616 | tf_op jit(solution)/shard_map/ppermute | solution.py:729
  5.1 6.4 %collective-permute-start.3 = (f32[176,128]{1,0:T(8,128)S(1)}, f32[176,128]{1,0:T(8,128)S(1)}, u32[]{:S(2)}, u32[]{:S(2)}) collective-permute-start(f32[176,128]{1,0:T(8,128)S(1)} %merge_gy.4.refs_2_.after.own.refs_0_.refs_7_.refs_1_), channel_id=1, source_target_pairs={{0,2},{1,3},{2,0},{3,1},{4,6},{5,7},{6,4},{7,5},{8,10},{9,11},{10,... | collective-permute-start | bytes 270344 | tf_op jit(solution)/shard_map/ppermute | solution.py:729
  8.1 1.1 %copy-start = (f32[3,32,16,128]{3,2,1,0:T(8,128)S(1)}, f32[3,32,16,128]{3,2,1,0:T(8,128)}, u32[]{:S(2)}) copy-start(f32[3,32,16,128]{3,2,1,0:T(8,128)} %param.8) | copy-start | bytes 2359300
  8.1 1.4 %copy-start.1 = (s32[3,32,16,128]{3,2,1,0:T(8,128)S(1)}, s32[3,32,16,128]{3,2,1,0:T(8,128)}, u32[]{:S(2)}) copy-start(s32[3,32,16,128]{3,2,1,0:T(8,128)} %param.9) | copy-start | bytes 2359300
  8.1 5.3 %collective-permute-start.2 = (f32[128,128]{1,0:T(8,128)S(1)}, f32[128,128]{1,0:T(8,128)S(1)}, u32[]{:S(2)}, u32[]{:S(2)}) collective-permute-start(f32[128,128]{1,0:T(8,128)S(1)} %merge_gy.5.refs_1_.own), channel_id=1, source_target_pairs={{0,2},{1,3},{2,0},{3,1},{4,6},{5,7},{6,4},{7,5},{8,10},{9,11},{10,... | collective-permute-start | bytes 196616 | tf_op jit(solution)/shard_map/ppermute | solution.py:729
  9.9 4.3 %collective-permute-start.7 = (f32[80,128]{1,0:T(8,128)S(1)}, f32[80,128]{1,0:T(8,128)S(1)}, u32[]{:S(2)}, u32[]{:S(2)}) collective-permute-start(f32[80,128]{1,0:T(8,128)S(1)} %get-tuple-element.64.refs_0_), channel_id=1, source_target_pairs={{0,8},{8,0},{16,24},{24,16},{1,9},{9,1},{17,25},{25,17},{2,10},{10... | collective-permute-start | bytes 122888 | tf_op jit(solution)/shard_map/ppermute | solution.py:729
  11.5 4.2 %collective-permute-start.5 = (f32[80,128]{1,0:T(8,128)S(1)}, f32[80,128]{1,0:T(8,128)S(1)}, u32[]{:S(2)}, u32[]{:S(2)}) collective-permute-start(f32[80,128]{1,0:T(8,128)S(1)} %get-tuple-element.65.refs_2_), channel_id=1, source_target_pairs={{0,4},{1,5},{2,6},{3,7},{4,0},{5,1},{6,2},{7,3},{8,12},{9,13},{10,... | collective-permute-start | bytes 122888 | tf_op jit(solution)/shard_map/ppermute | solution.py:729
  13.4 4.0 %collective-permute-start.4 = (f32[64,128]{1,0:T(8,128)S(1)}, f32[64,128]{1,0:T(8,128)S(1)}, u32[]{:S(2)}, u32[]{:S(2)}) collective-permute-start(f32[64,128]{1,0:T(8,128)S(1)} %get-tuple-element.67.refs_6_), channel_id=1, source_target_pairs={{0,4},{1,5},{2,6},{3,7},{4,0},{5,1},{6,2},{7,3},{8,12},{9,13},{10,... | collective-permute-start | bytes 98312 | tf_op jit(solution)/shard_map/ppermute | solution.py:729
  15.8 1.7 %collective-permute-start.8 = (f32[128,128]{1,0:T(8,128)S(1)}, f32[128,128]{1,0:T(8,128)S(1)}, u32[]{:S(2)}, u32[]{:S(2)}) collective-permute-start(f32[128,128]{1,0:T(8,128)S(1)} %get-tuple-element.77), channel_id=1, source_target_pairs={{0,1},{1,0},{2,3},{3,2},{4,5},{5,4},{6,7},{7,6},{8,9},{9,8},{10,11... | collective-permute-start | bytes 196616 | tf_op jit(solution)/shard_map/ppermute | solution.py:729
  17.5 2.3 %collective-permute-start.6 = (f32[128,128]{1,0:T(8,128)S(1)}, f32[128,128]{1,0:T(8,128)S(1)}, u32[]{:S(2)}, u32[]{:S(2)}) collective-permute-start(f32[128,128]{1,0:T(8,128)S(1)} %get-tuple-element.70), channel_id=1, source_target_pairs={{0,1},{1,0},{2,3},{3,2},{4,5},{5,4},{6,7},{7,6},{8,9},{9,8},{10,11... | collective-permute-start | bytes 196616 | tf_op jit(solution)/shard_map/ppermute | solution.py:729
  18.1 4.1 %collective-permute-start.10 = (f32[88,128]{1,0:T(8,128)S(1)}, f32[88,128]{1,0:T(8,128)S(1)}, u32[]{:S(2)}, u32[]{:S(2)}) collective-permute-start(f32[88,128]{1,0:T(8,128)S(1)} %get-tuple-element.86), channel_id=1, source_target_pairs={{0,8},{8,0},{16,24},{24,16},{1,9},{9,1},{17,25},{25,17},{2,10},{10... | collective-permute-start | bytes 135176 | tf_op jit(solution)/shard_map/ppermute | solution.py:729
  20.6 4.4 %collective-permute-start.9 = (f32[144,128]{1,0:T(8,128)S(1)}, f32[144,128]{1,0:T(8,128)S(1)}, u32[]{:S(2)}, u32[]{:S(2)}) collective-permute-start(f32[144,128]{1,0:T(8,128)S(1)} %get-tuple-element.84.refs_0_.own), channel_id=1, source_target_pairs={{0,8},{8,0},{16,24},{24,16},{1,9},{9,1},{17,25},{25,17},{2,10},{10... | collective-permute-start | bytes 221192 | tf_op jit(solution)/shard_map/ppermute | solution.py:729
  22.3 6.0 %collective-permute-start.12 = (f32[80,128]{1,0:T(8,128)S(1)}, f32[80,128]{1,0:T(8,128)S(1)}, u32[]{:S(2)}, u32[]{:S(2)}) collective-permute-start(f32[80,128]{1,0:T(8,128)S(1)} %get-tuple-element.91), channel_id=1, source_target_pairs={{0,16},{8,24},{16,0},{24,8},{1,17},{9,25},{17,1},{25,9},{2,18},{10... | collective-permute-start | bytes 122888 | tf_op jit(solution)/shard_map/ppermute | solution.py:729
  25.1 5.1 %collective-permute-start.11 = (f32[72,128]{1,0:T(8,128)S(1)}, f32[72,128]{1,0:T(8,128)S(1)}, u32[]{:S(2)}, u32[]{:S(2)}) collective-permute-start(f32[72,128]{1,0:T(8,128)S(1)} %get-tuple-element.89), channel_id=1, source_target_pairs={{0,16},{8,24},{16,0},{24,8},{1,17},{9,25},{17,1},{25,9},{2,18},{10... | collective-permute-start | bytes 110600 | tf_op jit(solution)/shard_map/ppermute | solution.py:729

commit v15 on v14

--- a/solution.py
+++ b/solution.py
@@ -293,10 +293,11 @@
     send[pl.ds(row, half), :] = pick(mine, high, low)
 
 
-def z_part(dims, lay, me_ref, cot, phi, psi, w, left, right, arrived, turned, az, keep, send):
+def z_part(
+    dims, lay, me_ref, sums, cot, phi, psi, w, left, right, arrived, turned, az, keep, send
+):
     nx, ny = dims
     tiles = nx * ny // LANES
-    sums = sum_matrix()
     mine = me_ref[0] & 1
     for c in range(len(lay.sizes)):
         arrived(c)
@@ -380,6 +381,7 @@
     for c in range(count):
         pltpu.make_async_copy(cot_any.at[c], cot.at[c], in_sems.at[c]).start()
     ahead.start()
+    sums = sum_matrix()
 
     for i, (source, target) in enumerate(small[:2]):
         pltpu.make_async_copy(source, target, sems.at[i]).wait()
@@ -415,13 +417,13 @@
     def arrived(c):
         pltpu.make_async_copy(cot_any.at[c], cot.at[c], in_sems.at[c]).wait()
 
-    z_part(dims, lay, me_ref, cot, phi, psi, w, left, right, arrived, turned, az, keep, send)
+    z_part(dims, lay, me_ref, sums, cot, phi, psi, w, left, right, arrived, turned, az, keep, send)
     ahead.wait()
 
 
 def next_z_kernel(dims, lay, me_ref, cot, phi, psi, w, left, right, keep, send, turned, az):
     z_part(
-        dims, lay, me_ref, cot, phi, psi, w, left, right, lambda c: None, turned, az, keep, send
+        dims, lay, me_ref, sum_matrix(), cot, phi, psi, w, left, right, lambda c: None, turned, az, keep, send
     )
 
 

time: 32 us -> 32 us (level)
  no operation moved by 1% of the time
where the time goes in v15:
time: 32 us; the launch traced here: 31.8 us
  starting transfers between devices  17 us (53%)
  Pallas kernels  9.42 us (29%)
  waiting for transfers between devices  4.89 us (15%)
  local copies, waits for them, and re-layouts  0.47 us (1%)
    ppermute x13, starting transfers between devices, exchange(): return lax.ppermute(rows, axis, [(i, i ^ 1 << bit) for i in range(count)])  17 us
    pallas_call x15, Pallas kernels, call(): pl.pallas_call(kernel, name=name, out_shape=[held[s](shape, jnp.float32)...  9.42 us
    ppermute x13, waiting for transfers between devices, exchange(): return lax.ppermute(rows, axis, [(i, i ^ 1 << bit) for i in range(count)])  4.89 us
  transfers between devices with their start and end apart: 13, of which 5 were waited for; matrix products, arithmetic and copies ran while one was open for 0% of the time, Pallas kernels for 15%

profile of v15, /device:TPU:0, one launch (start us, length us, event | category | flops | bytes accessed | tf_op | source)
XLA Modules:
  0.0 31.8 jit_solution(339008609292154336)
XLA Ops:
  0.0 2.9 %z_solve_lead.1 = (f32[176,128]{1,0:T(8,128)S(1)}, f32[176,128]{1,0:T(8,128)S(1)}, f32[2,512,128]{2,1,0:T(8,128)S(1)}, f32[512,128]{1,0:T(8,128)S(1)}, f32[512,1...) custom-call(s32[1]{0:T(128)} %bitcast.me_ref, ...), custom_call_target="tpu_custom_call" | custom-call | flops 1000000000 | bytes 10000000 | tf_op jit(solution)/shard_map/z_solve_lead/pallas_call | solution.py:713
  2.9 0.5 %collective-permute-start.1 = (f32[176,128]{1,0:T(8,128)S(1)}, f32[176,128]{1,0:T(8,128)S(1)}, u32[]{:S(2)}, u32[]{:S(2)}) collective-permute-start(f32[176,128]{1,0:T(8,128)S(1)} %get-tuple-element.63), channel_id=1, source_target_pairs={{0,1},{1,0},{2,3},{3,2},{4,5},{5,4},{6,7},{7,6},{8,9},{9,8},{10,11... | collective-permute-start | bytes 270344 | tf_op jit(solution)/shard_map/ppermute | solution.py:731
  3.4 1.5 %z_solve_next.1 = (f32[128,128]{1,0:T(8,128)S(1)}, f32[128,128]{1,0:T(8,128)S(1)}, f32[4,512,128]{2,1,0:T(8,128)S(1)}) custom-call(s32[1]{0:T(128)} %bitcast.me_ref, f32[4,512,128]{2,1,0:T(8,128)S(1)} %get-tuple-element.53.cot, f32[512,128]{1,0:T(8,128)S(1)} %get-tuple-element.54.phi, f32[512,128]{1,0:T(8,128)S(1)} %get-tuple-element.55.psi, ...), custom_call_target="tpu_custom_call" | custom-call | flops 1000000000 | bytes 10000000 | tf_op jit(solution)/shard_map/z_solve_next/pallas_call | solution.py:713
  5.1 3.0 %collective-permute-start.3 = (f32[176,128]{1,0:T(8,128)S(1)}, f32[176,128]{1,0:T(8,128)S(1)}, u32[]{:S(2)}, u32[]{:S(2)}) collective-permute-start(f32[176,128]{1,0:T(8,128)S(1)} %merge_gy.4.refs_2_.after.own.refs_0_.refs_7_.refs_1_), channel_id=1, source_target_pairs={{0,2},{1,3},{2,0},{3,1},{4,6},{5,7},{6,4},{7,5},{8,10},{9,11},{10,... | collective-permute-start | bytes 270344 | tf_op jit(solution)/shard_map/ppermute | solution.py:731
  8.1 0.9 %collective-permute-start.2 = (f32[128,128]{1,0:T(8,128)S(1)}, f32[128,128]{1,0:T(8,128)S(1)}, u32[]{:S(2)}, u32[]{:S(2)}) collective-permute-start(f32[128,128]{1,0:T(8,128)S(1)} %merge_gy.5.refs_1_.own), channel_id=1, source_target_pairs={{0,2},{1,3},{2,0},{3,1},{4,6},{5,7},{6,4},{7,5},{8,10},{9,11},{10,... | collective-permute-start | bytes 196616 | tf_op jit(solution)/shard_map/ppermute | solution.py:731
  9.0 0.2 copy-done
  9.2 0.2 copy-done.1
  9.5 0.4 %x_coefficients.1 = (f32[80,128]{1,0:T(8,128)S(1)}, f32[512,128]{1,0:T(8,128)S(1)}, f32[512,128]{1,0:T(8,128)S(1)}, f32[512,128]{1,0:T(8,128)S(1)}, f32[16,128]{...) custom-call(f32[512,128]{1,0:T(8,128)S(1)} %get-tuple-element.56.w, ...), custom_call_target="tpu_custom_call" | custom-call | flops 1000000000 | bytes 10000000 | tf_op jit(solution)/shard_map/x_coefficients/pallas_call | solution.py:713
  9.9 1.6 %collective-permute-start.7 = (f32[80,128]{1,0:T(8,128)S(1)}, f32[80,128]{1,0:T(8,128)S(1)}, u32[]{:S(2)}, u32[]{:S(2)}) collective-permute-start(f32[80,128]{1,0:T(8,128)S(1)} %get-tuple-element.64.refs_0_), channel_id=1, source_target_pairs={{0,8},{8,0},{16,24},{24,16},{1,9},{9,1},{17,25},{25,17},{2,10},{10... | collective-permute-start | bytes 122888 | tf_op jit(solution)/shard_map/ppermute | solution.py:731
  11.6 1.9 %collective-permute-start.5 = (f32[80,128]{1,0:T(8,128)S(1)}, f32[80,128]{1,0:T(8,128)S(1)}, u32[]{:S(2)}, u32[]{:S(2)}) collective-permute-start(f32[80,128]{1,0:T(8,128)S(1)} %get-tuple-element.65.refs_2_), channel_id=1, source_target_pairs={{0,4},{1,5},{2,6},{3,7},{4,0},{5,1},{6,2},{7,3},{8,12},{9,13},{10,... | collective-permute-start | bytes 122888 | tf_op jit(solution)/shard_map/ppermute | solution.py:731
  13.4 0.7 %collective-permute-start.4 = (f32[64,128]{1,0:T(8,128)S(1)}, f32[64,128]{1,0:T(8,128)S(1)}, u32[]{:S(2)}, u32[]{:S(2)}) collective-permute-start(f32[64,128]{1,0:T(8,128)S(1)} %get-tuple-element.67.refs_6_), channel_id=1, source_target_pairs={{0,4},{1,5},{2,6},{3,7},{4,0},{5,1},{6,2},{7,3},{8,12},{9,13},{10,... | collective-permute-start | bytes 98312 | tf_op jit(solution)/shard_map/ppermute | solution.py:731
  14.2 1.6 %collective-permute-done.5.refs_11_.refs_5_ = f32[80,128]{1,0:T(8,128)S(1)} collective-permute-done((f32[80,128]{1,0:T(8,128)S(1)}, f32[80,128]{1,0:T(8,128)S(1)}, u32[]{:S(2)}, u32[]{:S(2)}) %collective-permute-start.5) | collective-permute-done | bytes 40992 | tf_op jit(solution)/shard_map/ppermute | solution.py:731
  15.9 1.5 %collective-permute-done.4.refs_5_ = f32[64,128]{1,0:T(8,128)S(1)} collective-permute-done((f32[64,128]{1,0:T(8,128)S(1)}, f32[64,128]{1,0:T(8,128)S(1)}, u32[]{:S(2)}, u32[]{:S(2)}) %collective-permute-start.4) | collective-permute-done | bytes 32800 | tf_op jit(solution)/shard_map/ppermute | solution.py:731
  17.6 0.6 %y_solve_lead.1 = (f32[168,128]{1,0:T(8,128)S(1)}, f32[88,128]{1,0:T(8,128)S(1)}, f32[2,512,128]{2,1,0:T(8,128)S(1)}, f32[256,128]{1,0:T(8,128)S(1)}, f32[256,12...) custom-call(s32[1]{0:T(128)} %bitcast.me_ref, ...), custom_call_target="tpu_custom_call" | custom-call | flops 1000000000 | bytes 10000000 | tf_op jit(solution)/shard_map/y_solve_lead/pallas_call | solution.py:713
  18.1 1.7 %collective-permute-start.10 = (f32[88,128]{1,0:T(8,128)S(1)}, f32[88,128]{1,0:T(8,128)S(1)}, u32[]{:S(2)}, u32[]{:S(2)}) collective-permute-start(f32[88,128]{1,0:T(8,128)S(1)} %get-tuple-element.86), channel_id=1, source_target_pairs={{0,8},{8,0},{16,24},{24,16},{1,9},{9,1},{17,25},{25,17},{2,10},{10... | collective-permute-start | bytes 135176 | tf_op jit(solution)/shard_map/ppermute | solution.py:731
  19.9 0.8 %y_solve_next.1 = (f32[144,128]{1,0:T(8,128)S(1)}, f32[4,512,128]{2,1,0:T(8,128)S(1)}, f32[256,128]{1,0:T(8,128)S(1)}, f32[256,128]{1,0:T(8,128)S(1)}, f32[256,128]{1,0:T(8,128)S(1)}) custom-call(s32[1]{0:T(128)} %bitcast.me_ref, f32[4,512,128]{2,1,0:T(8,128)S(1)} %get-tuple-element.59.az, f32[128,128]{1,0:T(8,128)S(1)} %get-tuple-element.69.own, ...), custom_call_target="tpu_custom_call" | custom-call | flops 1000000000 | bytes 10000000 | tf_op jit(solution)/shard_map/y_solve_next/pallas_call | solution.py:713
  20.7 0.7 %collective-permute-start.9 = (f32[144,128]{1,0:T(8,128)S(1)}, f32[144,128]{1,0:T(8,128)S(1)}, u32[]{:S(2)}, u32[]{:S(2)}) collective-permute-start(f32[144,128]{1,0:T(8,128)S(1)} %get-tuple-element.84.refs_0_.own), channel_id=1, source_target_pairs={{0,8},{8,0},{16,24},{24,16},{1,9},{9,1},{17,25},{25,17},{2,10},{10... | collective-permute-start | bytes 221192 | tf_op jit(solution)/shard_map/ppermute | solution.py:731
  21.4 0.9 %collective-permute-done.10.slim = f32[88,128]{1,0:T(8,128)S(1)} collective-permute-done((f32[88,128]{1,0:T(8,128)S(1)}, f32[88,128]{1,0:T(8,128)S(1)}, u32[]{:S(2)}, u32[]{:S(2)}) %collective-permute-start.10) | collective-permute-done | bytes 45088 | tf_op jit(solution)/shard_map/ppermute | solution.py:731
  22.3 2.7 %collective-permute-start.12 = (f32[80,128]{1,0:T(8,128)S(1)}, f32[80,128]{1,0:T(8,128)S(1)}, u32[]{:S(2)}, u32[]{:S(2)}) collective-permute-start(f32[80,128]{1,0:T(8,128)S(1)} %get-tuple-element.91), channel_id=1, source_target_pairs={{0,16},{8,24},{16,0},{24,8},{1,17},{9,25},{17,1},{25,9},{2,18},{10... | collective-permute-start | bytes 122888 | tf_op jit(solution)/shard_map/ppermute | solution.py:731
  24.9 0.2 collective-permute-done.9.other.refs_2_
  25.2 3.0 %collective-permute-start.11 = (f32[72,128]{1,0:T(8,128)S(1)}, f32[72,128]{1,0:T(8,128)S(1)}, u32[]{:S(2)}, u32[]{:S(2)}) collective-permute-start(f32[72,128]{1,0:T(8,128)S(1)} %get-tuple-element.89), channel_id=1, source_target_pairs={{0,16},{8,24},{16,0},{24,8},{1,17},{9,25},{17,1},{25,9},{2,18},{10... | collective-permute-start | bytes 110600 | tf_op jit(solution)/shard_map/ppermute | solution.py:731
  28.2 1.3 %x_solve.2.refs_15_ = f32[6,512,128]{2,1,0:T(8,128)} custom-call(s32[1]{0:T(128)} %bitcast.me_ref, f32[168,128]{1,0:T(8,128)S(1)} %get-tuple-element.85.own.refs_0_.refs_4_, f32[168,128]{1,0:T(8,128)S(1)} %get-tuple-element.90.refs_1_.refs_5_, f32[168,128]{1,0:T(8,128)S(1)} %get-tuple-element.87.refs_1_.refs_2_.refs_6_, ...), custom_call_target="tpu_custom_call" | custom-call | flops 1000000000 | bytes 10000000 | tf_op jit(solution)/shard_map/x_solve/pallas_call | solution.py:713
  29.5 0.7 %collective-permute-done.11.refs_3_ = f32[72,128]{1,0:T(8,128)S(1)} collective-permute-done((f32[72,128]{1,0:T(8,128)S(1)}, f32[72,128]{1,0:T(8,128)S(1)}, u32[]{:S(2)}, u32[]{:S(2)}) %collective-permute-start.11) | collective-permute-done | bytes 36896 | tf_op jit(solution)/shard_map/ppermute | solution.py:731
  30.2 1.7 %x_solve.3 = f32[6,512,128]{2,1,0:T(8,128)} custom-call(s32[1]{0:T(128)} %bitcast.me_ref, f32[144,128]{1,0:T(8,128)S(1)} %get-tuple-element.84.refs_0_.own, f32[144,128]{1,0:T(8,128)S(1)} %get-tuple-element.88.refs_1_, f32[144,128]{1,0:T(8,128)S(1)} %collective-permute-done.9.other.refs_2_, ...), custom_call_target="tpu_custom_call", output_to_operand_aliasing={{}: (16, {})} | custom-call | flops 1000000000 | bytes 10000000 | tf_op jit(solution)/shard_map/x_solve/pallas_call | solution.py:713
  (21 shorter events, 0.6 us)
Async XLA Ops:
  2.9 2.2 %collective-permute-start.1 = (f32[176,128]{1,0:T(8,128)S(1)}, f32[176,128]{1,0:T(8,128)S(1)}, u32[]{:S(2)}, u32[]{:S(2)}) collective-permute-start(f32[176,128]{1,0:T(8,128)S(1)} %get-tuple-element.63), channel_id=1, source_target_pairs={{0,1},{1,0},{2,3},{3,2},{4,5},{5,4},{6,7},{7,6},{8,9},{9,8},{10,11... | collective-permute-start | bytes 270344 | tf_op jit(solution)/shard_map/ppermute | solution.py:731
  5.0 3.2 %collective-permute-start = (f32[128,128]{1,0:T(8,128)S(1)}, f32[128,128]{1,0:T(8,128)S(1)}, u32[]{:S(2)}, u32[]{:S(2)}) collective-permute-start(f32[128,128]{1,0:T(8,128)S(1)} %get-tuple-element.61.refs_0_), channel_id=1, source_target_pairs={{0,1},{1,0},{2,3},{3,2},{4,5},{5,4},{6,7},{7,6},{8,9},{9,8},{10,11... | collective-permute-start | bytes 196616 | tf_op jit(solution)/shard_map/ppermute | solution.py:731
  5.1 6.4 %collective-permute-start.3 = (f32[176,128]{1,0:T(8,128)S(1)}, f32[176,128]{1,0:T(8,128)S(1)}, u32[]{:S(2)}, u32[]{:S(2)}) collective-permute-start(f32[176,128]{1,0:T(8,128)S(1)} %merge_gy.4.refs_2_.after.own.refs_0_.refs_7_.refs_1_), channel_id=1, source_target_pairs={{0,2},{1,3},{2,0},{3,1},{4,6},{5,7},{6,4},{7,5},{8,10},{9,11},{10,... | collective-permute-start | bytes 270344 | tf_op jit(solution)/shard_map/ppermute | solution.py:731
  8.1 1.1 %copy-start = (f32[3,32,16,128]{3,2,1,0:T(8,128)S(1)}, f32[3,32,16,128]{3,2,1,0:T(8,128)}, u32[]{:S(2)}) copy-start(f32[3,32,16,128]{3,2,1,0:T(8,128)} %param.8) | copy-start | bytes 2359300
  8.1 1.4 %copy-start.1 = (s32[3,32,16,128]{3,2,1,0:T(8,128)S(1)}, s32[3,32,16,128]{3,2,1,0:T(8,128)}, u32[]{:S(2)}) copy-start(s32[3,32,16,128]{3,2,1,0:T(8,128)} %param.9) | copy-start | bytes 2359300
  8.1 5.3 %collective-permute-start.2 = (f32[128,128]{1,0:T(8,128)S(1)}, f32[128,128]{1,0:T(8,128)S(1)}, u32[]{:S(2)}, u32[]{:S(2)}) collective-permute-start(f32[128,128]{1,0:T(8,128)S(1)} %merge_gy.5.refs_1_.own), channel_id=1, source_target_pairs={{0,2},{1,3},{2,0},{3,1},{4,6},{5,7},{6,4},{7,5},{8,10},{9,11},{10,... | collective-permute-start | bytes 196616 | tf_op jit(solution)/shard_map/ppermute | solution.py:731
  9.9 4.3 %collective-permute-start.7 = (f32[80,128]{1,0:T(8,128)S(1)}, f32[80,128]{1,0:T(8,128)S(1)}, u32[]{:S(2)}, u32[]{:S(2)}) collective-permute-start(f32[80,128]{1,0:T(8,128)S(1)} %get-tuple-element.64.refs_0_), channel_id=1, source_target_pairs={{0,8},{8,0},{16,24},{24,16},{1,9},{9,1},{17,25},{25,17},{2,10},{10... | collective-permute-start | bytes 122888 | tf_op jit(solution)/shard_map/ppermute | solution.py:731
  11.6 4.3 %collective-permute-start.5 = (f32[80,128]{1,0:T(8,128)S(1)}, f32[80,128]{1,0:T(8,128)S(1)}, u32[]{:S(2)}, u32[]{:S(2)}) collective-permute-start(f32[80,128]{1,0:T(8,128)S(1)} %get-tuple-element.65.refs_2_), channel_id=1, source_target_pairs={{0,4},{1,5},{2,6},{3,7},{4,0},{5,1},{6,2},{7,3},{8,12},{9,13},{10,... | collective-permute-start | bytes 122888 | tf_op jit(solution)/shard_map/ppermute | solution.py:731
  13.4 4.0 %collective-permute-start.4 = (f32[64,128]{1,0:T(8,128)S(1)}, f32[64,128]{1,0:T(8,128)S(1)}, u32[]{:S(2)}, u32[]{:S(2)}) collective-permute-start(f32[64,128]{1,0:T(8,128)S(1)} %get-tuple-element.67.refs_6_), channel_id=1, source_target_pairs={{0,4},{1,5},{2,6},{3,7},{4,0},{5,1},{6,2},{7,3},{8,12},{9,13},{10,... | collective-permute-start | bytes 98312 | tf_op jit(solution)/shard_map/ppermute | solution.py:731
  15.9 1.7 %collective-permute-start.8 = (f32[128,128]{1,0:T(8,128)S(1)}, f32[128,128]{1,0:T(8,128)S(1)}, u32[]{:S(2)}, u32[]{:S(2)}) collective-permute-start(f32[128,128]{1,0:T(8,128)S(1)} %get-tuple-element.77), channel_id=1, source_target_pairs={{0,1},{1,0},{2,3},{3,2},{4,5},{5,4},{6,7},{7,6},{8,9},{9,8},{10,11... | collective-permute-start | bytes 196616 | tf_op jit(solution)/shard_map/ppermute | solution.py:731
  17.5 2.4 %collective-permute-start.6 = (f32[128,128]{1,0:T(8,128)S(1)}, f32[128,128]{1,0:T(8,128)S(1)}, u32[]{:S(2)}, u32[]{:S(2)}) collective-permute-start(f32[128,128]{1,0:T(8,128)S(1)} %get-tuple-element.70), channel_id=1, source_target_pairs={{0,1},{1,0},{2,3},{3,2},{4,5},{5,4},{6,7},{7,6},{8,9},{9,8},{10,11... | collective-permute-start | bytes 196616 | tf_op jit(solution)/shard_map/ppermute | solution.py:731
  18.1 4.1 %collective-permute-start.10 = (f32[88,128]{1,0:T(8,128)S(1)}, f32[88,128]{1,0:T(8,128)S(1)}, u32[]{:S(2)}, u32[]{:S(2)}) collective-permute-start(f32[88,128]{1,0:T(8,128)S(1)} %get-tuple-element.86), channel_id=1, source_target_pairs={{0,8},{8,0},{16,24},{24,16},{1,9},{9,1},{17,25},{25,17},{2,10},{10... | collective-permute-start | bytes 135176 | tf_op jit(solution)/shard_map/ppermute | solution.py:731
  20.7 4.4 %collective-permute-start.9 = (f32[144,128]{1,0:T(8,128)S(1)}, f32[144,128]{1,0:T(8,128)S(1)}, u32[]{:S(2)}, u32[]{:S(2)}) collective-permute-start(f32[144,128]{1,0:T(8,128)S(1)} %get-tuple-element.84.refs_0_.own), channel_id=1, source_target_pairs={{0,8},{8,0},{16,24},{24,16},{1,9},{9,1},{17,25},{25,17},{2,10},{10... | collective-permute-start | bytes 221192 | tf_op jit(solution)/shard_map/ppermute | solution.py:731
  22.3 5.9 %collective-permute-start.12 = (f32[80,128]{1,0:T(8,128)S(1)}, f32[80,128]{1,0:T(8,128)S(1)}, u32[]{:S(2)}, u32[]{:S(2)}) collective-permute-start(f32[80,128]{1,0:T(8,128)S(1)} %get-tuple-element.91), channel_id=1, source_target_pairs={{0,16},{8,24},{16,0},{24,8},{1,17},{9,25},{17,1},{25,9},{2,18},{10... | collective-permute-start | bytes 122888 | tf_op jit(solution)/shard_map/ppermute | solution.py:731
  25.2 5.0 %collective-permute-start.11 = (f32[72,128]{1,0:T(8,128)S(1)}, f32[72,128]{1,0:T(8,128)S(1)}, u32[]{:S(2)}, u32[]{:S(2)}) collective-permute-start(f32[72,128]{1,0:T(8,128)S(1)} %get-tuple-element.89), channel_id=1, source_target_pairs={{0,16},{8,24},{16,0},{24,8},{1,17},{9,25},{17,1},{25,9},{2,18},{10... | collective-permute-start | bytes 110600 | tf_op jit(solution)/shard_map/ppermute | solution.py:731

commit v16 on v15

--- a/solution.py
+++ b/solution.py
@@ -677,7 +677,7 @@
                 out[c, pl.ds(pl.multiple_of(x * ny + t * TILE, TILE), TILE), :] = part
         return carry
 
-    parts = 8
+    parts = 16
     share = nx // parts
 
     def copy(part):
@@ -898,7 +898,7 @@
             [(comps, rows, nz)],
             [
                 vmem(counts[g], rows, nz), vmem(counts[g], rows + 2 * ny, nz), vmem(nx * TILE, nz),
-                pltpu.SemaphoreType.DMA((8,)),
+                pltpu.SemaphoreType.DMA((16,)),
             ],
             spaces=spaces,
             out_spaces="h",

time: 32 us -> 32 us (level)
  no operation moved by 1% of the time
where the time goes in v16:
time: 32 us; the launch traced here: 31.9 us
  starting transfers between devices  17 us (53%)
  Pallas kernels  9.52 us (30%)
  waiting for transfers between devices  4.83 us (15%)
  local copies, waits for them, and re-layouts  0.47 us (1%)
    ppermute x13, starting transfers between devices, exchange(): return lax.ppermute(rows, axis, [(i, i ^ 1 << bit) for i in range(count)])  17 us
    pallas_call x15, Pallas kernels, call(): pl.pallas_call(kernel, name=name, out_shape=[held[s](shape, jnp.float32)...  9.52 us
    ppermute x13, waiting for transfers between devices, exchange(): return lax.ppermute(rows, axis, [(i, i ^ 1 << bit) for i in range(count)])  4.83 us
  transfers between devices with their start and end apart: 13, of which 5 were waited for; matrix products, arithmetic and copies ran while one was open for 0% of the time, Pallas kernels for 15%

profile of v16, /device:TPU:0, one launch (start us, length us, event | category | flops | bytes accessed | tf_op | source)
XLA Modules:
  0.0 31.9 jit_solution(5287901450614818438)
XLA Ops:
  0.0 2.9 %z_solve_lead.1 = (f32[176,128]{1,0:T(8,128)S(1)}, f32[176,128]{1,0:T(8,128)S(1)}, f32[2,512,128]{2,1,0:T(8,128)S(1)}, f32[512,128]{1,0:T(8,128)S(1)}, f32[512,1...) custom-call(s32[1]{0:T(128)} %bitcast.me_ref, ...), custom_call_target="tpu_custom_call" | custom-call | flops 1000000000 | bytes 10000000 | tf_op jit(solution)/shard_map/z_solve_lead/pallas_call | solution.py:713
  2.9 0.5 %collective-permute-start.1 = (f32[176,128]{1,0:T(8,128)S(1)}, f32[176,128]{1,0:T(8,128)S(1)}, u32[]{:S(2)}, u32[]{:S(2)}) collective-permute-start(f32[176,128]{1,0:T(8,128)S(1)} %get-tuple-element.63), channel_id=1, source_target_pairs={{0,1},{1,0},{2,3},{3,2},{4,5},{5,4},{6,7},{7,6},{8,9},{9,8},{10,11... | collective-permute-start | bytes 270344 | tf_op jit(solution)/shard_map/ppermute | solution.py:731
  3.4 1.5 %z_solve_next.1 = (f32[128,128]{1,0:T(8,128)S(1)}, f32[128,128]{1,0:T(8,128)S(1)}, f32[4,512,128]{2,1,0:T(8,128)S(1)}) custom-call(s32[1]{0:T(128)} %bitcast.me_ref, f32[4,512,128]{2,1,0:T(8,128)S(1)} %get-tuple-element.53.cot, f32[512,128]{1,0:T(8,128)S(1)} %get-tuple-element.54.phi, f32[512,128]{1,0:T(8,128)S(1)} %get-tuple-element.55.psi, ...), custom_call_target="tpu_custom_call" | custom-call | flops 1000000000 | bytes 10000000 | tf_op jit(solution)/shard_map/z_solve_next/pallas_call | solution.py:713
  5.1 3.0 %collective-permute-start.3 = (f32[176,128]{1,0:T(8,128)S(1)}, f32[176,128]{1,0:T(8,128)S(1)}, u32[]{:S(2)}, u32[]{:S(2)}) collective-permute-start(f32[176,128]{1,0:T(8,128)S(1)} %merge_gy.4.refs_2_.after.own.refs_0_.refs_7_.refs_1_), channel_id=1, source_target_pairs={{0,2},{1,3},{2,0},{3,1},{4,6},{5,7},{6,4},{7,5},{8,10},{9,11},{10,... | collective-permute-start | bytes 270344 | tf_op jit(solution)/shard_map/ppermute | solution.py:731
  8.1 0.9 %collective-permute-start.2 = (f32[128,128]{1,0:T(8,128)S(1)}, f32[128,128]{1,0:T(8,128)S(1)}, u32[]{:S(2)}, u32[]{:S(2)}) collective-permute-start(f32[128,128]{1,0:T(8,128)S(1)} %merge_gy.5.refs_1_.own), channel_id=1, source_target_pairs={{0,2},{1,3},{2,0},{3,1},{4,6},{5,7},{6,4},{7,5},{8,10},{9,11},{10,... | collective-permute-start | bytes 196616 | tf_op jit(solution)/shard_map/ppermute | solution.py:731
  9.0 0.2 copy-done
  9.2 0.2 copy-done.1
  9.5 0.4 %x_coefficients.1 = (f32[80,128]{1,0:T(8,128)S(1)}, f32[512,128]{1,0:T(8,128)S(1)}, f32[512,128]{1,0:T(8,128)S(1)}, f32[512,128]{1,0:T(8,128)S(1)}, f32[16,128]{...) custom-call(f32[512,128]{1,0:T(8,128)S(1)} %get-tuple-element.56.w, ...), custom_call_target="tpu_custom_call" | custom-call | flops 1000000000 | bytes 10000000 | tf_op jit(solution)/shard_map/x_coefficients/pallas_call | solution.py:713
  9.9 1.6 %collective-permute-start.7 = (f32[80,128]{1,0:T(8,128)S(1)}, f32[80,128]{1,0:T(8,128)S(1)}, u32[]{:S(2)}, u32[]{:S(2)}) collective-permute-start(f32[80,128]{1,0:T(8,128)S(1)} %get-tuple-element.64.refs_0_), channel_id=1, source_target_pairs={{0,8},{8,0},{16,24},{24,16},{1,9},{9,1},{17,25},{25,17},{2,10},{10... | collective-permute-start | bytes 122888 | tf_op jit(solution)/shard_map/ppermute | solution.py:731
  11.6 1.9 %collective-permute-start.5 = (f32[80,128]{1,0:T(8,128)S(1)}, f32[80,128]{1,0:T(8,128)S(1)}, u32[]{:S(2)}, u32[]{:S(2)}) collective-permute-start(f32[80,128]{1,0:T(8,128)S(1)} %get-tuple-element.65.refs_2_), channel_id=1, source_target_pairs={{0,4},{1,5},{2,6},{3,7},{4,0},{5,1},{6,2},{7,3},{8,12},{9,13},{10,... | collective-permute-start | bytes 122888 | tf_op jit(solution)/shard_map/ppermute | solution.py:731
  13.4 0.7 %collective-permute-start.4 = (f32[64,128]{1,0:T(8,128)S(1)}, f32[64,128]{1,0:T(8,128)S(1)}, u32[]{:S(2)}, u32[]{:S(2)}) collective-permute-start(f32[64,128]{1,0:T(8,128)S(1)} %get-tuple-element.67.refs_6_), channel_id=1, source_target_pairs={{0,4},{1,5},{2,6},{3,7},{4,0},{5,1},{6,2},{7,3},{8,12},{9,13},{10,... | collective-permute-start | bytes 98312 | tf_op jit(solution)/shard_map/ppermute | solution.py:731
  14.2 1.6 %collective-permute-done.5.refs_11_.refs_5_ = f32[80,128]{1,0:T(8,128)S(1)} collective-permute-done((f32[80,128]{1,0:T(8,128)S(1)}, f32[80,128]{1,0:T(8,128)S(1)}, u32[]{:S(2)}, u32[]{:S(2)}) %collective-permute-start.5) | collective-permute-done | bytes 40992 | tf_op jit(solution)/shard_map/ppermute | solution.py:731
  15.9 1.5 %collective-permute-done.4.refs_5_ = f32[64,128]{1,0:T(8,128)S(1)} collective-permute-done((f32[64,128]{1,0:T(8,128)S(1)}, f32[64,128]{1,0:T(8,128)S(1)}, u32[]{:S(2)}, u32[]{:S(2)}) %collective-permute-start.4) | collective-permute-done | bytes 32800 | tf_op jit(solution)/shard_map/ppermute | solution.py:731
  17.6 0.6 %y_solve_lead.1 = (f32[168,128]{1,0:T(8,128)S(1)}, f32[88,128]{1,0:T(8,128)S(1)}, f32[2,512,128]{2,1,0:T(8,128)S(1)}, f32[256,128]{1,0:T(8,128)S(1)}, f32[256,12...) custom-call(s32[1]{0:T(128)} %bitcast.me_ref, ...), custom_call_target="tpu_custom_call" | custom-call | flops 1000000000 | bytes 10000000 | tf_op jit(solution)/shard_map/y_solve_lead/pallas_call | solution.py:713
  18.1 1.7 %collective-permute-start.10 = (f32[88,128]{1,0:T(8,128)S(1)}, f32[88,128]{1,0:T(8,128)S(1)}, u32[]{:S(2)}, u32[]{:S(2)}) collective-permute-start(f32[88,128]{1,0:T(8,128)S(1)} %get-tuple-element.86), channel_id=1, source_target_pairs={{0,8},{8,0},{16,24},{24,16},{1,9},{9,1},{17,25},{25,17},{2,10},{10... | collective-permute-start | bytes 135176 | tf_op jit(solution)/shard_map/ppermute | solution.py:731
  19.9 0.8 %y_solve_next.1 = (f32[144,128]{1,0:T(8,128)S(1)}, f32[4,512,128]{2,1,0:T(8,128)S(1)}, f32[256,128]{1,0:T(8,128)S(1)}, f32[256,128]{1,0:T(8,128)S(1)}, f32[256,128]{1,0:T(8,128)S(1)}) custom-call(s32[1]{0:T(128)} %bitcast.me_ref, f32[4,512,128]{2,1,0:T(8,128)S(1)} %get-tuple-element.59.az, f32[128,128]{1,0:T(8,128)S(1)} %get-tuple-element.69.own, ...), custom_call_target="tpu_custom_call" | custom-call | flops 1000000000 | bytes 10000000 | tf_op jit(solution)/shard_map/y_solve_next/pallas_call | solution.py:713
  20.7 0.7 %collective-permute-start.9 = (f32[144,128]{1,0:T(8,128)S(1)}, f32[144,128]{1,0:T(8,128)S(1)}, u32[]{:S(2)}, u32[]{:S(2)}) collective-permute-start(f32[144,128]{1,0:T(8,128)S(1)} %get-tuple-element.84.refs_0_.own), channel_id=1, source_target_pairs={{0,8},{8,0},{16,24},{24,16},{1,9},{9,1},{17,25},{25,17},{2,10},{10... | collective-permute-start | bytes 221192 | tf_op jit(solution)/shard_map/ppermute | solution.py:731
  21.4 0.9 %collective-permute-done.10.slim = f32[88,128]{1,0:T(8,128)S(1)} collective-permute-done((f32[88,128]{1,0:T(8,128)S(1)}, f32[88,128]{1,0:T(8,128)S(1)}, u32[]{:S(2)}, u32[]{:S(2)}) %collective-permute-start.10) | collective-permute-done | bytes 45088 | tf_op jit(solution)/shard_map/ppermute | solution.py:731
  22.3 2.7 %collective-permute-start.12 = (f32[80,128]{1,0:T(8,128)S(1)}, f32[80,128]{1,0:T(8,128)S(1)}, u32[]{:S(2)}, u32[]{:S(2)}) collective-permute-start(f32[80,128]{1,0:T(8,128)S(1)} %get-tuple-element.91), channel_id=1, source_target_pairs={{0,16},{8,24},{16,0},{24,8},{1,17},{9,25},{17,1},{25,9},{2,18},{10... | collective-permute-start | bytes 122888 | tf_op jit(solution)/shard_map/ppermute | solution.py:731
  24.9 0.2 collective-permute-done.9.other.refs_2_
  25.2 3.0 %collective-permute-start.11 = (f32[72,128]{1,0:T(8,128)S(1)}, f32[72,128]{1,0:T(8,128)S(1)}, u32[]{:S(2)}, u32[]{:S(2)}) collective-permute-start(f32[72,128]{1,0:T(8,128)S(1)} %get-tuple-element.89), channel_id=1, source_target_pairs={{0,16},{8,24},{16,0},{24,8},{1,17},{9,25},{17,1},{25,9},{2,18},{10... | collective-permute-start | bytes 110600 | tf_op jit(solution)/shard_map/ppermute | solution.py:731
  28.2 1.3 %x_solve.2.refs_15_ = f32[6,512,128]{2,1,0:T(8,128)} custom-call(s32[1]{0:T(128)} %bitcast.me_ref, f32[168,128]{1,0:T(8,128)S(1)} %get-tuple-element.85.own.refs_0_.refs_4_, f32[168,128]{1,0:T(8,128)S(1)} %get-tuple-element.90.refs_1_.refs_5_, f32[168,128]{1,0:T(8,128)S(1)} %get-tuple-element.87.refs_1_.refs_2_.refs_6_, ...), custom_call_target="tpu_custom_call" | custom-call | flops 1000000000 | bytes 10000000 | tf_op jit(solution)/shard_map/x_solve/pallas_call | solution.py:713
  29.5 0.6 %collective-permute-done.11.refs_3_ = f32[72,128]{1,0:T(8,128)S(1)} collective-permute-done((f32[72,128]{1,0:T(8,128)S(1)}, f32[72,128]{1,0:T(8,128)S(1)}, u32[]{:S(2)}, u32[]{:S(2)}) %collective-permute-start.11) | collective-permute-done | bytes 36896 | tf_op jit(solution)/shard_map/ppermute | solution.py:731
  30.2 1.7 %x_solve.3 = f32[6,512,128]{2,1,0:T(8,128)} custom-call(s32[1]{0:T(128)} %bitcast.me_ref, f32[144,128]{1,0:T(8,128)S(1)} %get-tuple-element.84.refs_0_.own, f32[144,128]{1,0:T(8,128)S(1)} %get-tuple-element.88.refs_1_, f32[144,128]{1,0:T(8,128)S(1)} %collective-permute-done.9.other.refs_2_, ...), custom_call_target="tpu_custom_call", output_to_operand_aliasing={{}: (16, {})} | custom-call | flops 1000000000 | bytes 10000000 | tf_op jit(solution)/shard_map/x_solve/pallas_call | solution.py:713
  (21 shorter events, 0.6 us)
Async XLA Ops:
  2.9 2.2 %collective-permute-start.1 = (f32[176,128]{1,0:T(8,128)S(1)}, f32[176,128]{1,0:T(8,128)S(1)}, u32[]{:S(2)}, u32[]{:S(2)}) collective-permute-start(f32[176,128]{1,0:T(8,128)S(1)} %get-tuple-element.63), channel_id=1, source_target_pairs={{0,1},{1,0},{2,3},{3,2},{4,5},{5,4},{6,7},{7,6},{8,9},{9,8},{10,11... | collective-permute-start | bytes 270344 | tf_op jit(solution)/shard_map/ppermute | solution.py:731
  5.0 3.2 %collective-permute-start = (f32[128,128]{1,0:T(8,128)S(1)}, f32[128,128]{1,0:T(8,128)S(1)}, u32[]{:S(2)}, u32[]{:S(2)}) collective-permute-start(f32[128,128]{1,0:T(8,128)S(1)} %get-tuple-element.61.refs_0_), channel_id=1, source_target_pairs={{0,1},{1,0},{2,3},{3,2},{4,5},{5,4},{6,7},{7,6},{8,9},{9,8},{10,11... | collective-permute-start | bytes 196616 | tf_op jit(solution)/shard_map/ppermute | solution.py:731
  5.1 6.4 %collective-permute-start.3 = (f32[176,128]{1,0:T(8,128)S(1)}, f32[176,128]{1,0:T(8,128)S(1)}, u32[]{:S(2)}, u32[]{:S(2)}) collective-permute-start(f32[176,128]{1,0:T(8,128)S(1)} %merge_gy.4.refs_2_.after.own.refs_0_.refs_7_.refs_1_), channel_id=1, source_target_pairs={{0,2},{1,3},{2,0},{3,1},{4,6},{5,7},{6,4},{7,5},{8,10},{9,11},{10,... | collective-permute-start | bytes 270344 | tf_op jit(solution)/shard_map/ppermute | solution.py:731
  8.1 1.1 %copy-start = (f32[3,32,16,128]{3,2,1,0:T(8,128)S(1)}, f32[3,32,16,128]{3,2,1,0:T(8,128)}, u32[]{:S(2)}) copy-start(f32[3,32,16,128]{3,2,1,0:T(8,128)} %param.8) | copy-start | bytes 2359300
  8.1 1.4 %copy-start.1 = (s32[3,32,16,128]{3,2,1,0:T(8,128)S(1)}, s32[3,32,16,128]{3,2,1,0:T(8,128)}, u32[]{:S(2)}) copy-start(s32[3,32,16,128]{3,2,1,0:T(8,128)} %param.9) | copy-start | bytes 2359300
  8.1 5.3 %collective-permute-start.2 = (f32[128,128]{1,0:T(8,128)S(1)}, f32[128,128]{1,0:T(8,128)S(1)}, u32[]{:S(2)}, u32[]{:S(2)}) collective-permute-start(f32[128,128]{1,0:T(8,128)S(1)} %merge_gy.5.refs_1_.own), channel_id=1, source_target_pairs={{0,2},{1,3},{2,0},{3,1},{4,6},{5,7},{6,4},{7,5},{8,10},{9,11},{10,... | collective-permute-start | bytes 196616 | tf_op jit(solution)/shard_map/ppermute | solution.py:731
  9.9 4.3 %collective-permute-start.7 = (f32[80,128]{1,0:T(8,128)S(1)}, f32[80,128]{1,0:T(8,128)S(1)}, u32[]{:S(2)}, u32[]{:S(2)}) collective-permute-start(f32[80,128]{1,0:T(8,128)S(1)} %get-tuple-element.64.refs_0_), channel_id=1, source_target_pairs={{0,8},{8,0},{16,24},{24,16},{1,9},{9,1},{17,25},{25,17},{2,10},{10... | collective-permute-start | bytes 122888 | tf_op jit(solution)/shard_map/ppermute | solution.py:731
  11.6 4.3 %collective-permute-start.5 = (f32[80,128]{1,0:T(8,128)S(1)}, f32[80,128]{1,0:T(8,128)S(1)}, u32[]{:S(2)}, u32[]{:S(2)}) collective-permute-start(f32[80,128]{1,0:T(8,128)S(1)} %get-tuple-element.65.refs_2_), channel_id=1, source_target_pairs={{0,4},{1,5},{2,6},{3,7},{4,0},{5,1},{6,2},{7,3},{8,12},{9,13},{10,... | collective-permute-start | bytes 122888 | tf_op jit(solution)/shard_map/ppermute | solution.py:731
  13.4 4.0 %collective-permute-start.4 = (f32[64,128]{1,0:T(8,128)S(1)}, f32[64,128]{1,0:T(8,128)S(1)}, u32[]{:S(2)}, u32[]{:S(2)}) collective-permute-start(f32[64,128]{1,0:T(8,128)S(1)} %get-tuple-element.67.refs_6_), channel_id=1, source_target_pairs={{0,4},{1,5},{2,6},{3,7},{4,0},{5,1},{6,2},{7,3},{8,12},{9,13},{10,... | collective-permute-start | bytes 98312 | tf_op jit(solution)/shard_map/ppermute | solution.py:731
  15.9 1.7 %collective-permute-start.8 = (f32[128,128]{1,0:T(8,128)S(1)}, f32[128,128]{1,0:T(8,128)S(1)}, u32[]{:S(2)}, u32[]{:S(2)}) collective-permute-start(f32[128,128]{1,0:T(8,128)S(1)} %get-tuple-element.77), channel_id=1, source_target_pairs={{0,1},{1,0},{2,3},{3,2},{4,5},{5,4},{6,7},{7,6},{8,9},{9,8},{10,11... | collective-permute-start | bytes 196616 | tf_op jit(solution)/shard_map/ppermute | solution.py:731
  17.5 2.4 %collective-permute-start.6 = (f32[128,128]{1,0:T(8,128)S(1)}, f32[128,128]{1,0:T(8,128)S(1)}, u32[]{:S(2)}, u32[]{:S(2)}) collective-permute-start(f32[128,128]{1,0:T(8,128)S(1)} %get-tuple-element.70), channel_id=1, source_target_pairs={{0,1},{1,0},{2,3},{3,2},{4,5},{5,4},{6,7},{7,6},{8,9},{9,8},{10,11... | collective-permute-start | bytes 196616 | tf_op jit(solution)/shard_map/ppermute | solution.py:731
  18.1 4.1 %collective-permute-start.10 = (f32[88,128]{1,0:T(8,128)S(1)}, f32[88,128]{1,0:T(8,128)S(1)}, u32[]{:S(2)}, u32[]{:S(2)}) collective-permute-start(f32[88,128]{1,0:T(8,128)S(1)} %get-tuple-element.86), channel_id=1, source_target_pairs={{0,8},{8,0},{16,24},{24,16},{1,9},{9,1},{17,25},{25,17},{2,10},{10... | collective-permute-start | bytes 135176 | tf_op jit(solution)/shard_map/ppermute | solution.py:731
  20.7 4.4 %collective-permute-start.9 = (f32[144,128]{1,0:T(8,128)S(1)}, f32[144,128]{1,0:T(8,128)S(1)}, u32[]{:S(2)}, u32[]{:S(2)}) collective-permute-start(f32[144,128]{1,0:T(8,128)S(1)} %get-tuple-element.84.refs_0_.own), channel_id=1, source_target_pairs={{0,8},{8,0},{16,24},{24,16},{1,9},{9,1},{17,25},{25,17},{2,10},{10... | collective-permute-start | bytes 221192 | tf_op jit(solution)/shard_map/ppermute | solution.py:731
  22.3 5.9 %collective-permute-start.12 = (f32[80,128]{1,0:T(8,128)S(1)}, f32[80,128]{1,0:T(8,128)S(1)}, u32[]{:S(2)}, u32[]{:S(2)}) collective-permute-start(f32[80,128]{1,0:T(8,128)S(1)} %get-tuple-element.91), channel_id=1, source_target_pairs={{0,16},{8,24},{16,0},{24,8},{1,17},{9,25},{17,1},{25,9},{2,18},{10... | collective-permute-start | bytes 122888 | tf_op jit(solution)/shard_map/ppermute | solution.py:731
  25.2 5.0 %collective-permute-start.11 = (f32[72,128]{1,0:T(8,128)S(1)}, f32[72,128]{1,0:T(8,128)S(1)}, u32[]{:S(2)}, u32[]{:S(2)}) collective-permute-start(f32[72,128]{1,0:T(8,128)S(1)} %get-tuple-element.89), channel_id=1, source_target_pairs={{0,16},{8,24},{16,0},{24,8},{1,17},{9,25},{17,1},{25,9},{2,18},{10... | collective-permute-start | bytes 110600 | tf_op jit(solution)/shard_map/ppermute | solution.py:731
